TPU v7x, 32 devices: a whole 2x2x4 slice. The times are simulated.
32 devices in a mesh: groups: 2 (over x), seq: 16 (over z, y, core).
Axes of the slice: x: 2, y: 2, z: 4, core: 2. Of those that a mesh axis runs over, the one named last changes fastest.
Arguments:
- activations: bfloat16 [4096, 8192], P(('groups', 'seq')), parts along dimension 0, may hold values from -6 to 6
- out_grads: bfloat16 [4096, 28672], P('groups', 'seq'), parts along dimension 0, may hold values from -6 to 6
- proj_in: bfloat16 [8192, 64], replicated, may hold values from -0.0625 to 0.0625
- proj_out: bfloat16 [28672, 64], P('seq'), may hold values from -0.03125 to 0.03125
- queries: bfloat16 [128, 4096], P('seq'), may hold values from -0.09375 to 0.09375
- doc_length: int32 [32], P('groups'), parts along dimension 0, may hold values from 1 to 1024, 2048 in all
- valid_count: int32 [32], P('groups'), parts along dimension 0, may hold values from 1 to 1024
Outputs:
- token_scores: float32 [4096, 128], P(('groups', 'seq')), parts along dimension 0
- doc_scores: float32 [32, 128], P('groups', 'seq'), parts along dimension 0
There are 2 independent parts, one for each index of `groups`. A program takes and returns all parts, laid end to end along the dimension named above; an argument that names none is the same for every part. Nothing has to cross between parts.
Inputs may be any that keep to these rules, and one draw needn't show every extreme that they name: `doc_length`: the lengths sum to 2048; the longest is exactly 1024.
All inputs are finite; a program needn't handle non-finite values.
Results may differ from a plain program's by a relative error of at most 0.0029.
Values may be sent and summed in bfloat16 or wider, within the bound.
No kernel may reach another device: no remote copies, remote signals or barrier semaphores. Data moves between devices by JAX's collectives and lax.ppermute only.
A program may use at most 64 MiB of HBM per device.

v0:
```python
import jax
import jax.numpy as jnp
from jax import lax
from jax.sharding import PartitionSpec as P


def document_mask(glob_rows, doc_length, valid_count):
    ends = jnp.cumsum(doc_length)
    starts = ends - doc_length
    used = jnp.minimum(valid_count, doc_length)
    upper = starts + used
    inside = (glob_rows[None, :] >= starts[:, None]) & (glob_rows[None, :] < upper[:, None])
    return (inside.astype(jnp.float32), used)


def outer_rows(grad_rows, act_rows):
    width = act_rows.shape[1]
    count = act_rows.shape[0]
    return (
        (grad_rows[:, :, None] * act_rows[:, None, :])
        .reshape(count, width * width)
        .astype(jnp.bfloat16)
    )


def against(outer, panel):
    return lax.dot_general(
        outer, panel, (((1,), (1,)), ((), ())), preferred_element_type=jnp.float32
    )


def body(activations, out_grads, proj_in, proj_out, queries, doc_length, valid_count):
    rows = activations.shape[0]
    first = lax.axis_index("seq") * rows
    act_proj = jnp.dot(activations, proj_in, preferred_element_type=jnp.float32)
    grad_proj = lax.psum_scatter(
        jnp.dot(out_grads, proj_out, preferred_element_type=jnp.float32),
        "seq",
        scatter_dimension=0,
        tiled=True,
    )
    local_outer = outer_rows(grad_proj, act_proj)
    own_rows = first + jnp.arange(rows, dtype=jnp.int32)
    local_member, used = document_mask(own_rows, doc_length, valid_count)
    scale = 1.0 / jnp.sqrt(used.astype(jnp.float32))
    token_scores = against(local_outer, lax.all_gather(queries, "seq", axis=0, tiled=True))
    partial_outer = jnp.dot(
        local_member.astype(jnp.bfloat16), local_outer, preferred_element_type=jnp.float32
    )
    doc_outer = lax.psum(partial_outer, "seq")
    raw = lax.dot_general(
        doc_outer,
        queries.astype(jnp.float32),
        (((1,), (1,)), ((), ())),
        precision=lax.Precision.HIGHEST,
    )
    doc_scores = raw * scale[:, None]
    return (token_scores, doc_scores)


def solution(mesh):
    placed = (
        P(("groups", "seq"), None),
        P("groups", "seq"),
        P(),
        P("seq", None),
        P("seq", None),
        P("groups"),
        P("groups"),
    )
    return jax.shard_map(
        body,
        mesh=mesh,
        in_specs=placed,
        out_specs=(P(("groups", "seq"), None), P("groups", "seq")),
        check_vma=False,
    )
```

profile of v0, /device:TPU:0, one launch (start us, length us, event | category | flops | bytes accessed | tf_op | source)
XLA Modules:
  0.0 213.6 jit_solution(8357546238865074203)
XLA Ops:
  7.2 0.0 copy-start
  7.2 0.0 reduce-scatter.2.cloned.1.call-start
  7.2 0.0 copy-start.3
  7.2 0.0 copy-start.4
  7.2 0.0 copy-start.1
  7.3 6.3 %fusion.4 = f32[2048,64]{0,1:T(8,128)} fusion(bf16[2048,1792]{1,0:T(8,128)(2,1)} %param.8, bf16[1792,64]{0,1:T(8,128)(2,1)} %param.10), kind=kOutput, calls=%fused_computation.10 | convolution fusion | flops 469762048 | bytes 8093696 | tf_op jit(solution)/shard_map/dot_general | solution.py:37
  13.6 0.0 reduce-scatter.2.cloned.1.call-update
  13.6 0.0 all-reduce.2.cloned.1.call-start
  13.7 0.0 copy-done.3
  13.7 0.1 copy.12
  13.8 0.1 reduce
  13.9 0.0 copy-done.4
  14.0 0.0 copy-done
  14.0 0.0 copy-done.1
  14.0 0.8 fusion.5
  14.8 0.0 copy-start.2
  14.8 57.4 %reduce-scatter.2.cloned.1.call-done = f32[128,64]{0,1:T(8,128)} async-done(((f32[2048,64]{0,1:T(8,128)}), f32[128,64]{0,1:T(8,128)}) %reduce-scatter.2.cloned.1.call-update) | async-done | bytes 32784 | tf_op jit(solution)/shard_map/reduce_scatter | solution.py:36
  72.3 1.0 multiply_convert_fusion
  73.3 1.2 fusion
  74.5 0.0 all-reduce.2.cloned.1.call-update
  74.5 0.0 all-gather.2.cloned.1.call-start
  74.5 0.7 all-gather.2.cloned.1.call-update
  75.2 88.6 %all-reduce.2.cloned.1.call-done = f32[16,4096]{1,0:T(8,128)} async-done(((f32[16,4096]{1,0:T(8,128)}), f32[16,4096]{1,0:T(8,128)}) %all-reduce.2.cloned.1.call-update) | async-done | bytes 262160 | tf_op jit(solution)/shard_map/psum | solution.py:50
  163.9 0.0 copy-done.2
  163.9 1.8 convolution_multiply_fusion
  165.7 39.1 %all-gather.2.cloned.1.call-done = bf16[128,4096]{1,0:T(8,128)(2,1)} async-done(((bf16[8,4096]{1,0:T(8,128)(2,1)}), bf16[128,4096]{1,0:T(8,128)(2,1)}) %all-gather.2.cloned.1.call-update) | async-done | bytes 1048592 | tf_op jit(solution)/shard_map/all_gather | solution.py:46
  204.7 2.3 %fusion.6 = f32[128,128]{1,0:T(8,128)} fusion(bf16[128,4096]{0,1:T(8,128)(2,1)S(1)} %bitcast.12, bf16[128,4096]{1,0:T(8,128)(2,1)} %all-gather.2.cloned.1.call-done), kind=kOutput, calls=%fused_computation.12 | convolution fusion | flops 134217728 | bytes 2162688 | tf_op jit(solution)/shard_map/dot_general | solution.py:27
  (4 shorter events, 0.1 us)
Async XLA Ops:
  7.2 6.8 %copy-start = (bf16[128,8192]{1,0:T(8,128)(2,1)S(1)}, bf16[128,8192]{1,0:T(8,128)(2,1)}, u32[]{:S(2)}) copy-start(bf16[128,8192]{1,0:T(8,128)(2,1)} %param.7) | copy-start | bytes 6291460
  7.2 65.1 %reduce-scatter.2.cloned.1.call-start = ((), (), s32[]{:S(2)}) async-start(), calls=%async_computation.1 | async-start | bytes 557056 | tf_op jit(solution)/shard_map/reduce_scatter | solution.py:36
  7.2 6.5 %copy-start.3 = (s32[16]{0:T(128)S(1)}, s32[16]{0:T(128)}, u32[]{:S(2)}) copy-start(s32[16]{0:T(128)} %param.12) | copy-start | bytes 196
  7.2 6.7 %copy-start.4 = (s32[16]{0:T(128)S(1)}, s32[16]{0:T(128)}, u32[]{:S(2)}) copy-start(s32[16]{0:T(128)} %param.13) | copy-start | bytes 196
  7.2 6.7 %copy-start.1 = (bf16[8192,64]{0,1:T(8,128)(2,1)S(1)}, bf16[8192,64]{0,1:T(8,128)(2,1)}, u32[]{:S(2)}) copy-start(bf16[8192,64]{0,1:T(8,128)(2,1)} %param.9) | copy-start | bytes 3145732
  13.6 150.3 %all-reduce.2.cloned.1.call-start = ((), (), s32[]{:S(2)}) async-start(), calls=%async_computation.3 | async-start | bytes 524288 | tf_op jit(solution)/shard_map/psum | solution.py:50
  14.8 149.1 %copy-start.2 = (bf16[8,4096]{1,0:T(8,128)(2,1)S(1)}, bf16[8,4096]{1,0:T(8,128)(2,1)}, u32[]{:S(2)}) copy-start(bf16[8,4096]{1,0:T(8,128)(2,1)} %param.11) | copy-start | bytes 196612
  74.5 130.3 %all-gather.2.cloned.1.call-start = ((), (), s32[]{:S(2)}) async-start(), calls=%async_computation.2 | async-start | bytes 1114112 | tf_op jit(solution)/shard_map/all_gather | solution.py:46
Sparse Core Ops, SparseCore 0:
  13.7 58.4 reduce-scatter.1
  76.0 87.7 all-reduce.1
  166.3 38.4 all-gather.1
where the time goes:
time: 214 us
  waiting for transfers between devices  186 us (87%)
  between operations  13.9 us (6%)
  matrix products  12.5 us (6%)
    psum x1, waiting for transfers between devices, body(): doc_outer = lax.psum(partial_outer, 'seq')  88.6 us
    reduce_scatter x1, waiting for transfers between devices, body(): lax.psum_scatter(jnp.dot(out_grads, proj_out, preferred_element_type=jnp....  57.4 us
    all_gather x1, waiting for transfers between devices, body(): lax.all_gather(queries, 'seq', axis=0, tiled=True)  39.1 us
    dot_general x1, matrix products, body(): jnp.dot(out_grads, proj_out, preferred_element_type=jnp.float32)  6.34 us
  transfers between devices with their start and end apart: 3, of which 3 were waited for; matrix products, arithmetic and copies ran while one was open for 1% of the time, Pallas kernels for 0%

commit v1 on v0

v1 whole, which is shorter than its diff:
```python
import jax
import jax.numpy as jnp
from jax import lax
from jax.sharding import PartitionSpec as P


def document_mask(glob_rows, doc_length, valid_count):
    ends = jnp.cumsum(doc_length)
    starts = ends - doc_length
    used = jnp.minimum(valid_count, doc_length)
    upper = starts + used
    inside = (glob_rows[None, :] >= starts[:, None]) & (glob_rows[None, :] < upper[:, None])
    return (inside.astype(jnp.float32), used)


def gather_xor(block, size, order):
    place = [0]
    for bit in order:
        got = lax.ppermute(block, "seq", [(i, i ^ bit) for i in range(size)])
        block = jnp.concatenate([block, got], axis=0)
        place = place + [p ^ bit for p in place]
    return block, place


def link_order(size):
    bits = []
    bit = 2
    while bit < size:
        bits.append(bit)
        bit *= 2
    return bits[1:] + bits[:1] + [1]


def body(size, activations, out_grads, proj_in, proj_out, queries, doc_length, valid_count):
    rows = activations.shape[0]
    width = proj_in.shape[1]
    own_q = queries.shape[0]
    me = lax.axis_index("seq")
    panel, place = gather_xor(queries, size, link_order(size))

    grad_part = lax.dot_general(
        proj_out, out_grads, (((0,), (1,)), ((), ())), preferred_element_type=jnp.float32
    )
    pieces = grad_part.reshape(width, size, rows).transpose(1, 0, 2)
    got = lax.all_to_all(pieces, "seq", 0, 0, tiled=True)
    act_proj = lax.dot_general(
        proj_in, activations, (((0,), (1,)), ((), ())), preferred_element_type=jnp.float32
    )
    grad_proj = got.sum(axis=0)
    outer = (
        (grad_proj[:, None, :] * act_proj[None, :, :])
        .reshape(width * width, rows)
        .astype(jnp.bfloat16)
    )
    scores = jnp.dot(panel, outer, preferred_element_type=jnp.float32)
    blocks = scores.reshape(size, own_q, rows)
    inverse = [0] * size
    for k, p in enumerate(place):
        inverse[p] = k
    turn = jnp.asarray(inverse, jnp.int32)[jnp.arange(size, dtype=jnp.int32) ^ me]
    blocks = blocks[turn]
    token_scores = blocks.reshape(size * own_q, rows).T
    own_rows = me * rows + jnp.arange(rows, dtype=jnp.int32)
    member, used = document_mask(own_rows, doc_length, valid_count)
    scale = 1.0 / jnp.sqrt(used.astype(jnp.float32))
    partial = lax.dot_general(
        blocks, member, (((2,), (1,)), ((), ())), precision=lax.Precision.HIGHEST
    )
    doc_raw = lax.all_to_all(partial, "seq", 0, 0, tiled=True).sum(axis=0)
    doc_scores = (doc_raw * scale[None, :]).T
    return (token_scores, doc_scores)


def solution(mesh):
    size = mesh.shape["seq"]
    placed = (
        P(("groups", "seq"), None),
        P("groups", "seq"),
        P(),
        P("seq", None),
        P("seq", None),
        P("groups"),
        P("groups"),
    )

    def run(*args):
        return body(size, *args)

    return jax.shard_map(
        run,
        mesh=mesh,
        in_specs=placed,
        out_specs=(P(("groups", "seq"), None), P("groups", "seq")),
        check_vma=False,
    )
```

time: 214 us -> 63.7 us (0.30)
  waiting for transfers between devices: 186 us -> 26 us
  starting transfers between devices: 0.12 us -> 16.3 us
  between operations: 13.9 us -> 0.85 us
  local copies, waits for them, and re-layouts: 0.11 us -> 8.73 us
  matrix products: 12.5 us -> 9.46 us
    psum x1 -> x0, waiting for transfers between devices: 88.6 us -> none  [body(): doc_outer = lax.psum(partial_outer, 'seq')]
    reduce_scatter x1 -> x0, waiting for transfers between devices: 57.4 us -> none  [body(): lax.psum_scatter(jnp.dot(out_grads, proj_out, preferred_element_type=jnp....]
    all_gather x1 -> x0, waiting for transfers between devices: 39.1 us -> none  [body(): lax.all_gather(queries, 'seq', axis=0, tiled=True)]
    ppermute x0 -> x4, waiting for transfers between devices: none -> 20.4 us  [gather_xor(): got = lax.ppermute(block, 'seq', [(i, i ^ bit) for i in range(size)])]
    all_to_all x0 -> x2, starting transfers between devices: none -> 8.74 us  [the longest x1 4.93 us: body(): got = lax.all_to_all(pieces, 'seq', 0, 0, tiled=True)]
    ppermute x0 -> x4, starting transfers between devices: none -> 7.58 us  [gather_xor(): got = lax.ppermute(block, 'seq', [(i, i ^ bit) for i in range(size)])]
    all_to_all x0 -> x2, waiting for transfers between devices: none -> 5.67 us  [the longest x1 5.66 us: body(): doc_raw = lax.all_to_all(partial, 'seq', 0, 0, tiled=True).sum(axis=0)]
    unnamed x10 -> x16, local copies, waits for them, and re-layouts: 0.03 us -> 3.42 us
  transfers between devices with their start and end apart: 3 -> 6, of which waited for: 3 -> 4; matrix products, arithmetic and copies ran while one was open for 1% -> 21% of each run, Pallas kernels for 0% -> 0%
where the time goes in v1:
time: 63.7 us; the launch traced here: 63.2 us
  waiting for transfers between devices  26 us (41%)
  starting transfers between devices  16.3 us (26%)
  matrix products  9.46 us (15%)
  local copies, waits for them, and re-layouts  8.73 us (14%)
  other arithmetic  1.87 us (3%)
  between operations  0.85 us (1%)
    ppermute x4, waiting for transfers between devices, gather_xor(): got = lax.ppermute(block, 'seq', [(i, i ^ bit) for i in range(size)])  20.4 us
    ppermute x4, starting transfers between devices, gather_xor(): got = lax.ppermute(block, 'seq', [(i, i ^ bit) for i in range(size)])  7.58 us
    all_to_all x1, waiting for transfers between devices, body(): doc_raw = lax.all_to_all(partial, 'seq', 0, 0, tiled=True).sum(axis=0)  5.66 us
    dot_general x1, matrix products, body(): lax.dot_general(proj_out, out_grads, (((0,), (1,)), ((), ())), preferred_...  5.52 us
    all_to_all x1, starting transfers between devices, body(): got = lax.all_to_all(pieces, 'seq', 0, 0, tiled=True)  4.93 us
    all_to_all x1, starting transfers between devices, body(): doc_raw = lax.all_to_all(partial, 'seq', 0, 0, tiled=True).sum(axis=0)  3.81 us
    unnamed x16, local copies, waits for them, and re-layouts  3.42 us
    dot_general x1, matrix products, body(): lax.dot_general(proj_in, activations, (((0,), (1,)), ((), ())), preferred...  2.07 us
  transfers between devices with their start and end apart: 6, of which 4 were waited for; matrix products, arithmetic and copies ran while one was open for 21% of the time, Pallas kernels for 0%

profile of v1, /device:TPU:0, one launch (start us, length us, event | category | flops | bytes accessed | tf_op | source)
XLA Modules:
  0.0 63.2 jit_solution(2976851293228482734)
XLA Ops:
  0.6 0.0 copy-start
  0.6 3.1 %collective-permute-start = (bf16[8,4096]{1,0:T(8,128)(2,1)}, bf16[8,4096]{1,0:T(8,128)(2,1)S(1)}, u32[]{:S(2)}, u32[]{:S(2)}) collective-permute-start(bf16[8,4096]{1,0:T(8,128)(2,1)} %param.12), channel_id=1, source_target_pairs={{0,4},{1,5},{2,6},{3,7},{4,0},{5,1},{6,2},{7,3},{8,12},{9,13},{10,... | collective-permute-start | bytes 196616 | tf_op jit(solution)/shard_map/ppermute | solution.py:19
  3.7 5.5 %convolution_bitcast_fusion = f32[8,16,8,128]{3,2,1,0:T(8,128)S(1)} fusion(bf16[1792,64]{0,1:T(8,128)(2,1)} %param.11, bf16[2048,1792]{1,0:T(8,128)(2,1)} %param.9), kind=kOutput, calls=%fused_computation.3 | convolution fusion | flops 469762048 | bytes 8093696 | tf_op jit(solution)/shard_map/dot_general | solution.py:41
  9.3 0.0 copy-start.2
  9.3 0.0 copy-start.1
  9.3 0.0 copy-start.3
  9.3 0.9 %copy.19 = f32[8,16,8,128]{3,2,0,1:T(8,128)} copy(f32[8,16,8,128]{3,2,1,0:T(8,128)S(1)} %convolution_bitcast_fusion) | data formatting | bytes 1048576 | tf_op jit(solution)/shard_map/reshape | solution.py:44
  10.2 4.9 %all-to-all-start = ((f32[16,64,128]{2,1,0:T(8,128)}), f32[16,64,128]{2,1,0:T(8,128)S(1)}, u32[]{:S(2)}, u32[]{:S(2)}) async-start(f32[16,64,128]{2,1,0:T(8,128)} %bitcast.33), calls=%async_computation | async-start | bytes 1048576 | tf_op jit(solution)/shard_map/all_to_all | solution.py:45
  15.1 0.0 copy-done.2
  15.1 0.0 copy-start.4
  15.1 0.6 constant_dynamic-update-slice_fusion.4
  15.8 0.0 copy-done.1
  15.8 0.7 %gather_fusion = s32[16]{0:T(128)S(1)} fusion(s32[16]{0:T(128)S(1)} %copy-done.1, s32[1024]{0:T(1024)S(1)} %pad_clamp_fusion.1), kind=kCustom, calls=%fused_computation | custom fusion | bytes 192 | tf_op jit(solution)/shard_map/gather | solution.py:60
  16.5 0.0 copy-done.3
  16.5 0.1 copy.16
  16.6 0.1 reduce
  16.7 0.0 copy-done
  16.7 2.1 %fusion.12 = f32[64,128]{1,0:T(8,128)S(1)} fusion(bf16[8192,64]{0,1:T(8,128)(2,1)} %param.10, bf16[128,8192]{1,0:T(8,128)(2,1)S(1)} %copy-done), kind=kOutput, calls=%fused_computation.33 | convolution fusion | flops 134217728 | bytes 3178496 | tf_op jit(solution)/shard_map/dot_general | solution.py:46
  18.8 0.0 copy-done.4
  18.8 0.0 collective-permute-done
  18.8 2.9 %collective-permute-start.1 = (bf16[16,4096]{1,0:T(8,128)(2,1)S(1)}, bf16[16,4096]{1,0:T(8,128)(2,1)S(1)}, u32[]{:S(2)}, u32[]{:S(2)}) collective-permute-start(bf16[16,4096]{1,0:T(8,128)(2,1)S(1)} %pad_maximum_fusion.2), channel_id=1, source_target_pairs={{0,8},{1,9},{2,10},{3,11},{4,12},{5,13},{6,14},{7,15},{8,0},{9,1},... | collective-permute-start | bytes 393224 | tf_op jit(solution)/shard_map/ppermute | solution.py:19
  21.7 0.6 constant_dynamic-update-slice_fusion.3
  22.4 13.6 %collective-permute-done.1 = bf16[16,4096]{1,0:T(8,128)(2,1)S(1)} collective-permute-done((bf16[16,4096]{1,0:T(8,128)(2,1)S(1)}, bf16[16,4096]{1,0:T(8,128)(2,1)S(1)}, u32[]{:S(2)}, u32[]{:S(2)}) %collective-permute-start.1) | collective-permute-done | bytes 131104 | tf_op jit(solution)/shard_map/ppermute | solution.py:19
  36.0 1.5 %collective-permute-start.2 = (bf16[32,4096]{1,0:T(8,128)(2,1)S(1)}, bf16[32,4096]{1,0:T(8,128)(2,1)S(1)}, u32[]{:S(2)}, u32[]{:S(2)}) collective-permute-start(bf16[32,4096]{1,0:T(8,128)(2,1)S(1)} %pad_maximum_fusion.1), channel_id=1, source_target_pairs={{0,2},{1,3},{2,0},{3,1},{4,6},{5,7},{6,4},{7,5},{8,10},{9,11},{10,... | collective-permute-start | bytes 786440 | tf_op jit(solution)/shard_map/ppermute | solution.py:19
  37.6 0.7 %constant_dynamic-update-slice_fusion.2 = bf16[128,4096]{1,0:T(8,128)(2,1)} fusion(bf16[128,4096]{1,0:T(8,128)(2,1)} %constant_dynamic-update-slice_fusion.3, bf16[16,4096]{1,0:T(8,128)(2,1)S(1)} %collective-permute-done.1), kind=kLoop, calls=%fused_computation.12 | loop fusion | bytes 262144
  38.2 5.7 %collective-permute-done.2 = bf16[32,4096]{1,0:T(8,128)(2,1)S(1)} collective-permute-done((bf16[32,4096]{1,0:T(8,128)(2,1)S(1)}, bf16[32,4096]{1,0:T(8,128)(2,1)S(1)}, u32[]{:S(2)}, u32[]{:S(2)}) %collective-permute-start.2) | collective-permute-done | bytes 262176 | tf_op jit(solution)/shard_map/ppermute | solution.py:19
  44.0 0.1 collective-permute-start.3
  44.1 0.7 %constant_dynamic-update-slice_fusion.1 = bf16[128,4096]{1,0:T(8,128)(2,1)} fusion(bf16[128,4096]{1,0:T(8,128)(2,1)} %constant_dynamic-update-slice_fusion.2, bf16[32,4096]{1,0:T(8,128)(2,1)S(1)} %collective-permute-done.2), kind=kLoop, calls=%fused_computation.11 | loop fusion | bytes 524288
  44.8 0.0 all-to-all-done
  44.8 0.3 multiply_convert_fusion
  45.1 1.0 %collective-permute-done.3 = bf16[64,4096]{1,0:T(8,128)(2,1)} collective-permute-done((bf16[64,4096]{1,0:T(8,128)(2,1)S(1)}, bf16[64,4096]{1,0:T(8,128)(2,1)}, u32[]{:S(2)}, u32[]{:S(2)}) %collective-permute-start.3) | collective-permute-done | bytes 524320 | tf_op jit(solution)/shard_map/ppermute | solution.py:19
  46.1 1.9 %constant_dynamic-update-slice_fusion = bf16[128,4096]{1,0:T(8,128)(2,1)} fusion(bf16[128,4096]{1,0:T(8,128)(2,1)} %constant_dynamic-update-slice_fusion.1, bf16[64,4096]{1,0:T(8,128)(2,1)} %collective-permute-done.3), kind=kLoop, calls=%fused_computation.10 | loop fusion | bytes 1048576 | tf_op jit(solution)/shard_map/concatenate | solution.py:20
  48.0 1.6 %fusion = f32[16,8,128]{2,1,0:T(8,128)S(1)} fusion(bf16[4096,128,1]{1,0,2:T(8,128)(2,1)S(1)} %bitcast.34, bf16[128,4096]{1,0:T(8,128)(2,1)} %constant_dynamic-update-slice_fusion), kind=kOutput, calls=%fused_computation.4 | convolution fusion | flops 134217728 | bytes 2162688 | tf_op jit(solution)/shard_map/dot_general | solution.py:55
  49.6 0.6 gather_fusion.1
  50.2 0.2 fusion.2
  50.4 0.7 %reshape.112 = f32[16,1,128]{2,1,0:T(1,128)} reshape(f32[16,8,16]{2,1,0:T(8,128)S(1)} %fusion.2) | data formatting | bytes 16384
  51.1 3.8 %all-to-all-start.1 = ((f32[16,1,128]{2,1,0:T(1,128)}), f32[16,1,128]{2,1,0:T(1,128)S(1)}, u32[]{:S(2)}, u32[]{:S(2)}) async-start(f32[16,1,128]{2,1,0:T(1,128)} %reshape.112), calls=%async_computation.1 | async-start | bytes 16384 | tf_op jit(solution)/shard_map/all_to_all | solution.py:69
  55.0 0.7 %copy.15 = f32[128,128]{0,1:T(8,128)} copy(f32[128,128]{1,0:T(8,128)S(1)} %bitcast.35) | data formatting | bytes 131072 | tf_op jit(solution)/shard_map/reshape | solution.py:62
  55.7 5.7 %all-to-all-done.1 = f32[16,1,128]{2,1,0:T(1,128)S(1)} async-done(((f32[16,1,128]{2,1,0:T(1,128)}), f32[16,1,128]{2,1,0:T(1,128)S(1)}, u32[]{:S(2)}, u32[]{:S(2)}) %all-to-all-start.1) | async-done | bytes 8224 | tf_op jit(solution)/shard_map/all_to_all | solution.py:69
  61.4 0.5 broadcast.76
  61.9 0.7 %reduce.1 = f32[16,128]{1,0:T(8,128)S(1)} reduce(f32[16,1,128]{2,1,0:T(1,128)S(1)} %all-to-all-done.1, f32[]{:T(128)} %broadcast.76), dimensions={1}, to_apply=%all_to_all.7.reduce_sub_computation | reduce | bytes 16388 | tf_op jit(solution)/shard_map/all_to_all | solution.py:69
  62.5 0.1 reshape.113
  62.6 0.6 multiply_bitcast_fusion
  (13 shorter events, 0.2 us)
Async XLA Ops:
  0.6 16.1 %copy-start = (bf16[128,8192]{1,0:T(8,128)(2,1)S(1)}, bf16[128,8192]{1,0:T(8,128)(2,1)}, u32[]{:S(2)}) copy-start(bf16[128,8192]{1,0:T(8,128)(2,1)} %param.8) | copy-start | bytes 6291460
  0.6 18.2 %collective-permute-start = (bf16[8,4096]{1,0:T(8,128)(2,1)}, bf16[8,4096]{1,0:T(8,128)(2,1)S(1)}, u32[]{:S(2)}, u32[]{:S(2)}) collective-permute-start(bf16[8,4096]{1,0:T(8,128)(2,1)} %param.12), channel_id=1, source_target_pairs={{0,4},{1,5},{2,6},{3,7},{4,0},{5,1},{6,2},{7,3},{8,12},{9,13},{10,... | collective-permute-start | bytes 196616 | tf_op jit(solution)/shard_map/ppermute | solution.py:19
  9.3 5.8 %copy-start.2 = (bf16[8,4096]{1,0:T(8,128)(2,1)S(1)}, bf16[8,4096]{1,0:T(8,128)(2,1)}, u32[]{:S(2)}) copy-start(bf16[8,4096]{1,0:T(8,128)(2,1)} %param.12) | copy-start | bytes 196612
  9.3 6.5 %copy-start.1 = (s32[16]{0:T(128)S(1)}, s32[16]{0:T(128)}, u32[]{:S(2)}) copy-start(s32[16]{0:T(128)} %constant.18.clone) | copy-start | bytes 196
  9.3 7.2 %copy-start.3 = (s32[16]{0:T(128)S(1)}, s32[16]{0:T(128)}, u32[]{:S(2)}) copy-start(s32[16]{0:T(128)} %param.13) | copy-start | bytes 196
  10.2 34.6 %all-to-all-start = ((f32[16,64,128]{2,1,0:T(8,128)}), f32[16,64,128]{2,1,0:T(8,128)S(1)}, u32[]{:S(2)}, u32[]{:S(2)}) async-start(f32[16,64,128]{2,1,0:T(8,128)} %bitcast.33), calls=%async_computation | async-start | bytes 1048576 | tf_op jit(solution)/shard_map/all_to_all | solution.py:45
  15.1 3.7 %copy-start.4 = (s32[16]{0:T(128)S(1)}, s32[16]{0:T(128)}, u32[]{:S(2)}) copy-start(s32[16]{0:T(128)} %param.14) | copy-start | bytes 196
  18.8 17.2 %collective-permute-start.1 = (bf16[16,4096]{1,0:T(8,128)(2,1)S(1)}, bf16[16,4096]{1,0:T(8,128)(2,1)S(1)}, u32[]{:S(2)}, u32[]{:S(2)}) collective-permute-start(bf16[16,4096]{1,0:T(8,128)(2,1)S(1)} %pad_maximum_fusion.2), channel_id=1, source_target_pairs={{0,8},{1,9},{2,10},{3,11},{4,12},{5,13},{6,14},{7,15},{8,0},{9,1},... | collective-permute-start | bytes 393224 | tf_op jit(solution)/shard_map/ppermute | solution.py:19
  36.0 7.9 %collective-permute-start.2 = (bf16[32,4096]{1,0:T(8,128)(2,1)S(1)}, bf16[32,4096]{1,0:T(8,128)(2,1)S(1)}, u32[]{:S(2)}, u32[]{:S(2)}) collective-permute-start(bf16[32,4096]{1,0:T(8,128)(2,1)S(1)} %pad_maximum_fusion.1), channel_id=1, source_target_pairs={{0,2},{1,3},{2,0},{3,1},{4,6},{5,7},{6,4},{7,5},{8,10},{9,11},{10,... | collective-permute-start | bytes 786440 | tf_op jit(solution)/shard_map/ppermute | solution.py:19
  44.0 2.1 %collective-permute-start.3 = (bf16[64,4096]{1,0:T(8,128)(2,1)S(1)}, bf16[64,4096]{1,0:T(8,128)(2,1)}, u32[]{:S(2)}, u32[]{:S(2)}) collective-permute-start(bf16[64,4096]{1,0:T(8,128)(2,1)S(1)} %pad_maximum_fusion), channel_id=1, source_target_pairs={{0,1},{1,0},{2,3},{3,2},{4,5},{5,4},{6,7},{7,6},{8,9},{9,8},{10,11... | collective-permute-start | bytes 1572872 | tf_op jit(solution)/shard_map/ppermute | solution.py:19
  51.1 10.2 %all-to-all-start.1 = ((f32[16,1,128]{2,1,0:T(1,128)}), f32[16,1,128]{2,1,0:T(1,128)S(1)}, u32[]{:S(2)}, u32[]{:S(2)}) async-start(f32[16,1,128]{2,1,0:T(1,128)} %reshape.112), calls=%async_computation.1 | async-start | bytes 16384 | tf_op jit(solution)/shard_map/all_to_all | solution.py:69

commit v2 on v0

v2 whole, which is shorter than its diff:
```python
import functools

import jax
import jax.numpy as jnp
from jax import lax
from jax.experimental import pallas as pl
from jax.experimental.pallas import tpu as pltpu
from jax.sharding import PartitionSpec as P

MIB = 1 << 20


def bit_groups(size):
    bits = [1 << k for k in range(size.bit_length() - 1)]
    groups = [bits[:1]]
    rest = bits[1:]
    if len(rest) % 2:
        groups.append(rest[:1])
        rest = rest[1:]
    while rest:
        groups.append(rest[:2])
        rest = rest[2:]
    return [g for g in groups if g]


def offset_of(part, bits):
    last = len(bits) - 1
    return sum(bit for k, bit in enumerate(bits) if (part >> (last - k)) & 1)


def reverse_bits(position, size):
    count = size.bit_length() - 1
    total = 0
    for k in range(count):
        total = total + (((position >> k) & 1) << (count - 1 - k))
    return total


def swap(value, offset, size):
    return lax.ppermute(value, "seq", [(i, i ^ offset) for i in range(size)])


def stage_parts(current, bits, size):
    count = 1 << len(bits)
    depth = current.shape[0] // count
    parts = [current[:depth]]
    for k in range(1, count):
        parts.append(swap(current[k * depth : (k + 1) * depth], offset_of(k, bits), size))
    return parts


def grad_kernel(per_step, me_ref, proj_ref, *refs):
    del me_ref
    out_ref = refs[per_step]
    for k in range(per_step):
        rows = lax.dot_general(
            refs[k][...],
            proj_ref[...],
            (((1,), (1,)), ((), ())),
            preferred_element_type=jnp.float32,
        )
        out_ref[k] = rows.T


def grad_blocks(me, proj, out_grads, rows, size, first, count):
    width, depth = proj.shape
    per_step = min(2, count)

    def place(k, step, me_ref):
        return (reverse_bits(first + step * per_step + k, size) ^ me_ref[0], 0)

    return pl.pallas_call(
        functools.partial(grad_kernel, per_step),
        grid_spec=pltpu.PrefetchScalarGridSpec(
            num_scalar_prefetch=1,
            grid=(count // per_step,),
            in_specs=[pl.BlockSpec((width, depth), lambda step, me_ref: (0, 0))]
            + [pl.BlockSpec((rows, depth), functools.partial(place, k)) for k in range(per_step)],
            out_specs=pl.BlockSpec((per_step, width, rows), lambda step, me_ref: (step, 0, 0)),
        ),
        out_shape=jax.ShapeDtypeStruct((count, width, rows), jnp.float32),
        compiler_params=pltpu.CompilerParams(vmem_limit_bytes=52 * MIB),
        cost_estimate=pl.CostEstimate(
            flops=2 * count * rows * depth * width,
            bytes_accessed=2 * count * rows * depth,
            transcendentals=0,
        ),
    )(me, proj, *([out_grads] * per_step))


def score_kernel(
    size,
    halves,
    sums,
    panels,
    place,
    me_ref,
    group_ref,
    length_ref,
    valid_ref,
    act_ref,
    *refs,
):
    grad_refs = refs[:sums]
    panel_refs = refs[sums : sums + panels]
    token_ref, doc_ref, outer_ref, turned_ref = refs[sums + panels :]
    me = me_ref[0]
    act = act_ref[...]
    width, rows = act.shape
    grad = grad_refs[0][0]
    for ref in grad_refs[1:]:
        grad = grad + ref[0]
    for i in range(width):
        outer_ref[i * width : (i + 1) * width] = (act * grad[i : i + 1]).astype(jnp.bfloat16)
    depth = width * width // halves
    scores = None
    for h in range(halves):
        start = (group_ref[0] ^ h) * depth if halves > 1 else 0
        part = jnp.concatenate([panel_refs[h][...], panel_refs[halves + h][...]], axis=0)
        term = jnp.dot(
            part,
            outer_ref[pl.ds(pl.multiple_of(start, depth), depth)],
            preferred_element_type=jnp.float32,
        )
        scores = term if scores is None else scores + term
    own_q = scores.shape[0] // size
    for k, p in enumerate(place):
        spot = pl.multiple_of((me ^ p) * own_q, own_q)
        turned_ref[pl.ds(spot, own_q)] = scores[k * own_q : (k + 1) * own_q]
    turned = turned_ref[...]
    token_ref[...] = turned.T

    docs = length_ref.shape[0]
    doc_of = lax.broadcasted_iota(jnp.int32, (docs, rows), 0)
    lower = jnp.zeros((docs, rows), jnp.int32)
    used = jnp.zeros((docs, rows), jnp.int32)
    start = jnp.int32(0)
    for d in range(docs):
        lower = jnp.where(doc_of == d, start, lower)
        used = jnp.where(doc_of == d, jnp.minimum(valid_ref[d], length_ref[d]), used)
        start = start + length_ref[d]
    token = me * rows + lax.broadcasted_iota(jnp.int32, (docs, rows), 1)
    inside = (token >= lower) & (token < lower + used)
    member = jnp.where(inside, 1.0 / jnp.sqrt(used.astype(jnp.float32)), 0.0)
    partial = lax.dot_general(
        turned,
        member,
        (((1,), (1,)), ((), ())),
        precision=lax.Precision.HIGHEST,
        preferred_element_type=jnp.float32,
    )
    turned_ref[:, :docs] = partial
    for p in range(size):
        spot = pl.multiple_of((me ^ reverse_bits(p, size)) * own_q, own_q)
        doc_ref[p] = turned_ref[pl.ds(spot, own_q), :docs]


def score(me, group, lengths, valid, act, grads, panels, place, size, own_q):
    width, rows = act.shape
    docs = lengths.shape[0]
    halves = len(panels) // 2
    smem = pl.BlockSpec(memory_space=pltpu.SMEM)
    vmem = pl.BlockSpec(memory_space=pltpu.VMEM)
    count = size * own_q
    return pl.pallas_call(
        functools.partial(score_kernel, size, halves, len(grads), len(panels), place),
        in_specs=[smem] * 4 + [vmem] * (1 + len(grads) + len(panels)),
        out_specs=(vmem, vmem),
        out_shape=(
            jax.ShapeDtypeStruct((rows, count), jnp.float32),
            jax.ShapeDtypeStruct((size, own_q, docs), jnp.float32),
        ),
        scratch_shapes=[
            pltpu.VMEM((width * width, rows), jnp.bfloat16),
            pltpu.VMEM((count, rows), jnp.float32),
        ],
        compiler_params=pltpu.CompilerParams(vmem_limit_bytes=32 * MIB),
        cost_estimate=pl.CostEstimate(
            flops=2 * rows * width * width * count,
            bytes_accessed=2 * count * width * width,
            transcendentals=0,
        ),
    )(me, group, lengths, valid, act, *grads, *panels)


def gather_queries(queries, size, groups, group):
    if groups == 2:
        half = queries.shape[1] // 2
        panel = lax.dynamic_slice(queries, (0, group * half), (queries.shape[0], half))
    else:
        panel = queries
    place = [0]
    stages = bit_groups(size)
    for bits in stages[:0:-1]:
        offsets = [offset_of(k, bits) for k in range(1, 1 << len(bits))]
        panel = jnp.concatenate([panel] + [swap(panel, o, size) for o in offsets], axis=0)
        place = [p ^ o for o in [0] + offsets for p in place]
    panels = [panel]
    if groups == 2:
        panels.append(lax.ppermute(panel, "groups", [(0, 1), (1, 0)]))
    panels = panels + [swap(part, 1, size) for part in panels]
    return panels, tuple(place + [p ^ 1 for p in place])


def body(size, groups, activations, out_grads, proj_in, proj_out, queries, doc_length, valid_count):
    rows = activations.shape[0]
    me = lax.axis_index("seq").astype(jnp.int32)
    group = lax.axis_index("groups").astype(jnp.int32)
    panels, place = gather_queries(queries, size, groups, group)

    proj = proj_out.T
    half = size // 2
    stages = bit_groups(size)
    theirs = grad_blocks(me[None], proj, out_grads, rows, size, half, half)
    from_core = swap(theirs, 1, size)
    current = grad_blocks(me[None], proj, out_grads, rows, size, 0, half) + from_core
    for bits in stages[1:-1]:
        parts = stage_parts(current, bits, size)
        current = functools.reduce(jnp.add, parts)
    grads = stage_parts(current, stages[-1], size)

    act = lax.dot_general(
        proj_in, activations, (((0,), (1,)), ((), ())), preferred_element_type=jnp.float32
    )
    token_scores, doc = score(
        me[None],
        group[None],
        doc_length,
        valid_count,
        act,
        grads,
        panels,
        place,
        size,
        queries.shape[0],
    )
    bits = [b for g in stages for b in g]
    for k in range(0, len(bits), 2):
        doc = functools.reduce(jnp.add, stage_parts(doc, bits[k : k + 2], size))
    return (token_scores, doc[0].T)


def solution(mesh):
    size = mesh.shape["seq"]
    groups = mesh.shape["groups"]
    placed = (
        P(("groups", "seq"), None),
        P("groups", "seq"),
        P(),
        P("seq", None),
        P("seq", None),
        P("groups"),
        P("groups"),
    )
    return jax.shard_map(
        functools.partial(body, size, groups),
        mesh=mesh,
        in_specs=placed,
        out_specs=(P(("groups", "seq"), None), P("groups", "seq")),
        check_vma=False,
    )
```

time: 214 us -> 48.7 us (0.23)
  waiting for transfers between devices: 186 us -> 14 us
  starting transfers between devices: 0.12 us -> 20.8 us
  between operations: 13.9 us -> 0.83 us
  matrix products: 12.5 us -> 0.89 us
  Pallas kernels: 0 us -> 9.29 us
    psum x1 -> x0, waiting for transfers between devices: 88.6 us -> none  [body(): doc_outer = lax.psum(partial_outer, 'seq')]
    reduce_scatter x1 -> x0, waiting for transfers between devices: 57.4 us -> none  [body(): lax.psum_scatter(jnp.dot(out_grads, proj_out, preferred_element_type=jnp....]
    all_gather x1 -> x0, waiting for transfers between devices: 39.1 us -> none  [body(): lax.all_gather(queries, 'seq', axis=0, tiled=True)]
    ppermute x0 -> x18, starting transfers between devices: none -> 20.8 us  [the longest x17 19 us: swap(): return lax.ppermute(value, 'seq', [(i, i ^ offset) for i in range(size)])]
    ppermute x0 -> x18, waiting for transfers between devices: none -> 14 us  [the longest x17 12.2 us: swap(): return lax.ppermute(value, 'seq', [(i, i ^ offset) for i in range(size)])]
    dot_general x5 -> x1, matrix products: 12.5 us -> 0.89 us  [body(): lax.dot_general(proj_in, activations, (((0,), (1,)), ((), ())), preferred...]
    pallas_call x0 -> x3, Pallas kernels: none -> 9.29 us  [the longest x2 7.4 us: grad_blocks(): pl.pallas_call(functools.partial(grad_kernel, per_step), grid_spec=pltpu....]
  transfers between devices with their start and end apart: 3 -> 18, of which waited for: 3 -> 10; matrix products, arithmetic and copies ran while one was open for 1% -> 2% of each run, Pallas kernels for 0% -> 15%
where the time goes in v2:
time: 48.7 us; the launch traced here: 48.5 us
  starting transfers between devices  20.8 us (43%)
  waiting for transfers between devices  14 us (29%)
  Pallas kernels  9.29 us (19%)
  local copies, waits for them, and re-layouts  1.93 us (4%)
  matrix products  0.89 us (2%)
  between operations  0.83 us (2%)
  other arithmetic  0.66 us (1%)
    ppermute x17, starting transfers between devices, swap(): return lax.ppermute(value, 'seq', [(i, i ^ offset) for i in range(size)])  19 us
    ppermute x17, waiting for transfers between devices, swap(): return lax.ppermute(value, 'seq', [(i, i ^ offset) for i in range(size)])  12.2 us
    pallas_call x2, Pallas kernels, grad_blocks(): pl.pallas_call(functools.partial(grad_kernel, per_step), grid_spec=pltpu....  7.4 us
    unnamed x14, local copies, waits for them, and re-layouts  1.89 us
    pallas_call x1, Pallas kernels, score(): pl.pallas_call(functools.partial(score_kernel, size, halves, len(grads),...  1.89 us
    ppermute x1, waiting for transfers between devices, gather_queries(): panels.append(lax.ppermute(panel, 'groups', [(0, 1), (1, 0)]))  1.86 us
    ppermute x1, starting transfers between devices, gather_queries(): panels.append(lax.ppermute(panel, 'groups', [(0, 1), (1, 0)]))  1.77 us
  transfers between devices with their start and end apart: 18, of which 10 were waited for; matrix products, arithmetic and copies ran while one was open for 2% of the time, Pallas kernels for 15%

profile of v2, /device:TPU:0, one launch (start us, length us, event | category | flops | bytes accessed | tf_op | source)
XLA Modules:
  0.0 48.5 jit_solution(10592831317392949070)
XLA Ops:
  0.6 0.0 copy-start
  0.7 0.9 %constant_dynamic-update-slice_fusion.4 = (bf16[64,2048]{1,0:T(8,128)(2,1)S(1)}, bf16[8,2048]{1,0:T(8,128)(2,1)S(1)}) fusion(bf16[8,4096]{1,0:T(8,128)(2,1)} %param.11, s32[]{:T(128)S(6)} %select_n.3), kind=kLoop, calls=%fused_computation.7 | loop fusion | bytes 98308
  1.6 5.0 %collective-permute-start.7 = (bf16[8,2048]{1,0:T(8,128)(2,1)S(1)}, bf16[8,2048]{1,0:T(8,128)(2,1)S(1)}, u32[]{:S(2)}, u32[]{:S(2)}) collective-permute-start(bf16[8,2048]{1,0:T(8,128)(2,1)S(1)} %get-tuple-element.7), channel_id=1, source_target_pairs={{0,12},{1,13},{2,14},{3,15},{4,8},{5,9},{6,10},{7,11},{8,4},{9,5},... | collective-permute-start | bytes 98312 | tf_op jit(solution)/shard_map/ppermute | solution.py:40
  6.6 0.0 collective-permute-start.6
  6.6 0.6 %collective-permute-start.5 = (bf16[8,2048]{1,0:T(8,128)(2,1)S(1)}, bf16[8,2048]{1,0:T(8,128)(2,1)S(1)}, u32[]{:S(2)}, u32[]{:S(2)}) collective-permute-start(bf16[8,2048]{1,0:T(8,128)(2,1)S(1)} %get-tuple-element.7), channel_id=1, source_target_pairs={{0,8},{1,9},{2,10},{3,11},{4,12},{5,13},{6,14},{7,15},{8,0},{9,1},... | collective-permute-start | bytes 98312 | tf_op jit(solution)/shard_map/ppermute | solution.py:40
  7.2 0.9 %copy-done.1 = bf16[1792,64]{0,1:T(8,128)(2,1)S(1)} copy-done((bf16[1792,64]{0,1:T(8,128)(2,1)S(1)}, bf16[1792,64]{0,1:T(8,128)(2,1)}, u32[]{:S(2)}) %copy-start.1) | copy-done | bytes 229400
  8.1 3.7 %shard_map.87 = f32[8,64,128]{2,1,0:T(8,128)S(1)} custom-call(s32[1]{0:T(128)} %bitcast.me_ref, bf16[64,1792]{1,0:T(8,128)(2,1)S(1)} %bitcast.9, bf16[2048,1792]{1,0:T(8,128)(2,1)} %refs_1_.3, bf16[2048,1792]{1,0:T(8,128)(2,1)} %refs_1_.3), custom_call_target="tpu_custom_call" | custom-call | flops 234881024 | bytes 3670016 | tf_op jit(solution)/shard_map/pallas_call | solution.py:72
  11.8 0.1 collective-permute-start
  11.9 3.7 %shard_map.86 = f32[8,64,128]{2,1,0:T(8,128)S(1)} custom-call(s32[1]{0:T(128)} %bitcast.me_ref, bf16[64,1792]{1,0:T(8,128)(2,1)S(1)} %bitcast.10, bf16[2048,1792]{1,0:T(8,128)(2,1)} %refs_1_.3, bf16[2048,1792]{1,0:T(8,128)(2,1)} %refs_1_.3), custom_call_target="tpu_custom_call" | custom-call | flops 234881024 | bytes 3670016 | tf_op jit(solution)/shard_map/pallas_call | solution.py:72
  15.6 0.0 copy-start.4
  15.6 0.0 collective-permute-done.7
  15.6 0.0 collective-permute-done.6
  15.7 0.0 collective-permute-done.5
  15.7 1.8 %collective-permute-start.8 = (bf16[32,2048]{1,0:T(8,128)(2,1)S(1)}, bf16[32,2048]{1,0:T(8,128)(2,1)S(1)}, u32[]{:S(2)}, u32[]{:S(2)}) collective-permute-start(bf16[32,2048]{1,0:T(8,128)(2,1)S(1)} %pad_maximum_fusion), channel_id=1, source_target_pairs={{0,2},{1,3},{2,0},{3,1},{4,6},{5,7},{6,4},{7,5},{8,10},{9,11},{10,... | collective-permute-start | bytes 393224 | tf_op jit(solution)/shard_map/ppermute | solution.py:40
  17.5 0.0 collective-permute-done
  17.6 0.0 copy-start.2
  17.6 0.0 copy-start.3
  17.6 0.4 collective-permute-start.1
  17.9 4.1 %collective-permute-done.8 = bf16[32,2048]{1,0:T(8,128)(2,1)S(1)} collective-permute-done((bf16[32,2048]{1,0:T(8,128)(2,1)S(1)}, bf16[32,2048]{1,0:T(8,128)(2,1)S(1)}, u32[]{:S(2)}, u32[]{:S(2)}) %collective-permute-start.8) | collective-permute-done | bytes 131104 | tf_op jit(solution)/shard_map/ppermute | solution.py:40
  22.1 0.1 collective-permute-start.10
  22.1 1.8 %collective-permute-start.9 = (bf16[64,2048]{1,0:T(8,128)(2,1)S(1)}, bf16[64,2048]{1,0:T(8,128)(2,1)S(1)}, u32[]{:S(2)}, u32[]{:S(2)}) collective-permute-start(bf16[64,2048]{1,0:T(8,128)(2,1)S(1)} %constant_dynamic-update-slice_fusion.refs_4_), channel_id=1, source_target_pairs={{0,16},{16,0},{1,17},{17,1},{2,18},{18,2},{3,19},{19,3},{4,20},{20... | collective-permute-start | bytes 786440 | tf_op jit(solution)/shard_map/ppermute | solution.py:200
  23.9 0.5 %collective-permute-done.1 = f32[4,64,128]{2,1,0:T(8,128)S(1)} collective-permute-done((f32[4,64,128]{2,1,0:T(8,128)S(1)}, f32[4,64,128]{2,1,0:T(8,128)S(1)}, u32[]{:S(2)}, u32[]{:S(2)}) %collective-permute-start.1) | collective-permute-done | bytes 131104 | tf_op jit(solution)/shard_map/ppermute | solution.py:40
  24.5 3.9 %collective-permute-start.4 = (f32[1,64,128]{2,1,0:T(8,128)S(1)}, f32[1,64,128]{2,1,0:T(8,128)S(1)}, u32[]{:S(2)}, u32[]{:S(2)}) collective-permute-start(f32[1,64,128]{2,1,0:T(8,128)S(1)} %get-tuple-element.8), channel_id=1, source_target_pairs={{0,12},{1,13},{2,14},{3,15},{4,8},{5,9},{6,10},{7,11},{8,4},{9,5},... | collective-permute-start | bytes 98312 | tf_op jit(solution)/shard_map/ppermute | solution.py:40
  28.4 0.0 collective-permute-start.3
  28.4 0.6 %collective-permute-start.2 = (f32[1,64,128]{2,1,0:T(8,128)S(1)}, f32[1,64,128]{2,1,0:T(8,128)S(1)}, u32[]{:S(2)}, u32[]{:S(2)}) collective-permute-start(f32[1,64,128]{2,1,0:T(8,128)S(1)} %get-tuple-element.10), channel_id=1, source_target_pairs={{0,8},{1,9},{2,10},{3,11},{4,12},{5,13},{6,14},{7,15},{8,0},{9,1},... | collective-permute-start | bytes 98312 | tf_op jit(solution)/shard_map/ppermute | solution.py:40
  29.0 1.9 %collective-permute-done.9.refs_5_ = bf16[64,2048]{1,0:T(8,128)(2,1)S(1)} collective-permute-done((bf16[64,2048]{1,0:T(8,128)(2,1)S(1)}, bf16[64,2048]{1,0:T(8,128)(2,1)S(1)}, u32[]{:S(2)}, u32[]{:S(2)}) %collective-permute-start.9) | collective-permute-done | bytes 262176 | tf_op jit(solution)/shard_map/ppermute | solution.py:200
  30.9 0.0 collective-permute-start.11
  30.9 0.0 copy-done.4
  30.9 0.9 %fusion.6.act_ref = f32[64,128]{1,0:T(8,128)S(1)} fusion(bf16[8192,64]{0,1:T(8,128)(2,1)S(1)} %copy-done.4, bf16[128,8192]{1,0:T(8,128)(2,1)S(1)} %copy-done), kind=kOutput, calls=%fused_computation.16 | convolution fusion | flops 134217728 | bytes 3178496 | tf_op jit(solution)/shard_map/dot_general | solution.py:222
  31.8 0.0 collective-permute-done.4.refs_3_
  31.8 0.5 %collective-permute-done.3.refs_2_ = f32[1,64,128]{2,1,0:T(8,128)S(1)} collective-permute-done((f32[1,64,128]{2,1,0:T(8,128)S(1)}, f32[1,64,128]{2,1,0:T(8,128)S(1)}, u32[]{:S(2)}, u32[]{:S(2)}) %collective-permute-start.3) | collective-permute-done | bytes 32800 | tf_op jit(solution)/shard_map/ppermute | solution.py:40
  32.3 0.9 %collective-permute-done.2.refs_1_ = f32[1,64,128]{2,1,0:T(8,128)S(1)} collective-permute-done((f32[1,64,128]{2,1,0:T(8,128)S(1)}, f32[1,64,128]{2,1,0:T(8,128)S(1)}, u32[]{:S(2)}, u32[]{:S(2)}) %collective-permute-start.2) | collective-permute-done | bytes 32800 | tf_op jit(solution)/shard_map/ppermute | solution.py:40
  33.2 0.0 collective-permute-done.10.refs_6_
  33.2 0.0 collective-permute-done.11.refs_7_
  33.2 1.9 %shard_map.88 = (f32[128,128]{1,0:T(8,128)}, f32[16,8,16]{2,1,0:T(8,128)S(1)}) custom-call(s32[1]{0:T(128)} %bitcast.me_ref, s32[1]{0:T(128)} %bitcast.1.group_ref, s32[16]{0:T(128)S(1)} %copy-done.2, s32[16]{0:T(128)S(1)} %copy-done.3, f32[64,128]{1,0:T(8,128)S(1)} %fusion.6.act_ref, f32[1,64,128]{2,1,0:T(8,128)S(1)} %get-tuple-element.11.refs_0_, ...), custom_call_target="tpu_custom_call" | custom-call | flops 134217728 | bytes 1048576 | tf_op jit(solution)/shard_map/pallas_call | solution.py:165
  35.1 1.5 %collective-permute-start.12 = (f32[4,8,16]{2,1,0:T(8,128)S(1)}, f32[4,8,16]{2,1,0:T(8,128)S(1)}, u32[]{:S(2)}, u32[]{:S(2)}) collective-permute-start(f32[4,8,16]{2,1,0:T(8,128)S(1)} %get-tuple-element.12), channel_id=1, source_target_pairs={{0,2},{1,3},{2,0},{3,1},{4,6},{5,7},{6,4},{7,5},{8,10},{9,11},{10,... | collective-permute-start | bytes 6152 | tf_op jit(solution)/shard_map/ppermute | solution.py:40
  36.6 0.0 collective-permute-start.14
  36.6 0.6 %collective-permute-start.13 = (f32[4,8,16]{2,1,0:T(8,128)S(1)}, f32[4,8,16]{2,1,0:T(8,128)S(1)}, u32[]{:S(2)}, u32[]{:S(2)}) collective-permute-start(f32[4,8,16]{2,1,0:T(8,128)S(1)} %get-tuple-element.14), channel_id=1, source_target_pairs={{0,1},{1,0},{2,3},{3,2},{4,5},{5,4},{6,7},{7,6},{8,9},{9,8},{10,11... | collective-permute-start | bytes 6152 | tf_op jit(solution)/shard_map/ppermute | solution.py:40
  37.2 1.6 %collective-permute-done.12 = f32[4,8,16]{2,1,0:T(8,128)S(1)} collective-permute-done((f32[4,8,16]{2,1,0:T(8,128)S(1)}, f32[4,8,16]{2,1,0:T(8,128)S(1)}, u32[]{:S(2)}, u32[]{:S(2)}) %collective-permute-start.12) | collective-permute-done | bytes 2080 | tf_op jit(solution)/shard_map/ppermute | solution.py:40
  38.8 0.9 %collective-permute-done.14 = f32[4,8,16]{2,1,0:T(8,128)S(1)} collective-permute-done((f32[4,8,16]{2,1,0:T(8,128)S(1)}, f32[4,8,16]{2,1,0:T(8,128)S(1)}, u32[]{:S(2)}, u32[]{:S(2)}) %collective-permute-start.14) | collective-permute-done | bytes 2080 | tf_op jit(solution)/shard_map/ppermute | solution.py:40
  39.8 0.0 collective-permute-done.13
  39.8 1.8 %collective-permute-start.15 = (f32[1,8,16]{2,1,0:T(8,128)S(1)}, f32[1,8,16]{2,1,0:T(8,128)S(1)}, u32[]{:S(2)}, u32[]{:S(2)}) collective-permute-start(f32[1,8,16]{2,1,0:T(8,128)S(1)} %get-tuple-element.15), channel_id=1, source_target_pairs={{0,8},{1,9},{2,10},{3,11},{4,12},{5,13},{6,14},{7,15},{8,0},{9,1},... | collective-permute-start | bytes 1544 | tf_op jit(solution)/shard_map/ppermute | solution.py:40
  41.6 2.6 %collective-permute-start.17 = (f32[1,8,16]{2,1,0:T(8,128)S(1)}, f32[1,8,16]{2,1,0:T(8,128)S(1)}, u32[]{:S(2)}, u32[]{:S(2)}) collective-permute-start(f32[1,8,16]{2,1,0:T(8,128)S(1)} %get-tuple-element.16), channel_id=1, source_target_pairs={{0,12},{1,13},{2,14},{3,15},{4,8},{5,9},{6,10},{7,11},{8,4},{9,5},... | collective-permute-start | bytes 1544 | tf_op jit(solution)/shard_map/ppermute | solution.py:40
  44.2 0.0 collective-permute-start.16
  44.3 0.1 collective-permute-done.15
  44.4 2.6 %collective-permute-done.17 = f32[1,8,16]{2,1,0:T(8,128)S(1)} collective-permute-done((f32[1,8,16]{2,1,0:T(8,128)S(1)}, f32[1,8,16]{2,1,0:T(8,128)S(1)}, u32[]{:S(2)}, u32[]{:S(2)}) %collective-permute-start.17) | collective-permute-done | bytes 544 | tf_op jit(solution)/shard_map/ppermute | solution.py:40
  47.0 0.9 %collective-permute-done.16 = f32[1,8,16]{2,1,0:T(8,128)S(1)} collective-permute-done((f32[1,8,16]{2,1,0:T(8,128)S(1)}, f32[1,8,16]{2,1,0:T(8,128)S(1)}, u32[]{:S(2)}, u32[]{:S(2)}) %collective-permute-start.16) | collective-permute-done | bytes 544 | tf_op jit(solution)/shard_map/ppermute | solution.py:40
  47.9 0.6 %fusion.2 = f32[16,8]{0,1:T(8,128)} fusion(f32[1,8,16]{2,1,0:T(8,128)S(1)} %collective-permute-done.17, f32[1,8,16]{2,1,0:T(8,128)S(1)} %collective-permute-done.16, f32[1,8,16]{2,1,0:T(8,128)S(1)} %collective-permute-done.15, f32[4,8,16]{2,1,0:T(8,128)S(1)} %add_add_fusion), kind=kLoop, calls=%fused_computation.11 | loop fusion | flops 384 | bytes 2560 | tf_op jit(solution)/shard_map/transpose | solution.py:240
  (16 shorter events, 0.1 us)
Async XLA Ops:
  0.6 30.2 %copy-start = (bf16[128,8192]{1,0:T(8,128)(2,1)S(1)}, bf16[128,8192]{1,0:T(8,128)(2,1)}, u32[]{:S(2)}) copy-start(bf16[128,8192]{1,0:T(8,128)(2,1)} %param.7) | copy-start | bytes 6291460
  1.6 14.1 %collective-permute-start.7 = (bf16[8,2048]{1,0:T(8,128)(2,1)S(1)}, bf16[8,2048]{1,0:T(8,128)(2,1)S(1)}, u32[]{:S(2)}, u32[]{:S(2)}) collective-permute-start(bf16[8,2048]{1,0:T(8,128)(2,1)S(1)} %get-tuple-element.7), channel_id=1, source_target_pairs={{0,12},{1,13},{2,14},{3,15},{4,8},{5,9},{6,10},{7,11},{8,4},{9,5},... | collective-permute-start | bytes 98312 | tf_op jit(solution)/shard_map/ppermute | solution.py:40
  6.6 9.0 %collective-permute-start.6 = (bf16[8,2048]{1,0:T(8,128)(2,1)S(1)}, bf16[8,2048]{1,0:T(8,128)(2,1)S(1)}, u32[]{:S(2)}, u32[]{:S(2)}) collective-permute-start(bf16[8,2048]{1,0:T(8,128)(2,1)S(1)} %get-tuple-element.7), channel_id=1, source_target_pairs={{0,4},{1,5},{2,6},{3,7},{4,0},{5,1},{6,2},{7,3},{8,12},{9,13},{10,... | collective-permute-start | bytes 98312 | tf_op jit(solution)/shard_map/ppermute | solution.py:40
  6.6 9.0 %collective-permute-start.5 = (bf16[8,2048]{1,0:T(8,128)(2,1)S(1)}, bf16[8,2048]{1,0:T(8,128)(2,1)S(1)}, u32[]{:S(2)}, u32[]{:S(2)}) collective-permute-start(bf16[8,2048]{1,0:T(8,128)(2,1)S(1)} %get-tuple-element.7), channel_id=1, source_target_pairs={{0,8},{1,9},{2,10},{3,11},{4,12},{5,13},{6,14},{7,15},{8,0},{9,1},... | collective-permute-start | bytes 98312 | tf_op jit(solution)/shard_map/ppermute | solution.py:40
  7.2 0.9 %copy-start.1 = (bf16[1792,64]{0,1:T(8,128)(2,1)S(1)}, bf16[1792,64]{0,1:T(8,128)(2,1)}, u32[]{:S(2)}) copy-start(bf16[1792,64]{0,1:T(8,128)(2,1)} %param.10) | copy-start | bytes 688132
  11.8 5.7 %collective-permute-start = (f32[8,64,128]{2,1,0:T(8,128)S(1)}, f32[8,64,128]{2,1,0:T(8,128)S(1)}, u32[]{:S(2)}, u32[]{:S(2)}) collective-permute-start(f32[8,64,128]{2,1,0:T(8,128)S(1)} %shard_map.87), channel_id=1, source_target_pairs={{0,1},{1,0},{2,3},{3,2},{4,5},{5,4},{6,7},{7,6},{8,9},{9,8},{10,11... | collective-permute-start | bytes 786440 | tf_op jit(solution)/shard_map/ppermute | solution.py:40
  15.6 15.2 %copy-start.4 = (bf16[8192,64]{0,1:T(8,128)(2,1)S(1)}, bf16[8192,64]{0,1:T(8,128)(2,1)}, u32[]{:S(2)}) copy-start(bf16[8192,64]{0,1:T(8,128)(2,1)} %param.9) | copy-start | bytes 3145732
  15.7 6.4 %collective-permute-start.8 = (bf16[32,2048]{1,0:T(8,128)(2,1)S(1)}, bf16[32,2048]{1,0:T(8,128)(2,1)S(1)}, u32[]{:S(2)}, u32[]{:S(2)}) collective-permute-start(bf16[32,2048]{1,0:T(8,128)(2,1)S(1)} %pad_maximum_fusion), channel_id=1, source_target_pairs={{0,2},{1,3},{2,0},{3,1},{4,6},{5,7},{6,4},{7,5},{8,10},{9,11},{10,... | collective-permute-start | bytes 393224 | tf_op jit(solution)/shard_map/ppermute | solution.py:40
  17.6 15.6 %copy-start.2 = (s32[16]{0:T(128)S(1)}, s32[16]{0:T(128)}, u32[]{:S(2)}) copy-start(s32[16]{0:T(128)} %length_ref.1) | copy-start | bytes 196
  17.6 15.6 %copy-start.3 = (s32[16]{0:T(128)S(1)}, s32[16]{0:T(128)}, u32[]{:S(2)}) copy-start(s32[16]{0:T(128)} %valid_ref.1) | copy-start | bytes 196
  17.6 6.8 %collective-permute-start.1 = (f32[4,64,128]{2,1,0:T(8,128)S(1)}, f32[4,64,128]{2,1,0:T(8,128)S(1)}, u32[]{:S(2)}, u32[]{:S(2)}) collective-permute-start(f32[4,64,128]{2,1,0:T(8,128)S(1)} %slice.57), channel_id=1, source_target_pairs={{0,2},{1,3},{2,0},{3,1},{4,6},{5,7},{6,4},{7,5},{8,10},{9,11},{10,... | collective-permute-start | bytes 393224 | tf_op jit(solution)/shard_map/ppermute | solution.py:40
  22.1 11.1 %collective-permute-start.10 = (bf16[64,2048]{1,0:T(8,128)(2,1)S(1)}, bf16[64,2048]{1,0:T(8,128)(2,1)S(1)}, u32[]{:S(2)}, u32[]{:S(2)}) collective-permute-start(bf16[64,2048]{1,0:T(8,128)(2,1)S(1)} %constant_dynamic-update-slice_fusion.refs_4_), channel_id=1, source_target_pairs={{0,1},{1,0},{2,3},{3,2},{4,5},{5,4},{6,7},{7,6},{8,9},{9,8},{10,11... | collective-permute-start | bytes 786440 | tf_op jit(solution)/shard_map/ppermute | solution.py:40
  22.1 8.7 %collective-permute-start.9 = (bf16[64,2048]{1,0:T(8,128)(2,1)S(1)}, bf16[64,2048]{1,0:T(8,128)(2,1)S(1)}, u32[]{:S(2)}, u32[]{:S(2)}) collective-permute-start(bf16[64,2048]{1,0:T(8,128)(2,1)S(1)} %constant_dynamic-update-slice_fusion.refs_4_), channel_id=1, source_target_pairs={{0,16},{16,0},{1,17},{17,1},{2,18},{18,2},{3,19},{19,3},{4,20},{20... | collective-permute-start | bytes 786440 | tf_op jit(solution)/shard_map/ppermute | solution.py:200
  24.5 7.3 %collective-permute-start.4 = (f32[1,64,128]{2,1,0:T(8,128)S(1)}, f32[1,64,128]{2,1,0:T(8,128)S(1)}, u32[]{:S(2)}, u32[]{:S(2)}) collective-permute-start(f32[1,64,128]{2,1,0:T(8,128)S(1)} %get-tuple-element.8), channel_id=1, source_target_pairs={{0,12},{1,13},{2,14},{3,15},{4,8},{5,9},{6,10},{7,11},{8,4},{9,5},... | collective-permute-start | bytes 98312 | tf_op jit(solution)/shard_map/ppermute | solution.py:40
  28.4 3.9 %collective-permute-start.3 = (f32[1,64,128]{2,1,0:T(8,128)S(1)}, f32[1,64,128]{2,1,0:T(8,128)S(1)}, u32[]{:S(2)}, u32[]{:S(2)}) collective-permute-start(f32[1,64,128]{2,1,0:T(8,128)S(1)} %get-tuple-element.9), channel_id=1, source_target_pairs={{0,4},{1,5},{2,6},{3,7},{4,0},{5,1},{6,2},{7,3},{8,12},{9,13},{10,... | collective-permute-start | bytes 98312 | tf_op jit(solution)/shard_map/ppermute | solution.py:40
  28.4 4.8 %collective-permute-start.2 = (f32[1,64,128]{2,1,0:T(8,128)S(1)}, f32[1,64,128]{2,1,0:T(8,128)S(1)}, u32[]{:S(2)}, u32[]{:S(2)}) collective-permute-start(f32[1,64,128]{2,1,0:T(8,128)S(1)} %get-tuple-element.10), channel_id=1, source_target_pairs={{0,8},{1,9},{2,10},{3,11},{4,12},{5,13},{6,14},{7,15},{8,0},{9,1},... | collective-permute-start | bytes 98312 | tf_op jit(solution)/shard_map/ppermute | solution.py:40
  30.9 2.3 %collective-permute-start.11 = (bf16[64,2048]{1,0:T(8,128)(2,1)S(1)}, bf16[64,2048]{1,0:T(8,128)(2,1)S(1)}, u32[]{:S(2)}, u32[]{:S(2)}) collective-permute-start(bf16[64,2048]{1,0:T(8,128)(2,1)S(1)} %collective-permute-done.9.refs_5_), channel_id=1, source_target_pairs={{0,1},{1,0},{2,3},{3,2},{4,5},{5,4},{6,7},{7,6},{8,9},{9,8},{10,11... | collective-permute-start | bytes 786440 | tf_op jit(solution)/shard_map/ppermute | solution.py:40
  35.1 3.7 %collective-permute-start.12 = (f32[4,8,16]{2,1,0:T(8,128)S(1)}, f32[4,8,16]{2,1,0:T(8,128)S(1)}, u32[]{:S(2)}, u32[]{:S(2)}) collective-permute-start(f32[4,8,16]{2,1,0:T(8,128)S(1)} %get-tuple-element.12), channel_id=1, source_target_pairs={{0,2},{1,3},{2,0},{3,1},{4,6},{5,7},{6,4},{7,5},{8,10},{9,11},{10,... | collective-permute-start | bytes 6152 | tf_op jit(solution)/shard_map/ppermute | solution.py:40
  36.6 3.2 %collective-permute-start.14 = (f32[4,8,16]{2,1,0:T(8,128)S(1)}, f32[4,8,16]{2,1,0:T(8,128)S(1)}, u32[]{:S(2)}, u32[]{:S(2)}) collective-permute-start(f32[4,8,16]{2,1,0:T(8,128)S(1)} %get-tuple-element.13), channel_id=1, source_target_pairs={{0,3},{1,2},{2,1},{3,0},{4,7},{5,6},{6,5},{7,4},{8,11},{9,10},{10,... | collective-permute-start | bytes 6152 | tf_op jit(solution)/shard_map/ppermute | solution.py:40
  36.6 3.2 %collective-permute-start.13 = (f32[4,8,16]{2,1,0:T(8,128)S(1)}, f32[4,8,16]{2,1,0:T(8,128)S(1)}, u32[]{:S(2)}, u32[]{:S(2)}) collective-permute-start(f32[4,8,16]{2,1,0:T(8,128)S(1)} %get-tuple-element.14), channel_id=1, source_target_pairs={{0,1},{1,0},{2,3},{3,2},{4,5},{5,4},{6,7},{7,6},{8,9},{9,8},{10,11... | collective-permute-start | bytes 6152 | tf_op jit(solution)/shard_map/ppermute | solution.py:40
  39.8 4.6 %collective-permute-start.15 = (f32[1,8,16]{2,1,0:T(8,128)S(1)}, f32[1,8,16]{2,1,0:T(8,128)S(1)}, u32[]{:S(2)}, u32[]{:S(2)}) collective-permute-start(f32[1,8,16]{2,1,0:T(8,128)S(1)} %get-tuple-element.15), channel_id=1, source_target_pairs={{0,8},{1,9},{2,10},{3,11},{4,12},{5,13},{6,14},{7,15},{8,0},{9,1},... | collective-permute-start | bytes 1544 | tf_op jit(solution)/shard_map/ppermute | solution.py:40
  41.6 5.4 %collective-permute-start.17 = (f32[1,8,16]{2,1,0:T(8,128)S(1)}, f32[1,8,16]{2,1,0:T(8,128)S(1)}, u32[]{:S(2)}, u32[]{:S(2)}) collective-permute-start(f32[1,8,16]{2,1,0:T(8,128)S(1)} %get-tuple-element.16), channel_id=1, source_target_pairs={{0,12},{1,13},{2,14},{3,15},{4,8},{5,9},{6,10},{7,11},{8,4},{9,5},... | collective-permute-start | bytes 1544 | tf_op jit(solution)/shard_map/ppermute | solution.py:40
  44.2 3.6 %collective-permute-start.16 = (f32[1,8,16]{2,1,0:T(8,128)S(1)}, f32[1,8,16]{2,1,0:T(8,128)S(1)}, u32[]{:S(2)}, u32[]{:S(2)}) collective-permute-start(f32[1,8,16]{2,1,0:T(8,128)S(1)} %get-tuple-element.17), channel_id=1, source_target_pairs={{0,4},{1,5},{2,6},{3,7},{4,0},{5,1},{6,2},{7,3},{8,12},{9,13},{10,... | collective-permute-start | bytes 1544 | tf_op jit(solution)/shard_map/ppermute | solution.py:40

commit v3 on v0

v3 whole, which is shorter than its diff:
```python
import functools

import jax
import jax.numpy as jnp
from jax import lax
from jax.experimental import pallas as pl
from jax.experimental.pallas import tpu as pltpu
from jax.sharding import PartitionSpec as P

MIB = 1 << 20


def swap(value, offset, size):
    return lax.ppermute(value, "seq", [(i, i ^ offset) for i in range(size)])


def grad_kernel(core_ref, proj_ref, grads_ref, out_ref):
    del core_ref
    count, rows, depth = grads_ref.shape
    made = lax.dot_general(
        grads_ref[...].reshape(count * rows, depth),
        proj_ref[...],
        (((1,), (1,)), ((), ())),
        preferred_element_type=jnp.float32,
    )
    for k in range(count):
        out_ref[k] = made[k * rows : (k + 1) * rows].T


def grad_blocks(core, proj, out_grads, per_step):
    width, depth = proj.shape
    chips, _, rows, _ = out_grads.shape
    return pl.pallas_call(
        grad_kernel,
        grid_spec=pltpu.PrefetchScalarGridSpec(
            num_scalar_prefetch=1,
            grid=(chips // per_step,),
            in_specs=[
                pl.BlockSpec((width, depth), lambda step, core_ref: (0, 0)),
                pl.BlockSpec(
                    (per_step, None, rows, depth),
                    lambda step, core_ref: (step, core_ref[0], 0, 0),
                ),
            ],
            out_specs=pl.BlockSpec((per_step, width, rows), lambda step, core_ref: (step, 0, 0)),
        ),
        out_shape=jax.ShapeDtypeStruct((chips, width, rows), jnp.float32),
        compiler_params=pltpu.CompilerParams(vmem_limit_bytes=52 * MIB),
        cost_estimate=pl.CostEstimate(
            flops=2 * chips * rows * depth * width,
            bytes_accessed=2 * chips * rows * depth,
            transcendentals=0,
        ),
    )(core, proj, out_grads)


def score_kernel(size, low, place, me_ref, length_ref, valid_ref, act_ref, grad_ref, *refs):
    panel_refs = refs[:-4]
    token_ref, doc_ref, outer_ref, turned_ref = refs[-4:]
    me = me_ref[0]
    act = act_ref[...]
    width, rows = act.shape
    grad = grad_ref[0]
    for k in range(1, grad_ref.shape[0]):
        grad = grad + grad_ref[k]
    for i in range(width):
        outer_ref[i * width : (i + 1) * width] = (act * grad[i : i + 1]).astype(jnp.bfloat16)
    panel = jnp.concatenate([ref[...] for ref in panel_refs], axis=0)
    scores = jnp.dot(panel, outer_ref[...], preferred_element_type=jnp.float32)
    own_q = scores.shape[0] // size
    for k, (high, offset) in enumerate(place):
        spot = pl.multiple_of((((me & (low - 1)) ^ offset) + high) * own_q, own_q)
        turned_ref[pl.ds(spot, own_q)] = scores[k * own_q : (k + 1) * own_q]
    turned = turned_ref[...]
    token_ref[...] = turned.T

    docs = length_ref.shape[0]
    doc_of = lax.broadcasted_iota(jnp.int32, (docs, rows), 0)
    lower = jnp.zeros((docs, rows), jnp.int32)
    used = jnp.zeros((docs, rows), jnp.int32)
    start = jnp.int32(0)
    for d in range(docs):
        lower = jnp.where(doc_of == d, start, lower)
        used = jnp.where(doc_of == d, jnp.minimum(valid_ref[d], length_ref[d]), used)
        start = start + length_ref[d]
    token = me * rows + lax.broadcasted_iota(jnp.int32, (docs, rows), 1)
    inside = (token >= lower) & (token < lower + used)
    member = jnp.where(inside, 1.0 / jnp.sqrt(used.astype(jnp.float32)), 0.0)
    partial = lax.dot_general(
        turned,
        member,
        (((1,), (1,)), ((), ())),
        precision=lax.Precision.HIGHEST,
        preferred_element_type=jnp.float32,
    )
    for k in range(size):
        doc_ref[k] = partial[k * own_q : (k + 1) * own_q]


def score(me, lengths, valid, act, grads, panels, low, place, size, own_q):
    width, rows = act.shape
    docs = lengths.shape[0]
    smem = pl.BlockSpec(memory_space=pltpu.SMEM)
    vmem = pl.BlockSpec(memory_space=pltpu.VMEM)
    count = size * own_q
    return pl.pallas_call(
        functools.partial(score_kernel, size, low, place),
        in_specs=[smem] * 3 + [vmem] * (2 + len(panels)),
        out_specs=(vmem, vmem),
        out_shape=(
            jax.ShapeDtypeStruct((rows, count), jnp.float32),
            jax.ShapeDtypeStruct((size, own_q, docs), jnp.float32),
        ),
        scratch_shapes=[
            pltpu.VMEM((width * width, rows), jnp.bfloat16),
            pltpu.VMEM((count, rows), jnp.float32),
        ],
        compiler_params=pltpu.CompilerParams(vmem_limit_bytes=32 * MIB),
        cost_estimate=pl.CostEstimate(
            flops=2 * rows * width * width * count,
            bytes_accessed=2 * count * width * width,
            transcendentals=0,
        ),
    )(me, lengths, valid, act, grads, *panels)


def gather_lines(queries, size):
    count = size.bit_length() - 1
    low = 1 << (count - count // 2)
    lines = [[low * k + i for k in range(size // low)] for i in range(low)]
    return lax.all_gather(queries, "seq", axis=0, tiled=True, axis_index_groups=lines), low


def gather_queries(panel, low, size):
    place = [(low * k, 0) for k in range(size // low)]
    offset = low // 2
    while offset > 1:
        panel = jnp.concatenate([panel, swap(panel, offset, size)], axis=0)
        place = place + [(high, o ^ offset) for high, o in place]
        offset //= 2
    place = place + [(high, o ^ 1) for high, o in place]
    return [panel, swap(panel, 1, size)], tuple(place)


def body(size, activations, out_grads, proj_in, proj_out, queries, doc_length, valid_count):
    rows = activations.shape[0]
    me = lax.axis_index("seq").astype(jnp.int32)
    panel, low = gather_lines(queries, size)

    proj = proj_out.T
    chips = size // 2
    split = out_grads.reshape(chips, 2, rows, out_grads.shape[1])
    core = (me & 1)[None]
    from_core = swap(grad_blocks(1 - core, proj, split, 2), 1, size)
    chip_sum = grad_blocks(core, proj, split, 2) + from_core
    alike = [[2 * k + c for k in range(chips)] for c in range(2)]
    grads = lax.all_to_all(chip_sum, "seq", 0, 0, tiled=True, axis_index_groups=alike)

    panel, _ = lax.optimization_barrier((panel, chip_sum))
    panels, place = gather_queries(panel, low, size)
    act = lax.dot_general(
        proj_in, activations, (((0,), (1,)), ((), ())), preferred_element_type=jnp.float32
    )
    token_scores, doc = score(
        me[None],
        doc_length,
        valid_count,
        act,
        grads,
        panels,
        low,
        place,
        size,
        queries.shape[0],
    )
    doc = lax.all_to_all(doc, "seq", 0, 0, tiled=True).sum(axis=0)
    return (token_scores, doc.T)


def solution(mesh):
    size = mesh.shape["seq"]
    placed = (
        P(("groups", "seq"), None),
        P("groups", "seq"),
        P(),
        P("seq", None),
        P("seq", None),
        P("groups"),
        P("groups"),
    )
    return jax.shard_map(
        functools.partial(body, size),
        mesh=mesh,
        in_specs=placed,
        out_specs=(P(("groups", "seq"), None), P("groups", "seq")),
        check_vma=False,
    )
```

time: 214 us -> 62.1 us (0.29)
  waiting for transfers between devices: 186 us -> 12.6 us
  blocking collectives: 0 us -> 25.2 us
  between operations: 13.9 us -> 0.75 us
  matrix products: 12.5 us -> 2.07 us
  Pallas kernels: 0 us -> 9.28 us
  starting transfers between devices: 0.12 us -> 7.94 us
    psum x1 -> x0, waiting for transfers between devices: 88.6 us -> none  [body(): doc_outer = lax.psum(partial_outer, 'seq')]
    reduce_scatter x1 -> x0, waiting for transfers between devices: 57.4 us -> none  [body(): lax.psum_scatter(jnp.dot(out_grads, proj_out, preferred_element_type=jnp....]
    all_gather x1 -> x0, waiting for transfers between devices: 39.1 us -> none  [body(): lax.all_gather(queries, 'seq', axis=0, tiled=True)]
    all_gather x0 -> x1, blocking collectives: none -> 15.3 us  [gather_lines(): lax.all_gather(queries, 'seq', axis=0, tiled=True, axis_index_groups=lines)]
    dot_general x5 -> x1, matrix products: 12.5 us -> 2.07 us  [body(): lax.dot_general(proj_in, activations, (((0,), (1,)), ((), ())), preferred...]
    all_to_all x0 -> x1, blocking collectives: none -> 9.9 us  [body(): doc = lax.all_to_all(doc, 'seq', 0, 0, tiled=True).sum(axis=0)]
    pallas_call x0 -> x3, Pallas kernels: none -> 9.28 us  [the longest x2 7.48 us: grad_blocks(): pl.pallas_call(grad_kernel, grid_spec=pltpu.PrefetchScalarGridSpec(num_sc...]
    all_to_all x0 -> x1, waiting for transfers between devices: none -> 7.49 us  [body(): lax.all_to_all(chip_sum, 'seq', 0, 0, tiled=True, axis_index_groups=alike)]
  transfers between devices with their start and end apart: 3 -> 4, of which waited for: 3 -> 2; matrix products, arithmetic and copies ran while one was open for 1% -> 3% of each run, Pallas kernels for 0% -> 6%
where the time goes in v3:
time: 62.1 us; the launch traced here: 61.6 us
  blocking collectives  25.2 us (41%)
  waiting for transfers between devices  12.6 us (20%)
  Pallas kernels  9.28 us (15%)
  starting transfers between devices  7.94 us (13%)
  matrix products  2.07 us (3%)
  other arithmetic  2.02 us (3%)
  local copies, waits for them, and re-layouts  1.82 us (3%)
  between operations  0.75 us (1%)
    all_gather x1, blocking collectives, gather_lines(): lax.all_gather(queries, 'seq', axis=0, tiled=True, axis_index_groups=lines)  15.3 us
    all_to_all x1, blocking collectives, body(): doc = lax.all_to_all(doc, 'seq', 0, 0, tiled=True).sum(axis=0)  9.9 us
    all_to_all x1, waiting for transfers between devices, body(): lax.all_to_all(chip_sum, 'seq', 0, 0, tiled=True, axis_index_groups=alike)  7.49 us
    pallas_call x2, Pallas kernels, grad_blocks(): pl.pallas_call(grad_kernel, grid_spec=pltpu.PrefetchScalarGridSpec(num_sc...  7.48 us
    all_to_all x1, starting transfers between devices, body(): lax.all_to_all(chip_sum, 'seq', 0, 0, tiled=True, axis_index_groups=alike)  5.83 us
    ppermute x3, waiting for transfers between devices, swap(): return lax.ppermute(value, 'seq', [(i, i ^ offset) for i in range(size)])  5.11 us
    ppermute x3, starting transfers between devices, swap(): return lax.ppermute(value, 'seq', [(i, i ^ offset) for i in range(size)])  2.11 us
    dot_general x1, matrix products, body(): lax.dot_general(proj_in, activations, (((0,), (1,)), ((), ())), preferred...  2.07 us
  transfers between devices with their start and end apart: 4, of which 2 were waited for; matrix products, arithmetic and copies ran while one was open for 3% of the time, Pallas kernels for 6%

profile of v3, /device:TPU:0, one launch (start us, length us, event | category | flops | bytes accessed | tf_op | source)
XLA Modules:
  0.0 61.6 jit_solution(2249455495379451355)
XLA Ops:
  0.6 0.0 copy-start
  0.6 0.0 copy-start.1
  0.7 1.1 %copy-done.1 = bf16[1792,64]{0,1:T(8,128)(2,1)S(1)} copy-done((bf16[1792,64]{0,1:T(8,128)(2,1)S(1)}, bf16[1792,64]{0,1:T(8,128)(2,1)}, u32[]{:S(2)}) %copy-start.1) | copy-done | bytes 229400
  1.7 0.0 copy-start.2
  1.7 3.8 %shard_map.87 = f32[8,64,128]{2,1,0:T(8,128)S(1)} custom-call(s32[1]{0:T(128)S(6)} %sub.3.core_ref, bf16[64,1792]{1,0:T(8,128)(2,1)S(1)} %bitcast.7, bf16[8,2,128,1792]{3,2,1,0:T(8,128)(2,1)} %bitcast.9), custom_call_target="tpu_custom_call" | custom-call | flops 234881024 | bytes 3670016 | tf_op jit(solution)/shard_map/pallas_call | solution.py:33
  5.5 0.0 copy-start.5
  5.5 0.5 collective-permute-start
  6.0 0.0 copy-done.2
  6.0 3.7 %shard_map.86 = f32[8,64,128]{2,1,0:T(8,128)S(1)} custom-call(s32[1]{0:T(128)} %bitcast.1.core_ref, bf16[64,1792]{1,0:T(8,128)(2,1)S(1)} %bitcast.8, bf16[8,2,128,1792]{3,2,1,0:T(8,128)(2,1)} %bitcast.10), custom_call_target="tpu_custom_call" | custom-call | flops 234881024 | bytes 3670016 | tf_op jit(solution)/shard_map/pallas_call | solution.py:33
  9.8 0.0 copy-done.5
  9.8 15.3 %all_gather.3 = bf16[32,4096]{1,0:T(8,128)(2,1)S(1)} all-gather(bf16[8,4096]{1,0:T(8,128)(2,1)S(1)} %copy-done.5), channel_id=1, replica_groups={{0,4,8,12},{1,5,9,13},{2,6,10,14},{3,7,11,15},{16,20,24,28},{17,21,25,2..., dimensions={0}, use_global_device_ids=true | all-gather | bytes 327680 | tf_op jit(solution)/shard_map/all_gather | solution.py:131
  25.0 0.0 collective-permute-done
  25.1 0.7 %add.3 = f32[8,64,128]{2,1,0:T(8,128)} add(f32[8,64,128]{2,1,0:T(8,128)S(1)} %shard_map.86, f32[8,64,128]{2,1,0:T(8,128)S(1)} %collective-permute-done) | non-fusion elementwise | flops 65536 | bytes 786432 | tf_op jit(solution)/shard_map/add | solution.py:155
  25.8 1.5 %collective-permute-start.1 = (bf16[32,4096]{1,0:T(8,128)(2,1)S(1)}, bf16[32,4096]{1,0:T(8,128)(2,1)S(1)}, u32[]{:S(2)}, u32[]{:S(2)}) collective-permute-start(bf16[32,4096]{1,0:T(8,128)(2,1)S(1)} %all_gather.3), channel_id=1, source_target_pairs={{0,2},{1,3},{2,0},{3,1},{4,6},{5,7},{6,4},{7,5},{8,10},{9,11},{10,... | collective-permute-start | bytes 786440 | tf_op jit(solution)/shard_map/ppermute | solution.py:14
  27.3 0.0 copy-start.3
  27.3 0.0 copy-start.4
  27.4 5.1 %collective-permute-done.1 = bf16[32,4096]{1,0:T(8,128)(2,1)S(1)} collective-permute-done((bf16[32,4096]{1,0:T(8,128)(2,1)S(1)}, bf16[32,4096]{1,0:T(8,128)(2,1)S(1)}, u32[]{:S(2)}, u32[]{:S(2)}) %collective-permute-start.1) | collective-permute-done | bytes 262176 | tf_op jit(solution)/shard_map/ppermute | solution.py:14
  32.5 0.1 collective-permute-start.2
  32.6 5.8 %all-to-all-start = ((f32[8,64,128]{2,1,0:T(8,128)}), f32[8,64,128]{2,1,0:T(8,128)S(1)}, u32[]{:S(2)}, u32[]{:S(2)}) async-start(f32[8,64,128]{2,1,0:T(8,128)} %add.3), calls=%async_computation | async-start | bytes 524288 | tf_op jit(solution)/shard_map/all_to_all | solution.py:157
  38.4 0.0 copy-done
  38.4 2.1 %fusion.act_ref = f32[64,128]{1,0:T(8,128)S(1)} fusion(bf16[8192,64]{0,1:T(8,128)(2,1)} %param.9, bf16[128,8192]{1,0:T(8,128)(2,1)S(1)} %copy-done), kind=kOutput, calls=%fused_computation.2 | convolution fusion | flops 134217728 | bytes 3178496 | tf_op jit(solution)/shard_map/dot_general | solution.py:161
  40.5 7.5 %all-to-all-done.grad_ref = f32[8,64,128]{2,1,0:T(8,128)S(1)} async-done(((f32[8,64,128]{2,1,0:T(8,128)}), f32[8,64,128]{2,1,0:T(8,128)S(1)}, u32[]{:S(2)}, u32[]{:S(2)}) %all-to-all-start) | async-done | bytes 262176 | tf_op jit(solution)/shard_map/all_to_all | solution.py:157
  48.0 0.0 collective-permute-done.2.refs_1_
  48.0 0.0 copy-done.3
  48.0 0.0 copy-done.4
  48.0 1.8 %shard_map.88 = (f32[128,128]{1,0:T(8,128)}, f32[16,8,16]{2,1,0:T(8,128)S(1)}) custom-call(s32[1]{0:T(128)} %bitcast.me_ref, s32[16]{0:T(128)S(1)} %copy-done.3, s32[16]{0:T(128)S(1)} %copy-done.4, f32[64,128]{1,0:T(8,128)S(1)} %fusion.act_ref, f32[8,64,128]{2,1,0:T(8,128)S(1)} %all-to-all-done.grad_ref, ...), custom_call_target="tpu_custom_call" | custom-call | flops 134217728 | bytes 1048576 | tf_op jit(solution)/shard_map/pallas_call | solution.py:106
  49.8 0.1 reshape.8
  49.9 9.9 %all_to_all.10 = f32[16,1,128]{2,1,0:T(1,128)S(1)} all-to-all(f32[16,1,128]{2,1,0:T(1,128)S(1)} %reshape.8), channel_id=1, replica_groups=mesh['groups'=2,'seq'=16] {'seq'}, dimensions={0} | all-to-all | bytes 16384 | tf_op jit(solution)/shard_map/all_to_all | solution.py:176
  59.8 0.5 broadcast
  60.3 0.7 %reduce = f32[16,128]{1,0:T(8,128)S(1)} reduce(f32[16,1,128]{2,1,0:T(1,128)S(1)} %all_to_all.10, f32[]{:T(128)} %broadcast), dimensions={1}, to_apply=%all_to_all.7.reduce_sub_computation | reduce | bytes 16388 | tf_op jit(solution)/shard_map/all_to_all | solution.py:176
  60.9 0.1 reshape.9
  61.0 0.6 reduce_sum.9
  (2 shorter events, 0.0 us)
Async XLA Ops:
  0.6 37.8 %copy-start = (bf16[128,8192]{1,0:T(8,128)(2,1)S(1)}, bf16[128,8192]{1,0:T(8,128)(2,1)}, u32[]{:S(2)}) copy-start(bf16[128,8192]{1,0:T(8,128)(2,1)} %param.7) | copy-start | bytes 6291460
  0.6 1.1 %copy-start.1 = (bf16[1792,64]{0,1:T(8,128)(2,1)S(1)}, bf16[1792,64]{0,1:T(8,128)(2,1)}, u32[]{:S(2)}) copy-start(bf16[1792,64]{0,1:T(8,128)(2,1)} %param.10) | copy-start | bytes 688132
  1.7 4.3 %copy-start.2 = (bf16[1792,64]{0,1:T(8,128)(2,1)S(1)}, bf16[1792,64]{0,1:T(8,128)(2,1)}, u32[]{:S(2)}) copy-start(bf16[1792,64]{0,1:T(8,128)(2,1)} %param.10) | copy-start | bytes 688132
  5.5 4.3 %copy-start.5 = (bf16[8,4096]{1,0:T(8,128)(2,1)S(1)}, bf16[8,4096]{1,0:T(8,128)(2,1)}, u32[]{:S(2)}) copy-start(bf16[8,4096]{1,0:T(8,128)(2,1)} %param.11) | copy-start | bytes 196612
  5.5 19.5 %collective-permute-start = (f32[8,64,128]{2,1,0:T(8,128)S(1)}, f32[8,64,128]{2,1,0:T(8,128)S(1)}, u32[]{:S(2)}, u32[]{:S(2)}) collective-permute-start(f32[8,64,128]{2,1,0:T(8,128)S(1)} %shard_map.87), channel_id=1, source_target_pairs={{0,1},{1,0},{2,3},{3,2},{4,5},{5,4},{6,7},{7,6},{8,9},{9,8},{10,11... | collective-permute-start | bytes 786440 | tf_op jit(solution)/shard_map/ppermute | solution.py:14
  25.8 6.7 %collective-permute-start.1 = (bf16[32,4096]{1,0:T(8,128)(2,1)S(1)}, bf16[32,4096]{1,0:T(8,128)(2,1)S(1)}, u32[]{:S(2)}, u32[]{:S(2)}) collective-permute-start(bf16[32,4096]{1,0:T(8,128)(2,1)S(1)} %all_gather.3), channel_id=1, source_target_pairs={{0,2},{1,3},{2,0},{3,1},{4,6},{5,7},{6,4},{7,5},{8,10},{9,11},{10,... | collective-permute-start | bytes 786440 | tf_op jit(solution)/shard_map/ppermute | solution.py:14
  27.3 20.6 %copy-start.3 = (s32[16]{0:T(128)S(1)}, s32[16]{0:T(128)}, u32[]{:S(2)}) copy-start(s32[16]{0:T(128)} %length_ref.1) | copy-start | bytes 196
  27.3 20.6 %copy-start.4 = (s32[16]{0:T(128)S(1)}, s32[16]{0:T(128)}, u32[]{:S(2)}) copy-start(s32[16]{0:T(128)} %valid_ref.1) | copy-start | bytes 196
  32.5 15.5 %collective-permute-start.2 = (bf16[64,4096]{1,0:T(8,128)(2,1)S(1)}, bf16[64,4096]{1,0:T(8,128)(2,1)S(1)}, u32[]{:S(2)}, u32[]{:S(2)}) collective-permute-start(bf16[64,4096]{1,0:T(8,128)(2,1)S(1)} %constant_dynamic-update-slice_fusion.refs_0_), channel_id=1, source_target_pairs={{0,1},{1,0},{2,3},{3,2},{4,5},{5,4},{6,7},{7,6},{8,9},{9,8},{10,11... | collective-permute-start | bytes 1572872 | tf_op jit(solution)/shard_map/ppermute | solution.py:14
  32.6 15.4 %all-to-all-start = ((f32[8,64,128]{2,1,0:T(8,128)}), f32[8,64,128]{2,1,0:T(8,128)S(1)}, u32[]{:S(2)}, u32[]{:S(2)}) async-start(f32[8,64,128]{2,1,0:T(8,128)} %add.3), calls=%async_computation | async-start | bytes 524288 | tf_op jit(solution)/shard_map/all_to_all | solution.py:157

commit v4 on v0

v4 whole, which is shorter than its diff:
```python
import functools

import jax
import jax.numpy as jnp
from jax import lax
from jax.experimental import pallas as pl
from jax.experimental.pallas import tpu as pltpu
from jax.sharding import PartitionSpec as P

MIB = 1 << 20
SMEM = pl.BlockSpec(memory_space=pltpu.SMEM)
VMEM = pl.BlockSpec(memory_space=pltpu.VMEM)
HBM = pl.BlockSpec(memory_space=pltpu.HBM)


def swap(value, offset, size):
    return lax.ppermute(value, "seq", [(i, i ^ offset) for i in range(size)])


def grad_kernel(offsets, me_ref, proj_ref, grads_ref, out_ref, proj_buf, grads_buf, proj_sem, sems):
    count, rows, depth = grads_buf.shape
    load = pltpu.make_async_copy(proj_ref, proj_buf, proj_sem)
    load.start()
    copies = []
    for k, offset in enumerate(offsets):
        first = pl.multiple_of((me_ref[0] ^ offset) * rows, rows)
        copy = pltpu.make_async_copy(grads_ref.at[pl.ds(first, rows)], grads_buf.at[k], sems.at[k])
        copy.start()
        copies.append(copy)
    load.wait()
    for k in range(0, count, 2):
        copies[k].wait()
        copies[k + 1].wait()
        made = lax.dot_general(
            proj_buf[...],
            grads_buf[k : k + 2].reshape(2 * rows, depth),
            (((1,), (1,)), ((), ())),
            preferred_element_type=jnp.float32,
        )
        out_ref[k] = made[:, :rows]
        out_ref[k + 1] = made[:, rows:]


def grad_blocks(me, proj, out_grads, rows, offsets):
    width, depth = proj.shape
    count = len(offsets)
    return pl.pallas_call(
        functools.partial(grad_kernel, offsets),
        in_specs=[SMEM, HBM, HBM],
        out_specs=VMEM,
        out_shape=jax.ShapeDtypeStruct((count, width, rows), jnp.float32),
        scratch_shapes=[
            pltpu.VMEM((width, depth), jnp.bfloat16),
            pltpu.VMEM((count, rows, depth), jnp.bfloat16),
            pltpu.SemaphoreType.DMA,
            pltpu.SemaphoreType.DMA((count,)),
        ],
        compiler_params=pltpu.CompilerParams(vmem_limit_bytes=52 * MIB),
        cost_estimate=pl.CostEstimate(
            flops=2 * count * rows * depth * width,
            bytes_accessed=2 * count * rows * depth,
            transcendentals=0,
        ),
    )(me, proj, out_grads)


def inner_kernel(pieces, act_ref, *refs):
    out_ref = refs[pieces]
    columns = []
    for r in range(act_ref.shape[0]):
        act = act_ref[r]
        high = act.astype(jnp.bfloat16)
        low = (act - high.astype(jnp.float32)).astype(jnp.bfloat16)
        none = jnp.zeros_like(high)
        columns.append(jnp.concatenate([high, none, low, none], axis=0))
        columns.append(jnp.concatenate([none, high, none, low], axis=0))
    table = jnp.concatenate(columns, axis=1)
    pair = 2 * act_ref.shape[1]
    rows = []
    for k in range(refs[0].shape[1] // pair):
        for ref in refs[:pieces]:
            rows.append(ref[:, k * pair : (k + 1) * pair])
    left = jnp.concatenate(rows, axis=0)
    left = jnp.concatenate([left, left], axis=1)
    out_ref[...] = jnp.dot(left, table, preferred_element_type=jnp.float32)


def inner(act, panels, steps):
    halves, width, rows = act.shape
    count = sum(p.shape[0] for p in panels)
    pairs = panels[0].shape[1] // (2 * width)
    total = pairs * count
    if steps == 1:
        grid = {"in_specs": [VMEM] * (1 + len(panels)), "out_specs": VMEM}
    else:
        grid = {
            "grid": (steps,),
            "in_specs": [VMEM]
            + [pl.BlockSpec((p.shape[0], p.shape[1] // steps), lambda s: (0, s)) for p in panels],
            "out_specs": pl.BlockSpec((total // steps, 2 * halves * rows), lambda s: (s, 0)),
        }
    return pl.pallas_call(
        functools.partial(inner_kernel, len(panels)),
        out_shape=jax.ShapeDtypeStruct((total, 2 * halves * rows), jnp.float32),
        compiler_params=pltpu.CompilerParams(vmem_limit_bytes=32 * MIB),
        cost_estimate=pl.CostEstimate(
            flops=16 * total * width * halves * rows,
            bytes_accessed=8 * total * halves * rows,
            transcendentals=0,
        ),
        **grid,
    )(act, *panels)


def score_kernel(steps, top, me_ref, length_ref, valid_ref, own_ref, other_ref, inner_ref, token_ref, doc_ref, grad_ref):
    halves, width, rows = own_ref.shape
    count = token_ref.shape[1]
    pairs = inner_ref.shape[0] // count
    step = pl.program_id(0) if steps > 1 else 0

    def begin():
        for r in range(halves):
            grad_ref[r] = own_ref[r] + other_ref[halves - 1 - r]

    if steps == 1:
        begin()
    else:
        pl.when(step == 0)(begin)

    for r in range(halves):
        total = None
        for k in range(pairs):
            for parity in range(2):
                if steps == 1:
                    line = grad_ref[r, 2 * k + parity : 2 * k + parity + 1]
                else:
                    line = grad_ref[r, pl.ds(2 * (step * pairs + k) + parity, 1)]
                column = (2 * r + parity) * rows
                term = line * inner_ref[k * count : (k + 1) * count, column : column + rows]
                total = term if total is None else total + term
        if steps == 1:
            token_ref[r] = total
        else:
            token_ref[r] = jnp.where(step == 0, total, token_ref[r] + total)

    def finish():
        me = me_ref[0]
        docs = length_ref.shape[0]
        doc_of = lax.broadcasted_iota(jnp.int32, (docs, rows), 0)
        lower = jnp.zeros((docs, rows), jnp.int32)
        used = jnp.zeros((docs, rows), jnp.int32)
        start = jnp.int32(0)
        for d in range(docs):
            lower = jnp.where(doc_of == d, start, lower)
            used = jnp.where(doc_of == d, jnp.minimum(valid_ref[d], length_ref[d]), used)
            start = start + length_ref[d]
        scale = 1.0 / jnp.sqrt(used.astype(jnp.float32))
        partial = None
        for r in range(halves):
            token = (me ^ (top * r)) * rows + lax.broadcasted_iota(jnp.int32, (docs, rows), 1)
            inside = (token >= lower) & (token < lower + used)
            term = lax.dot_general(
                token_ref[r],
                jnp.where(inside, scale, 0.0),
                (((1,), (1,)), ((), ())),
                precision=lax.Precision.HIGHEST,
                preferred_element_type=jnp.float32,
            )
            partial = term if partial is None else partial + term
        own_q = doc_ref.shape[1]
        for k in range(doc_ref.shape[0]):
            doc_ref[k] = partial[k * own_q : (k + 1) * own_q]

    if steps == 1:
        finish()
    else:
        pl.when(step == steps - 1)(finish)


def score(me, lengths, valid, own, other, products, top, own_q, steps):
    halves, width, rows = own.shape
    docs = lengths.shape[0]
    count = 2 * products.shape[0] // width
    if steps == 1:
        grid = {"in_specs": [SMEM] * 3 + [VMEM] * 3, "out_specs": (VMEM, VMEM)}
    else:
        block = (products.shape[0] // steps, products.shape[1])
        grid = {
            "grid": (steps,),
            "in_specs": [SMEM] * 3 + [VMEM] * 2 + [pl.BlockSpec(block, lambda s: (s, 0))],
            "out_specs": (VMEM, VMEM),
        }
    return pl.pallas_call(
        functools.partial(score_kernel, steps, top),
        out_shape=(
            jax.ShapeDtypeStruct((halves, count, rows), jnp.float32),
            jax.ShapeDtypeStruct((count // own_q, own_q, docs), jnp.float32),
        ),
        scratch_shapes=[pltpu.VMEM((halves, width, rows), jnp.float32)],
        compiler_params=pltpu.CompilerParams(vmem_limit_bytes=32 * MIB),
        cost_estimate=pl.CostEstimate(
            flops=2 * products.shape[0] * products.shape[1],
            bytes_accessed=4 * products.shape[0] * products.shape[1],
            transcendentals=0,
        ),
        **grid,
    )(me, lengths, valid, own, other, products)


def place_kernel(place, top, own_q, me_ref, own_ref, other_ref, out_ref, turned_ref):
    for r, ref in enumerate((own_ref, other_ref)):
        for k, offset in enumerate(place):
            spot = pl.multiple_of((me_ref[0] ^ (offset + top * r)) * own_q, own_q)
            turned_ref[pl.ds(spot, own_q)] = ref[k * own_q : (k + 1) * own_q]
    out_ref[...] = turned_ref[...].T


def place_tokens(me, own, other, place, top, own_q):
    count, rows = own.shape
    return pl.pallas_call(
        functools.partial(place_kernel, place, top, own_q),
        in_specs=[SMEM, VMEM, VMEM],
        out_specs=VMEM,
        out_shape=jax.ShapeDtypeStruct((rows, 2 * count), jnp.float32),
        scratch_shapes=[pltpu.VMEM((2 * count, rows), jnp.float32)],
    )(me, own, other)


def body(size, activations, out_grads, proj_in, proj_out, queries, doc_length, valid_count):
    rows = activations.shape[0]
    width = proj_in.shape[1]
    own_q = queries.shape[0]
    me = lax.axis_index("seq").astype(jnp.int32)[None]
    top = size // 2
    middle = [1 << k for k in range(1, top.bit_length() - 1)]

    panel, place = queries, [0]
    panels = []
    for bit in middle[::-1]:
        got = swap(panel, bit, size)
        place = place + [p ^ bit for p in place]
        panel = jnp.concatenate([panel, got], axis=0)
    panels = [panel, swap(panel, 1, size)]
    place = tuple(place + [p ^ 1 for p in place])

    proj = pltpu.with_memory_space_constraint(proj_out.T, pltpu.HBM)
    spots = [2 * m + top * r for m in range(top // 2) for r in range(2)]
    from_core = swap(grad_blocks(me, proj, out_grads, rows, [s + 1 for s in spots]), 1, size)
    chip_sums = grad_blocks(me, proj, out_grads, rows, spots) + from_core
    sums = chip_sums
    for bit in middle[::-1]:
        half = sums.shape[0] // 2
        sums = sums[:half] + swap(sums[half:], bit, size)
    across = swap(sums, top, size)

    late, _ = lax.optimization_barrier((proj_in, chip_sums))
    act = lax.dot_general(
        late, activations, (((0,), (1,)), ((), ())), preferred_element_type=jnp.float32
    )
    act = jnp.stack([act, swap(act, top, size)])
    steps = max(1, 8 * width * top * own_q * rows // (4 * MIB))
    products = inner(act, panels, steps)
    tokens, doc = score(me, doc_length, valid_count, sums, across, products, top, own_q, steps)
    others = swap(tokens[1], top, size)
    token_scores = place_tokens(me, tokens[0], others, place, top, own_q)
    for bit in [1] + middle:
        half = doc.shape[0] // 2
        if half == 1:
            doc, _ = lax.optimization_barrier((doc, others))
        doc = doc[:half] + swap(doc[half:], bit, size)
    return (token_scores, doc[0].T)


def solution(mesh):
    size = mesh.shape["seq"]
    placed = (
        P(("groups", "seq"), None),
        P("groups", "seq"),
        P(),
        P("seq", None),
        P("seq", None),
        P("groups"),
        P("groups"),
    )
    return jax.shard_map(
        functools.partial(body, size),
        mesh=mesh,
        in_specs=placed,
        out_specs=(P(("groups", "seq"), None), P("groups", "seq")),
        check_vma=False,
    )
```

time: 214 us -> 44 us (0.21)
  waiting for transfers between devices: 186 us -> 14.1 us
  starting transfers between devices: 0.12 us -> 13.8 us
  between operations: 13.9 us -> 0.82 us
  Pallas kernels: 0 us -> 12.3 us
  matrix products: 12.5 us -> 0.88 us
    psum x1 -> x0, waiting for transfers between devices: 88.6 us -> none  [body(): doc_outer = lax.psum(partial_outer, 'seq')]
    reduce_scatter x1 -> x0, waiting for transfers between devices: 57.4 us -> none  [body(): lax.psum_scatter(jnp.dot(out_grads, proj_out, preferred_element_type=jnp....]
    all_gather x1 -> x0, waiting for transfers between devices: 39.1 us -> none  [body(): lax.all_gather(queries, 'seq', axis=0, tiled=True)]
    ppermute x0 -> x12, waiting for transfers between devices: none -> 14.1 us  [swap(): return lax.ppermute(value, 'seq', [(i, i ^ offset) for i in range(size)])]
    ppermute x0 -> x12, starting transfers between devices: none -> 13.8 us  [swap(): return lax.ppermute(value, 'seq', [(i, i ^ offset) for i in range(size)])]
    pallas_call x0 -> x5, Pallas kernels: none -> 12.3 us  [the longest x2 8.86 us: grad_blocks(): pl.pallas_call(functools.partial(grad_kernel, offsets), in_specs=[SMEM, H...]
    dot_general x5 -> x1, matrix products: 12.5 us -> 0.88 us  [body(): lax.dot_general(late, activations, (((0,), (1,)), ((), ())), preferred_el...]
  transfers between devices with their start and end apart: 3 -> 12, of which waited for: 3 -> 8; matrix products, arithmetic and copies ran while one was open for 1% -> 4% of each run, Pallas kernels for 0% -> 25%
where the time goes in v4:
time: 44 us; the launch traced here: 43.8 us
  waiting for transfers between devices  14.1 us (32%)
  starting transfers between devices  13.8 us (31%)
  Pallas kernels  12.3 us (28%)
  local copies, waits for them, and re-layouts  1.29 us (3%)
  matrix products  0.88 us (2%)
  between operations  0.82 us (2%)
  other arithmetic  0.68 us (2%)
    ppermute x12, waiting for transfers between devices, swap(): return lax.ppermute(value, 'seq', [(i, i ^ offset) for i in range(size)])  14.1 us
    ppermute x12, starting transfers between devices, swap(): return lax.ppermute(value, 'seq', [(i, i ^ offset) for i in range(size)])  13.8 us
    pallas_call x2, Pallas kernels, grad_blocks(): pl.pallas_call(functools.partial(grad_kernel, offsets), in_specs=[SMEM, H...  8.86 us
    pallas_call x1, Pallas kernels, place_tokens(): pl.pallas_call(functools.partial(place_kernel, place, top, own_q), in_spe...  1.52 us
    pallas_call x1, Pallas kernels, score(): pl.pallas_call(functools.partial(score_kernel, steps, top), out_shape=(ja...  1.25 us
  transfers between devices with their start and end apart: 12, of which 8 were waited for; matrix products, arithmetic and copies ran while one was open for 4% of the time, Pallas kernels for 25%

profile of v4, /device:TPU:0, one launch (start us, length us, event | category | flops | bytes accessed | tf_op | source)
XLA Modules:
  0.0 43.8 jit_solution(3736009203365436789)
XLA Ops:
  0.6 0.0 copy-start
  0.6 3.1 %collective-permute-start.5 = (bf16[8,4096]{1,0:T(8,128)(2,1)}, bf16[8,4096]{1,0:T(8,128)(2,1)S(1)}, u32[]{:S(2)}, u32[]{:S(2)}) collective-permute-start(bf16[8,4096]{1,0:T(8,128)(2,1)} %param.11), channel_id=1, source_target_pairs={{0,4},{1,5},{2,6},{3,7},{4,0},{5,1},{6,2},{7,3},{8,12},{9,13},{10,... | collective-permute-start | bytes 196616 | tf_op jit(solution)/shard_map/ppermute | solution.py:17
  3.7 0.0 copy-start.4
  3.7 4.4 %shard_map.87 = f32[8,64,128]{2,1,0:T(8,128)S(1)} custom-call(s32[1]{0:T(128)} %bitcast.me_ref, bf16[64,1792]{1,0:T(8,128)(2,1)} %bitcast.14, bf16[2048,1792]{1,0:T(8,128)(2,1)} %grads_ref.3), custom_call_target="tpu_custom_call" | custom-call | flops 234881024 | bytes 3670016 | tf_op jit(solution)/shard_map/pallas_call | solution.py:47
  8.2 0.1 collective-permute-start
  8.3 0.0 copy-done.4
  8.3 4.4 %shard_map.86 = f32[8,64,128]{2,1,0:T(8,128)S(1)} custom-call(s32[1]{0:T(128)} %bitcast.me_ref, bf16[64,1792]{1,0:T(8,128)(2,1)} %bitcast.15, bf16[2048,1792]{1,0:T(8,128)(2,1)} %grads_ref.3), custom_call_target="tpu_custom_call" | custom-call | flops 234881024 | bytes 3670016 | tf_op jit(solution)/shard_map/pallas_call | solution.py:47
  12.7 0.0 copy-start.3
  12.7 0.0 collective-permute-done.5
  12.8 1.6 %collective-permute-start.6 = (bf16[16,4096]{1,0:T(8,128)(2,1)S(1)}, bf16[16,4096]{1,0:T(8,128)(2,1)S(1)}, u32[]{:S(2)}, u32[]{:S(2)}) collective-permute-start(bf16[16,4096]{1,0:T(8,128)(2,1)S(1)} %pad_maximum_fusion), channel_id=1, source_target_pairs={{0,2},{1,3},{2,0},{3,1},{4,6},{5,7},{6,4},{7,5},{8,10},{9,11},{10,... | collective-permute-start | bytes 393224 | tf_op jit(solution)/shard_map/ppermute | solution.py:17
  14.4 0.0 collective-permute-done
  14.4 0.6 %collective-permute-start.1 = (f32[4,64,128]{2,1,0:T(8,128)S(1)}, f32[4,64,128]{2,1,0:T(8,128)S(1)}, u32[]{:S(2)}, u32[]{:S(2)}) collective-permute-start(f32[4,64,128]{2,1,0:T(8,128)S(1)} %slice.49), channel_id=1, source_target_pairs={{0,4},{1,5},{2,6},{3,7},{4,0},{5,1},{6,2},{7,3},{8,12},{9,13},{10,... | collective-permute-start | bytes 393224 | tf_op jit(solution)/shard_map/ppermute | solution.py:17
  15.0 3.7 %collective-permute-done.6 = bf16[16,4096]{1,0:T(8,128)(2,1)S(1)} collective-permute-done((bf16[16,4096]{1,0:T(8,128)(2,1)S(1)}, bf16[16,4096]{1,0:T(8,128)(2,1)S(1)}, u32[]{:S(2)}, u32[]{:S(2)}) %collective-permute-start.6) | collective-permute-done | bytes 131104 | tf_op jit(solution)/shard_map/ppermute | solution.py:17
  18.7 0.1 collective-permute-start.7
  18.8 1.3 %collective-permute-done.1 = f32[4,64,128]{2,1,0:T(8,128)S(1)} collective-permute-done((f32[4,64,128]{2,1,0:T(8,128)S(1)}, f32[4,64,128]{2,1,0:T(8,128)S(1)}, u32[]{:S(2)}, u32[]{:S(2)}) %collective-permute-start.1) | collective-permute-done | bytes 131104 | tf_op jit(solution)/shard_map/ppermute | solution.py:17
  20.1 0.6 %collective-permute-start.2 = (f32[2,64,128]{2,1,0:T(8,128)S(1)}, f32[2,64,128]{2,1,0:T(8,128)S(1)}, u32[]{:S(2)}, u32[]{:S(2)}) collective-permute-start(f32[2,64,128]{2,1,0:T(8,128)S(1)} %slice.51), channel_id=1, source_target_pairs={{0,2},{1,3},{2,0},{3,1},{4,6},{5,7},{6,4},{7,5},{8,10},{9,11},{10,... | collective-permute-start | bytes 196616 | tf_op jit(solution)/shard_map/ppermute | solution.py:17
  20.7 0.0 copy-done
  20.7 0.0 copy-done.3
  20.7 0.9 %fusion = f32[64,128]{1,0:T(8,128)S(1)} fusion(bf16[8192,64]{0,1:T(8,128)(2,1)S(1)} %copy-done.3, bf16[128,8192]{1,0:T(8,128)(2,1)S(1)} %copy-done), kind=kOutput, calls=%fused_computation.12 | convolution fusion | flops 134217728 | bytes 3178496 | tf_op jit(solution)/shard_map/dot_general | solution.py:257
  21.6 2.7 %collective-permute-start.4 = (f32[64,128]{1,0:T(8,128)S(1)}, f32[64,128]{1,0:T(8,128)S(1)}, u32[]{:S(2)}, u32[]{:S(2)}) collective-permute-start(f32[64,128]{1,0:T(8,128)S(1)} %fusion), channel_id=1, source_target_pairs={{0,8},{1,9},{2,10},{3,11},{4,12},{5,13},{6,14},{7,15},{8,0},{9,1},... | collective-permute-start | bytes 98312 | tf_op jit(solution)/shard_map/ppermute | solution.py:17
  24.2 0.2 collective-permute-done.2
  24.5 2.6 %collective-permute-start.3 = (f32[2,64,128]{2,1,0:T(8,128)S(1)}, f32[2,64,128]{2,1,0:T(8,128)S(1)}, u32[]{:S(2)}, u32[]{:S(2)}) collective-permute-start(f32[2,64,128]{2,1,0:T(8,128)S(1)} %slice_add_fusion.1.own_ref), channel_id=1, source_target_pairs={{0,8},{1,9},{2,10},{3,11},{4,12},{5,13},{6,14},{7,15},{8,0},{9,1},... | collective-permute-start | bytes 196616 | tf_op jit(solution)/shard_map/ppermute | solution.py:17
  27.1 0.0 collective-permute-done.4
  27.1 0.0 copy-start.1
  27.1 0.0 copy-start.2
  27.1 0.0 collective-permute-done.7.refs_1_
  27.2 0.7 %shard_map.88.inner_ref = f32[2048,512]{1,0:T(8,128)S(1)} custom-call(f32[2,64,128]{2,1,0:T(8,128)S(1)} %pad_maximum_fusion.1.act_ref, bf16[32,4096]{1,0:T(8,128)(2,1)S(1)} %constant_dynamic-update-slice_fusion.refs_0_, bf16[32,4096]{1,0:T(8,128)(2,1)S(1)} %collective-permute-done.7.refs_1_), custom_call_target="tpu_custom_call" | custom-call | flops 536870912 | bytes 4194304 | tf_op jit(solution)/shard_map/pallas_call | solution.py:102
  27.9 2.5 %collective-permute-done.3.other_ref = f32[2,64,128]{2,1,0:T(8,128)S(1)} collective-permute-done((f32[2,64,128]{2,1,0:T(8,128)S(1)}, f32[2,64,128]{2,1,0:T(8,128)S(1)}, u32[]{:S(2)}, u32[]{:S(2)}) %collective-permute-start.3) | collective-permute-done | bytes 65568 | tf_op jit(solution)/shard_map/ppermute | solution.py:17
  30.4 0.0 copy-done.1
  30.4 0.0 copy-done.2
  30.4 1.3 %shard_map.89 = (f32[2,64,128]{2,1,0:T(8,128)S(1)}, f32[8,8,16]{2,1,0:T(8,128)S(1)}) custom-call(s32[1]{0:T(128)} %bitcast.me_ref, s32[16]{0:T(128)S(1)} %copy-done.1, s32[16]{0:T(128)S(1)} %copy-done.2, f32[2,64,128]{2,1,0:T(8,128)S(1)} %slice_add_fusion.1.own_ref, f32[2,64,128]{2,1,0:T(8,128)S(1)} %collective-permute-done.3.other_ref, ...), custom_call_target="tpu_custom_call" | custom-call | flops 2097152 | bytes 4194304 | tf_op jit(solution)/shard_map/pallas_call | solution.py:193
  31.6 0.1 collective-permute-start.9
  31.7 1.2 %collective-permute-done.9 = f32[4,8,16]{2,1,0:T(8,128)S(1)} collective-permute-done((f32[4,8,16]{2,1,0:T(8,128)S(1)}, f32[4,8,16]{2,1,0:T(8,128)S(1)}, u32[]{:S(2)}, u32[]{:S(2)}) %collective-permute-start.9) | collective-permute-done | bytes 2080 | tf_op jit(solution)/shard_map/ppermute | solution.py:17
  32.9 1.3 %collective-permute-start.10 = (f32[2,8,16]{2,1,0:T(8,128)S(1)}, f32[2,8,16]{2,1,0:T(8,128)S(1)}, u32[]{:S(2)}, u32[]{:S(2)}) collective-permute-start(f32[2,8,16]{2,1,0:T(8,128)S(1)} %slice.53), channel_id=1, source_target_pairs={{0,2},{1,3},{2,0},{3,1},{4,6},{5,7},{6,4},{7,5},{8,10},{9,11},{10,... | collective-permute-start | bytes 3080 | tf_op jit(solution)/shard_map/ppermute | solution.py:17
  34.2 0.6 %slice_bitcast_fusion = (f32[64,128]{1,0:T(8,128)S(1)}, f32[64,128]{1,0:T(8,128)}) fusion(f32[2,64,128]{2,1,0:T(8,128)S(1)} %get-tuple-element.7), kind=kLoop, calls=%fused_computation.4 | loop fusion | bytes 131072 | tf_op jit(solution)/shard_map/squeeze | solution.py:264
  34.8 1.1 %collective-permute-start.8 = (f32[64,128]{1,0:T(8,128)S(1)}, f32[64,128]{1,0:T(8,128)S(1)}, u32[]{:S(2)}, u32[]{:S(2)}) collective-permute-start(f32[64,128]{1,0:T(8,128)S(1)} %get-tuple-element.10), channel_id=1, source_target_pairs={{0,8},{1,9},{2,10},{3,11},{4,12},{5,13},{6,14},{7,15},{8,0},{9,1},... | collective-permute-start | bytes 98312 | tf_op jit(solution)/shard_map/ppermute | solution.py:17
  35.9 0.6 %collective-permute-done.10 = f32[2,8,16]{2,1,0:T(8,128)S(1)} collective-permute-done((f32[2,8,16]{2,1,0:T(8,128)S(1)}, f32[2,8,16]{2,1,0:T(8,128)S(1)}, u32[]{:S(2)}, u32[]{:S(2)}) %collective-permute-start.10) | collective-permute-done | bytes 1056 | tf_op jit(solution)/shard_map/ppermute | solution.py:17
  36.5 3.1 %collective-permute-done.8.other_ref = f32[64,128]{1,0:T(8,128)S(1)} collective-permute-done((f32[64,128]{1,0:T(8,128)S(1)}, f32[64,128]{1,0:T(8,128)S(1)}, u32[]{:S(2)}, u32[]{:S(2)}) %collective-permute-start.8) | collective-permute-done | bytes 32800 | tf_op jit(solution)/shard_map/ppermute | solution.py:17
  39.6 0.0 copy-start.5
  39.6 0.0 collective-permute-start.11
  39.6 0.6 %copy-done.5 = f32[64,128]{1,0:T(8,128)} copy-done((f32[64,128]{1,0:T(8,128)}, f32[64,128]{1,0:T(8,128)S(1)}, u32[]{:S(2)}) %copy-start.5) | copy-done | bytes 32792
  40.2 1.5 %shard_map.90 = f32[128,128]{1,0:T(8,128)} custom-call(s32[1]{0:T(128)} %bitcast.me_ref, f32[64,128]{1,0:T(8,128)} %get-tuple-element.11.own_ref, f32[64,128]{1,0:T(8,128)} %copy-done.5), custom_call_target="tpu_custom_call" | custom-call | tf_op jit(solution)/shard_map/pallas_call | solution.py:220
  41.8 1.5 %collective-permute-done.11 = f32[1,8,16]{2,1,0:T(8,128)S(1)} collective-permute-done((f32[1,8,16]{2,1,0:T(8,128)S(1)}, f32[1,8,16]{2,1,0:T(8,128)S(1)}, u32[]{:S(2)}, u32[]{:S(2)}) %collective-permute-start.11) | collective-permute-done | bytes 544 | tf_op jit(solution)/shard_map/ppermute | solution.py:17
  43.2 0.6 %add_bitcast_fusion = f32[16,8]{0,1:T(8,128)} fusion(f32[1,8,16]{2,1,0:T(8,128)S(1)} %collective-permute-done.11, f32[2,8,16]{2,1,0:T(8,128)S(1)} %slice_add_fusion.3), kind=kLoop, calls=%fused_computation.11 | loop fusion | flops 128 | bytes 1536 | tf_op jit(solution)/shard_map/transpose | solution.py:271
  (15 shorter events, 0.1 us)
Async XLA Ops:
  0.6 20.1 %copy-start = (bf16[128,8192]{1,0:T(8,128)(2,1)S(1)}, bf16[128,8192]{1,0:T(8,128)(2,1)}, u32[]{:S(2)}) copy-start(bf16[128,8192]{1,0:T(8,128)(2,1)} %param.7) | copy-start | bytes 6291460
  0.6 12.1 %collective-permute-start.5 = (bf16[8,4096]{1,0:T(8,128)(2,1)}, bf16[8,4096]{1,0:T(8,128)(2,1)S(1)}, u32[]{:S(2)}, u32[]{:S(2)}) collective-permute-start(bf16[8,4096]{1,0:T(8,128)(2,1)} %param.11), channel_id=1, source_target_pairs={{0,4},{1,5},{2,6},{3,7},{4,0},{5,1},{6,2},{7,3},{8,12},{9,13},{10,... | collective-permute-start | bytes 196616 | tf_op jit(solution)/shard_map/ppermute | solution.py:17
  3.7 4.5 %copy-start.4 = (bf16[8,4096]{1,0:T(8,128)(2,1)S(1)}, bf16[8,4096]{1,0:T(8,128)(2,1)}, u32[]{:S(2)}) copy-start(bf16[8,4096]{1,0:T(8,128)(2,1)} %param.11) | copy-start | bytes 196612
  8.2 6.2 %collective-permute-start = (f32[8,64,128]{2,1,0:T(8,128)S(1)}, f32[8,64,128]{2,1,0:T(8,128)S(1)}, u32[]{:S(2)}, u32[]{:S(2)}) collective-permute-start(f32[8,64,128]{2,1,0:T(8,128)S(1)} %shard_map.87), channel_id=1, source_target_pairs={{0,1},{1,0},{2,3},{3,2},{4,5},{5,4},{6,7},{7,6},{8,9},{9,8},{10,11... | collective-permute-start | bytes 786440 | tf_op jit(solution)/shard_map/ppermute | solution.py:17
  12.7 8.0 %copy-start.3 = (bf16[8192,64]{0,1:T(8,128)(2,1)S(1)}, bf16[8192,64]{0,1:T(8,128)(2,1)}, u32[]{:S(2)}) copy-start(bf16[8192,64]{0,1:T(8,128)(2,1)} %param.9) | copy-start | bytes 3145732
  12.8 5.9 %collective-permute-start.6 = (bf16[16,4096]{1,0:T(8,128)(2,1)S(1)}, bf16[16,4096]{1,0:T(8,128)(2,1)S(1)}, u32[]{:S(2)}, u32[]{:S(2)}) collective-permute-start(bf16[16,4096]{1,0:T(8,128)(2,1)S(1)} %pad_maximum_fusion), channel_id=1, source_target_pairs={{0,2},{1,3},{2,0},{3,1},{4,6},{5,7},{6,4},{7,5},{8,10},{9,11},{10,... | collective-permute-start | bytes 393224 | tf_op jit(solution)/shard_map/ppermute | solution.py:17
  14.4 5.7 %collective-permute-start.1 = (f32[4,64,128]{2,1,0:T(8,128)S(1)}, f32[4,64,128]{2,1,0:T(8,128)S(1)}, u32[]{:S(2)}, u32[]{:S(2)}) collective-permute-start(f32[4,64,128]{2,1,0:T(8,128)S(1)} %slice.49), channel_id=1, source_target_pairs={{0,4},{1,5},{2,6},{3,7},{4,0},{5,1},{6,2},{7,3},{8,12},{9,13},{10,... | collective-permute-start | bytes 393224 | tf_op jit(solution)/shard_map/ppermute | solution.py:17
  18.7 8.4 %collective-permute-start.7 = (bf16[32,4096]{1,0:T(8,128)(2,1)S(1)}, bf16[32,4096]{1,0:T(8,128)(2,1)S(1)}, u32[]{:S(2)}, u32[]{:S(2)}) collective-permute-start(bf16[32,4096]{1,0:T(8,128)(2,1)S(1)} %constant_dynamic-update-slice_fusion.refs_0_), channel_id=1, source_target_pairs={{0,1},{1,0},{2,3},{3,2},{4,5},{5,4},{6,7},{7,6},{8,9},{9,8},{10,11... | collective-permute-start | bytes 786440 | tf_op jit(solution)/shard_map/ppermute | solution.py:17
  20.1 4.3 %collective-permute-start.2 = (f32[2,64,128]{2,1,0:T(8,128)S(1)}, f32[2,64,128]{2,1,0:T(8,128)S(1)}, u32[]{:S(2)}, u32[]{:S(2)}) collective-permute-start(f32[2,64,128]{2,1,0:T(8,128)S(1)} %slice.51), channel_id=1, source_target_pairs={{0,2},{1,3},{2,0},{3,1},{4,6},{5,7},{6,4},{7,5},{8,10},{9,11},{10,... | collective-permute-start | bytes 196616 | tf_op jit(solution)/shard_map/ppermute | solution.py:17
  21.6 5.5 %collective-permute-start.4 = (f32[64,128]{1,0:T(8,128)S(1)}, f32[64,128]{1,0:T(8,128)S(1)}, u32[]{:S(2)}, u32[]{:S(2)}) collective-permute-start(f32[64,128]{1,0:T(8,128)S(1)} %fusion), channel_id=1, source_target_pairs={{0,8},{1,9},{2,10},{3,11},{4,12},{5,13},{6,14},{7,15},{8,0},{9,1},... | collective-permute-start | bytes 98312 | tf_op jit(solution)/shard_map/ppermute | solution.py:17
  24.5 5.9 %collective-permute-start.3 = (f32[2,64,128]{2,1,0:T(8,128)S(1)}, f32[2,64,128]{2,1,0:T(8,128)S(1)}, u32[]{:S(2)}, u32[]{:S(2)}) collective-permute-start(f32[2,64,128]{2,1,0:T(8,128)S(1)} %slice_add_fusion.1.own_ref), channel_id=1, source_target_pairs={{0,8},{1,9},{2,10},{3,11},{4,12},{5,13},{6,14},{7,15},{8,0},{9,1},... | collective-permute-start | bytes 196616 | tf_op jit(solution)/shard_map/ppermute | solution.py:17
  27.1 3.2 %copy-start.1 = (s32[16]{0:T(128)S(1)}, s32[16]{0:T(128)}, u32[]{:S(2)}) copy-start(s32[16]{0:T(128)} %length_ref.1) | copy-start | bytes 196
  27.1 3.2 %copy-start.2 = (s32[16]{0:T(128)S(1)}, s32[16]{0:T(128)}, u32[]{:S(2)}) copy-start(s32[16]{0:T(128)} %valid_ref.1) | copy-start | bytes 196
  31.6 1.2 %collective-permute-start.9 = (f32[4,8,16]{2,1,0:T(8,128)S(1)}, f32[4,8,16]{2,1,0:T(8,128)S(1)}, u32[]{:S(2)}, u32[]{:S(2)}) collective-permute-start(f32[4,8,16]{2,1,0:T(8,128)S(1)} %slice.43), channel_id=1, source_target_pairs={{0,1},{1,0},{2,3},{3,2},{4,5},{5,4},{6,7},{7,6},{8,9},{9,8},{10,11... | collective-permute-start | bytes 6152 | tf_op jit(solution)/shard_map/ppermute | solution.py:17
  32.9 3.7 %collective-permute-start.10 = (f32[2,8,16]{2,1,0:T(8,128)S(1)}, f32[2,8,16]{2,1,0:T(8,128)S(1)}, u32[]{:S(2)}, u32[]{:S(2)}) collective-permute-start(f32[2,8,16]{2,1,0:T(8,128)S(1)} %slice.53), channel_id=1, source_target_pairs={{0,2},{1,3},{2,0},{3,1},{4,6},{5,7},{6,4},{7,5},{8,10},{9,11},{10,... | collective-permute-start | bytes 3080 | tf_op jit(solution)/shard_map/ppermute | solution.py:17
  34.8 4.8 %collective-permute-start.8 = (f32[64,128]{1,0:T(8,128)S(1)}, f32[64,128]{1,0:T(8,128)S(1)}, u32[]{:S(2)}, u32[]{:S(2)}) collective-permute-start(f32[64,128]{1,0:T(8,128)S(1)} %get-tuple-element.10), channel_id=1, source_target_pairs={{0,8},{1,9},{2,10},{3,11},{4,12},{5,13},{6,14},{7,15},{8,0},{9,1},... | collective-permute-start | bytes 98312 | tf_op jit(solution)/shard_map/ppermute | solution.py:17
  39.6 0.6 %copy-start.5 = (f32[64,128]{1,0:T(8,128)}, f32[64,128]{1,0:T(8,128)S(1)}, u32[]{:S(2)}) copy-start(f32[64,128]{1,0:T(8,128)S(1)} %collective-permute-done.8.other_ref) | copy-start | bytes 98308
  39.6 3.6 %collective-permute-start.11 = (f32[1,8,16]{2,1,0:T(8,128)S(1)}, f32[1,8,16]{2,1,0:T(8,128)S(1)}, u32[]{:S(2)}, u32[]{:S(2)}) collective-permute-start(f32[1,8,16]{2,1,0:T(8,128)S(1)} %slice.47), channel_id=1, source_target_pairs={{0,4},{1,5},{2,6},{3,7},{4,0},{5,1},{6,2},{7,3},{8,12},{9,13},{10,... | collective-permute-start | bytes 1544 | tf_op jit(solution)/shard_map/ppermute | solution.py:17

commit v5 on v4

v5 whole, which is shorter than its diff:
```python
import functools

import jax
import jax.numpy as jnp
from jax import lax
from jax.experimental import pallas as pl
from jax.experimental.pallas import tpu as pltpu
from jax.sharding import PartitionSpec as P

MIB = 1 << 20
SMEM = pl.BlockSpec(memory_space=pltpu.SMEM)
VMEM = pl.BlockSpec(memory_space=pltpu.VMEM)
HBM = pl.BlockSpec(memory_space=pltpu.HBM)


def swap(value, offset, size):
    return lax.ppermute(value, "seq", [(i, i ^ offset) for i in range(size)])


def grad_kernel(offsets, me_ref, proj_ref, grads_ref, out_ref, proj_buf, table, grads_buf, proj_sem, sems):
    halves, total, depth = grads_buf.shape
    count = len(offsets) // halves
    rows = total // count
    width = proj_buf.shape[0]
    load = pltpu.make_async_copy(proj_ref, proj_buf, proj_sem)
    load.start()
    copies = []
    for k, offset in enumerate(offsets):
        first = pl.multiple_of((me_ref[0] ^ offset) * rows, rows)
        copy = pltpu.make_async_copy(
            grads_ref.at[pl.ds(first, rows)],
            grads_buf.at[k % halves, pl.ds((k // halves) * rows, rows)],
            sems.at[k],
        )
        copy.start()
        copies.append(copy)
    load.wait()
    turned = proj_buf[...].T
    none = jnp.zeros_like(turned)
    for r in range(halves):
        table[r] = jnp.concatenate([turned if c == r else none for c in range(halves)], axis=1)
    for k in range(0, count, 2):
        for copy in copies[k * halves : (k + 2) * halves]:
            copy.wait()
        made = None
        for r in range(halves):
            part = jnp.dot(
                grads_buf[r, k * rows : (k + 2) * rows],
                table[r],
                preferred_element_type=jnp.float32,
            )
            made = part if made is None else made + part
        out_ref[k] = made[:rows]
        out_ref[k + 1] = made[rows:]


def grad_blocks(me, proj, out_grads, rows, offsets):
    width, depth = proj.shape
    count = len(offsets) // 2
    return pl.pallas_call(
        functools.partial(grad_kernel, offsets),
        in_specs=[SMEM, HBM, HBM],
        out_specs=VMEM,
        out_shape=jax.ShapeDtypeStruct((count, rows, 2 * width), jnp.float32),
        scratch_shapes=[
            pltpu.VMEM((width, depth), jnp.bfloat16),
            pltpu.VMEM((2, depth, 2 * width), jnp.bfloat16),
            pltpu.VMEM((2, count * rows, depth), jnp.bfloat16),
            pltpu.SemaphoreType.DMA,
            pltpu.SemaphoreType.DMA((2 * count,)),
        ],
        compiler_params=pltpu.CompilerParams(vmem_limit_bytes=52 * MIB),
        cost_estimate=pl.CostEstimate(
            flops=4 * count * rows * depth * width,
            bytes_accessed=4 * count * rows * depth,
            transcendentals=0,
        ),
    )(me, proj, out_grads)


def inner_kernel(pieces, act_ref, *refs):
    out_ref = refs[pieces]
    columns = []
    for r in range(act_ref.shape[0]):
        act = act_ref[r]
        high = act.astype(jnp.bfloat16)
        low = (act - high.astype(jnp.float32)).astype(jnp.bfloat16)
        none = jnp.zeros_like(high)
        columns.append(jnp.concatenate([high, none, low, none], axis=0))
        columns.append(jnp.concatenate([none, high, none, low], axis=0))
    table = jnp.concatenate(columns, axis=1)
    pair = 2 * act_ref.shape[1]
    rows = []
    for k in range(refs[0].shape[1] // pair):
        for ref in refs[:pieces]:
            rows.append(ref[:, k * pair : (k + 1) * pair])
    left = jnp.concatenate(rows, axis=0)
    left = jnp.concatenate([left, left], axis=1)
    out_ref[...] = jnp.dot(left, table, preferred_element_type=jnp.float32)


def inner(act, panels, steps):
    halves, width, rows = act.shape
    count = sum(p.shape[0] for p in panels)
    pairs = panels[0].shape[1] // (2 * width)
    total = pairs * count
    if steps == 1:
        grid = {"in_specs": [VMEM] * (1 + len(panels)), "out_specs": VMEM}
    else:
        grid = {
            "grid": (steps,),
            "in_specs": [VMEM]
            + [pl.BlockSpec((p.shape[0], p.shape[1] // steps), lambda s: (0, s)) for p in panels],
            "out_specs": pl.BlockSpec((total // steps, 2 * halves * rows), lambda s: (s, 0)),
        }
    return pl.pallas_call(
        functools.partial(inner_kernel, len(panels)),
        out_shape=jax.ShapeDtypeStruct((total, 2 * halves * rows), jnp.float32),
        compiler_params=pltpu.CompilerParams(vmem_limit_bytes=32 * MIB),
        cost_estimate=pl.CostEstimate(
            flops=16 * total * width * halves * rows,
            bytes_accessed=8 * total * halves * rows,
            transcendentals=0,
        ),
        **grid,
    )(act, *panels)


def score_kernel(
    steps, split, me_ref, length_ref, valid_ref, own_ref, other_ref, inner_ref, own_tok, other_tok, doc_ref, grad_ref
):
    rows, wide = own_ref.shape
    halves, width = 2, wide // 2
    count = own_tok.shape[0]
    pairs = inner_ref.shape[0] // count
    step = pl.program_id(0) if steps > 1 else 0
    tokens = (own_tok, other_tok)

    def begin():
        other = other_ref[...].T
        grad_ref[...] = own_ref[...].T + jnp.concatenate([other[width:], other[:width]], axis=0)

    if steps == 1:
        begin()
    else:
        pl.when(step == 0)(begin)

    for r in range(halves):
        total = None
        for k in range(pairs):
            for parity in range(2):
                feature = 2 * k + parity
                if steps == 1:
                    line = grad_ref[r * width + feature : r * width + feature + 1]
                else:
                    line = grad_ref[pl.ds(r * width + 2 * pairs * step + feature, 1)]
                column = (2 * r + parity) * rows
                term = line * inner_ref[k * count : (k + 1) * count, column : column + rows]
                total = term if total is None else total + term
        if steps == 1:
            tokens[r][...] = total
        else:
            tokens[r][...] = jnp.where(step == 0, total, tokens[r][...] + total)

    def finish():
        me = me_ref[0]
        docs = length_ref.shape[0]
        doc_of = lax.broadcasted_iota(jnp.int32, (docs, rows), 0)
        lower = jnp.zeros((docs, rows), jnp.int32)
        upper = jnp.zeros((docs, rows), jnp.int32)
        start = jnp.int32(0)
        for d in range(docs):
            lower = jnp.where(doc_of == d, start, lower)
            used = jnp.minimum(valid_ref[d], length_ref[d])
            upper = jnp.where(doc_of == d, start + used, upper)
            start = start + length_ref[d]
        members, parts = [], []
        for r in range(halves):
            token = (me ^ (split * r)) * rows + lax.broadcasted_iota(jnp.int32, (docs, rows), 1)
            inside = (token >= lower) & (token < upper)
            members.append(jnp.where(inside, 1.0, 0.0).astype(jnp.bfloat16))
            left = tokens[r][...]
            for _ in range(3):
                part = left.astype(jnp.bfloat16)
                left = left - part.astype(jnp.float32)
                parts.append(part)
        partial = lax.dot_general(
            jnp.concatenate(parts, axis=1),
            jnp.concatenate([m for m in members for _ in range(3)], axis=1),
            (((1,), (1,)), ((), ())),
            preferred_element_type=jnp.float32,
        )
        own_q = doc_ref.shape[1]
        for k in range(doc_ref.shape[0]):
            doc_ref[k] = partial[k * own_q : (k + 1) * own_q]

    if steps == 1:
        finish()
    else:
        pl.when(step == steps - 1)(finish)


def score(me, lengths, valid, own, other, products, split, own_q, steps):
    rows, wide = own.shape
    docs = lengths.shape[0]
    count = 4 * products.shape[0] // wide
    if steps == 1:
        grid = {"in_specs": [SMEM] * 3 + [VMEM] * 3, "out_specs": (VMEM,) * 3}
    else:
        block = (products.shape[0] // steps, products.shape[1])
        grid = {
            "grid": (steps,),
            "in_specs": [SMEM] * 3 + [VMEM] * 2 + [pl.BlockSpec(block, lambda s: (s, 0))],
            "out_specs": (VMEM,) * 3,
        }
    return pl.pallas_call(
        functools.partial(score_kernel, steps, split),
        out_shape=(
            jax.ShapeDtypeStruct((count, rows), jnp.float32),
            jax.ShapeDtypeStruct((count, rows), jnp.float32),
            jax.ShapeDtypeStruct((count // own_q, own_q, docs), jnp.float32),
        ),
        scratch_shapes=[pltpu.VMEM((wide, rows), jnp.float32)],
        compiler_params=pltpu.CompilerParams(vmem_limit_bytes=32 * MIB),
        cost_estimate=pl.CostEstimate(
            flops=2 * products.shape[0] * products.shape[1],
            bytes_accessed=4 * products.shape[0] * products.shape[1],
            transcendentals=0,
        ),
        **grid,
    )(me, lengths, valid, own, other, products)


def last_kernel(
    place, split, me_ref, length_ref, valid_ref, own_ref, other_ref, doc_ref, more_ref, token_out, doc_out, turned_ref
):
    own_q, docs = doc_out.shape
    for r, ref in enumerate((own_ref, other_ref)):
        for k, offset in enumerate(place):
            spot = pl.multiple_of((me_ref[0] ^ (offset + split * r)) * own_q, own_q)
            turned_ref[pl.ds(spot, own_q)] = ref[k * own_q : (k + 1) * own_q]
    token_out[...] = turned_ref[...].T
    doc_of = lax.broadcasted_iota(jnp.int32, (own_q, docs), 1)
    used = jnp.zeros((own_q, docs), jnp.int32)
    for d in range(docs):
        used = jnp.where(doc_of == d, jnp.minimum(valid_ref[d], length_ref[d]), used)
    doc_out[...] = (doc_ref[0] + more_ref[0]) * (1.0 / jnp.sqrt(used.astype(jnp.float32)))


def last(me, lengths, valid, own, other, doc, more, place, split):
    count, rows = own.shape
    _, own_q, docs = doc.shape
    return pl.pallas_call(
        functools.partial(last_kernel, place, split),
        in_specs=[SMEM] * 3 + [VMEM] * 4,
        out_specs=(VMEM, VMEM),
        out_shape=(
            jax.ShapeDtypeStruct((rows, 2 * count), jnp.float32),
            jax.ShapeDtypeStruct((own_q, docs), jnp.float32),
        ),
        scratch_shapes=[pltpu.VMEM((2 * count, rows), jnp.float32)],
    )(me, lengths, valid, own, other, doc, more)


def offset_of(number, bits):
    last_bit = len(bits) - 1
    return sum(bit for k, bit in enumerate(bits) if (number >> (last_bit - k)) & 1)


def body(size, activations, out_grads, proj_in, proj_out, queries, doc_length, valid_count):
    rows = activations.shape[0]
    width = proj_in.shape[1]
    own_q = queries.shape[0]
    me = lax.axis_index("seq").astype(jnp.int32)[None]
    split = size // 4
    middle = [1 << k for k in range(1, size.bit_length() - 1) if 1 << k != split]

    panel, place = queries, [0]
    got = swap(panel, middle[-1], size)

    proj = pltpu.with_memory_space_constraint(proj_out.T, pltpu.HBM)
    spots = [offset_of(m, middle) + split * r for m in range(size // 4) for r in range(2)]
    from_core = swap(grad_blocks(me, proj, out_grads, rows, [s + 1 for s in spots]), 1, size)
    sums = grad_blocks(me, proj, out_grads, rows, spots) + from_core
    late, _ = lax.optimization_barrier((proj_in, sums))
    for k, bit in enumerate(middle):
        half = sums.shape[0] // 2
        sent = swap(sums[half:].astype(jnp.bfloat16), bit, size)
        sums = sums[:half] + sent.astype(jnp.float32)
        if k == 0:
            got, _ = lax.optimization_barrier((got, sums))
    own = sums[0]
    across = swap(own, split, size)

    panel = jnp.concatenate([panel, got], axis=0)
    place = [0, middle[-1]]
    for bit in middle[-2::-1]:
        panel = jnp.concatenate([panel, swap(panel, bit, size)], axis=0)
        place = place + [p ^ bit for p in place]
    panels = [panel, swap(panel, 1, size)]
    place = tuple(place + [p ^ 1 for p in place])

    act = lax.dot_general(
        late, activations, (((0,), (1,)), ((), ())), preferred_element_type=jnp.float32
    )
    act = jnp.stack([act, swap(act, split, size)])
    steps = max(1, 4 * width * size * own_q * rows // (4 * MIB))
    products = inner(act, panels, steps)
    mine, theirs, doc = score(
        me, doc_length, valid_count, own, across, products, split, own_q, steps
    )
    others = swap(theirs, split, size)
    bits = [1] + middle
    for bit in bits[:-1]:
        half = doc.shape[0] // 2
        doc = doc[:half] + swap(doc[half:], bit, size)
    more = swap(doc[1:], bits[-1], size)
    token_scores, doc = last(
        me, doc_length, valid_count, mine, others, doc[:1], more, place, split
    )
    return (token_scores, doc.T)


def solution(mesh):
    size = mesh.shape["seq"]
    placed = (
        P(("groups", "seq"), None),
        P("groups", "seq"),
        P(),
        P("seq", None),
        P("seq", None),
        P("groups"),
        P("groups"),
    )
    return jax.shard_map(
        functools.partial(body, size),
        mesh=mesh,
        in_specs=placed,
        out_specs=(P(("groups", "seq"), None), P("groups", "seq")),
        check_vma=False,
    )
```

time: 44 us -> 41.6 us (0.945)
  Pallas kernels: 12.3 us -> 10.5 us
  waiting for transfers between devices: 14.1 us -> 13.2 us
  local copies, waits for them, and re-layouts: 1.29 us -> 1.91 us
  other arithmetic: 0.68 us -> 0.08 us
    pallas_call x2, Pallas kernels: 8.86 us -> 7.19 us  [grad_blocks(): pl.pallas_call(functools.partial(grad_kernel, offsets), in_specs=[SMEM, H...]
    ppermute x12, waiting for transfers between devices: 14.1 us -> 13.2 us  [swap(): return lax.ppermute(value, 'seq', [(i, i ^ offset) for i in range(size)])]
    unnamed x14 -> x18, local copies, waits for them, and re-layouts: 0.64 us -> 1.28 us
    squeeze x1 -> x0, local copies, waits for them, and re-layouts: 0.61 us -> none  [body(): others = swap(tokens[1], top, size)]
    slice x2 -> x3, local copies, waits for them, and re-layouts: 0.02 us -> 0.62 us  [the longest x1 0.6 us: body(): more = swap(doc[1:], bits[-1], size)]
    transpose x1 -> x0, other arithmetic: 0.6 us -> none  [body(): return (token_scores, doc[0].T)]
  transfers between devices with their start and end apart: 12 -> 12, of which waited for: 8 -> 7; matrix products, arithmetic and copies ran while one was open for 4% -> 4% of each run, Pallas kernels for 25% -> 19%
where the time goes in v5:
time: 41.6 us; the launch traced here: 41.4 us
  starting transfers between devices  14 us (34%)
  waiting for transfers between devices  13.2 us (32%)
  Pallas kernels  10.5 us (25%)
  local copies, waits for them, and re-layouts  1.91 us (5%)
  matrix products  0.88 us (2%)
  between operations  0.82 us (2%)
    ppermute x12, starting transfers between devices, swap(): return lax.ppermute(value, 'seq', [(i, i ^ offset) for i in range(size)])  14 us
    ppermute x12, waiting for transfers between devices, swap(): return lax.ppermute(value, 'seq', [(i, i ^ offset) for i in range(size)])  13.2 us
    pallas_call x2, Pallas kernels, grad_blocks(): pl.pallas_call(functools.partial(grad_kernel, offsets), in_specs=[SMEM, H...  7.19 us
    pallas_call x1, Pallas kernels, last(): pl.pallas_call(functools.partial(last_kernel, place, split), in_specs=[SM...  1.56 us
    unnamed x18, local copies, waits for them, and re-layouts  1.28 us
    pallas_call x1, Pallas kernels, score(): pl.pallas_call(functools.partial(score_kernel, steps, split), out_shape=(...  1.08 us
    dot_general x1, matrix products, body(): lax.dot_general(late, activations, (((0,), (1,)), ((), ())), preferred_el...  0.88 us
  transfers between devices with their start and end apart: 12, of which 7 were waited for; matrix products, arithmetic and copies ran while one was open for 4% of the time, Pallas kernels for 19%

profile of v5, /device:TPU:0, one launch (start us, length us, event | category | flops | bytes accessed | tf_op | source)
XLA Modules:
  0.0 41.4 jit_solution(1852317432471425706)
XLA Ops:
  0.6 0.0 copy-start
  0.6 4.1 %collective-permute-start.5 = (bf16[8,4096]{1,0:T(8,128)(2,1)}, bf16[8,4096]{1,0:T(8,128)(2,1)S(1)}, u32[]{:S(2)}, u32[]{:S(2)}) collective-permute-start(bf16[8,4096]{1,0:T(8,128)(2,1)} %param.11), channel_id=1, source_target_pairs={{0,8},{1,9},{2,10},{3,11},{4,12},{5,13},{6,14},{7,15},{8,0},{9,1},... | collective-permute-start | bytes 196616 | tf_op jit(solution)/shard_map/ppermute | solution.py:17
  4.7 3.6 %shard_map.87 = f32[4,128,128]{2,1,0:T(8,128)S(1)} custom-call(s32[1]{0:T(128)} %bitcast.me_ref, bf16[64,1792]{1,0:T(8,128)(2,1)} %bitcast.9, bf16[2048,1792]{1,0:T(8,128)(2,1)} %grads_ref.3), custom_call_target="tpu_custom_call" | custom-call | flops 234881024 | bytes 3670016 | tf_op jit(solution)/shard_map/pallas_call | solution.py:60
  8.3 0.0 copy-start.5
  8.3 0.0 copy-start.4
  8.3 0.1 collective-permute-start
  8.4 3.6 %shard_map.86 = f32[4,128,128]{2,1,0:T(8,128)S(1)} custom-call(s32[1]{0:T(128)} %bitcast.me_ref, bf16[64,1792]{1,0:T(8,128)(2,1)} %bitcast.10, bf16[2048,1792]{1,0:T(8,128)(2,1)} %grads_ref.3), custom_call_target="tpu_custom_call" | custom-call | flops 234881024 | bytes 3670016 | tf_op jit(solution)/shard_map/pallas_call | solution.py:60
  12.1 0.0 copy-done.5
  12.1 0.0 collective-permute-done
  12.1 1.6 %collective-permute-start.1 = (bf16[2,128,128]{2,1,0:T(8,128)(2,1)S(1)}, bf16[2,128,128]{2,1,0:T(8,128)(2,1)S(1)}, u32[]{:S(2)}, u32[]{:S(2)}) collective-permute-start(bf16[2,128,128]{2,1,0:T(8,128)(2,1)S(1)} %slice.58), channel_id=1, source_target_pairs={{0,2},{1,3},{2,0},{3,1},{4,6},{5,7},{6,4},{7,5},{8,10},{9,11},{10,... | collective-permute-start | bytes 196616 | tf_op jit(solution)/shard_map/ppermute | solution.py:17
  13.7 0.0 copy-done
  13.7 0.0 copy-done.4
  13.7 0.9 %fusion.2 = f32[64,128]{1,0:T(8,128)S(1)} fusion(bf16[8192,64]{0,1:T(8,128)(2,1)S(1)} %copy-done.4, bf16[128,8192]{1,0:T(8,128)(2,1)S(1)} %copy-done), kind=kOutput, calls=%fused_computation.13 | convolution fusion | flops 134217728 | bytes 3178496 | tf_op jit(solution)/shard_map/dot_general | solution.py:303
  14.6 1.6 %collective-permute-start.4 = (f32[64,128]{1,0:T(8,128)S(1)}, f32[64,128]{1,0:T(8,128)S(1)}, u32[]{:S(2)}, u32[]{:S(2)}) collective-permute-start(f32[64,128]{1,0:T(8,128)S(1)} %fusion.2), channel_id=1, source_target_pairs={{0,4},{1,5},{2,6},{3,7},{4,0},{5,1},{6,2},{7,3},{8,12},{9,13},{10,... | collective-permute-start | bytes 98312 | tf_op jit(solution)/shard_map/ppermute | solution.py:17
  16.3 0.4 collective-permute-done.1
  16.7 0.0 collective-permute-done.5
  16.7 1.6 %collective-permute-start.6 = (bf16[16,4096]{1,0:T(8,128)(2,1)S(1)}, bf16[16,4096]{1,0:T(8,128)(2,1)S(1)}, u32[]{:S(2)}, u32[]{:S(2)}) collective-permute-start(bf16[16,4096]{1,0:T(8,128)(2,1)S(1)} %pad_maximum_fusion), channel_id=1, source_target_pairs={{0,2},{1,3},{2,0},{3,1},{4,6},{5,7},{6,4},{7,5},{8,10},{9,11},{10,... | collective-permute-start | bytes 393224 | tf_op jit(solution)/shard_map/ppermute | solution.py:17
  18.3 0.6 %collective-permute-start.2 = (bf16[1,128,128]{2,1,0:T(8,128)(2,1)S(1)}, bf16[1,128,128]{2,1,0:T(8,128)(2,1)S(1)}, u32[]{:S(2)}, u32[]{:S(2)}) collective-permute-start(bf16[1,128,128]{2,1,0:T(8,128)(2,1)S(1)} %slice.59), channel_id=1, source_target_pairs={{0,8},{1,9},{2,10},{3,11},{4,12},{5,13},{6,14},{7,15},{8,0},{9,1},... | collective-permute-start | bytes 98312 | tf_op jit(solution)/shard_map/ppermute | solution.py:17
  18.9 2.9 %collective-permute-done.6 = bf16[16,4096]{1,0:T(8,128)(2,1)S(1)} collective-permute-done((bf16[16,4096]{1,0:T(8,128)(2,1)S(1)}, bf16[16,4096]{1,0:T(8,128)(2,1)S(1)}, u32[]{:S(2)}, u32[]{:S(2)}) %collective-permute-start.6) | collective-permute-done | bytes 131104 | tf_op jit(solution)/shard_map/ppermute | solution.py:17
  21.8 0.1 collective-permute-start.7
  21.9 1.3 %collective-permute-done.2 = bf16[1,128,128]{2,1,0:T(8,128)(2,1)S(1)} collective-permute-done((bf16[1,128,128]{2,1,0:T(8,128)(2,1)S(1)}, bf16[1,128,128]{2,1,0:T(8,128)(2,1)S(1)}, u32[]{:S(2)}, u32[]{:S(2)}) %collective-permute-start.2) | collective-permute-done | bytes 32800 | tf_op jit(solution)/shard_map/ppermute | solution.py:17
  23.2 1.6 %collective-permute-start.3 = (f32[128,128]{1,0:T(8,128)S(1)}, f32[128,128]{1,0:T(8,128)S(1)}, u32[]{:S(2)}, u32[]{:S(2)}) collective-permute-start(f32[128,128]{1,0:T(8,128)S(1)} %fusion.own_ref), channel_id=1, source_target_pairs={{0,4},{1,5},{2,6},{3,7},{4,0},{5,1},{6,2},{7,3},{8,12},{9,13},{10,... | collective-permute-start | bytes 196616 | tf_op jit(solution)/shard_map/ppermute | solution.py:17
  24.8 0.0 collective-permute-done.4
  24.8 0.0 copy-start.2
  24.8 0.0 copy-start.3
  24.9 0.0 collective-permute-done.7.refs_1_
  24.9 0.7 %shard_map.88.inner_ref = f32[2048,512]{1,0:T(8,128)S(1)} custom-call(f32[2,64,128]{2,1,0:T(8,128)S(1)} %pad_maximum_fusion.1.act_ref, bf16[32,4096]{1,0:T(8,128)(2,1)S(1)} %constant_dynamic-update-slice_fusion.refs_0_, bf16[32,4096]{1,0:T(8,128)(2,1)S(1)} %collective-permute-done.7.refs_1_), custom_call_target="tpu_custom_call" | custom-call | flops 536870912 | bytes 4194304 | tf_op jit(solution)/shard_map/pallas_call | solution.py:116
  25.6 1.9 %collective-permute-done.3.other_ref = f32[128,128]{1,0:T(8,128)S(1)} collective-permute-done((f32[128,128]{1,0:T(8,128)S(1)}, f32[128,128]{1,0:T(8,128)S(1)}, u32[]{:S(2)}, u32[]{:S(2)}) %collective-permute-start.3) | collective-permute-done | bytes 65568 | tf_op jit(solution)/shard_map/ppermute | solution.py:17
  27.5 0.0 copy-done.2
  27.5 0.0 copy-done.3
  27.5 1.1 %shard_map.89 = (f32[64,128]{1,0:T(8,128)S(1)}, f32[64,128]{1,0:T(8,128)S(1)}, f32[8,8,16]{2,1,0:T(8,128)S(1)}) custom-call(s32[1]{0:T(128)} %bitcast.me_ref, s32[16]{0:T(128)S(1)} %copy-done.2, s32[16]{0:T(128)S(1)} %copy-done.3, f32[128,128]{1,0:T(8,128)S(1)} %fusion.own_ref, f32[128,128]{1,0:T(8,128)S(1)} %collective-permute-done.3.other_ref, ...), custom_call_target="tpu_custom_call" | custom-call | flops 2097152 | bytes 4194304 | tf_op jit(solution)/shard_map/pallas_call | solution.py:216
  28.6 0.0 copy-start.1
  28.6 0.6 %copy-done.1 = f32[64,128]{1,0:T(8,128)} copy-done((f32[64,128]{1,0:T(8,128)}, f32[64,128]{1,0:T(8,128)S(1)}, u32[]{:S(2)}) %copy-start.1) | copy-done | bytes 32792
  29.2 0.0 collective-permute-start.9
  29.2 1.2 %collective-permute-done.9 = f32[4,8,16]{2,1,0:T(8,128)S(1)} collective-permute-done((f32[4,8,16]{2,1,0:T(8,128)S(1)}, f32[4,8,16]{2,1,0:T(8,128)S(1)}, u32[]{:S(2)}, u32[]{:S(2)}) %collective-permute-start.9) | collective-permute-done | bytes 2080 | tf_op jit(solution)/shard_map/ppermute | solution.py:17
  30.4 0.5 %collective-permute-start.10 = (f32[2,8,16]{2,1,0:T(8,128)S(1)}, f32[2,8,16]{2,1,0:T(8,128)S(1)}, u32[]{:S(2)}, u32[]{:S(2)}) collective-permute-start(f32[2,8,16]{2,1,0:T(8,128)S(1)} %slice.47), channel_id=1, source_target_pairs={{0,2},{1,3},{2,0},{3,1},{4,6},{5,7},{6,4},{7,5},{8,10},{9,11},{10,... | collective-permute-start | bytes 3080 | tf_op jit(solution)/shard_map/ppermute | solution.py:17
  30.9 1.6 %collective-permute-start.8 = (f32[64,128]{1,0:T(8,128)S(1)}, f32[64,128]{1,0:T(8,128)S(1)}, u32[]{:S(2)}, u32[]{:S(2)}) collective-permute-start(f32[64,128]{1,0:T(8,128)S(1)} %get-tuple-element.12), channel_id=1, source_target_pairs={{0,4},{1,5},{2,6},{3,7},{4,0},{5,1},{6,2},{7,3},{8,12},{9,13},{10,... | collective-permute-start | bytes 98312 | tf_op jit(solution)/shard_map/ppermute | solution.py:17
  32.5 1.6 %collective-permute-done.10 = f32[2,8,16]{2,1,0:T(8,128)S(1)} collective-permute-done((f32[2,8,16]{2,1,0:T(8,128)S(1)}, f32[2,8,16]{2,1,0:T(8,128)S(1)}, u32[]{:S(2)}, u32[]{:S(2)}) %collective-permute-start.10) | collective-permute-done | bytes 1056 | tf_op jit(solution)/shard_map/ppermute | solution.py:17
  34.1 0.6 %fusion.1 = (f32[1,8,16]{2,1,0:T(8,128)S(1)}, f32[1,8,16]{2,1,0:T(8,128)}) fusion(f32[2,8,16]{2,1,0:T(8,128)S(1)} %slice_add_fusion.3), kind=kLoop, calls=%fused_computation.12 | loop fusion | bytes 2048 | tf_op jit(solution)/shard_map/slice | solution.py:317
  34.7 0.6 %collective-permute-start.11 = (f32[1,8,16]{2,1,0:T(8,128)S(1)}, f32[1,8,16]{2,1,0:T(8,128)S(1)}, u32[]{:S(2)}, u32[]{:S(2)}) collective-permute-start(f32[1,8,16]{2,1,0:T(8,128)S(1)} %get-tuple-element.16), channel_id=1, source_target_pairs={{0,8},{1,9},{2,10},{3,11},{4,12},{5,13},{6,14},{7,15},{8,0},{9,1},... | collective-permute-start | bytes 1544 | tf_op jit(solution)/shard_map/ppermute | solution.py:17
  35.2 3.9 %collective-permute-done.11.more_ref = f32[1,8,16]{2,1,0:T(8,128)S(1)} collective-permute-done((f32[1,8,16]{2,1,0:T(8,128)S(1)}, f32[1,8,16]{2,1,0:T(8,128)S(1)}, u32[]{:S(2)}, u32[]{:S(2)}) %collective-permute-start.11) | collective-permute-done | bytes 544 | tf_op jit(solution)/shard_map/ppermute | solution.py:17
  39.2 0.0 copy-start.7
  39.2 0.0 collective-permute-done.8.other_ref
  39.2 0.0 copy-start.6
  39.2 0.6 %copy-done.7 = f32[1,8,16]{2,1,0:T(8,128)} copy-done((f32[1,8,16]{2,1,0:T(8,128)}, f32[1,8,16]{2,1,0:T(8,128)S(1)}, u32[]{:S(2)}) %copy-start.7) | copy-done | bytes 536
  39.8 0.0 copy-done.6
  39.8 1.6 %shard_map.90 = (f32[128,128]{1,0:T(8,128)}, f32[8,16]{1,0:T(8,128)}) custom-call(s32[1]{0:T(128)} %bitcast.me_ref, s32[16]{0:T(128)} %length_ref.3, s32[16]{0:T(128)} %valid_ref.3, f32[64,128]{1,0:T(8,128)} %copy-done.1, f32[64,128]{1,0:T(8,128)} %copy-done.6, f32[1,8,16]{2,1,0:T(8,128)} %get-tuple-element.17.doc_ref, f32[1,8,16]{2,1,0:T(8,128)} %copy-done.7), custom_call_target="tpu_custom_call" | custom-call | tf_op jit(solution)/shard_map/pallas_call | solution.py:253
  (14 shorter events, 0.1 us)
Async XLA Ops:
  0.6 13.1 %copy-start = (bf16[128,8192]{1,0:T(8,128)(2,1)S(1)}, bf16[128,8192]{1,0:T(8,128)(2,1)}, u32[]{:S(2)}) copy-start(bf16[128,8192]{1,0:T(8,128)(2,1)} %param.7) | copy-start | bytes 6291460
  0.6 16.0 %collective-permute-start.5 = (bf16[8,4096]{1,0:T(8,128)(2,1)}, bf16[8,4096]{1,0:T(8,128)(2,1)S(1)}, u32[]{:S(2)}, u32[]{:S(2)}) collective-permute-start(bf16[8,4096]{1,0:T(8,128)(2,1)} %param.11), channel_id=1, source_target_pairs={{0,8},{1,9},{2,10},{3,11},{4,12},{5,13},{6,14},{7,15},{8,0},{9,1},... | collective-permute-start | bytes 196616 | tf_op jit(solution)/shard_map/ppermute | solution.py:17
  8.3 3.7 %copy-start.5 = (bf16[8,4096]{1,0:T(8,128)(2,1)S(1)}, bf16[8,4096]{1,0:T(8,128)(2,1)}, u32[]{:S(2)}) copy-start(bf16[8,4096]{1,0:T(8,128)(2,1)} %param.11) | copy-start | bytes 196612
  8.3 5.4 %copy-start.4 = (bf16[8192,64]{0,1:T(8,128)(2,1)S(1)}, bf16[8192,64]{0,1:T(8,128)(2,1)}, u32[]{:S(2)}) copy-start(bf16[8192,64]{0,1:T(8,128)(2,1)} %param.9) | copy-start | bytes 3145732
  8.3 3.7 %collective-permute-start = (f32[4,128,128]{2,1,0:T(8,128)S(1)}, f32[4,128,128]{2,1,0:T(8,128)S(1)}, u32[]{:S(2)}, u32[]{:S(2)}) collective-permute-start(f32[4,128,128]{2,1,0:T(8,128)S(1)} %shard_map.87), channel_id=1, source_target_pairs={{0,1},{1,0},{2,3},{3,2},{4,5},{5,4},{6,7},{7,6},{8,9},{9,8},{10,11... | collective-permute-start | bytes 786440 | tf_op jit(solution)/shard_map/ppermute | solution.py:17
  12.1 4.5 %collective-permute-start.1 = (bf16[2,128,128]{2,1,0:T(8,128)(2,1)S(1)}, bf16[2,128,128]{2,1,0:T(8,128)(2,1)S(1)}, u32[]{:S(2)}, u32[]{:S(2)}) collective-permute-start(bf16[2,128,128]{2,1,0:T(8,128)(2,1)S(1)} %slice.58), channel_id=1, source_target_pairs={{0,2},{1,3},{2,0},{3,1},{4,6},{5,7},{6,4},{7,5},{8,10},{9,11},{10,... | collective-permute-start | bytes 196616 | tf_op jit(solution)/shard_map/ppermute | solution.py:17
  14.6 10.2 %collective-permute-start.4 = (f32[64,128]{1,0:T(8,128)S(1)}, f32[64,128]{1,0:T(8,128)S(1)}, u32[]{:S(2)}, u32[]{:S(2)}) collective-permute-start(f32[64,128]{1,0:T(8,128)S(1)} %fusion.2), channel_id=1, source_target_pairs={{0,4},{1,5},{2,6},{3,7},{4,0},{5,1},{6,2},{7,3},{8,12},{9,13},{10,... | collective-permute-start | bytes 98312 | tf_op jit(solution)/shard_map/ppermute | solution.py:17
  16.7 5.1 %collective-permute-start.6 = (bf16[16,4096]{1,0:T(8,128)(2,1)S(1)}, bf16[16,4096]{1,0:T(8,128)(2,1)S(1)}, u32[]{:S(2)}, u32[]{:S(2)}) collective-permute-start(bf16[16,4096]{1,0:T(8,128)(2,1)S(1)} %pad_maximum_fusion), channel_id=1, source_target_pairs={{0,2},{1,3},{2,0},{3,1},{4,6},{5,7},{6,4},{7,5},{8,10},{9,11},{10,... | collective-permute-start | bytes 393224 | tf_op jit(solution)/shard_map/ppermute | solution.py:17
  18.3 4.9 %collective-permute-start.2 = (bf16[1,128,128]{2,1,0:T(8,128)(2,1)S(1)}, bf16[1,128,128]{2,1,0:T(8,128)(2,1)S(1)}, u32[]{:S(2)}, u32[]{:S(2)}) collective-permute-start(bf16[1,128,128]{2,1,0:T(8,128)(2,1)S(1)} %slice.59), channel_id=1, source_target_pairs={{0,8},{1,9},{2,10},{3,11},{4,12},{5,13},{6,14},{7,15},{8,0},{9,1},... | collective-permute-start | bytes 98312 | tf_op jit(solution)/shard_map/ppermute | solution.py:17
  21.8 3.1 %collective-permute-start.7 = (bf16[32,4096]{1,0:T(8,128)(2,1)S(1)}, bf16[32,4096]{1,0:T(8,128)(2,1)S(1)}, u32[]{:S(2)}, u32[]{:S(2)}) collective-permute-start(bf16[32,4096]{1,0:T(8,128)(2,1)S(1)} %constant_dynamic-update-slice_fusion.refs_0_), channel_id=1, source_target_pairs={{0,1},{1,0},{2,3},{3,2},{4,5},{5,4},{6,7},{7,6},{8,9},{9,8},{10,11... | collective-permute-start | bytes 786440 | tf_op jit(solution)/shard_map/ppermute | solution.py:17
  23.2 4.3 %collective-permute-start.3 = (f32[128,128]{1,0:T(8,128)S(1)}, f32[128,128]{1,0:T(8,128)S(1)}, u32[]{:S(2)}, u32[]{:S(2)}) collective-permute-start(f32[128,128]{1,0:T(8,128)S(1)} %fusion.own_ref), channel_id=1, source_target_pairs={{0,4},{1,5},{2,6},{3,7},{4,0},{5,1},{6,2},{7,3},{8,12},{9,13},{10,... | collective-permute-start | bytes 196616 | tf_op jit(solution)/shard_map/ppermute | solution.py:17
  24.8 2.7 %copy-start.2 = (s32[16]{0:T(128)S(1)}, s32[16]{0:T(128)}, u32[]{:S(2)}) copy-start(s32[16]{0:T(128)} %length_ref.3) | copy-start | bytes 196
  24.8 2.7 %copy-start.3 = (s32[16]{0:T(128)S(1)}, s32[16]{0:T(128)}, u32[]{:S(2)}) copy-start(s32[16]{0:T(128)} %valid_ref.3) | copy-start | bytes 196
  28.6 0.6 %copy-start.1 = (f32[64,128]{1,0:T(8,128)}, f32[64,128]{1,0:T(8,128)S(1)}, u32[]{:S(2)}) copy-start(f32[64,128]{1,0:T(8,128)S(1)} %get-tuple-element.11.own_ref) | copy-start | bytes 98308
  29.2 1.2 %collective-permute-start.9 = (f32[4,8,16]{2,1,0:T(8,128)S(1)}, f32[4,8,16]{2,1,0:T(8,128)S(1)}, u32[]{:S(2)}, u32[]{:S(2)}) collective-permute-start(f32[4,8,16]{2,1,0:T(8,128)S(1)} %slice.37), channel_id=1, source_target_pairs={{0,1},{1,0},{2,3},{3,2},{4,5},{5,4},{6,7},{7,6},{8,9},{9,8},{10,11... | collective-permute-start | bytes 6152 | tf_op jit(solution)/shard_map/ppermute | solution.py:17
  30.4 3.7 %collective-permute-start.10 = (f32[2,8,16]{2,1,0:T(8,128)S(1)}, f32[2,8,16]{2,1,0:T(8,128)S(1)}, u32[]{:S(2)}, u32[]{:S(2)}) collective-permute-start(f32[2,8,16]{2,1,0:T(8,128)S(1)} %slice.47), channel_id=1, source_target_pairs={{0,2},{1,3},{2,0},{3,1},{4,6},{5,7},{6,4},{7,5},{8,10},{9,11},{10,... | collective-permute-start | bytes 3080 | tf_op jit(solution)/shard_map/ppermute | solution.py:17
  30.9 8.3 %collective-permute-start.8 = (f32[64,128]{1,0:T(8,128)S(1)}, f32[64,128]{1,0:T(8,128)S(1)}, u32[]{:S(2)}, u32[]{:S(2)}) collective-permute-start(f32[64,128]{1,0:T(8,128)S(1)} %get-tuple-element.12), channel_id=1, source_target_pairs={{0,4},{1,5},{2,6},{3,7},{4,0},{5,1},{6,2},{7,3},{8,12},{9,13},{10,... | collective-permute-start | bytes 98312 | tf_op jit(solution)/shard_map/ppermute | solution.py:17
  34.7 4.5 %collective-permute-start.11 = (f32[1,8,16]{2,1,0:T(8,128)S(1)}, f32[1,8,16]{2,1,0:T(8,128)S(1)}, u32[]{:S(2)}, u32[]{:S(2)}) collective-permute-start(f32[1,8,16]{2,1,0:T(8,128)S(1)} %get-tuple-element.16), channel_id=1, source_target_pairs={{0,8},{1,9},{2,10},{3,11},{4,12},{5,13},{6,14},{7,15},{8,0},{9,1},... | collective-permute-start | bytes 1544 | tf_op jit(solution)/shard_map/ppermute | solution.py:17
  39.2 0.6 %copy-start.7 = (f32[1,8,16]{2,1,0:T(8,128)}, f32[1,8,16]{2,1,0:T(8,128)S(1)}, u32[]{:S(2)}) copy-start(f32[1,8,16]{2,1,0:T(8,128)S(1)} %collective-permute-done.11.more_ref) | copy-start | bytes 1540
  39.2 0.6 %copy-start.6 = (f32[64,128]{1,0:T(8,128)}, f32[64,128]{1,0:T(8,128)S(1)}, u32[]{:S(2)}) copy-start(f32[64,128]{1,0:T(8,128)S(1)} %collective-permute-done.8.other_ref) | copy-start | bytes 98308

commit v6 on v5

--- a/solution.py
+++ b/solution.py
@@ -32,7 +32,7 @@
             grads_buf.at[k % halves, pl.ds((k // halves) * rows, rows)],
             sems.at[k],
         )
-        copy.start()
+        copy.start(priority=k % 2)
         copies.append(copy)
     load.wait()
     turned = proj_buf[...].T
@@ -259,6 +259,7 @@
             jax.ShapeDtypeStruct((own_q, docs), jnp.float32),
         ),
         scratch_shapes=[pltpu.VMEM((2 * count, rows), jnp.float32)],
+        compiler_params=pltpu.CompilerParams(vmem_limit_bytes=16 * MIB),
     )(me, lengths, valid, own, other, doc, more)
 
 

time: 41.6 us -> 38.7 us (0.930)
  local copies, waits for them, and re-layouts: 1.91 us -> 0.09 us
  Pallas kernels: 10.5 us -> 9.44 us
    unnamed x18 -> x12, local copies, waits for them, and re-layouts: 1.28 us -> 0.05 us
    pallas_call x2, Pallas kernels: 7.19 us -> 6.36 us  [grad_blocks(): pl.pallas_call(functools.partial(grad_kernel, offsets), in_specs=[SMEM, H...]
    slice x1, local copies, waits for them, and re-layouts: 0.6 us -> 0.01 us  [body(): more = swap(doc[1:], bits[-1], size)]
  transfers between devices with their start and end apart: 12 -> 12, of which waited for: 7 -> 7; matrix products, arithmetic and copies ran while one was open for 4% -> 3% of each run, Pallas kernels for 19% -> 18%
where the time goes in v6:
time: 38.7 us; the launch traced here: 38.5 us
  starting transfers between devices  14 us (36%)
  waiting for transfers between devices  13.2 us (34%)
  Pallas kernels  9.44 us (24%)
  matrix products  0.88 us (2%)
  between operations  0.83 us (2%)
    ppermute x12, starting transfers between devices, swap(): return lax.ppermute(value, 'seq', [(i, i ^ offset) for i in range(size)])  14 us
    ppermute x12, waiting for transfers between devices, swap(): return lax.ppermute(value, 'seq', [(i, i ^ offset) for i in range(size)])  13.2 us
    pallas_call x2, Pallas kernels, grad_blocks(): pl.pallas_call(functools.partial(grad_kernel, offsets), in_specs=[SMEM, H...  6.36 us
    pallas_call x1, Pallas kernels, last(): pl.pallas_call(functools.partial(last_kernel, place, split), in_specs=[SM...  1.29 us
    pallas_call x1, Pallas kernels, score(): pl.pallas_call(functools.partial(score_kernel, steps, split), out_shape=(...  1.08 us
    dot_general x1, matrix products, body(): lax.dot_general(late, activations, (((0,), (1,)), ((), ())), preferred_el...  0.88 us
  transfers between devices with their start and end apart: 12, of which 7 were waited for; matrix products, arithmetic and copies ran while one was open for 3% of the time, Pallas kernels for 18%

profile of v6, /device:TPU:0, one launch (start us, length us, event | category | flops | bytes accessed | tf_op | source)
XLA Modules:
  0.0 38.5 jit_solution(9173170548618332141)
XLA Ops:
  0.6 0.0 copy-start
  0.6 4.1 %collective-permute-start.5 = (bf16[8,4096]{1,0:T(8,128)(2,1)}, bf16[8,4096]{1,0:T(8,128)(2,1)S(1)}, u32[]{:S(2)}, u32[]{:S(2)}) collective-permute-start(bf16[8,4096]{1,0:T(8,128)(2,1)} %param.11), channel_id=1, source_target_pairs={{0,8},{1,9},{2,10},{3,11},{4,12},{5,13},{6,14},{7,15},{8,0},{9,1},... | collective-permute-start | bytes 196616 | tf_op jit(solution)/shard_map/ppermute | solution.py:17
  4.7 3.1 %shard_map.87 = f32[4,128,128]{2,1,0:T(8,128)S(1)} custom-call(s32[1]{0:T(128)} %bitcast.me_ref, bf16[64,1792]{1,0:T(8,128)(2,1)} %bitcast.9, bf16[2048,1792]{1,0:T(8,128)(2,1)} %grads_ref.3), custom_call_target="tpu_custom_call" | custom-call | flops 234881024 | bytes 3670016 | tf_op jit(solution)/shard_map/pallas_call | solution.py:60
  7.9 0.0 copy-start.4
  7.9 0.0 copy-start.3
  7.9 0.1 collective-permute-start
  8.0 3.2 %shard_map.86 = f32[4,128,128]{2,1,0:T(8,128)S(1)} custom-call(s32[1]{0:T(128)} %bitcast.me_ref, bf16[64,1792]{1,0:T(8,128)(2,1)} %bitcast.10, bf16[2048,1792]{1,0:T(8,128)(2,1)} %grads_ref.3), custom_call_target="tpu_custom_call" | custom-call | flops 234881024 | bytes 3670016 | tf_op jit(solution)/shard_map/pallas_call | solution.py:60
  11.2 0.0 copy-done.4
  11.3 0.0 collective-permute-done
  11.3 1.6 %collective-permute-start.1 = (bf16[2,128,128]{2,1,0:T(8,128)(2,1)S(1)}, bf16[2,128,128]{2,1,0:T(8,128)(2,1)S(1)}, u32[]{:S(2)}, u32[]{:S(2)}) collective-permute-start(bf16[2,128,128]{2,1,0:T(8,128)(2,1)S(1)} %slice.58), channel_id=1, source_target_pairs={{0,2},{1,3},{2,0},{3,1},{4,6},{5,7},{6,4},{7,5},{8,10},{9,11},{10,... | collective-permute-start | bytes 196616 | tf_op jit(solution)/shard_map/ppermute | solution.py:17
  12.9 0.0 copy-done
  12.9 0.0 copy-done.3
  12.9 0.9 %fusion.2 = f32[64,128]{1,0:T(8,128)S(1)} fusion(bf16[8192,64]{0,1:T(8,128)(2,1)S(1)} %copy-done.3, bf16[128,8192]{1,0:T(8,128)(2,1)S(1)} %copy-done), kind=kOutput, calls=%fused_computation.13 | convolution fusion | flops 134217728 | bytes 3178496 | tf_op jit(solution)/shard_map/dot_general | solution.py:304
  13.8 1.6 %collective-permute-start.4 = (f32[64,128]{1,0:T(8,128)S(1)}, f32[64,128]{1,0:T(8,128)S(1)}, u32[]{:S(2)}, u32[]{:S(2)}) collective-permute-start(f32[64,128]{1,0:T(8,128)S(1)} %fusion.2), channel_id=1, source_target_pairs={{0,4},{1,5},{2,6},{3,7},{4,0},{5,1},{6,2},{7,3},{8,12},{9,13},{10,... | collective-permute-start | bytes 98312 | tf_op jit(solution)/shard_map/ppermute | solution.py:17
  15.4 0.4 collective-permute-done.1
  15.8 0.0 collective-permute-done.5
  15.9 1.6 %collective-permute-start.6 = (bf16[16,4096]{1,0:T(8,128)(2,1)S(1)}, bf16[16,4096]{1,0:T(8,128)(2,1)S(1)}, u32[]{:S(2)}, u32[]{:S(2)}) collective-permute-start(bf16[16,4096]{1,0:T(8,128)(2,1)S(1)} %pad_maximum_fusion), channel_id=1, source_target_pairs={{0,2},{1,3},{2,0},{3,1},{4,6},{5,7},{6,4},{7,5},{8,10},{9,11},{10,... | collective-permute-start | bytes 393224 | tf_op jit(solution)/shard_map/ppermute | solution.py:17
  17.5 0.6 %collective-permute-start.2 = (bf16[1,128,128]{2,1,0:T(8,128)(2,1)S(1)}, bf16[1,128,128]{2,1,0:T(8,128)(2,1)S(1)}, u32[]{:S(2)}, u32[]{:S(2)}) collective-permute-start(bf16[1,128,128]{2,1,0:T(8,128)(2,1)S(1)} %slice.59), channel_id=1, source_target_pairs={{0,8},{1,9},{2,10},{3,11},{4,12},{5,13},{6,14},{7,15},{8,0},{9,1},... | collective-permute-start | bytes 98312 | tf_op jit(solution)/shard_map/ppermute | solution.py:17
  18.1 2.9 %collective-permute-done.6 = bf16[16,4096]{1,0:T(8,128)(2,1)S(1)} collective-permute-done((bf16[16,4096]{1,0:T(8,128)(2,1)S(1)}, bf16[16,4096]{1,0:T(8,128)(2,1)S(1)}, u32[]{:S(2)}, u32[]{:S(2)}) %collective-permute-start.6) | collective-permute-done | bytes 131104 | tf_op jit(solution)/shard_map/ppermute | solution.py:17
  21.0 0.1 collective-permute-start.7
  21.1 1.3 %collective-permute-done.2 = bf16[1,128,128]{2,1,0:T(8,128)(2,1)S(1)} collective-permute-done((bf16[1,128,128]{2,1,0:T(8,128)(2,1)S(1)}, bf16[1,128,128]{2,1,0:T(8,128)(2,1)S(1)}, u32[]{:S(2)}, u32[]{:S(2)}) %collective-permute-start.2) | collective-permute-done | bytes 32800 | tf_op jit(solution)/shard_map/ppermute | solution.py:17
  22.4 1.6 %collective-permute-start.3 = (f32[128,128]{1,0:T(8,128)S(1)}, f32[128,128]{1,0:T(8,128)S(1)}, u32[]{:S(2)}, u32[]{:S(2)}) collective-permute-start(f32[128,128]{1,0:T(8,128)S(1)} %fusion.own_ref), channel_id=1, source_target_pairs={{0,4},{1,5},{2,6},{3,7},{4,0},{5,1},{6,2},{7,3},{8,12},{9,13},{10,... | collective-permute-start | bytes 196616 | tf_op jit(solution)/shard_map/ppermute | solution.py:17
  24.0 0.0 collective-permute-done.4
  24.0 0.0 copy-start.1
  24.0 0.0 copy-start.2
  24.0 0.0 collective-permute-done.7.refs_1_
  24.0 0.7 %shard_map.88.inner_ref = f32[2048,512]{1,0:T(8,128)S(1)} custom-call(f32[2,64,128]{2,1,0:T(8,128)S(1)} %pad_maximum_fusion.1.act_ref, bf16[32,4096]{1,0:T(8,128)(2,1)S(1)} %constant_dynamic-update-slice_fusion.refs_0_, bf16[32,4096]{1,0:T(8,128)(2,1)S(1)} %collective-permute-done.7.refs_1_), custom_call_target="tpu_custom_call" | custom-call | flops 536870912 | bytes 4194304 | tf_op jit(solution)/shard_map/pallas_call | solution.py:116
  24.8 1.9 %collective-permute-done.3.other_ref = f32[128,128]{1,0:T(8,128)S(1)} collective-permute-done((f32[128,128]{1,0:T(8,128)S(1)}, f32[128,128]{1,0:T(8,128)S(1)}, u32[]{:S(2)}, u32[]{:S(2)}) %collective-permute-start.3) | collective-permute-done | bytes 65568 | tf_op jit(solution)/shard_map/ppermute | solution.py:17
  26.7 0.0 copy-done.1
  26.7 0.0 copy-done.2
  26.7 1.1 %shard_map.89 = (f32[64,128]{1,0:T(8,128)S(1)}, f32[64,128]{1,0:T(8,128)S(1)}, f32[8,8,16]{2,1,0:T(8,128)S(1)}) custom-call(s32[1]{0:T(128)} %bitcast.me_ref, s32[16]{0:T(128)S(1)} %copy-done.1, s32[16]{0:T(128)S(1)} %copy-done.2, f32[128,128]{1,0:T(8,128)S(1)} %fusion.own_ref, f32[128,128]{1,0:T(8,128)S(1)} %collective-permute-done.3.other_ref, ...), custom_call_target="tpu_custom_call" | custom-call | flops 2097152 | bytes 4194304 | tf_op jit(solution)/shard_map/pallas_call | solution.py:216
  27.8 0.1 collective-permute-start.9
  27.9 1.2 %collective-permute-done.9 = f32[4,8,16]{2,1,0:T(8,128)S(1)} collective-permute-done((f32[4,8,16]{2,1,0:T(8,128)S(1)}, f32[4,8,16]{2,1,0:T(8,128)S(1)}, u32[]{:S(2)}, u32[]{:S(2)}) %collective-permute-start.9) | collective-permute-done | bytes 2080 | tf_op jit(solution)/shard_map/ppermute | solution.py:17
  29.0 0.5 %collective-permute-start.10 = (f32[2,8,16]{2,1,0:T(8,128)S(1)}, f32[2,8,16]{2,1,0:T(8,128)S(1)}, u32[]{:S(2)}, u32[]{:S(2)}) collective-permute-start(f32[2,8,16]{2,1,0:T(8,128)S(1)} %slice.47), channel_id=1, source_target_pairs={{0,2},{1,3},{2,0},{3,1},{4,6},{5,7},{6,4},{7,5},{8,10},{9,11},{10,... | collective-permute-start | bytes 3080 | tf_op jit(solution)/shard_map/ppermute | solution.py:17
  29.6 1.6 %collective-permute-start.8 = (f32[64,128]{1,0:T(8,128)S(1)}, f32[64,128]{1,0:T(8,128)S(1)}, u32[]{:S(2)}, u32[]{:S(2)}) collective-permute-start(f32[64,128]{1,0:T(8,128)S(1)} %get-tuple-element.12), channel_id=1, source_target_pairs={{0,4},{1,5},{2,6},{3,7},{4,0},{5,1},{6,2},{7,3},{8,12},{9,13},{10,... | collective-permute-start | bytes 98312 | tf_op jit(solution)/shard_map/ppermute | solution.py:17
  31.1 1.6 %collective-permute-done.10 = f32[2,8,16]{2,1,0:T(8,128)S(1)} collective-permute-done((f32[2,8,16]{2,1,0:T(8,128)S(1)}, f32[2,8,16]{2,1,0:T(8,128)S(1)}, u32[]{:S(2)}, u32[]{:S(2)}) %collective-permute-start.10) | collective-permute-done | bytes 1056 | tf_op jit(solution)/shard_map/ppermute | solution.py:17
  32.7 0.6 %collective-permute-start.11 = (f32[1,8,16]{2,1,0:T(8,128)S(1)}, f32[1,8,16]{2,1,0:T(8,128)S(1)}, u32[]{:S(2)}, u32[]{:S(2)}) collective-permute-start(f32[1,8,16]{2,1,0:T(8,128)S(1)} %get-tuple-element.16), channel_id=1, source_target_pairs={{0,8},{1,9},{2,10},{3,11},{4,12},{5,13},{6,14},{7,15},{8,0},{9,1},... | collective-permute-start | bytes 1544 | tf_op jit(solution)/shard_map/ppermute | solution.py:17
  33.3 3.9 %collective-permute-done.11.more_ref = f32[1,8,16]{2,1,0:T(8,128)S(1)} collective-permute-done((f32[1,8,16]{2,1,0:T(8,128)S(1)}, f32[1,8,16]{2,1,0:T(8,128)S(1)}, u32[]{:S(2)}, u32[]{:S(2)}) %collective-permute-start.11) | collective-permute-done | bytes 544 | tf_op jit(solution)/shard_map/ppermute | solution.py:17
  37.2 0.0 collective-permute-done.8.other_ref
  37.2 1.3 %shard_map.90 = (f32[128,128]{1,0:T(8,128)}, f32[8,16]{1,0:T(8,128)}) custom-call(s32[1]{0:T(128)} %bitcast.me_ref, s32[16]{0:T(128)S(1)} %copy-done.1, s32[16]{0:T(128)S(1)} %copy-done.2, f32[64,128]{1,0:T(8,128)S(1)} %get-tuple-element.11.own_ref, f32[64,128]{1,0:T(8,128)S(1)} %collective-permute-done.8.other_ref, ...), custom_call_target="tpu_custom_call" | custom-call | tf_op jit(solution)/shard_map/pallas_call | solution.py:253
  (15 shorter events, 0.1 us)
Async XLA Ops:
  0.6 12.3 %copy-start = (bf16[128,8192]{1,0:T(8,128)(2,1)S(1)}, bf16[128,8192]{1,0:T(8,128)(2,1)}, u32[]{:S(2)}) copy-start(bf16[128,8192]{1,0:T(8,128)(2,1)} %param.7) | copy-start | bytes 6291460
  0.6 15.2 %collective-permute-start.5 = (bf16[8,4096]{1,0:T(8,128)(2,1)}, bf16[8,4096]{1,0:T(8,128)(2,1)S(1)}, u32[]{:S(2)}, u32[]{:S(2)}) collective-permute-start(bf16[8,4096]{1,0:T(8,128)(2,1)} %param.11), channel_id=1, source_target_pairs={{0,8},{1,9},{2,10},{3,11},{4,12},{5,13},{6,14},{7,15},{8,0},{9,1},... | collective-permute-start | bytes 196616 | tf_op jit(solution)/shard_map/ppermute | solution.py:17
  7.9 3.3 %copy-start.4 = (bf16[8,4096]{1,0:T(8,128)(2,1)S(1)}, bf16[8,4096]{1,0:T(8,128)(2,1)}, u32[]{:S(2)}) copy-start(bf16[8,4096]{1,0:T(8,128)(2,1)} %param.11) | copy-start | bytes 196612
  7.9 5.0 %copy-start.3 = (bf16[8192,64]{0,1:T(8,128)(2,1)S(1)}, bf16[8192,64]{0,1:T(8,128)(2,1)}, u32[]{:S(2)}) copy-start(bf16[8192,64]{0,1:T(8,128)(2,1)} %param.9) | copy-start | bytes 3145732
  7.9 3.3 %collective-permute-start = (f32[4,128,128]{2,1,0:T(8,128)S(1)}, f32[4,128,128]{2,1,0:T(8,128)S(1)}, u32[]{:S(2)}, u32[]{:S(2)}) collective-permute-start(f32[4,128,128]{2,1,0:T(8,128)S(1)} %shard_map.87), channel_id=1, source_target_pairs={{0,1},{1,0},{2,3},{3,2},{4,5},{5,4},{6,7},{7,6},{8,9},{9,8},{10,11... | collective-permute-start | bytes 786440 | tf_op jit(solution)/shard_map/ppermute | solution.py:17
  11.3 4.5 %collective-permute-start.1 = (bf16[2,128,128]{2,1,0:T(8,128)(2,1)S(1)}, bf16[2,128,128]{2,1,0:T(8,128)(2,1)S(1)}, u32[]{:S(2)}, u32[]{:S(2)}) collective-permute-start(bf16[2,128,128]{2,1,0:T(8,128)(2,1)S(1)} %slice.58), channel_id=1, source_target_pairs={{0,2},{1,3},{2,0},{3,1},{4,6},{5,7},{6,4},{7,5},{8,10},{9,11},{10,... | collective-permute-start | bytes 196616 | tf_op jit(solution)/shard_map/ppermute | solution.py:17
  13.8 10.2 %collective-permute-start.4 = (f32[64,128]{1,0:T(8,128)S(1)}, f32[64,128]{1,0:T(8,128)S(1)}, u32[]{:S(2)}, u32[]{:S(2)}) collective-permute-start(f32[64,128]{1,0:T(8,128)S(1)} %fusion.2), channel_id=1, source_target_pairs={{0,4},{1,5},{2,6},{3,7},{4,0},{5,1},{6,2},{7,3},{8,12},{9,13},{10,... | collective-permute-start | bytes 98312 | tf_op jit(solution)/shard_map/ppermute | solution.py:17
  15.9 5.1 %collective-permute-start.6 = (bf16[16,4096]{1,0:T(8,128)(2,1)S(1)}, bf16[16,4096]{1,0:T(8,128)(2,1)S(1)}, u32[]{:S(2)}, u32[]{:S(2)}) collective-permute-start(bf16[16,4096]{1,0:T(8,128)(2,1)S(1)} %pad_maximum_fusion), channel_id=1, source_target_pairs={{0,2},{1,3},{2,0},{3,1},{4,6},{5,7},{6,4},{7,5},{8,10},{9,11},{10,... | collective-permute-start | bytes 393224 | tf_op jit(solution)/shard_map/ppermute | solution.py:17
  17.5 4.9 %collective-permute-start.2 = (bf16[1,128,128]{2,1,0:T(8,128)(2,1)S(1)}, bf16[1,128,128]{2,1,0:T(8,128)(2,1)S(1)}, u32[]{:S(2)}, u32[]{:S(2)}) collective-permute-start(bf16[1,128,128]{2,1,0:T(8,128)(2,1)S(1)} %slice.59), channel_id=1, source_target_pairs={{0,8},{1,9},{2,10},{3,11},{4,12},{5,13},{6,14},{7,15},{8,0},{9,1},... | collective-permute-start | bytes 98312 | tf_op jit(solution)/shard_map/ppermute | solution.py:17
  21.0 3.1 %collective-permute-start.7 = (bf16[32,4096]{1,0:T(8,128)(2,1)S(1)}, bf16[32,4096]{1,0:T(8,128)(2,1)S(1)}, u32[]{:S(2)}, u32[]{:S(2)}) collective-permute-start(bf16[32,4096]{1,0:T(8,128)(2,1)S(1)} %constant_dynamic-update-slice_fusion.refs_0_), channel_id=1, source_target_pairs={{0,1},{1,0},{2,3},{3,2},{4,5},{5,4},{6,7},{7,6},{8,9},{9,8},{10,11... | collective-permute-start | bytes 786440 | tf_op jit(solution)/shard_map/ppermute | solution.py:17
  22.4 4.3 %collective-permute-start.3 = (f32[128,128]{1,0:T(8,128)S(1)}, f32[128,128]{1,0:T(8,128)S(1)}, u32[]{:S(2)}, u32[]{:S(2)}) collective-permute-start(f32[128,128]{1,0:T(8,128)S(1)} %fusion.own_ref), channel_id=1, source_target_pairs={{0,4},{1,5},{2,6},{3,7},{4,0},{5,1},{6,2},{7,3},{8,12},{9,13},{10,... | collective-permute-start | bytes 196616 | tf_op jit(solution)/shard_map/ppermute | solution.py:17
  24.0 2.7 %copy-start.1 = (s32[16]{0:T(128)S(1)}, s32[16]{0:T(128)}, u32[]{:S(2)}) copy-start(s32[16]{0:T(128)} %length_ref.3) | copy-start | bytes 196
  24.0 2.7 %copy-start.2 = (s32[16]{0:T(128)S(1)}, s32[16]{0:T(128)}, u32[]{:S(2)}) copy-start(s32[16]{0:T(128)} %valid_ref.3) | copy-start | bytes 196
  27.8 1.2 %collective-permute-start.9 = (f32[4,8,16]{2,1,0:T(8,128)S(1)}, f32[4,8,16]{2,1,0:T(8,128)S(1)}, u32[]{:S(2)}, u32[]{:S(2)}) collective-permute-start(f32[4,8,16]{2,1,0:T(8,128)S(1)} %slice.37), channel_id=1, source_target_pairs={{0,1},{1,0},{2,3},{3,2},{4,5},{5,4},{6,7},{7,6},{8,9},{9,8},{10,11... | collective-permute-start | bytes 6152 | tf_op jit(solution)/shard_map/ppermute | solution.py:17
  29.0 3.7 %collective-permute-start.10 = (f32[2,8,16]{2,1,0:T(8,128)S(1)}, f32[2,8,16]{2,1,0:T(8,128)S(1)}, u32[]{:S(2)}, u32[]{:S(2)}) collective-permute-start(f32[2,8,16]{2,1,0:T(8,128)S(1)} %slice.47), channel_id=1, source_target_pairs={{0,2},{1,3},{2,0},{3,1},{4,6},{5,7},{6,4},{7,5},{8,10},{9,11},{10,... | collective-permute-start | bytes 3080 | tf_op jit(solution)/shard_map/ppermute | solution.py:17
  29.6 7.7 %collective-permute-start.8 = (f32[64,128]{1,0:T(8,128)S(1)}, f32[64,128]{1,0:T(8,128)S(1)}, u32[]{:S(2)}, u32[]{:S(2)}) collective-permute-start(f32[64,128]{1,0:T(8,128)S(1)} %get-tuple-element.12), channel_id=1, source_target_pairs={{0,4},{1,5},{2,6},{3,7},{4,0},{5,1},{6,2},{7,3},{8,12},{9,13},{10,... | collective-permute-start | bytes 98312 | tf_op jit(solution)/shard_map/ppermute | solution.py:17
  32.7 4.5 %collective-permute-start.11 = (f32[1,8,16]{2,1,0:T(8,128)S(1)}, f32[1,8,16]{2,1,0:T(8,128)S(1)}, u32[]{:S(2)}, u32[]{:S(2)}) collective-permute-start(f32[1,8,16]{2,1,0:T(8,128)S(1)} %get-tuple-element.16), channel_id=1, source_target_pairs={{0,8},{1,9},{2,10},{3,11},{4,12},{5,13},{6,14},{7,15},{8,0},{9,1},... | collective-permute-start | bytes 1544 | tf_op jit(solution)/shard_map/ppermute | solution.py:17

commit v7 on v6

--- a/solution.py
+++ b/solution.py
@@ -13,17 +13,21 @@
 HBM = pl.BlockSpec(memory_space=pltpu.HBM)
 
 
-def swap(value, offset, size):
-    return lax.ppermute(value, "seq", [(i, i ^ offset) for i in range(size)])
-
-
-def grad_kernel(offsets, me_ref, proj_ref, grads_ref, out_ref, proj_buf, table, grads_buf, proj_sem, sems):
+def swap(value, offset, size, cores=(0, 1)):
+    pairs = [(i, i ^ offset) for i in range(size) if i % 2 in cores]
+    return lax.ppermute(value, "seq", pairs)
+
+
+def grad_kernel(offsets, fresh, me_ref, proj_ref, grads_ref, out_ref, *refs):
+    if fresh:
+        table, proj_buf, grads_buf, sems, proj_sem = refs
+        load = pltpu.make_async_copy(proj_ref, proj_buf, proj_sem)
+        load.start()
+    else:
+        table, (grads_buf, sems) = proj_ref, refs
     halves, total, depth = grads_buf.shape
     count = len(offsets) // halves
     rows = total // count
-    width = proj_buf.shape[0]
-    load = pltpu.make_async_copy(proj_ref, proj_buf, proj_sem)
-    load.start()
     copies = []
     for k, offset in enumerate(offsets):
         first = pl.multiple_of((me_ref[0] ^ offset) * rows, rows)
@@ -34,11 +38,12 @@
         )
         copy.start(priority=k % 2)
         copies.append(copy)
-    load.wait()
-    turned = proj_buf[...].T
-    none = jnp.zeros_like(turned)
-    for r in range(halves):
-        table[r] = jnp.concatenate([turned if c == r else none for c in range(halves)], axis=1)
+    if fresh:
+        load.wait()
+        turned = proj_buf[...].T
+        none = jnp.zeros_like(turned)
+        for r in range(halves):
+            table[r] = jnp.concatenate([turned if c == r else none for c in range(halves)], axis=1)
     for k in range(0, count, 2):
         for copy in copies[k * halves : (k + 2) * halves]:
             copy.wait()
@@ -54,22 +59,25 @@
         out_ref[k + 1] = made[rows:]
 
 
-def grad_blocks(me, proj, out_grads, rows, offsets):
-    width, depth = proj.shape
+def grad_blocks(me, proj, out_grads, rows, offsets, fresh):
+    depth = out_grads.shape[1]
+    width = proj.shape[0] if fresh else proj.shape[2] // 2
     count = len(offsets) // 2
+    made = jax.ShapeDtypeStruct((count, rows, 2 * width), jnp.float32)
+    table = jax.ShapeDtypeStruct((2, depth, 2 * width), jnp.bfloat16)
+    scratch = [
+        pltpu.VMEM((2, count * rows, depth), jnp.bfloat16),
+        pltpu.SemaphoreType.DMA((2 * count,)),
+    ]
+    if fresh:
+        scratch = [pltpu.VMEM((width, depth), jnp.bfloat16)] + scratch + [pltpu.SemaphoreType.DMA]
     return pl.pallas_call(
-        functools.partial(grad_kernel, offsets),
-        in_specs=[SMEM, HBM, HBM],
-        out_specs=VMEM,
-        out_shape=jax.ShapeDtypeStruct((count, rows, 2 * width), jnp.float32),
-        scratch_shapes=[
-            pltpu.VMEM((width, depth), jnp.bfloat16),
-            pltpu.VMEM((2, depth, 2 * width), jnp.bfloat16),
-            pltpu.VMEM((2, count * rows, depth), jnp.bfloat16),
-            pltpu.SemaphoreType.DMA,
-            pltpu.SemaphoreType.DMA((2 * count,)),
-        ],
-        compiler_params=pltpu.CompilerParams(vmem_limit_bytes=52 * MIB),
+        functools.partial(grad_kernel, offsets, fresh),
+        in_specs=[SMEM, HBM if fresh else VMEM, HBM],
+        out_specs=(VMEM, VMEM) if fresh else VMEM,
+        out_shape=(made, table) if fresh else made,
+        scratch_shapes=scratch,
+        compiler_params=pltpu.CompilerParams(vmem_limit_bytes=48 * MIB),
         cost_estimate=pl.CostEstimate(
             flops=4 * count * rows * depth * width,
             bytes_accessed=4 * count * rows * depth,
@@ -244,7 +252,8 @@
     used = jnp.zeros((own_q, docs), jnp.int32)
     for d in range(docs):
         used = jnp.where(doc_of == d, jnp.minimum(valid_ref[d], length_ref[d]), used)
-    doc_out[...] = (doc_ref[0] + more_ref[0]) * (1.0 / jnp.sqrt(used.astype(jnp.float32)))
+    doc = jnp.where(me_ref[0] % 2 == 1, doc_ref[0], more_ref[0])
+    doc_out[...] = doc * (1.0 / jnp.sqrt(used.astype(jnp.float32)))
 
 
 def last(me, lengths, valid, own, other, doc, more, place, split):
@@ -276,13 +285,13 @@
     split = size // 4
     middle = [1 << k for k in range(1, size.bit_length() - 1) if 1 << k != split]
 
-    panel, place = queries, [0]
-    got = swap(panel, middle[-1], size)
-
     proj = pltpu.with_memory_space_constraint(proj_out.T, pltpu.HBM)
     spots = [offset_of(m, middle) + split * r for m in range(size // 4) for r in range(2)]
-    from_core = swap(grad_blocks(me, proj, out_grads, rows, [s + 1 for s in spots]), 1, size)
-    sums = grad_blocks(me, proj, out_grads, rows, spots) + from_core
+    theirs, table = grad_blocks(me, proj, out_grads, rows, [s + 1 for s in spots], True)
+    from_core = swap(theirs, 1, size)
+    panel, _ = lax.optimization_barrier((queries, theirs))
+    got = swap(panel, middle[-1], size)
+    sums = grad_blocks(me, table, out_grads, rows, spots, False) + from_core
     late, _ = lax.optimization_barrier((proj_in, sums))
     for k, bit in enumerate(middle):
         half = sums.shape[0] // 2
@@ -311,13 +320,17 @@
         me, doc_length, valid_count, own, across, products, split, own_q, steps
     )
     others = swap(theirs, split, size)
-    bits = [1] + middle
-    for bit in bits[:-1]:
-        half = doc.shape[0] // 2
-        doc = doc[:half] + swap(doc[half:], bit, size)
-    more = swap(doc[1:], bits[-1], size)
+    half = doc.shape[0] // 2
+    from_even = swap(doc, 1, size, (0,))
+    doc = doc + jnp.concatenate([from_even[half:], from_even[:half]], axis=0)
+    doc = doc.reshape((2, half) + doc.shape[1:])
+    for bit in middle:
+        half //= 2
+        doc = doc[:, :half] + swap(doc[:, half:], bit, size, (1,))
+    own_doc, even_doc = doc[0], doc[1]
+    from_odd = swap(even_doc, 1, size, (1,))
     token_scores, doc = last(
-        me, doc_length, valid_count, mine, others, doc[:1], more, place, split
+        me, doc_length, valid_count, mine, others, own_doc, from_odd, place, split
     )
     return (token_scores, doc.T)
 

time: 38.7 us -> 43.7 us (1.13)
  starting transfers between devices: 14 us -> 16.7 us
  waiting for transfers between devices: 13.2 us -> 15.4 us
    ppermute x12 -> x13, starting transfers between devices: 14 us -> 16.7 us  [swap(): return lax.ppermute(value, 'seq', pairs)]
    ppermute x12 -> x13, waiting for transfers between devices: 13.2 us -> 15.4 us  [swap(): return lax.ppermute(value, 'seq', pairs)]
  transfers between devices with their start and end apart: 12 -> 13, of which waited for: 7 -> 6; matrix products, arithmetic and copies ran while one was open for 3% -> 2% of each run, Pallas kernels for 18% -> 9%
where the time goes in v7:
time: 43.7 us; the launch traced here: 43.5 us
  starting transfers between devices  16.7 us (38%)
  waiting for transfers between devices  15.4 us (35%)
  Pallas kernels  9.55 us (22%)
  matrix products  0.88 us (2%)
  between operations  0.85 us (2%)
    ppermute x13, starting transfers between devices, swap(): return lax.ppermute(value, 'seq', pairs)  16.7 us
    ppermute x13, waiting for transfers between devices, swap(): return lax.ppermute(value, 'seq', pairs)  15.4 us
    pallas_call x2, Pallas kernels, grad_blocks(): pl.pallas_call(functools.partial(grad_kernel, offsets, fresh), in_specs=[...  6.48 us
    pallas_call x1, Pallas kernels, last(): pl.pallas_call(functools.partial(last_kernel, place, split), in_specs=[SM...  1.29 us
    pallas_call x1, Pallas kernels, score(): pl.pallas_call(functools.partial(score_kernel, steps, split), out_shape=(...  1.08 us
    dot_general x1, matrix products, body(): lax.dot_general(late, activations, (((0,), (1,)), ((), ())), preferred_el...  0.88 us
  transfers between devices with their start and end apart: 13, of which 6 were waited for; matrix products, arithmetic and copies ran while one was open for 2% of the time, Pallas kernels for 9%

profile of v7, /device:TPU:0, one launch (start us, length us, event | category | flops | bytes accessed | tf_op | source)
XLA Modules:
  0.0 43.5 jit_solution(8002254648230584789)
XLA Ops:
  0.6 0.0 copy-start
  0.6 0.0 copy-start.4
  0.7 3.3 %shard_map.86 = (f32[4,128,128]{2,1,0:T(8,128)S(1)}, bf16[2,1792,128]{2,1,0:T(8,128)(2,1)S(1)}) custom-call(s32[1]{0:T(128)} %bitcast.me_ref, bf16[64,1792]{1,0:T(8,128)(2,1)} %bitcast.14, bf16[2048,1792]{1,0:T(8,128)(2,1)} %grads_ref.3), custom_call_target="tpu_custom_call" | custom-call | flops 234881024 | bytes 3670016 | tf_op jit(solution)/shard_map/pallas_call | solution.py:74
  4.0 0.5 %collective-permute-start = (f32[4,128,128]{2,1,0:T(8,128)S(1)}, f32[4,128,128]{2,1,0:T(8,128)S(1)}, u32[]{:S(2)}, u32[]{:S(2)}) collective-permute-start(f32[4,128,128]{2,1,0:T(8,128)S(1)} %get-tuple-element.13), channel_id=1, source_target_pairs={{0,1},{1,0},{2,3},{3,2},{4,5},{5,4},{6,7},{7,6},{8,9},{9,8},{10,11... | collective-permute-start | bytes 786440 | tf_op jit(solution)/shard_map/ppermute | solution.py:18
  4.5 0.0 copy-done.4
  4.5 3.7 %collective-permute-start.5 = (bf16[8,4096]{1,0:T(8,128)(2,1)S(1)}, bf16[8,4096]{1,0:T(8,128)(2,1)S(1)}, u32[]{:S(2)}, u32[]{:S(2)}) collective-permute-start(bf16[8,4096]{1,0:T(8,128)(2,1)S(1)} %copy-done.4), channel_id=1, source_target_pairs={{0,8},{1,9},{2,10},{3,11},{4,12},{5,13},{6,14},{7,15},{8,0},{9,1},... | collective-permute-start | bytes 196616 | tf_op jit(solution)/shard_map/ppermute | solution.py:18
  8.2 0.0 copy-start.3
  8.2 3.1 %shard_map.87 = f32[4,128,128]{2,1,0:T(8,128)S(1)} custom-call(s32[1]{0:T(128)} %bitcast.me_ref, bf16[2,1792,128]{2,1,0:T(8,128)(2,1)S(1)} %get-tuple-element.12.proj_ref, bf16[2048,1792]{1,0:T(8,128)(2,1)} %grads_ref.3), custom_call_target="tpu_custom_call" | custom-call | flops 234881024 | bytes 3670016 | tf_op jit(solution)/shard_map/pallas_call | solution.py:74
  11.4 0.0 collective-permute-done
  11.4 1.6 %collective-permute-start.1 = (bf16[2,128,128]{2,1,0:T(8,128)(2,1)S(1)}, bf16[2,128,128]{2,1,0:T(8,128)(2,1)S(1)}, u32[]{:S(2)}, u32[]{:S(2)}) collective-permute-start(bf16[2,128,128]{2,1,0:T(8,128)(2,1)S(1)} %slice.72), channel_id=1, source_target_pairs={{0,2},{1,3},{2,0},{3,1},{4,6},{5,7},{6,4},{7,5},{8,10},{9,11},{10,... | collective-permute-start | bytes 196616 | tf_op jit(solution)/shard_map/ppermute | solution.py:18
  13.0 0.0 copy-done
  13.0 0.0 copy-done.3
  13.0 0.9 %fusion.2 = f32[64,128]{1,0:T(8,128)S(1)} fusion(bf16[8192,64]{0,1:T(8,128)(2,1)S(1)} %copy-done.3, bf16[128,8192]{1,0:T(8,128)(2,1)S(1)} %copy-done), kind=kOutput, calls=%fused_computation.16 | convolution fusion | flops 134217728 | bytes 3178496 | tf_op jit(solution)/shard_map/dot_general | solution.py:313
  13.9 1.6 %collective-permute-start.4 = (f32[64,128]{1,0:T(8,128)S(1)}, f32[64,128]{1,0:T(8,128)S(1)}, u32[]{:S(2)}, u32[]{:S(2)}) collective-permute-start(f32[64,128]{1,0:T(8,128)S(1)} %fusion.2), channel_id=1, source_target_pairs={{0,4},{1,5},{2,6},{3,7},{4,0},{5,1},{6,2},{7,3},{8,12},{9,13},{10,... | collective-permute-start | bytes 98312 | tf_op jit(solution)/shard_map/ppermute | solution.py:18
  15.5 0.2 collective-permute-done.1
  15.8 0.0 collective-permute-done.5
  15.8 1.6 %collective-permute-start.6 = (bf16[16,4096]{1,0:T(8,128)(2,1)S(1)}, bf16[16,4096]{1,0:T(8,128)(2,1)S(1)}, u32[]{:S(2)}, u32[]{:S(2)}) collective-permute-start(bf16[16,4096]{1,0:T(8,128)(2,1)S(1)} %pad_maximum_fusion), channel_id=1, source_target_pairs={{0,2},{1,3},{2,0},{3,1},{4,6},{5,7},{6,4},{7,5},{8,10},{9,11},{10,... | collective-permute-start | bytes 393224 | tf_op jit(solution)/shard_map/ppermute | solution.py:18
  17.4 0.4 collective-permute-start.2
  17.8 3.0 %collective-permute-done.6 = bf16[16,4096]{1,0:T(8,128)(2,1)S(1)} collective-permute-done((bf16[16,4096]{1,0:T(8,128)(2,1)S(1)}, bf16[16,4096]{1,0:T(8,128)(2,1)S(1)}, u32[]{:S(2)}, u32[]{:S(2)}) %collective-permute-start.6) | collective-permute-done | bytes 131104 | tf_op jit(solution)/shard_map/ppermute | solution.py:18
  20.9 0.1 collective-permute-start.7
  20.9 1.4 %collective-permute-done.2 = bf16[1,128,128]{2,1,0:T(8,128)(2,1)S(1)} collective-permute-done((bf16[1,128,128]{2,1,0:T(8,128)(2,1)S(1)}, bf16[1,128,128]{2,1,0:T(8,128)(2,1)S(1)}, u32[]{:S(2)}, u32[]{:S(2)}) %collective-permute-start.2) | collective-permute-done | bytes 32800 | tf_op jit(solution)/shard_map/ppermute | solution.py:18
  22.3 1.6 %collective-permute-start.3 = (f32[128,128]{1,0:T(8,128)S(1)}, f32[128,128]{1,0:T(8,128)S(1)}, u32[]{:S(2)}, u32[]{:S(2)}) collective-permute-start(f32[128,128]{1,0:T(8,128)S(1)} %fusion.own_ref), channel_id=1, source_target_pairs={{0,4},{1,5},{2,6},{3,7},{4,0},{5,1},{6,2},{7,3},{8,12},{9,13},{10,... | collective-permute-start | bytes 196616 | tf_op jit(solution)/shard_map/ppermute | solution.py:18
  23.9 0.0 collective-permute-done.4
  23.9 0.0 copy-start.1
  24.0 0.0 copy-start.2
  24.0 0.0 collective-permute-done.7.refs_1_
  24.0 0.7 %shard_map.88.inner_ref = f32[2048,512]{1,0:T(8,128)S(1)} custom-call(f32[2,64,128]{2,1,0:T(8,128)S(1)} %pad_maximum_fusion.1.act_ref, bf16[32,4096]{1,0:T(8,128)(2,1)S(1)} %constant_dynamic-update-slice_fusion.refs_0_, bf16[32,4096]{1,0:T(8,128)(2,1)S(1)} %collective-permute-done.7.refs_1_), custom_call_target="tpu_custom_call" | custom-call | flops 536870912 | bytes 4194304 | tf_op jit(solution)/shard_map/pallas_call | solution.py:124
  24.7 1.9 %collective-permute-done.3.other_ref = f32[128,128]{1,0:T(8,128)S(1)} collective-permute-done((f32[128,128]{1,0:T(8,128)S(1)}, f32[128,128]{1,0:T(8,128)S(1)}, u32[]{:S(2)}, u32[]{:S(2)}) %collective-permute-start.3) | collective-permute-done | bytes 65568 | tf_op jit(solution)/shard_map/ppermute | solution.py:18
  26.6 0.0 copy-done.1
  26.6 0.0 copy-done.2
  26.6 1.1 %shard_map.89 = (f32[64,128]{1,0:T(8,128)S(1)}, f32[64,128]{1,0:T(8,128)S(1)}, f32[8,8,16]{2,1,0:T(8,128)S(1)}) custom-call(s32[1]{0:T(128)} %bitcast.me_ref, s32[16]{0:T(128)S(1)} %copy-done.1, s32[16]{0:T(128)S(1)} %copy-done.2, f32[128,128]{1,0:T(8,128)S(1)} %fusion.own_ref, f32[128,128]{1,0:T(8,128)S(1)} %collective-permute-done.3.other_ref, ...), custom_call_target="tpu_custom_call" | custom-call | flops 2097152 | bytes 4194304 | tf_op jit(solution)/shard_map/pallas_call | solution.py:224
  27.7 1.3 %collective-permute-start.9 = (f32[8,8,16]{2,1,0:T(8,128)S(1)}, f32[8,8,16]{2,1,0:T(8,128)S(1)}, u32[]{:S(2)}, u32[]{:S(2)}) collective-permute-start(f32[8,8,16]{2,1,0:T(8,128)S(1)} %get-tuple-element.19), channel_id=1, source_target_pairs={{0,1},{2,3},{4,5},{6,7},{8,9},{10,11},{12,13},{14,15},{16,17},{18,... | collective-permute-start | bytes 12296 | tf_op jit(solution)/shard_map/ppermute | solution.py:18
  29.0 0.8 %collective-permute-done.9 = f32[8,8,16]{2,1,0:T(8,128)S(1)} collective-permute-done((f32[8,8,16]{2,1,0:T(8,128)S(1)}, f32[8,8,16]{2,1,0:T(8,128)S(1)}, u32[]{:S(2)}, u32[]{:S(2)}) %collective-permute-start.9) | collective-permute-done | bytes 4128 | tf_op jit(solution)/shard_map/ppermute | solution.py:18
  29.9 0.7 %collective-permute-start.10 = (f32[2,2,8,16]{3,2,1,0:T(8,128)S(1)}, f32[2,2,8,16]{3,2,1,0:T(8,128)S(1)}, u32[]{:S(2)}, u32[]{:S(2)}) collective-permute-start(f32[2,2,8,16]{3,2,1,0:T(8,128)S(1)} %slice.57), channel_id=1, source_target_pairs={{1,3},{3,1},{5,7},{7,5},{9,11},{11,9},{13,15},{15,13},{17,19},{19,... | collective-permute-start | bytes 6152 | tf_op jit(solution)/shard_map/ppermute | solution.py:18
  30.6 0.0 collective-permute-done.10
  30.6 0.7 %collective-permute-start.11 = (f32[2,1,8,16]{3,2,1,0:T(8,128)S(1)}, f32[2,1,8,16]{3,2,1,0:T(8,128)S(1)}, u32[]{:S(2)}, u32[]{:S(2)}) collective-permute-start(f32[2,1,8,16]{3,2,1,0:T(8,128)S(1)} %slice.59), channel_id=1, source_target_pairs={{1,9},{3,11},{5,13},{7,15},{9,1},{11,3},{13,5},{15,7},{17,25},{19,... | collective-permute-start | bytes 3080 | tf_op jit(solution)/shard_map/ppermute | solution.py:18
  31.3 1.6 %collective-permute-start.8 = (f32[64,128]{1,0:T(8,128)S(1)}, f32[64,128]{1,0:T(8,128)S(1)}, u32[]{:S(2)}, u32[]{:S(2)}) collective-permute-start(f32[64,128]{1,0:T(8,128)S(1)} %get-tuple-element.18), channel_id=1, source_target_pairs={{0,4},{1,5},{2,6},{3,7},{4,0},{5,1},{6,2},{7,3},{8,12},{9,13},{10,... | collective-permute-start | bytes 98312 | tf_op jit(solution)/shard_map/ppermute | solution.py:18
  32.9 0.0 collective-permute-done.11
  32.9 1.3 %collective-permute-start.12 = (f32[1,8,16]{2,1,0:T(8,128)S(1)}, f32[1,8,16]{2,1,0:T(8,128)S(1)}, u32[]{:S(2)}, u32[]{:S(2)}) collective-permute-start(f32[1,8,16]{2,1,0:T(8,128)S(1)} %get-tuple-element.24), channel_id=1, source_target_pairs={{1,0},{3,2},{5,4},{7,6},{9,8},{11,10},{13,12},{15,14},{17,16},{19,... | collective-permute-start | bytes 1544 | tf_op jit(solution)/shard_map/ppermute | solution.py:18
  34.2 8.0 %collective-permute-done.12.more_ref = f32[1,8,16]{2,1,0:T(8,128)S(1)} collective-permute-done((f32[1,8,16]{2,1,0:T(8,128)S(1)}, f32[1,8,16]{2,1,0:T(8,128)S(1)}, u32[]{:S(2)}, u32[]{:S(2)}) %collective-permute-start.12) | collective-permute-done | bytes 544 | tf_op jit(solution)/shard_map/ppermute | solution.py:18
  42.2 0.0 collective-permute-done.8.other_ref
  42.2 1.3 %shard_map.90 = (f32[128,128]{1,0:T(8,128)}, f32[8,16]{1,0:T(8,128)}) custom-call(s32[1]{0:T(128)} %bitcast.me_ref, s32[16]{0:T(128)S(1)} %copy-done.1, s32[16]{0:T(128)S(1)} %copy-done.2, f32[64,128]{1,0:T(8,128)S(1)} %get-tuple-element.17.own_ref, f32[64,128]{1,0:T(8,128)S(1)} %collective-permute-done.8.other_ref, ...), custom_call_target="tpu_custom_call" | custom-call | tf_op jit(solution)/shard_map/pallas_call | solution.py:262
  (17 shorter events, 0.1 us)
Async XLA Ops:
  0.6 12.4 %copy-start = (bf16[128,8192]{1,0:T(8,128)(2,1)S(1)}, bf16[128,8192]{1,0:T(8,128)(2,1)}, u32[]{:S(2)}) copy-start(bf16[128,8192]{1,0:T(8,128)(2,1)} %param.7) | copy-start | bytes 6291460
  0.6 3.9 %copy-start.4 = (bf16[8,4096]{1,0:T(8,128)(2,1)S(1)}, bf16[8,4096]{1,0:T(8,128)(2,1)}, u32[]{:S(2)}) copy-start(bf16[8,4096]{1,0:T(8,128)(2,1)} %param.11) | copy-start | bytes 196612
  4.0 7.4 %collective-permute-start = (f32[4,128,128]{2,1,0:T(8,128)S(1)}, f32[4,128,128]{2,1,0:T(8,128)S(1)}, u32[]{:S(2)}, u32[]{:S(2)}) collective-permute-start(f32[4,128,128]{2,1,0:T(8,128)S(1)} %get-tuple-element.13), channel_id=1, source_target_pairs={{0,1},{1,0},{2,3},{3,2},{4,5},{5,4},{6,7},{7,6},{8,9},{9,8},{10,11... | collective-permute-start | bytes 786440 | tf_op jit(solution)/shard_map/ppermute | solution.py:18
  4.5 11.3 %collective-permute-start.5 = (bf16[8,4096]{1,0:T(8,128)(2,1)S(1)}, bf16[8,4096]{1,0:T(8,128)(2,1)S(1)}, u32[]{:S(2)}, u32[]{:S(2)}) collective-permute-start(bf16[8,4096]{1,0:T(8,128)(2,1)S(1)} %copy-done.4), channel_id=1, source_target_pairs={{0,8},{1,9},{2,10},{3,11},{4,12},{5,13},{6,14},{7,15},{8,0},{9,1},... | collective-permute-start | bytes 196616 | tf_op jit(solution)/shard_map/ppermute | solution.py:18
  8.2 4.8 %copy-start.3 = (bf16[8192,64]{0,1:T(8,128)(2,1)S(1)}, bf16[8192,64]{0,1:T(8,128)(2,1)}, u32[]{:S(2)}) copy-start(bf16[8192,64]{0,1:T(8,128)(2,1)} %param.9) | copy-start | bytes 3145732
  11.4 4.3 %collective-permute-start.1 = (bf16[2,128,128]{2,1,0:T(8,128)(2,1)S(1)}, bf16[2,128,128]{2,1,0:T(8,128)(2,1)S(1)}, u32[]{:S(2)}, u32[]{:S(2)}) collective-permute-start(bf16[2,128,128]{2,1,0:T(8,128)(2,1)S(1)} %slice.72), channel_id=1, source_target_pairs={{0,2},{1,3},{2,0},{3,1},{4,6},{5,7},{6,4},{7,5},{8,10},{9,11},{10,... | collective-permute-start | bytes 196616 | tf_op jit(solution)/shard_map/ppermute | solution.py:18
  13.9 10.0 %collective-permute-start.4 = (f32[64,128]{1,0:T(8,128)S(1)}, f32[64,128]{1,0:T(8,128)S(1)}, u32[]{:S(2)}, u32[]{:S(2)}) collective-permute-start(f32[64,128]{1,0:T(8,128)S(1)} %fusion.2), channel_id=1, source_target_pairs={{0,4},{1,5},{2,6},{3,7},{4,0},{5,1},{6,2},{7,3},{8,12},{9,13},{10,... | collective-permute-start | bytes 98312 | tf_op jit(solution)/shard_map/ppermute | solution.py:18
  15.8 5.0 %collective-permute-start.6 = (bf16[16,4096]{1,0:T(8,128)(2,1)S(1)}, bf16[16,4096]{1,0:T(8,128)(2,1)S(1)}, u32[]{:S(2)}, u32[]{:S(2)}) collective-permute-start(bf16[16,4096]{1,0:T(8,128)(2,1)S(1)} %pad_maximum_fusion), channel_id=1, source_target_pairs={{0,2},{1,3},{2,0},{3,1},{4,6},{5,7},{6,4},{7,5},{8,10},{9,11},{10,... | collective-permute-start | bytes 393224 | tf_op jit(solution)/shard_map/ppermute | solution.py:18
  17.4 4.9 %collective-permute-start.2 = (bf16[1,128,128]{2,1,0:T(8,128)(2,1)S(1)}, bf16[1,128,128]{2,1,0:T(8,128)(2,1)S(1)}, u32[]{:S(2)}, u32[]{:S(2)}) collective-permute-start(bf16[1,128,128]{2,1,0:T(8,128)(2,1)S(1)} %slice.73), channel_id=1, source_target_pairs={{0,8},{1,9},{2,10},{3,11},{4,12},{5,13},{6,14},{7,15},{8,0},{9,1},... | collective-permute-start | bytes 98312 | tf_op jit(solution)/shard_map/ppermute | solution.py:18
  20.9 3.1 %collective-permute-start.7 = (bf16[32,4096]{1,0:T(8,128)(2,1)S(1)}, bf16[32,4096]{1,0:T(8,128)(2,1)S(1)}, u32[]{:S(2)}, u32[]{:S(2)}) collective-permute-start(bf16[32,4096]{1,0:T(8,128)(2,1)S(1)} %constant_dynamic-update-slice_fusion.refs_0_), channel_id=1, source_target_pairs={{0,1},{1,0},{2,3},{3,2},{4,5},{5,4},{6,7},{7,6},{8,9},{9,8},{10,11... | collective-permute-start | bytes 786440 | tf_op jit(solution)/shard_map/ppermute | solution.py:18
  22.3 4.3 %collective-permute-start.3 = (f32[128,128]{1,0:T(8,128)S(1)}, f32[128,128]{1,0:T(8,128)S(1)}, u32[]{:S(2)}, u32[]{:S(2)}) collective-permute-start(f32[128,128]{1,0:T(8,128)S(1)} %fusion.own_ref), channel_id=1, source_target_pairs={{0,4},{1,5},{2,6},{3,7},{4,0},{5,1},{6,2},{7,3},{8,12},{9,13},{10,... | collective-permute-start | bytes 196616 | tf_op jit(solution)/shard_map/ppermute | solution.py:18
  23.9 2.7 %copy-start.1 = (s32[16]{0:T(128)S(1)}, s32[16]{0:T(128)}, u32[]{:S(2)}) copy-start(s32[16]{0:T(128)} %length_ref.3) | copy-start | bytes 196
  24.0 2.7 %copy-start.2 = (s32[16]{0:T(128)S(1)}, s32[16]{0:T(128)}, u32[]{:S(2)}) copy-start(s32[16]{0:T(128)} %valid_ref.3) | copy-start | bytes 196
  27.7 2.1 %collective-permute-start.9 = (f32[8,8,16]{2,1,0:T(8,128)S(1)}, f32[8,8,16]{2,1,0:T(8,128)S(1)}, u32[]{:S(2)}, u32[]{:S(2)}) collective-permute-start(f32[8,8,16]{2,1,0:T(8,128)S(1)} %get-tuple-element.19), channel_id=1, source_target_pairs={{0,1},{2,3},{4,5},{6,7},{8,9},{10,11},{12,13},{14,15},{16,17},{18,... | collective-permute-start | bytes 12296 | tf_op jit(solution)/shard_map/ppermute | solution.py:18
  29.9 0.7 %collective-permute-start.10 = (f32[2,2,8,16]{3,2,1,0:T(8,128)S(1)}, f32[2,2,8,16]{3,2,1,0:T(8,128)S(1)}, u32[]{:S(2)}, u32[]{:S(2)}) collective-permute-start(f32[2,2,8,16]{3,2,1,0:T(8,128)S(1)} %slice.57), channel_id=1, source_target_pairs={{1,3},{3,1},{5,7},{7,5},{9,11},{11,9},{13,15},{15,13},{17,19},{19,... | collective-permute-start | bytes 6152 | tf_op jit(solution)/shard_map/ppermute | solution.py:18
  30.6 2.3 %collective-permute-start.11 = (f32[2,1,8,16]{3,2,1,0:T(8,128)S(1)}, f32[2,1,8,16]{3,2,1,0:T(8,128)S(1)}, u32[]{:S(2)}, u32[]{:S(2)}) collective-permute-start(f32[2,1,8,16]{3,2,1,0:T(8,128)S(1)} %slice.59), channel_id=1, source_target_pairs={{1,9},{3,11},{5,13},{7,15},{9,1},{11,3},{13,5},{15,7},{17,25},{19,... | collective-permute-start | bytes 3080 | tf_op jit(solution)/shard_map/ppermute | solution.py:18
  31.3 11.0 %collective-permute-start.8 = (f32[64,128]{1,0:T(8,128)S(1)}, f32[64,128]{1,0:T(8,128)S(1)}, u32[]{:S(2)}, u32[]{:S(2)}) collective-permute-start(f32[64,128]{1,0:T(8,128)S(1)} %get-tuple-element.18), channel_id=1, source_target_pairs={{0,4},{1,5},{2,6},{3,7},{4,0},{5,1},{6,2},{7,3},{8,12},{9,13},{10,... | collective-permute-start | bytes 98312 | tf_op jit(solution)/shard_map/ppermute | solution.py:18
  32.9 9.3 %collective-permute-start.12 = (f32[1,8,16]{2,1,0:T(8,128)S(1)}, f32[1,8,16]{2,1,0:T(8,128)S(1)}, u32[]{:S(2)}, u32[]{:S(2)}) collective-permute-start(f32[1,8,16]{2,1,0:T(8,128)S(1)} %get-tuple-element.24), channel_id=1, source_target_pairs={{1,0},{3,2},{5,4},{7,6},{9,8},{11,10},{13,12},{15,14},{17,16},{19,... | collective-permute-start | bytes 1544 | tf_op jit(solution)/shard_map/ppermute | solution.py:18

commit v8 on v6

--- a/solution.py
+++ b/solution.py
@@ -10,66 +10,50 @@
 MIB = 1 << 20
 SMEM = pl.BlockSpec(memory_space=pltpu.SMEM)
 VMEM = pl.BlockSpec(memory_space=pltpu.VMEM)
-HBM = pl.BlockSpec(memory_space=pltpu.HBM)
 
 
 def swap(value, offset, size):
     return lax.ppermute(value, "seq", [(i, i ^ offset) for i in range(size)])
 
 
-def grad_kernel(offsets, me_ref, proj_ref, grads_ref, out_ref, proj_buf, table, grads_buf, proj_sem, sems):
-    halves, total, depth = grads_buf.shape
-    count = len(offsets) // halves
-    rows = total // count
-    width = proj_buf.shape[0]
-    load = pltpu.make_async_copy(proj_ref, proj_buf, proj_sem)
-    load.start()
-    copies = []
-    for k, offset in enumerate(offsets):
-        first = pl.multiple_of((me_ref[0] ^ offset) * rows, rows)
-        copy = pltpu.make_async_copy(
-            grads_ref.at[pl.ds(first, rows)],
-            grads_buf.at[k % halves, pl.ds((k // halves) * rows, rows)],
-            sems.at[k],
-        )
-        copy.start(priority=k % 2)
-        copies.append(copy)
-    load.wait()
-    turned = proj_buf[...].T
-    none = jnp.zeros_like(turned)
-    for r in range(halves):
-        table[r] = jnp.concatenate([turned if c == r else none for c in range(halves)], axis=1)
+def grad_kernel(offsets, fresh, me_ref, proj_ref, grads_ref, out_ref, *refs):
+    table = refs[0] if fresh else proj_ref
+    halves = table.shape[0]
+    count, rows, _ = out_ref.shape
+    if fresh:
+        turned = proj_ref[...].T
+        none = jnp.zeros_like(turned)
+        for r in range(halves):
+            table[r] = jnp.concatenate([turned if c == r else none for c in range(halves)], axis=1)
     for k in range(0, count, 2):
-        for copy in copies[k * halves : (k + 2) * halves]:
-            copy.wait()
         made = None
         for r in range(halves):
+            left = []
+            for offset in (offsets[k * halves + r], offsets[(k + 1) * halves + r]):
+                first = pl.multiple_of((me_ref[0] ^ offset) * rows, rows)
+                left.append(grads_ref[pl.ds(first, rows)])
             part = jnp.dot(
-                grads_buf[r, k * rows : (k + 2) * rows],
-                table[r],
-                preferred_element_type=jnp.float32,
+                jnp.concatenate(left, axis=0), table[r], preferred_element_type=jnp.float32
             )
             made = part if made is None else made + part
         out_ref[k] = made[:rows]
         out_ref[k + 1] = made[rows:]
 
 
-def grad_blocks(me, proj, out_grads, rows, offsets):
-    width, depth = proj.shape
+def grad_blocks(me, proj, out_grads, rows, offsets, fresh):
+    depth = out_grads.shape[1]
+    width = proj.shape[0] if fresh else proj.shape[2] // 2
     count = len(offsets) // 2
+    made = jax.ShapeDtypeStruct((count, rows, 2 * width), jnp.float32)
+    table = jax.ShapeDtypeStruct((2, depth, 2 * width), jnp.bfloat16)
+    held = jax.ShapeDtypeStruct(out_grads.shape, out_grads.dtype)
     return pl.pallas_call(
-        functools.partial(grad_kernel, offsets),
-        in_specs=[SMEM, HBM, HBM],
-        out_specs=VMEM,
-        out_shape=jax.ShapeDtypeStruct((count, rows, 2 * width), jnp.float32),
-        scratch_shapes=[
-            pltpu.VMEM((width, depth), jnp.bfloat16),
-            pltpu.VMEM((2, depth, 2 * width), jnp.bfloat16),
-            pltpu.VMEM((2, count * rows, depth), jnp.bfloat16),
-            pltpu.SemaphoreType.DMA,
-            pltpu.SemaphoreType.DMA((2 * count,)),
-        ],
-        compiler_params=pltpu.CompilerParams(vmem_limit_bytes=52 * MIB),
+        functools.partial(grad_kernel, offsets, fresh),
+        in_specs=[SMEM, VMEM, VMEM],
+        out_specs=(VMEM,) * 3 if fresh else VMEM,
+        out_shape=(made, table, held) if fresh else made,
+        input_output_aliases={2: 2} if fresh else {},
+        compiler_params=pltpu.CompilerParams(vmem_limit_bytes=24 * MIB),
         cost_estimate=pl.CostEstimate(
             flops=4 * count * rows * depth * width,
             bytes_accessed=4 * count * rows * depth,
@@ -276,13 +260,13 @@
     split = size // 4
     middle = [1 << k for k in range(1, size.bit_length() - 1) if 1 << k != split]
 
-    panel, place = queries, [0]
+    proj = proj_out.T
+    spots = [offset_of(m, middle) + split * r for m in range(size // 4) for r in range(2)]
+    theirs, table, held = grad_blocks(me, proj, out_grads, rows, [s + 1 for s in spots], True)
+    from_core = swap(theirs, 1, size)
+    panel = queries
     got = swap(panel, middle[-1], size)
-
-    proj = pltpu.with_memory_space_constraint(proj_out.T, pltpu.HBM)
-    spots = [offset_of(m, middle) + split * r for m in range(size // 4) for r in range(2)]
-    from_core = swap(grad_blocks(me, proj, out_grads, rows, [s + 1 for s in spots]), 1, size)
-    sums = grad_blocks(me, proj, out_grads, rows, spots) + from_core
+    sums = grad_blocks(me, table, held, rows, spots, False) + from_core
     late, _ = lax.optimization_barrier((proj_in, sums))
     for k, bit in enumerate(middle):
         half = sums.shape[0] // 2

time: 38.7 us -> 50.4 us (1.30)
  local copies, waits for them, and re-layouts: 0.09 us -> 15.8 us
  Pallas kernels: 9.44 us -> 5.69 us
    unnamed x12 -> x21, local copies, waits for them, and re-layouts: 0.05 us -> 15.8 us
    pallas_call x2, Pallas kernels: 6.36 us -> 2.62 us  [grad_blocks(): pl.pallas_call(functools.partial(grad_kernel, offsets, fresh), in_specs=[...]
    ppermute x12, starting transfers between devices: 14 us -> 13.5 us  [swap(): return lax.ppermute(value, 'seq', [(i, i ^ offset) for i in range(size)])]
  transfers between devices with their start and end apart: 12 -> 12, of which waited for: 7 -> 7; matrix products, arithmetic and copies ran while one was open for 3% -> 2% of each run, Pallas kernels for 18% -> 4%
where the time goes in v8:
time: 50.4 us; the launch traced here: 50.2 us
  local copies, waits for them, and re-layouts  15.8 us (31%)
  starting transfers between devices  13.5 us (27%)
  waiting for transfers between devices  13.5 us (27%)
  Pallas kernels  5.69 us (11%)
  matrix products  0.89 us (2%)
  between operations  0.81 us (2%)
    unnamed x21, local copies, waits for them, and re-layouts  15.8 us
    ppermute x12, starting transfers between devices, swap(): return lax.ppermute(value, 'seq', [(i, i ^ offset) for i in range(size)])  13.5 us
    ppermute x12, waiting for transfers between devices, swap(): return lax.ppermute(value, 'seq', [(i, i ^ offset) for i in range(size)])  13.5 us
    pallas_call x2, Pallas kernels, grad_blocks(): pl.pallas_call(functools.partial(grad_kernel, offsets, fresh), in_specs=[...  2.62 us
    pallas_call x1, Pallas kernels, last(): pl.pallas_call(functools.partial(last_kernel, place, split), in_specs=[SM...  1.29 us
    pallas_call x1, Pallas kernels, score(): pl.pallas_call(functools.partial(score_kernel, steps, split), out_shape=(...  1.08 us
  transfers between devices with their start and end apart: 12, of which 7 were waited for; matrix products, arithmetic and copies ran while one was open for 2% of the time, Pallas kernels for 4%

profile of v8, /device:TPU:0, one launch (start us, length us, event | category | flops | bytes accessed | tf_op | source)
XLA Modules:
  0.0 50.2 jit_solution(10953258156766975095)
XLA Ops:
  0.6 0.0 copy-start
  0.6 0.0 copy-start.4
  0.7 0.0 copy-start.8
  0.7 6.6 %copy.14.grads_ref = bf16[2048,1792]{1,0:T(8,128)(2,1)} copy(bf16[2048,1792]{1,0:T(8,128)(2,1)} %param.8) | data formatting | bytes 14680064
  7.3 0.0 copy-done.4
  7.3 0.0 copy-start.1
  7.3 3.1 %copy-done.1 = bf16[2048,1792]{1,0:T(8,128)(2,1)S(1)} copy-done((bf16[2048,1792]{1,0:T(8,128)(2,1)S(1)}, bf16[2048,1792]{1,0:T(8,128)(2,1)}, u32[]{:S(2)}) %copy-start.1) | copy-done | bytes 7340056
  10.4 1.5 %shard_map.86 = (f32[4,128,128]{2,1,0:T(8,128)S(1)}, bf16[2,1792,128]{2,1,0:T(8,128)(2,1)S(1)}, bf16[2048,1792]{1,0:T(8,128)(2,1)S(1)}) custom-call(s32[1]{0:T(128)} %bitcast.me_ref, bf16[64,1792]{1,0:T(8,128)(2,1)S(1)} %bitcast.9, bf16[2048,1792]{1,0:T(8,128)(2,1)S(1)} %copy-done.1), custom_call_target="tpu_custom_call", output_to_operand_aliasing={{2}: (2, {})} | custom-call | flops 234881024 | bytes 3670016 | tf_op jit(solution)/shard_map/pallas_call | solution.py:50
  11.9 0.0 copy-start.2
  11.9 2.9 %copy-done.2 = bf16[2048,1792]{1,0:T(8,128)(2,1)} copy-done((bf16[2048,1792]{1,0:T(8,128)(2,1)}, bf16[2048,1792]{1,0:T(8,128)(2,1)S(1)}, u32[]{:S(2)}) %copy-start.2) | copy-done | bytes 7340056
  14.9 0.4 collective-permute-start
  15.3 0.0 copy-done.8
  15.3 3.6 %collective-permute-start.5 = (bf16[8,4096]{1,0:T(8,128)(2,1)S(1)}, bf16[8,4096]{1,0:T(8,128)(2,1)S(1)}, u32[]{:S(2)}, u32[]{:S(2)}) collective-permute-start(bf16[8,4096]{1,0:T(8,128)(2,1)S(1)} %copy-done.8), channel_id=1, source_target_pairs={{0,8},{1,9},{2,10},{3,11},{4,12},{5,13},{6,14},{7,15},{8,0},{9,1},... | collective-permute-start | bytes 196616 | tf_op jit(solution)/shard_map/ppermute | solution.py:16
  18.9 3.1 %copy-done.3 = bf16[2048,1792]{1,0:T(8,128)(2,1)S(1)} copy-done((bf16[2048,1792]{1,0:T(8,128)(2,1)S(1)}, bf16[2048,1792]{1,0:T(8,128)(2,1)}, u32[]{:S(2)}) %copy-start.3) | copy-done | bytes 7340056
  22.0 0.0 copy-start.7
  22.0 1.1 %shard_map.87 = f32[4,128,128]{2,1,0:T(8,128)S(1)} custom-call(s32[1]{0:T(128)} %bitcast.me_ref, bf16[2,1792,128]{2,1,0:T(8,128)(2,1)S(1)} %get-tuple-element.12.proj_ref, bf16[2048,1792]{1,0:T(8,128)(2,1)S(1)} %copy-done.3), custom_call_target="tpu_custom_call" | custom-call | flops 234881024 | bytes 3670016 | tf_op jit(solution)/shard_map/pallas_call | solution.py:50
  23.1 0.0 collective-permute-done
  23.2 0.0 copy-start.5
  23.2 0.0 copy-start.6
  23.2 1.6 %collective-permute-start.1 = (bf16[2,128,128]{2,1,0:T(8,128)(2,1)S(1)}, bf16[2,128,128]{2,1,0:T(8,128)(2,1)S(1)}, u32[]{:S(2)}, u32[]{:S(2)}) collective-permute-start(bf16[2,128,128]{2,1,0:T(8,128)(2,1)S(1)} %slice.58), channel_id=1, source_target_pairs={{0,2},{1,3},{2,0},{3,1},{4,6},{5,7},{6,4},{7,5},{8,10},{9,11},{10,... | collective-permute-start | bytes 196616 | tf_op jit(solution)/shard_map/ppermute | solution.py:16
  24.8 0.0 copy-done
  24.8 0.0 copy-done.7
  24.8 0.9 %fusion.2 = f32[64,128]{1,0:T(8,128)S(1)} fusion(bf16[8192,64]{0,1:T(8,128)(2,1)S(1)} %copy-done.7, bf16[128,8192]{1,0:T(8,128)(2,1)S(1)} %copy-done), kind=kOutput, calls=%fused_computation.13 | convolution fusion | flops 134217728 | bytes 3178496 | tf_op jit(solution)/shard_map/dot_general | solution.py:288
  25.7 1.6 %collective-permute-start.4 = (f32[64,128]{1,0:T(8,128)S(1)}, f32[64,128]{1,0:T(8,128)S(1)}, u32[]{:S(2)}, u32[]{:S(2)}) collective-permute-start(f32[64,128]{1,0:T(8,128)S(1)} %fusion.2), channel_id=1, source_target_pairs={{0,4},{1,5},{2,6},{3,7},{4,0},{5,1},{6,2},{7,3},{8,12},{9,13},{10,... | collective-permute-start | bytes 98312 | tf_op jit(solution)/shard_map/ppermute | solution.py:16
  27.3 0.2 collective-permute-done.1
  27.5 0.0 collective-permute-done.5
  27.6 1.6 %collective-permute-start.6 = (bf16[16,4096]{1,0:T(8,128)(2,1)S(1)}, bf16[16,4096]{1,0:T(8,128)(2,1)S(1)}, u32[]{:S(2)}, u32[]{:S(2)}) collective-permute-start(bf16[16,4096]{1,0:T(8,128)(2,1)S(1)} %pad_maximum_fusion), channel_id=1, source_target_pairs={{0,2},{1,3},{2,0},{3,1},{4,6},{5,7},{6,4},{7,5},{8,10},{9,11},{10,... | collective-permute-start | bytes 393224 | tf_op jit(solution)/shard_map/ppermute | solution.py:16
  29.2 0.4 collective-permute-start.2
  29.6 3.0 %collective-permute-done.6 = bf16[16,4096]{1,0:T(8,128)(2,1)S(1)} collective-permute-done((bf16[16,4096]{1,0:T(8,128)(2,1)S(1)}, bf16[16,4096]{1,0:T(8,128)(2,1)S(1)}, u32[]{:S(2)}, u32[]{:S(2)}) %collective-permute-start.6) | collective-permute-done | bytes 131104 | tf_op jit(solution)/shard_map/ppermute | solution.py:16
  32.6 0.1 collective-permute-start.7
  32.7 1.4 %collective-permute-done.2 = bf16[1,128,128]{2,1,0:T(8,128)(2,1)S(1)} collective-permute-done((bf16[1,128,128]{2,1,0:T(8,128)(2,1)S(1)}, bf16[1,128,128]{2,1,0:T(8,128)(2,1)S(1)}, u32[]{:S(2)}, u32[]{:S(2)}) %collective-permute-start.2) | collective-permute-done | bytes 32800 | tf_op jit(solution)/shard_map/ppermute | solution.py:16
  34.1 1.6 %collective-permute-start.3 = (f32[128,128]{1,0:T(8,128)S(1)}, f32[128,128]{1,0:T(8,128)S(1)}, u32[]{:S(2)}, u32[]{:S(2)}) collective-permute-start(f32[128,128]{1,0:T(8,128)S(1)} %fusion.own_ref), channel_id=1, source_target_pairs={{0,4},{1,5},{2,6},{3,7},{4,0},{5,1},{6,2},{7,3},{8,12},{9,13},{10,... | collective-permute-start | bytes 196616 | tf_op jit(solution)/shard_map/ppermute | solution.py:16
  35.7 0.0 collective-permute-done.4
  35.7 0.0 collective-permute-done.7.refs_1_
  35.7 0.7 %shard_map.88.inner_ref = f32[2048,512]{1,0:T(8,128)S(1)} custom-call(f32[2,64,128]{2,1,0:T(8,128)S(1)} %pad_maximum_fusion.1.act_ref, bf16[32,4096]{1,0:T(8,128)(2,1)S(1)} %constant_dynamic-update-slice_fusion.refs_0_, bf16[32,4096]{1,0:T(8,128)(2,1)S(1)} %collective-permute-done.7.refs_1_), custom_call_target="tpu_custom_call" | custom-call | flops 536870912 | bytes 4194304 | tf_op jit(solution)/shard_map/pallas_call | solution.py:100
  36.4 2.0 %collective-permute-done.3.other_ref = f32[128,128]{1,0:T(8,128)S(1)} collective-permute-done((f32[128,128]{1,0:T(8,128)S(1)}, f32[128,128]{1,0:T(8,128)S(1)}, u32[]{:S(2)}, u32[]{:S(2)}) %collective-permute-start.3) | collective-permute-done | bytes 65568 | tf_op jit(solution)/shard_map/ppermute | solution.py:16
  38.4 0.0 copy-done.5
  38.4 0.0 copy-done.6
  38.4 1.1 %shard_map.89 = (f32[64,128]{1,0:T(8,128)S(1)}, f32[64,128]{1,0:T(8,128)S(1)}, f32[8,8,16]{2,1,0:T(8,128)S(1)}) custom-call(s32[1]{0:T(128)} %bitcast.me_ref, s32[16]{0:T(128)S(1)} %copy-done.5, s32[16]{0:T(128)S(1)} %copy-done.6, f32[128,128]{1,0:T(8,128)S(1)} %fusion.own_ref, f32[128,128]{1,0:T(8,128)S(1)} %collective-permute-done.3.other_ref, ...), custom_call_target="tpu_custom_call" | custom-call | flops 2097152 | bytes 4194304 | tf_op jit(solution)/shard_map/pallas_call | solution.py:200
  39.5 0.1 collective-permute-start.9
  39.6 1.2 %collective-permute-done.9 = f32[4,8,16]{2,1,0:T(8,128)S(1)} collective-permute-done((f32[4,8,16]{2,1,0:T(8,128)S(1)}, f32[4,8,16]{2,1,0:T(8,128)S(1)}, u32[]{:S(2)}, u32[]{:S(2)}) %collective-permute-start.9) | collective-permute-done | bytes 2080 | tf_op jit(solution)/shard_map/ppermute | solution.py:16
  40.8 0.5 %collective-permute-start.10 = (f32[2,8,16]{2,1,0:T(8,128)S(1)}, f32[2,8,16]{2,1,0:T(8,128)S(1)}, u32[]{:S(2)}, u32[]{:S(2)}) collective-permute-start(f32[2,8,16]{2,1,0:T(8,128)S(1)} %slice.47), channel_id=1, source_target_pairs={{0,2},{1,3},{2,0},{3,1},{4,6},{5,7},{6,4},{7,5},{8,10},{9,11},{10,... | collective-permute-start | bytes 3080 | tf_op jit(solution)/shard_map/ppermute | solution.py:16
  41.3 1.6 %collective-permute-start.8 = (f32[64,128]{1,0:T(8,128)S(1)}, f32[64,128]{1,0:T(8,128)S(1)}, u32[]{:S(2)}, u32[]{:S(2)}) collective-permute-start(f32[64,128]{1,0:T(8,128)S(1)} %get-tuple-element.18), channel_id=1, source_target_pairs={{0,4},{1,5},{2,6},{3,7},{4,0},{5,1},{6,2},{7,3},{8,12},{9,13},{10,... | collective-permute-start | bytes 98312 | tf_op jit(solution)/shard_map/ppermute | solution.py:16
  42.9 1.6 %collective-permute-done.10 = f32[2,8,16]{2,1,0:T(8,128)S(1)} collective-permute-done((f32[2,8,16]{2,1,0:T(8,128)S(1)}, f32[2,8,16]{2,1,0:T(8,128)S(1)}, u32[]{:S(2)}, u32[]{:S(2)}) %collective-permute-start.10) | collective-permute-done | bytes 1056 | tf_op jit(solution)/shard_map/ppermute | solution.py:16
  44.4 0.4 collective-permute-start.11
  44.8 4.1 %collective-permute-done.11.more_ref = f32[1,8,16]{2,1,0:T(8,128)S(1)} collective-permute-done((f32[1,8,16]{2,1,0:T(8,128)S(1)}, f32[1,8,16]{2,1,0:T(8,128)S(1)}, u32[]{:S(2)}, u32[]{:S(2)}) %collective-permute-start.11) | collective-permute-done | bytes 544 | tf_op jit(solution)/shard_map/ppermute | solution.py:16
  48.9 0.0 collective-permute-done.8.other_ref
  48.9 1.3 %shard_map.90 = (f32[128,128]{1,0:T(8,128)}, f32[8,16]{1,0:T(8,128)}) custom-call(s32[1]{0:T(128)} %bitcast.me_ref, s32[16]{0:T(128)S(1)} %copy-done.5, s32[16]{0:T(128)S(1)} %copy-done.6, f32[64,128]{1,0:T(8,128)S(1)} %get-tuple-element.17.own_ref, f32[64,128]{1,0:T(8,128)S(1)} %collective-permute-done.8.other_ref, ...), custom_call_target="tpu_custom_call" | custom-call | tf_op jit(solution)/shard_map/pallas_call | solution.py:237
  (16 shorter events, 0.1 us)
Async XLA Ops:
  0.6 24.2 %copy-start = (bf16[128,8192]{1,0:T(8,128)(2,1)S(1)}, bf16[128,8192]{1,0:T(8,128)(2,1)}, u32[]{:S(2)}) copy-start(bf16[128,8192]{1,0:T(8,128)(2,1)} %param.7) | copy-start | bytes 6291460
  0.6 6.7 %copy-start.4 = (bf16[1792,64]{0,1:T(8,128)(2,1)S(1)}, bf16[1792,64]{0,1:T(8,128)(2,1)}, u32[]{:S(2)}) copy-start(bf16[1792,64]{0,1:T(8,128)(2,1)} %param.10) | copy-start | bytes 688132
  0.7 14.7 %copy-start.8 = (bf16[8,4096]{1,0:T(8,128)(2,1)S(1)}, bf16[8,4096]{1,0:T(8,128)(2,1)}, u32[]{:S(2)}) copy-start(bf16[8,4096]{1,0:T(8,128)(2,1)} %param.11) | copy-start | bytes 196612
  7.3 3.1 %copy-start.1 = (bf16[2048,1792]{1,0:T(8,128)(2,1)S(1)}, bf16[2048,1792]{1,0:T(8,128)(2,1)}, u32[]{:S(2)}) copy-start(bf16[2048,1792]{1,0:T(8,128)(2,1)} %copy.14.grads_ref) | copy-start | bytes 22020100
  11.9 2.9 %copy-start.2 = (bf16[2048,1792]{1,0:T(8,128)(2,1)}, bf16[2048,1792]{1,0:T(8,128)(2,1)S(1)}, u32[]{:S(2)}) copy-start(bf16[2048,1792]{1,0:T(8,128)(2,1)S(1)} %get-tuple-element.13.grads_ref) | copy-start | bytes 22020100
  14.9 8.2 %collective-permute-start = (f32[4,128,128]{2,1,0:T(8,128)S(1)}, f32[4,128,128]{2,1,0:T(8,128)S(1)}, u32[]{:S(2)}, u32[]{:S(2)}) collective-permute-start(f32[4,128,128]{2,1,0:T(8,128)S(1)} %get-tuple-element.14), channel_id=1, source_target_pairs={{0,1},{1,0},{2,3},{3,2},{4,5},{5,4},{6,7},{7,6},{8,9},{9,8},{10,11... | collective-permute-start | bytes 786440 | tf_op jit(solution)/shard_map/ppermute | solution.py:16
  15.3 12.2 %collective-permute-start.5 = (bf16[8,4096]{1,0:T(8,128)(2,1)S(1)}, bf16[8,4096]{1,0:T(8,128)(2,1)S(1)}, u32[]{:S(2)}, u32[]{:S(2)}) collective-permute-start(bf16[8,4096]{1,0:T(8,128)(2,1)S(1)} %copy-done.8), channel_id=1, source_target_pairs={{0,8},{1,9},{2,10},{3,11},{4,12},{5,13},{6,14},{7,15},{8,0},{9,1},... | collective-permute-start | bytes 196616 | tf_op jit(solution)/shard_map/ppermute | solution.py:16
  18.9 3.1 %copy-start.3 = (bf16[2048,1792]{1,0:T(8,128)(2,1)S(1)}, bf16[2048,1792]{1,0:T(8,128)(2,1)}, u32[]{:S(2)}) copy-start(bf16[2048,1792]{1,0:T(8,128)(2,1)} %copy-done.2) | copy-start | bytes 22020100
  22.0 2.8 %copy-start.7 = (bf16[8192,64]{0,1:T(8,128)(2,1)S(1)}, bf16[8192,64]{0,1:T(8,128)(2,1)}, u32[]{:S(2)}) copy-start(bf16[8192,64]{0,1:T(8,128)(2,1)} %param.9) | copy-start | bytes 3145732
  23.2 15.2 %copy-start.5 = (s32[16]{0:T(128)S(1)}, s32[16]{0:T(128)}, u32[]{:S(2)}) copy-start(s32[16]{0:T(128)} %length_ref.3) | copy-start | bytes 196
  23.2 15.2 %copy-start.6 = (s32[16]{0:T(128)S(1)}, s32[16]{0:T(128)}, u32[]{:S(2)}) copy-start(s32[16]{0:T(128)} %valid_ref.3) | copy-start | bytes 196
  23.2 4.3 %collective-permute-start.1 = (bf16[2,128,128]{2,1,0:T(8,128)(2,1)S(1)}, bf16[2,128,128]{2,1,0:T(8,128)(2,1)S(1)}, u32[]{:S(2)}, u32[]{:S(2)}) collective-permute-start(bf16[2,128,128]{2,1,0:T(8,128)(2,1)S(1)} %slice.58), channel_id=1, source_target_pairs={{0,2},{1,3},{2,0},{3,1},{4,6},{5,7},{6,4},{7,5},{8,10},{9,11},{10,... | collective-permute-start | bytes 196616 | tf_op jit(solution)/shard_map/ppermute | solution.py:16
  25.7 10.0 %collective-permute-start.4 = (f32[64,128]{1,0:T(8,128)S(1)}, f32[64,128]{1,0:T(8,128)S(1)}, u32[]{:S(2)}, u32[]{:S(2)}) collective-permute-start(f32[64,128]{1,0:T(8,128)S(1)} %fusion.2), channel_id=1, source_target_pairs={{0,4},{1,5},{2,6},{3,7},{4,0},{5,1},{6,2},{7,3},{8,12},{9,13},{10,... | collective-permute-start | bytes 98312 | tf_op jit(solution)/shard_map/ppermute | solution.py:16
  27.6 5.0 %collective-permute-start.6 = (bf16[16,4096]{1,0:T(8,128)(2,1)S(1)}, bf16[16,4096]{1,0:T(8,128)(2,1)S(1)}, u32[]{:S(2)}, u32[]{:S(2)}) collective-permute-start(bf16[16,4096]{1,0:T(8,128)(2,1)S(1)} %pad_maximum_fusion), channel_id=1, source_target_pairs={{0,2},{1,3},{2,0},{3,1},{4,6},{5,7},{6,4},{7,5},{8,10},{9,11},{10,... | collective-permute-start | bytes 393224 | tf_op jit(solution)/shard_map/ppermute | solution.py:16
  29.2 4.9 %collective-permute-start.2 = (bf16[1,128,128]{2,1,0:T(8,128)(2,1)S(1)}, bf16[1,128,128]{2,1,0:T(8,128)(2,1)S(1)}, u32[]{:S(2)}, u32[]{:S(2)}) collective-permute-start(bf16[1,128,128]{2,1,0:T(8,128)(2,1)S(1)} %slice.59), channel_id=1, source_target_pairs={{0,8},{1,9},{2,10},{3,11},{4,12},{5,13},{6,14},{7,15},{8,0},{9,1},... | collective-permute-start | bytes 98312 | tf_op jit(solution)/shard_map/ppermute | solution.py:16
  32.6 3.1 %collective-permute-start.7 = (bf16[32,4096]{1,0:T(8,128)(2,1)S(1)}, bf16[32,4096]{1,0:T(8,128)(2,1)S(1)}, u32[]{:S(2)}, u32[]{:S(2)}) collective-permute-start(bf16[32,4096]{1,0:T(8,128)(2,1)S(1)} %constant_dynamic-update-slice_fusion.refs_0_), channel_id=1, source_target_pairs={{0,1},{1,0},{2,3},{3,2},{4,5},{5,4},{6,7},{7,6},{8,9},{9,8},{10,11... | collective-permute-start | bytes 786440 | tf_op jit(solution)/shard_map/ppermute | solution.py:16
  34.1 4.3 %collective-permute-start.3 = (f32[128,128]{1,0:T(8,128)S(1)}, f32[128,128]{1,0:T(8,128)S(1)}, u32[]{:S(2)}, u32[]{:S(2)}) collective-permute-start(f32[128,128]{1,0:T(8,128)S(1)} %fusion.own_ref), channel_id=1, source_target_pairs={{0,4},{1,5},{2,6},{3,7},{4,0},{5,1},{6,2},{7,3},{8,12},{9,13},{10,... | collective-permute-start | bytes 196616 | tf_op jit(solution)/shard_map/ppermute | solution.py:16
  39.5 1.2 %collective-permute-start.9 = (f32[4,8,16]{2,1,0:T(8,128)S(1)}, f32[4,8,16]{2,1,0:T(8,128)S(1)}, u32[]{:S(2)}, u32[]{:S(2)}) collective-permute-start(f32[4,8,16]{2,1,0:T(8,128)S(1)} %slice.37), channel_id=1, source_target_pairs={{0,1},{1,0},{2,3},{3,2},{4,5},{5,4},{6,7},{7,6},{8,9},{9,8},{10,11... | collective-permute-start | bytes 6152 | tf_op jit(solution)/shard_map/ppermute | solution.py:16
  40.8 3.7 %collective-permute-start.10 = (f32[2,8,16]{2,1,0:T(8,128)S(1)}, f32[2,8,16]{2,1,0:T(8,128)S(1)}, u32[]{:S(2)}, u32[]{:S(2)}) collective-permute-start(f32[2,8,16]{2,1,0:T(8,128)S(1)} %slice.47), channel_id=1, source_target_pairs={{0,2},{1,3},{2,0},{3,1},{4,6},{5,7},{6,4},{7,5},{8,10},{9,11},{10,... | collective-permute-start | bytes 3080 | tf_op jit(solution)/shard_map/ppermute | solution.py:16
  41.3 7.7 %collective-permute-start.8 = (f32[64,128]{1,0:T(8,128)S(1)}, f32[64,128]{1,0:T(8,128)S(1)}, u32[]{:S(2)}, u32[]{:S(2)}) collective-permute-start(f32[64,128]{1,0:T(8,128)S(1)} %get-tuple-element.18), channel_id=1, source_target_pairs={{0,4},{1,5},{2,6},{3,7},{4,0},{5,1},{6,2},{7,3},{8,12},{9,13},{10,... | collective-permute-start | bytes 98312 | tf_op jit(solution)/shard_map/ppermute | solution.py:16
  44.4 4.5 %collective-permute-start.11 = (f32[1,8,16]{2,1,0:T(8,128)S(1)}, f32[1,8,16]{2,1,0:T(8,128)S(1)}, u32[]{:S(2)}, u32[]{:S(2)}) collective-permute-start(f32[1,8,16]{2,1,0:T(8,128)S(1)} %get-tuple-element.22), channel_id=1, source_target_pairs={{0,8},{1,9},{2,10},{3,11},{4,12},{5,13},{6,14},{7,15},{8,0},{9,1},... | collective-permute-start | bytes 1544 | tf_op jit(solution)/shard_map/ppermute | solution.py:16

commit v9 on v7

--- a/solution.py
+++ b/solution.py
@@ -13,9 +13,8 @@
 HBM = pl.BlockSpec(memory_space=pltpu.HBM)
 
 
-def swap(value, offset, size, cores=(0, 1)):
-    pairs = [(i, i ^ offset) for i in range(size) if i % 2 in cores]
-    return lax.ppermute(value, "seq", pairs)
+def swap(value, offset, size):
+    return lax.ppermute(value, "seq", [(i, i ^ offset) for i in range(size)])
 
 
 def grad_kernel(offsets, fresh, me_ref, proj_ref, grads_ref, out_ref, *refs):
@@ -59,20 +58,74 @@
         out_ref[k + 1] = made[rows:]
 
 
+def paired_kernel(offsets, fresh, me_ref, proj_ref, grads_ref, out_ref, *refs):
+    if fresh:
+        table, proj_buf, grads_buf, sems, proj_sem = refs
+        load = pltpu.make_async_copy(proj_ref, proj_buf, proj_sem)
+        load.start()
+    else:
+        table, (grads_buf, sems) = proj_ref, refs
+    halves, total, pairs, _, lanes = grads_buf.shape
+    count, rows, wide = out_ref.shape
+    groups = rows // 8
+    copies = []
+    for k, offset in enumerate(offsets):
+        first = pl.multiple_of((me_ref[0] ^ offset) * groups, groups)
+        copy = pltpu.make_async_copy(
+            grads_ref.at[pl.ds(first, groups)],
+            grads_buf.at[k % halves, pl.ds((k // halves) * groups, groups)],
+            sems.at[k],
+        )
+        copy.start(priority=k % 2)
+        copies.append(copy)
+    if fresh:
+        load.wait()
+        turned = proj_buf[...].T
+        for p in range(pairs):
+            one = turned[2 * p * lanes : (2 * p + 1) * lanes]
+            two = turned[(2 * p + 1) * lanes : (2 * p + 2) * lanes]
+            table[0, p * lanes : (p + 1) * lanes] = jnp.concatenate([one, two], axis=1)
+            table[1, p * lanes : (p + 1) * lanes] = jnp.concatenate([two, one], axis=1)
+    lane = lax.broadcasted_iota(jnp.int32, (2 * rows, wide), 1)
+    for k in range(0, count, 2):
+        for copy in copies[k * halves : (k + 2) * halves]:
+            copy.wait()
+        sums = []
+        for r in range(halves):
+            left = [
+                grads_buf[r, k * groups : (k + 2) * groups, p].reshape(4 * rows, lanes)
+                for p in range(pairs)
+            ]
+            made = jnp.dot(
+                jnp.concatenate(left, axis=1), table[r], preferred_element_type=jnp.float32
+            ).reshape(2 * groups, 2, 8, wide)
+            one = made[:, 0].reshape(2 * rows, wide)
+            two = made[:, 1].reshape(2 * rows, wide)
+            sums.append(one + pltpu.roll(two, wide // 2, 1))
+        both = jnp.where(lane < wide // 2, sums[0], sums[1])
+        out_ref[k] = both[:rows]
+        out_ref[k + 1] = both[rows:]
+
+
 def grad_blocks(me, proj, out_grads, rows, offsets, fresh):
-    depth = out_grads.shape[1]
+    tokens, depth = out_grads.shape
     width = proj.shape[0] if fresh else proj.shape[2] // 2
     count = len(offsets) // 2
     made = jax.ShapeDtypeStruct((count, rows, 2 * width), jnp.float32)
-    table = jax.ShapeDtypeStruct((2, depth, 2 * width), jnp.bfloat16)
-    scratch = [
-        pltpu.VMEM((2, count * rows, depth), jnp.bfloat16),
-        pltpu.SemaphoreType.DMA((2 * count,)),
-    ]
+    if depth % 256 == 0 and rows % 8 == 0 and width == 64:
+        kernel, deep = paired_kernel, depth // 2
+        held = (2, count * rows // 8, depth // 256, 16, 128)
+        tiles = out_grads.reshape(tokens // 8, 8, depth // 128, 128).transpose(0, 2, 1, 3)
+        out_grads = tiles.reshape(tokens // 8, depth // 256, 16, 128)
+    else:
+        kernel, deep = grad_kernel, depth
+        held = (2, count * rows, depth)
+    table = jax.ShapeDtypeStruct((2, deep, 2 * width), jnp.bfloat16)
+    scratch = [pltpu.VMEM(held, jnp.bfloat16), pltpu.SemaphoreType.DMA((2 * count,))]
     if fresh:
         scratch = [pltpu.VMEM((width, depth), jnp.bfloat16)] + scratch + [pltpu.SemaphoreType.DMA]
     return pl.pallas_call(
-        functools.partial(grad_kernel, offsets, fresh),
+        functools.partial(kernel, offsets, fresh),
         in_specs=[SMEM, HBM if fresh else VMEM, HBM],
         out_specs=(VMEM, VMEM) if fresh else VMEM,
         out_shape=(made, table) if fresh else made,
@@ -83,7 +136,7 @@
             bytes_accessed=4 * count * rows * depth,
             transcendentals=0,
         ),
-    )(me, proj, out_grads)
+    )(me, proj, pltpu.with_memory_space_constraint(out_grads, pltpu.HBM))
 
 
 def inner_kernel(pieces, act_ref, *refs):
@@ -252,8 +305,7 @@
     used = jnp.zeros((own_q, docs), jnp.int32)
     for d in range(docs):
         used = jnp.where(doc_of == d, jnp.minimum(valid_ref[d], length_ref[d]), used)
-    doc = jnp.where(me_ref[0] % 2 == 1, doc_ref[0], more_ref[0])
-    doc_out[...] = doc * (1.0 / jnp.sqrt(used.astype(jnp.float32)))
+    doc_out[...] = (doc_ref[0] + more_ref[0]) * (1.0 / jnp.sqrt(used.astype(jnp.float32)))
 
 
 def last(me, lengths, valid, own, other, doc, more, place, split):
@@ -289,7 +341,7 @@
     spots = [offset_of(m, middle) + split * r for m in range(size // 4) for r in range(2)]
     theirs, table = grad_blocks(me, proj, out_grads, rows, [s + 1 for s in spots], True)
     from_core = swap(theirs, 1, size)
-    panel, _ = lax.optimization_barrier((queries, theirs))
+    panel = queries
     got = swap(panel, middle[-1], size)
     sums = grad_blocks(me, table, out_grads, rows, spots, False) + from_core
     late, _ = lax.optimization_barrier((proj_in, sums))
@@ -320,17 +372,13 @@
         me, doc_length, valid_count, own, across, products, split, own_q, steps
     )
     others = swap(theirs, split, size)
-    half = doc.shape[0] // 2
-    from_even = swap(doc, 1, size, (0,))
-    doc = doc + jnp.concatenate([from_even[half:], from_even[:half]], axis=0)
-    doc = doc.reshape((2, half) + doc.shape[1:])
-    for bit in middle:
-        half //= 2
-        doc = doc[:, :half] + swap(doc[:, half:], bit, size, (1,))
-    own_doc, even_doc = doc[0], doc[1]
-    from_odd = swap(even_doc, 1, size, (1,))
+    bits = [1] + middle
+    for bit in bits[:-1]:
+        half = doc.shape[0] // 2
+        doc = doc[:half] + swap(doc[half:], bit, size)
+    more = swap(doc[1:], bits[-1], size)
     token_scores, doc = last(
-        me, doc_length, valid_count, mine, others, own_doc, from_odd, place, split
+        me, doc_length, valid_count, mine, others, doc[:1], more, place, split
     )
     return (token_scores, doc.T)
 

time: 43.7 us -> 38.9 us (0.89)
  starting transfers between devices: 16.7 us -> 14 us
  waiting for transfers between devices: 15.4 us -> 13.2 us
    ppermute x13 -> x12, starting transfers between devices: 16.7 us -> 14 us  [swap(): return lax.ppermute(value, 'seq', [(i, i ^ offset) for i in range(size)])]
    ppermute x13 -> x12, waiting for transfers between devices: 15.4 us -> 13.2 us  [swap(): return lax.ppermute(value, 'seq', [(i, i ^ offset) for i in range(size)])]
  transfers between devices with their start and end apart: 13 -> 12, of which waited for: 6 -> 7; matrix products, arithmetic and copies ran while one was open for 2% -> 3% of each run, Pallas kernels for 9% -> 19%
where the time goes in v9:
time: 38.9 us; the launch traced here: 38.8 us
  starting transfers between devices  14 us (36%)
  waiting for transfers between devices  13.2 us (34%)
  Pallas kernels  9.67 us (25%)
  matrix products  0.88 us (2%)
  between operations  0.83 us (2%)
    ppermute x12, starting transfers between devices, swap(): return lax.ppermute(value, 'seq', [(i, i ^ offset) for i in range(size)])  14 us
    ppermute x12, waiting for transfers between devices, swap(): return lax.ppermute(value, 'seq', [(i, i ^ offset) for i in range(size)])  13.2 us
    pallas_call x2, Pallas kernels, grad_blocks(): pl.pallas_call(functools.partial(kernel, offsets, fresh), in_specs=[SMEM,...  6.6 us
    pallas_call x1, Pallas kernels, last(): pl.pallas_call(functools.partial(last_kernel, place, split), in_specs=[SM...  1.29 us
    pallas_call x1, Pallas kernels, score(): pl.pallas_call(functools.partial(score_kernel, steps, split), out_shape=(...  1.08 us
    dot_general x1, matrix products, body(): lax.dot_general(late, activations, (((0,), (1,)), ((), ())), preferred_el...  0.88 us
  transfers between devices with their start and end apart: 12, of which 7 were waited for; matrix products, arithmetic and copies ran while one was open for 3% of the time, Pallas kernels for 19%

profile of v9, /device:TPU:0, one launch (start us, length us, event | category | flops | bytes accessed | tf_op | source)
XLA Modules:
  0.0 38.8 jit_solution(6810806488170781711)
XLA Ops:
  0.6 0.0 copy-start
  0.6 4.1 %collective-permute-start.5 = (bf16[8,4096]{1,0:T(8,128)(2,1)}, bf16[8,4096]{1,0:T(8,128)(2,1)S(1)}, u32[]{:S(2)}, u32[]{:S(2)}) collective-permute-start(bf16[8,4096]{1,0:T(8,128)(2,1)} %param.11), channel_id=1, source_target_pairs={{0,8},{1,9},{2,10},{3,11},{4,12},{5,13},{6,14},{7,15},{8,0},{9,1},... | collective-permute-start | bytes 196616 | tf_op jit(solution)/shard_map/ppermute | solution.py:17
  4.7 3.3 %shard_map.86 = (f32[4,128,128]{2,1,0:T(8,128)S(1)}, bf16[2,896,128]{2,1,0:T(8,128)(2,1)S(1)}) custom-call(s32[1]{0:T(128)} %bitcast.me_ref, bf16[64,1792]{1,0:T(8,128)(2,1)} %bitcast.16, bf16[256,7,16,128]{3,2,1,0:T(8,128)(2,1)} %bitcast.14), custom_call_target="tpu_custom_call" | custom-call | flops 234881024 | bytes 3670016 | tf_op jit(solution)/shard_map/pallas_call | solution.py:127
  8.1 0.1 collective-permute-start
  8.1 0.0 copy-start.4
  8.1 0.0 copy-start.3
  8.2 3.3 %shard_map.87 = f32[4,128,128]{2,1,0:T(8,128)S(1)} custom-call(s32[1]{0:T(128)} %bitcast.me_ref, bf16[2,896,128]{2,1,0:T(8,128)(2,1)S(1)} %get-tuple-element.11.proj_ref, bf16[256,7,16,128]{3,2,1,0:T(8,128)(2,1)} %bitcast.15), custom_call_target="tpu_custom_call" | custom-call | flops 234881024 | bytes 3670016 | tf_op jit(solution)/shard_map/pallas_call | solution.py:127
  11.5 0.0 copy-done.4
  11.5 0.0 collective-permute-done
  11.6 1.6 %collective-permute-start.1 = (bf16[2,128,128]{2,1,0:T(8,128)(2,1)S(1)}, bf16[2,128,128]{2,1,0:T(8,128)(2,1)S(1)}, u32[]{:S(2)}, u32[]{:S(2)}) collective-permute-start(bf16[2,128,128]{2,1,0:T(8,128)(2,1)S(1)} %slice.58), channel_id=1, source_target_pairs={{0,2},{1,3},{2,0},{3,1},{4,6},{5,7},{6,4},{7,5},{8,10},{9,11},{10,... | collective-permute-start | bytes 196616 | tf_op jit(solution)/shard_map/ppermute | solution.py:17
  13.1 0.0 copy-done
  13.1 0.0 copy-done.3
  13.1 0.9 %fusion.2 = f32[64,128]{1,0:T(8,128)S(1)} fusion(bf16[8192,64]{0,1:T(8,128)(2,1)S(1)} %copy-done.3, bf16[128,8192]{1,0:T(8,128)(2,1)S(1)} %copy-done), kind=kOutput, calls=%fused_computation.13 | convolution fusion | flops 134217728 | bytes 3178496 | tf_op jit(solution)/shard_map/dot_general | solution.py:365
  14.0 1.6 %collective-permute-start.4 = (f32[64,128]{1,0:T(8,128)S(1)}, f32[64,128]{1,0:T(8,128)S(1)}, u32[]{:S(2)}, u32[]{:S(2)}) collective-permute-start(f32[64,128]{1,0:T(8,128)S(1)} %fusion.2), channel_id=1, source_target_pairs={{0,4},{1,5},{2,6},{3,7},{4,0},{5,1},{6,2},{7,3},{8,12},{9,13},{10,... | collective-permute-start | bytes 98312 | tf_op jit(solution)/shard_map/ppermute | solution.py:17
  15.7 0.4 %collective-permute-done.1 = bf16[2,128,128]{2,1,0:T(8,128)(2,1)S(1)} collective-permute-done((bf16[2,128,128]{2,1,0:T(8,128)(2,1)S(1)}, bf16[2,128,128]{2,1,0:T(8,128)(2,1)S(1)}, u32[]{:S(2)}, u32[]{:S(2)}) %collective-permute-start.1) | collective-permute-done | bytes 65568 | tf_op jit(solution)/shard_map/ppermute | solution.py:17
  16.1 0.0 collective-permute-done.5
  16.1 1.6 %collective-permute-start.6 = (bf16[16,4096]{1,0:T(8,128)(2,1)S(1)}, bf16[16,4096]{1,0:T(8,128)(2,1)S(1)}, u32[]{:S(2)}, u32[]{:S(2)}) collective-permute-start(bf16[16,4096]{1,0:T(8,128)(2,1)S(1)} %pad_maximum_fusion), channel_id=1, source_target_pairs={{0,2},{1,3},{2,0},{3,1},{4,6},{5,7},{6,4},{7,5},{8,10},{9,11},{10,... | collective-permute-start | bytes 393224 | tf_op jit(solution)/shard_map/ppermute | solution.py:17
  17.7 0.6 %collective-permute-start.2 = (bf16[1,128,128]{2,1,0:T(8,128)(2,1)S(1)}, bf16[1,128,128]{2,1,0:T(8,128)(2,1)S(1)}, u32[]{:S(2)}, u32[]{:S(2)}) collective-permute-start(bf16[1,128,128]{2,1,0:T(8,128)(2,1)S(1)} %slice.59), channel_id=1, source_target_pairs={{0,8},{1,9},{2,10},{3,11},{4,12},{5,13},{6,14},{7,15},{8,0},{9,1},... | collective-permute-start | bytes 98312 | tf_op jit(solution)/shard_map/ppermute | solution.py:17
  18.3 2.9 %collective-permute-done.6 = bf16[16,4096]{1,0:T(8,128)(2,1)S(1)} collective-permute-done((bf16[16,4096]{1,0:T(8,128)(2,1)S(1)}, bf16[16,4096]{1,0:T(8,128)(2,1)S(1)}, u32[]{:S(2)}, u32[]{:S(2)}) %collective-permute-start.6) | collective-permute-done | bytes 131104 | tf_op jit(solution)/shard_map/ppermute | solution.py:17
  21.3 0.1 collective-permute-start.7
  21.4 1.2 %collective-permute-done.2 = bf16[1,128,128]{2,1,0:T(8,128)(2,1)S(1)} collective-permute-done((bf16[1,128,128]{2,1,0:T(8,128)(2,1)S(1)}, bf16[1,128,128]{2,1,0:T(8,128)(2,1)S(1)}, u32[]{:S(2)}, u32[]{:S(2)}) %collective-permute-start.2) | collective-permute-done | bytes 32800 | tf_op jit(solution)/shard_map/ppermute | solution.py:17
  22.6 1.6 %collective-permute-start.3 = (f32[128,128]{1,0:T(8,128)S(1)}, f32[128,128]{1,0:T(8,128)S(1)}, u32[]{:S(2)}, u32[]{:S(2)}) collective-permute-start(f32[128,128]{1,0:T(8,128)S(1)} %fusion.own_ref), channel_id=1, source_target_pairs={{0,4},{1,5},{2,6},{3,7},{4,0},{5,1},{6,2},{7,3},{8,12},{9,13},{10,... | collective-permute-start | bytes 196616 | tf_op jit(solution)/shard_map/ppermute | solution.py:17
  24.3 0.0 collective-permute-done.4
  24.3 0.0 copy-start.1
  24.3 0.0 copy-start.2
  24.3 0.0 collective-permute-done.7.refs_1_
  24.3 0.7 %shard_map.88.inner_ref = f32[2048,512]{1,0:T(8,128)S(1)} custom-call(f32[2,64,128]{2,1,0:T(8,128)S(1)} %pad_maximum_fusion.1.act_ref, bf16[32,4096]{1,0:T(8,128)(2,1)S(1)} %constant_dynamic-update-slice_fusion.refs_0_, bf16[32,4096]{1,0:T(8,128)(2,1)S(1)} %collective-permute-done.7.refs_1_), custom_call_target="tpu_custom_call" | custom-call | flops 536870912 | bytes 4194304 | tf_op jit(solution)/shard_map/pallas_call | solution.py:177
  25.0 1.9 %collective-permute-done.3.other_ref = f32[128,128]{1,0:T(8,128)S(1)} collective-permute-done((f32[128,128]{1,0:T(8,128)S(1)}, f32[128,128]{1,0:T(8,128)S(1)}, u32[]{:S(2)}, u32[]{:S(2)}) %collective-permute-start.3) | collective-permute-done | bytes 65568 | tf_op jit(solution)/shard_map/ppermute | solution.py:17
  27.0 0.0 copy-done.1
  27.0 0.0 copy-done.2
  27.0 1.1 %shard_map.89 = (f32[64,128]{1,0:T(8,128)S(1)}, f32[64,128]{1,0:T(8,128)S(1)}, f32[8,8,16]{2,1,0:T(8,128)S(1)}) custom-call(s32[1]{0:T(128)} %bitcast.me_ref, s32[16]{0:T(128)S(1)} %copy-done.1, s32[16]{0:T(128)S(1)} %copy-done.2, f32[128,128]{1,0:T(8,128)S(1)} %fusion.own_ref, f32[128,128]{1,0:T(8,128)S(1)} %collective-permute-done.3.other_ref, ...), custom_call_target="tpu_custom_call" | custom-call | flops 2097152 | bytes 4194304 | tf_op jit(solution)/shard_map/pallas_call | solution.py:277
  28.1 0.1 collective-permute-start.9
  28.1 1.2 %collective-permute-done.9 = f32[4,8,16]{2,1,0:T(8,128)S(1)} collective-permute-done((f32[4,8,16]{2,1,0:T(8,128)S(1)}, f32[4,8,16]{2,1,0:T(8,128)S(1)}, u32[]{:S(2)}, u32[]{:S(2)}) %collective-permute-start.9) | collective-permute-done | bytes 2080 | tf_op jit(solution)/shard_map/ppermute | solution.py:17
  29.3 0.5 %collective-permute-start.10 = (f32[2,8,16]{2,1,0:T(8,128)S(1)}, f32[2,8,16]{2,1,0:T(8,128)S(1)}, u32[]{:S(2)}, u32[]{:S(2)}) collective-permute-start(f32[2,8,16]{2,1,0:T(8,128)S(1)} %slice.47), channel_id=1, source_target_pairs={{0,2},{1,3},{2,0},{3,1},{4,6},{5,7},{6,4},{7,5},{8,10},{9,11},{10,... | collective-permute-start | bytes 3080 | tf_op jit(solution)/shard_map/ppermute | solution.py:17
  29.8 1.6 %collective-permute-start.8 = (f32[64,128]{1,0:T(8,128)S(1)}, f32[64,128]{1,0:T(8,128)S(1)}, u32[]{:S(2)}, u32[]{:S(2)}) collective-permute-start(f32[64,128]{1,0:T(8,128)S(1)} %get-tuple-element.16), channel_id=1, source_target_pairs={{0,4},{1,5},{2,6},{3,7},{4,0},{5,1},{6,2},{7,3},{8,12},{9,13},{10,... | collective-permute-start | bytes 98312 | tf_op jit(solution)/shard_map/ppermute | solution.py:17
  31.4 1.6 %collective-permute-done.10 = f32[2,8,16]{2,1,0:T(8,128)S(1)} collective-permute-done((f32[2,8,16]{2,1,0:T(8,128)S(1)}, f32[2,8,16]{2,1,0:T(8,128)S(1)}, u32[]{:S(2)}, u32[]{:S(2)}) %collective-permute-start.10) | collective-permute-done | bytes 1056 | tf_op jit(solution)/shard_map/ppermute | solution.py:17
  33.0 0.6 %collective-permute-start.11 = (f32[1,8,16]{2,1,0:T(8,128)S(1)}, f32[1,8,16]{2,1,0:T(8,128)S(1)}, u32[]{:S(2)}, u32[]{:S(2)}) collective-permute-start(f32[1,8,16]{2,1,0:T(8,128)S(1)} %get-tuple-element.20), channel_id=1, source_target_pairs={{0,8},{1,9},{2,10},{3,11},{4,12},{5,13},{6,14},{7,15},{8,0},{9,1},... | collective-permute-start | bytes 1544 | tf_op jit(solution)/shard_map/ppermute | solution.py:17
  33.5 3.9 %collective-permute-done.11.more_ref = f32[1,8,16]{2,1,0:T(8,128)S(1)} collective-permute-done((f32[1,8,16]{2,1,0:T(8,128)S(1)}, f32[1,8,16]{2,1,0:T(8,128)S(1)}, u32[]{:S(2)}, u32[]{:S(2)}) %collective-permute-start.11) | collective-permute-done | bytes 544 | tf_op jit(solution)/shard_map/ppermute | solution.py:17
  37.5 0.0 collective-permute-done.8.other_ref
  37.5 1.3 %shard_map.90 = (f32[128,128]{1,0:T(8,128)}, f32[8,16]{1,0:T(8,128)}) custom-call(s32[1]{0:T(128)} %bitcast.me_ref, s32[16]{0:T(128)S(1)} %copy-done.1, s32[16]{0:T(128)S(1)} %copy-done.2, f32[64,128]{1,0:T(8,128)S(1)} %get-tuple-element.15.own_ref, f32[64,128]{1,0:T(8,128)S(1)} %collective-permute-done.8.other_ref, ...), custom_call_target="tpu_custom_call" | custom-call | tf_op jit(solution)/shard_map/pallas_call | solution.py:314
  (15 shorter events, 0.1 us)
Async XLA Ops:
  0.6 12.5 %copy-start = (bf16[128,8192]{1,0:T(8,128)(2,1)S(1)}, bf16[128,8192]{1,0:T(8,128)(2,1)}, u32[]{:S(2)}) copy-start(bf16[128,8192]{1,0:T(8,128)(2,1)} %param.7) | copy-start | bytes 6291460
  0.6 15.5 %collective-permute-start.5 = (bf16[8,4096]{1,0:T(8,128)(2,1)}, bf16[8,4096]{1,0:T(8,128)(2,1)S(1)}, u32[]{:S(2)}, u32[]{:S(2)}) collective-permute-start(bf16[8,4096]{1,0:T(8,128)(2,1)} %param.11), channel_id=1, source_target_pairs={{0,8},{1,9},{2,10},{3,11},{4,12},{5,13},{6,14},{7,15},{8,0},{9,1},... | collective-permute-start | bytes 196616 | tf_op jit(solution)/shard_map/ppermute | solution.py:17
  8.1 3.4 %collective-permute-start = (f32[4,128,128]{2,1,0:T(8,128)S(1)}, f32[4,128,128]{2,1,0:T(8,128)S(1)}, u32[]{:S(2)}, u32[]{:S(2)}) collective-permute-start(f32[4,128,128]{2,1,0:T(8,128)S(1)} %get-tuple-element.12), channel_id=1, source_target_pairs={{0,1},{1,0},{2,3},{3,2},{4,5},{5,4},{6,7},{7,6},{8,9},{9,8},{10,11... | collective-permute-start | bytes 786440 | tf_op jit(solution)/shard_map/ppermute | solution.py:17
  8.1 3.3 %copy-start.4 = (bf16[8,4096]{1,0:T(8,128)(2,1)S(1)}, bf16[8,4096]{1,0:T(8,128)(2,1)}, u32[]{:S(2)}) copy-start(bf16[8,4096]{1,0:T(8,128)(2,1)} %param.11) | copy-start | bytes 196612
  8.1 5.0 %copy-start.3 = (bf16[8192,64]{0,1:T(8,128)(2,1)S(1)}, bf16[8192,64]{0,1:T(8,128)(2,1)}, u32[]{:S(2)}) copy-start(bf16[8192,64]{0,1:T(8,128)(2,1)} %param.9) | copy-start | bytes 3145732
  11.6 4.5 %collective-permute-start.1 = (bf16[2,128,128]{2,1,0:T(8,128)(2,1)S(1)}, bf16[2,128,128]{2,1,0:T(8,128)(2,1)S(1)}, u32[]{:S(2)}, u32[]{:S(2)}) collective-permute-start(bf16[2,128,128]{2,1,0:T(8,128)(2,1)S(1)} %slice.58), channel_id=1, source_target_pairs={{0,2},{1,3},{2,0},{3,1},{4,6},{5,7},{6,4},{7,5},{8,10},{9,11},{10,... | collective-permute-start | bytes 196616 | tf_op jit(solution)/shard_map/ppermute | solution.py:17
  14.0 10.2 %collective-permute-start.4 = (f32[64,128]{1,0:T(8,128)S(1)}, f32[64,128]{1,0:T(8,128)S(1)}, u32[]{:S(2)}, u32[]{:S(2)}) collective-permute-start(f32[64,128]{1,0:T(8,128)S(1)} %fusion.2), channel_id=1, source_target_pairs={{0,4},{1,5},{2,6},{3,7},{4,0},{5,1},{6,2},{7,3},{8,12},{9,13},{10,... | collective-permute-start | bytes 98312 | tf_op jit(solution)/shard_map/ppermute | solution.py:17
  16.1 5.2 %collective-permute-start.6 = (bf16[16,4096]{1,0:T(8,128)(2,1)S(1)}, bf16[16,4096]{1,0:T(8,128)(2,1)S(1)}, u32[]{:S(2)}, u32[]{:S(2)}) collective-permute-start(bf16[16,4096]{1,0:T(8,128)(2,1)S(1)} %pad_maximum_fusion), channel_id=1, source_target_pairs={{0,2},{1,3},{2,0},{3,1},{4,6},{5,7},{6,4},{7,5},{8,10},{9,11},{10,... | collective-permute-start | bytes 393224 | tf_op jit(solution)/shard_map/ppermute | solution.py:17
  17.7 4.9 %collective-permute-start.2 = (bf16[1,128,128]{2,1,0:T(8,128)(2,1)S(1)}, bf16[1,128,128]{2,1,0:T(8,128)(2,1)S(1)}, u32[]{:S(2)}, u32[]{:S(2)}) collective-permute-start(bf16[1,128,128]{2,1,0:T(8,128)(2,1)S(1)} %slice.59), channel_id=1, source_target_pairs={{0,8},{1,9},{2,10},{3,11},{4,12},{5,13},{6,14},{7,15},{8,0},{9,1},... | collective-permute-start | bytes 98312 | tf_op jit(solution)/shard_map/ppermute | solution.py:17
  21.3 3.0 %collective-permute-start.7 = (bf16[32,4096]{1,0:T(8,128)(2,1)S(1)}, bf16[32,4096]{1,0:T(8,128)(2,1)S(1)}, u32[]{:S(2)}, u32[]{:S(2)}) collective-permute-start(bf16[32,4096]{1,0:T(8,128)(2,1)S(1)} %constant_dynamic-update-slice_fusion.refs_0_), channel_id=1, source_target_pairs={{0,1},{1,0},{2,3},{3,2},{4,5},{5,4},{6,7},{7,6},{8,9},{9,8},{10,11... | collective-permute-start | bytes 786440 | tf_op jit(solution)/shard_map/ppermute | solution.py:17
  22.6 4.3 %collective-permute-start.3 = (f32[128,128]{1,0:T(8,128)S(1)}, f32[128,128]{1,0:T(8,128)S(1)}, u32[]{:S(2)}, u32[]{:S(2)}) collective-permute-start(f32[128,128]{1,0:T(8,128)S(1)} %fusion.own_ref), channel_id=1, source_target_pairs={{0,4},{1,5},{2,6},{3,7},{4,0},{5,1},{6,2},{7,3},{8,12},{9,13},{10,... | collective-permute-start | bytes 196616 | tf_op jit(solution)/shard_map/ppermute | solution.py:17
  24.3 2.7 %copy-start.1 = (s32[16]{0:T(128)S(1)}, s32[16]{0:T(128)}, u32[]{:S(2)}) copy-start(s32[16]{0:T(128)} %length_ref.3) | copy-start | bytes 196
  24.3 2.7 %copy-start.2 = (s32[16]{0:T(128)S(1)}, s32[16]{0:T(128)}, u32[]{:S(2)}) copy-start(s32[16]{0:T(128)} %valid_ref.3) | copy-start | bytes 196
  28.1 1.2 %collective-permute-start.9 = (f32[4,8,16]{2,1,0:T(8,128)S(1)}, f32[4,8,16]{2,1,0:T(8,128)S(1)}, u32[]{:S(2)}, u32[]{:S(2)}) collective-permute-start(f32[4,8,16]{2,1,0:T(8,128)S(1)} %slice.37), channel_id=1, source_target_pairs={{0,1},{1,0},{2,3},{3,2},{4,5},{5,4},{6,7},{7,6},{8,9},{9,8},{10,11... | collective-permute-start | bytes 6152 | tf_op jit(solution)/shard_map/ppermute | solution.py:17
  29.3 3.7 %collective-permute-start.10 = (f32[2,8,16]{2,1,0:T(8,128)S(1)}, f32[2,8,16]{2,1,0:T(8,128)S(1)}, u32[]{:S(2)}, u32[]{:S(2)}) collective-permute-start(f32[2,8,16]{2,1,0:T(8,128)S(1)} %slice.47), channel_id=1, source_target_pairs={{0,2},{1,3},{2,0},{3,1},{4,6},{5,7},{6,4},{7,5},{8,10},{9,11},{10,... | collective-permute-start | bytes 3080 | tf_op jit(solution)/shard_map/ppermute | solution.py:17
  29.8 7.6 %collective-permute-start.8 = (f32[64,128]{1,0:T(8,128)S(1)}, f32[64,128]{1,0:T(8,128)S(1)}, u32[]{:S(2)}, u32[]{:S(2)}) collective-permute-start(f32[64,128]{1,0:T(8,128)S(1)} %get-tuple-element.16), channel_id=1, source_target_pairs={{0,4},{1,5},{2,6},{3,7},{4,0},{5,1},{6,2},{7,3},{8,12},{9,13},{10,... | collective-permute-start | bytes 98312 | tf_op jit(solution)/shard_map/ppermute | solution.py:17
  33.0 4.5 %collective-permute-start.11 = (f32[1,8,16]{2,1,0:T(8,128)S(1)}, f32[1,8,16]{2,1,0:T(8,128)S(1)}, u32[]{:S(2)}, u32[]{:S(2)}) collective-permute-start(f32[1,8,16]{2,1,0:T(8,128)S(1)} %get-tuple-element.20), channel_id=1, source_target_pairs={{0,8},{1,9},{2,10},{3,11},{4,12},{5,13},{6,14},{7,15},{8,0},{9,1},... | collective-permute-start | bytes 1544 | tf_op jit(solution)/shard_map/ppermute | solution.py:17

commit v10 on v6

--- a/solution.py
+++ b/solution.py
@@ -17,13 +17,12 @@
     return lax.ppermute(value, "seq", [(i, i ^ offset) for i in range(size)])
 
 
-def grad_kernel(offsets, me_ref, proj_ref, grads_ref, out_ref, proj_buf, table, grads_buf, proj_sem, sems):
+def grad_kernel(offsets, me_ref, proj_ref, grads_ref, out_ref, table, proj_buf, grads_buf, proj_sem, sems):
+    load = pltpu.make_async_copy(proj_ref, proj_buf, proj_sem)
+    load.start()
     halves, total, depth = grads_buf.shape
     count = len(offsets) // halves
     rows = total // count
-    width = proj_buf.shape[0]
-    load = pltpu.make_async_copy(proj_ref, proj_buf, proj_sem)
-    load.start()
     copies = []
     for k, offset in enumerate(offsets):
         first = pl.multiple_of((me_ref[0] ^ offset) * rows, rows)
@@ -39,43 +38,74 @@
     none = jnp.zeros_like(turned)
     for r in range(halves):
         table[r] = jnp.concatenate([turned if c == r else none for c in range(halves)], axis=1)
-    for k in range(0, count, 2):
-        for copy in copies[k * halves : (k + 2) * halves]:
-            copy.wait()
+    for k in range(count):
         made = None
         for r in range(halves):
+            copies[k * halves + r].wait()
             part = jnp.dot(
-                grads_buf[r, k * rows : (k + 2) * rows],
+                grads_buf[r, k * rows : (k + 1) * rows],
                 table[r],
                 preferred_element_type=jnp.float32,
             )
             made = part if made is None else made + part
+        out_ref[k] = made
+
+
+def held_kernel(offsets, me_ref, table, grads_ref, out_ref):
+    halves = table.shape[0]
+    count, rows, _ = out_ref.shape
+    for k in range(0, count, 2):
+        made = None
+        for r in range(halves):
+            left = []
+            for offset in (offsets[k * halves + r], offsets[(k + 1) * halves + r]):
+                first = pl.multiple_of((me_ref[0] ^ offset) * rows, rows)
+                left.append(grads_ref[pl.ds(first, rows)])
+            part = jnp.dot(
+                jnp.concatenate(left, axis=0), table[r], preferred_element_type=jnp.float32
+            )
+            made = part if made is None else made + part
         out_ref[k] = made[:rows]
         out_ref[k + 1] = made[rows:]
 
 
-def grad_blocks(me, proj, out_grads, rows, offsets):
+def grad_blocks(me, proj, out_grads, rows, offsets, table=None):
     width, depth = proj.shape
     count = len(offsets) // 2
+    made = jax.ShapeDtypeStruct((count, rows, 2 * width), jnp.float32)
+    shared = dict(
+        compiler_params=pltpu.CompilerParams(vmem_limit_bytes=24 * MIB),
+        cost_estimate=pl.CostEstimate(
+            flops=4 * count * rows * depth * width,
+            bytes_accessed=4 * count * rows * depth,
+            transcendentals=0,
+        ),
+    )
+    if table is not None:
+        return pl.pallas_call(
+            functools.partial(held_kernel, offsets),
+            in_specs=[SMEM, VMEM, VMEM],
+            out_specs=VMEM,
+            out_shape=made,
+            **shared,
+        )(me, table, out_grads)
     return pl.pallas_call(
         functools.partial(grad_kernel, offsets),
         in_specs=[SMEM, HBM, HBM],
-        out_specs=VMEM,
-        out_shape=jax.ShapeDtypeStruct((count, rows, 2 * width), jnp.float32),
+        out_specs=(VMEM, VMEM),
+        out_shape=(made, jax.ShapeDtypeStruct((2, depth, 2 * width), jnp.bfloat16)),
         scratch_shapes=[
             pltpu.VMEM((width, depth), jnp.bfloat16),
-            pltpu.VMEM((2, depth, 2 * width), jnp.bfloat16),
             pltpu.VMEM((2, count * rows, depth), jnp.bfloat16),
             pltpu.SemaphoreType.DMA,
             pltpu.SemaphoreType.DMA((2 * count,)),
         ],
-        compiler_params=pltpu.CompilerParams(vmem_limit_bytes=52 * MIB),
-        cost_estimate=pl.CostEstimate(
-            flops=4 * count * rows * depth * width,
-            bytes_accessed=4 * count * rows * depth,
-            transcendentals=0,
-        ),
-    )(me, proj, out_grads)
+        **shared,
+    )(
+        me,
+        pltpu.with_memory_space_constraint(proj, pltpu.HBM),
+        pltpu.with_memory_space_constraint(out_grads, pltpu.HBM),
+    )
 
 
 def inner_kernel(pieces, act_ref, *refs):
@@ -276,13 +306,13 @@
     split = size // 4
     middle = [1 << k for k in range(1, size.bit_length() - 1) if 1 << k != split]
 
-    panel, place = queries, [0]
+    proj = proj_out.T
+    spots = [offset_of(m, middle) + split * r for m in range(size // 4) for r in range(2)]
+    theirs, table = grad_blocks(me, proj, out_grads, rows, [s + 1 for s in spots])
+    from_core = swap(theirs, 1, size)
+    panel = queries
     got = swap(panel, middle[-1], size)
-
-    proj = pltpu.with_memory_space_constraint(proj_out.T, pltpu.HBM)
-    spots = [offset_of(m, middle) + split * r for m in range(size // 4) for r in range(2)]
-    from_core = swap(grad_blocks(me, proj, out_grads, rows, [s + 1 for s in spots]), 1, size)
-    sums = grad_blocks(me, proj, out_grads, rows, spots) + from_core
+    sums = grad_blocks(me, proj, out_grads, rows, spots, table) + from_core
     late, _ = lax.optimization_barrier((proj_in, sums))
     for k, bit in enumerate(middle):
         half = sums.shape[0] // 2

time: 38.7 us -> 37.5 us (0.969)
  Pallas kernels: 9.44 us -> 8.13 us
    pallas_call x2 -> x1, Pallas kernels: 6.36 us -> 3.96 us  [grad_blocks(): pl.pallas_call(functools.partial(grad_kernel, offsets), in_specs=[SMEM, H...]
    pallas_call x0 -> x1, Pallas kernels: none -> 1.1 us  [grad_blocks(): pl.pallas_call(functools.partial(held_kernel, offsets), in_specs=[SMEM, V...]
  transfers between devices with their start and end apart: 12 -> 12, of which waited for: 7 -> 8; matrix products, arithmetic and copies ran while one was open for 3% -> 3% of each run, Pallas kernels for 18% -> 15%
where the time goes in v10:
time: 37.5 us; the launch traced here: 37.4 us
  starting transfers between devices  13.7 us (37%)
  waiting for transfers between devices  13.5 us (36%)
  Pallas kernels  8.13 us (22%)
  matrix products  0.88 us (2%)
  between operations  0.8 us (2%)
    ppermute x12, starting transfers between devices, swap(): return lax.ppermute(value, 'seq', [(i, i ^ offset) for i in range(size)])  13.7 us
    ppermute x12, waiting for transfers between devices, swap(): return lax.ppermute(value, 'seq', [(i, i ^ offset) for i in range(size)])  13.5 us
    pallas_call x1, Pallas kernels, grad_blocks(): pl.pallas_call(functools.partial(grad_kernel, offsets), in_specs=[SMEM, H...  3.96 us
    pallas_call x1, Pallas kernels, last(): pl.pallas_call(functools.partial(last_kernel, place, split), in_specs=[SM...  1.29 us
    pallas_call x1, Pallas kernels, grad_blocks(): pl.pallas_call(functools.partial(held_kernel, offsets), in_specs=[SMEM, V...  1.1 us
    pallas_call x1, Pallas kernels, score(): pl.pallas_call(functools.partial(score_kernel, steps, split), out_shape=(...  1.08 us
    dot_general x1, matrix products, body(): lax.dot_general(late, activations, (((0,), (1,)), ((), ())), preferred_el...  0.88 us
  transfers between devices with their start and end apart: 12, of which 8 were waited for; matrix products, arithmetic and copies ran while one was open for 3% of the time, Pallas kernels for 15%

profile of v10, /device:TPU:0, one launch (start us, length us, event | category | flops | bytes accessed | tf_op | source)
XLA Modules:
  0.0 37.4 jit_solution(2331762783043146220)
XLA Ops:
  0.6 0.0 copy-start
  0.6 4.1 %collective-permute-start.5 = (bf16[8,4096]{1,0:T(8,128)(2,1)}, bf16[8,4096]{1,0:T(8,128)(2,1)S(1)}, u32[]{:S(2)}, u32[]{:S(2)}) collective-permute-start(bf16[8,4096]{1,0:T(8,128)(2,1)} %param.11), channel_id=1, source_target_pairs={{0,8},{1,9},{2,10},{3,11},{4,12},{5,13},{6,14},{7,15},{8,0},{9,1},... | collective-permute-start | bytes 196616 | tf_op jit(solution)/shard_map/ppermute | solution.py:17
  4.7 0.0 copy-start.1
  4.7 4.0 %shard_map.86 = (f32[4,128,128]{2,1,0:T(8,128)S(1)}, bf16[2,1792,128]{2,1,0:T(8,128)(2,1)S(1)}) custom-call(s32[1]{0:T(128)} %bitcast.me_ref, bf16[64,1792]{1,0:T(8,128)(2,1)} %bitcast.9, bf16[2048,1792]{1,0:T(8,128)(2,1)} %grads_ref.3), custom_call_target="tpu_custom_call" | custom-call | flops 234881024 | bytes 3670016 | tf_op jit(solution)/shard_map/pallas_call | solution.py:92
  8.7 0.1 collective-permute-start
  8.8 0.2 copy-done.1
  9.0 0.0 copy-start.5
  9.0 0.0 copy-start.4
  9.0 1.1 %shard_map.87 = f32[4,128,128]{2,1,0:T(8,128)S(1)} custom-call(s32[1]{0:T(128)} %bitcast.me_ref, bf16[2,1792,128]{2,1,0:T(8,128)(2,1)S(1)} %get-tuple-element.11.table, bf16[2048,1792]{1,0:T(8,128)(2,1)S(1)} %copy-done.1), custom_call_target="tpu_custom_call" | custom-call | flops 234881024 | bytes 3670016 | tf_op jit(solution)/shard_map/pallas_call | solution.py:85
  10.1 0.0 copy-done.5
  10.1 0.2 collective-permute-done
  10.4 1.6 %collective-permute-start.1 = (bf16[2,128,128]{2,1,0:T(8,128)(2,1)S(1)}, bf16[2,128,128]{2,1,0:T(8,128)(2,1)S(1)}, u32[]{:S(2)}, u32[]{:S(2)}) collective-permute-start(bf16[2,128,128]{2,1,0:T(8,128)(2,1)S(1)} %slice.58), channel_id=1, source_target_pairs={{0,2},{1,3},{2,0},{3,1},{4,6},{5,7},{6,4},{7,5},{8,10},{9,11},{10,... | collective-permute-start | bytes 196616 | tf_op jit(solution)/shard_map/ppermute | solution.py:17
  11.9 0.0 copy-done
  12.0 0.0 copy-done.4
  12.0 0.9 %fusion.2 = f32[64,128]{1,0:T(8,128)S(1)} fusion(bf16[8192,64]{0,1:T(8,128)(2,1)S(1)} %copy-done.4, bf16[128,8192]{1,0:T(8,128)(2,1)S(1)} %copy-done), kind=kOutput, calls=%fused_computation.13 | convolution fusion | flops 134217728 | bytes 3178496 | tf_op jit(solution)/shard_map/dot_general | solution.py:334
  12.8 1.6 %collective-permute-start.4 = (f32[64,128]{1,0:T(8,128)S(1)}, f32[64,128]{1,0:T(8,128)S(1)}, u32[]{:S(2)}, u32[]{:S(2)}) collective-permute-start(f32[64,128]{1,0:T(8,128)S(1)} %fusion.2), channel_id=1, source_target_pairs={{0,4},{1,5},{2,6},{3,7},{4,0},{5,1},{6,2},{7,3},{8,12},{9,13},{10,... | collective-permute-start | bytes 98312 | tf_op jit(solution)/shard_map/ppermute | solution.py:17
  14.5 0.2 collective-permute-done.1
  14.7 0.0 collective-permute-done.5
  14.7 1.6 %collective-permute-start.6 = (bf16[16,4096]{1,0:T(8,128)(2,1)S(1)}, bf16[16,4096]{1,0:T(8,128)(2,1)S(1)}, u32[]{:S(2)}, u32[]{:S(2)}) collective-permute-start(bf16[16,4096]{1,0:T(8,128)(2,1)S(1)} %pad_maximum_fusion), channel_id=1, source_target_pairs={{0,2},{1,3},{2,0},{3,1},{4,6},{5,7},{6,4},{7,5},{8,10},{9,11},{10,... | collective-permute-start | bytes 393224 | tf_op jit(solution)/shard_map/ppermute | solution.py:17
  16.3 0.5 %collective-permute-start.2 = (bf16[1,128,128]{2,1,0:T(8,128)(2,1)S(1)}, bf16[1,128,128]{2,1,0:T(8,128)(2,1)S(1)}, u32[]{:S(2)}, u32[]{:S(2)}) collective-permute-start(bf16[1,128,128]{2,1,0:T(8,128)(2,1)S(1)} %slice.59), channel_id=1, source_target_pairs={{0,8},{1,9},{2,10},{3,11},{4,12},{5,13},{6,14},{7,15},{8,0},{9,1},... | collective-permute-start | bytes 98312 | tf_op jit(solution)/shard_map/ppermute | solution.py:17
  16.8 3.0 %collective-permute-done.6 = bf16[16,4096]{1,0:T(8,128)(2,1)S(1)} collective-permute-done((bf16[16,4096]{1,0:T(8,128)(2,1)S(1)}, bf16[16,4096]{1,0:T(8,128)(2,1)S(1)}, u32[]{:S(2)}, u32[]{:S(2)}) %collective-permute-start.6) | collective-permute-done | bytes 131104 | tf_op jit(solution)/shard_map/ppermute | solution.py:17
  19.8 0.1 collective-permute-start.7
  19.9 1.4 %collective-permute-done.2 = bf16[1,128,128]{2,1,0:T(8,128)(2,1)S(1)} collective-permute-done((bf16[1,128,128]{2,1,0:T(8,128)(2,1)S(1)}, bf16[1,128,128]{2,1,0:T(8,128)(2,1)S(1)}, u32[]{:S(2)}, u32[]{:S(2)}) %collective-permute-start.2) | collective-permute-done | bytes 32800 | tf_op jit(solution)/shard_map/ppermute | solution.py:17
  21.2 1.6 %collective-permute-start.3 = (f32[128,128]{1,0:T(8,128)S(1)}, f32[128,128]{1,0:T(8,128)S(1)}, u32[]{:S(2)}, u32[]{:S(2)}) collective-permute-start(f32[128,128]{1,0:T(8,128)S(1)} %fusion.own_ref), channel_id=1, source_target_pairs={{0,4},{1,5},{2,6},{3,7},{4,0},{5,1},{6,2},{7,3},{8,12},{9,13},{10,... | collective-permute-start | bytes 196616 | tf_op jit(solution)/shard_map/ppermute | solution.py:17
  22.9 0.0 collective-permute-done.4
  22.9 0.0 copy-start.2
  22.9 0.0 copy-start.3
  22.9 0.0 collective-permute-done.7.refs_1_
  22.9 0.7 %shard_map.88.inner_ref = f32[2048,512]{1,0:T(8,128)S(1)} custom-call(f32[2,64,128]{2,1,0:T(8,128)S(1)} %pad_maximum_fusion.1.act_ref, bf16[32,4096]{1,0:T(8,128)(2,1)S(1)} %constant_dynamic-update-slice_fusion.refs_0_, bf16[32,4096]{1,0:T(8,128)(2,1)S(1)} %collective-permute-done.7.refs_1_), custom_call_target="tpu_custom_call" | custom-call | flops 536870912 | bytes 4194304 | tf_op jit(solution)/shard_map/pallas_call | solution.py:146
  23.6 1.9 %collective-permute-done.3.other_ref = f32[128,128]{1,0:T(8,128)S(1)} collective-permute-done((f32[128,128]{1,0:T(8,128)S(1)}, f32[128,128]{1,0:T(8,128)S(1)}, u32[]{:S(2)}, u32[]{:S(2)}) %collective-permute-start.3) | collective-permute-done | bytes 65568 | tf_op jit(solution)/shard_map/ppermute | solution.py:17
  25.6 0.0 copy-done.2
  25.6 0.0 copy-done.3
  25.6 1.1 %shard_map.89 = (f32[64,128]{1,0:T(8,128)S(1)}, f32[64,128]{1,0:T(8,128)S(1)}, f32[8,8,16]{2,1,0:T(8,128)S(1)}) custom-call(s32[1]{0:T(128)} %bitcast.me_ref, s32[16]{0:T(128)S(1)} %copy-done.2, s32[16]{0:T(128)S(1)} %copy-done.3, f32[128,128]{1,0:T(8,128)S(1)} %fusion.own_ref, f32[128,128]{1,0:T(8,128)S(1)} %collective-permute-done.3.other_ref, ...), custom_call_target="tpu_custom_call" | custom-call | flops 2097152 | bytes 4194304 | tf_op jit(solution)/shard_map/pallas_call | solution.py:246
  26.7 0.1 collective-permute-start.9
  26.7 1.2 %collective-permute-done.9 = f32[4,8,16]{2,1,0:T(8,128)S(1)} collective-permute-done((f32[4,8,16]{2,1,0:T(8,128)S(1)}, f32[4,8,16]{2,1,0:T(8,128)S(1)}, u32[]{:S(2)}, u32[]{:S(2)}) %collective-permute-start.9) | collective-permute-done | bytes 2080 | tf_op jit(solution)/shard_map/ppermute | solution.py:17
  27.9 0.5 %collective-permute-start.10 = (f32[2,8,16]{2,1,0:T(8,128)S(1)}, f32[2,8,16]{2,1,0:T(8,128)S(1)}, u32[]{:S(2)}, u32[]{:S(2)}) collective-permute-start(f32[2,8,16]{2,1,0:T(8,128)S(1)} %slice.47), channel_id=1, source_target_pairs={{0,2},{1,3},{2,0},{3,1},{4,6},{5,7},{6,4},{7,5},{8,10},{9,11},{10,... | collective-permute-start | bytes 3080 | tf_op jit(solution)/shard_map/ppermute | solution.py:17
  28.4 1.6 %collective-permute-start.8 = (f32[64,128]{1,0:T(8,128)S(1)}, f32[64,128]{1,0:T(8,128)S(1)}, u32[]{:S(2)}, u32[]{:S(2)}) collective-permute-start(f32[64,128]{1,0:T(8,128)S(1)} %get-tuple-element.16), channel_id=1, source_target_pairs={{0,4},{1,5},{2,6},{3,7},{4,0},{5,1},{6,2},{7,3},{8,12},{9,13},{10,... | collective-permute-start | bytes 98312 | tf_op jit(solution)/shard_map/ppermute | solution.py:17
  30.0 1.6 %collective-permute-done.10 = f32[2,8,16]{2,1,0:T(8,128)S(1)} collective-permute-done((f32[2,8,16]{2,1,0:T(8,128)S(1)}, f32[2,8,16]{2,1,0:T(8,128)S(1)}, u32[]{:S(2)}, u32[]{:S(2)}) %collective-permute-start.10) | collective-permute-done | bytes 1056 | tf_op jit(solution)/shard_map/ppermute | solution.py:17
  31.6 0.4 %collective-permute-start.11 = (f32[1,8,16]{2,1,0:T(8,128)S(1)}, f32[1,8,16]{2,1,0:T(8,128)S(1)}, u32[]{:S(2)}, u32[]{:S(2)}) collective-permute-start(f32[1,8,16]{2,1,0:T(8,128)S(1)} %get-tuple-element.20), channel_id=1, source_target_pairs={{0,8},{1,9},{2,10},{3,11},{4,12},{5,13},{6,14},{7,15},{8,0},{9,1},... | collective-permute-start | bytes 1544 | tf_op jit(solution)/shard_map/ppermute | solution.py:17
  32.0 4.1 %collective-permute-done.11.more_ref = f32[1,8,16]{2,1,0:T(8,128)S(1)} collective-permute-done((f32[1,8,16]{2,1,0:T(8,128)S(1)}, f32[1,8,16]{2,1,0:T(8,128)S(1)}, u32[]{:S(2)}, u32[]{:S(2)}) %collective-permute-start.11) | collective-permute-done | bytes 544 | tf_op jit(solution)/shard_map/ppermute | solution.py:17
  36.1 0.0 collective-permute-done.8.other_ref
  36.1 1.3 %shard_map.90 = (f32[128,128]{1,0:T(8,128)}, f32[8,16]{1,0:T(8,128)}) custom-call(s32[1]{0:T(128)} %bitcast.me_ref, s32[16]{0:T(128)S(1)} %copy-done.2, s32[16]{0:T(128)S(1)} %copy-done.3, f32[64,128]{1,0:T(8,128)S(1)} %get-tuple-element.15.own_ref, f32[64,128]{1,0:T(8,128)S(1)} %collective-permute-done.8.other_ref, ...), custom_call_target="tpu_custom_call" | custom-call | tf_op jit(solution)/shard_map/pallas_call | solution.py:283
  (15 shorter events, 0.1 us)
Async XLA Ops:
  0.6 11.3 %copy-start = (bf16[128,8192]{1,0:T(8,128)(2,1)S(1)}, bf16[128,8192]{1,0:T(8,128)(2,1)}, u32[]{:S(2)}) copy-start(bf16[128,8192]{1,0:T(8,128)(2,1)} %param.7) | copy-start | bytes 6291460
  0.6 14.1 %collective-permute-start.5 = (bf16[8,4096]{1,0:T(8,128)(2,1)}, bf16[8,4096]{1,0:T(8,128)(2,1)S(1)}, u32[]{:S(2)}, u32[]{:S(2)}) collective-permute-start(bf16[8,4096]{1,0:T(8,128)(2,1)} %param.11), channel_id=1, source_target_pairs={{0,8},{1,9},{2,10},{3,11},{4,12},{5,13},{6,14},{7,15},{8,0},{9,1},... | collective-permute-start | bytes 196616 | tf_op jit(solution)/shard_map/ppermute | solution.py:17
  4.7 4.3 %copy-start.1 = (bf16[2048,1792]{1,0:T(8,128)(2,1)S(1)}, bf16[2048,1792]{1,0:T(8,128)(2,1)}, u32[]{:S(2)}) copy-start(bf16[2048,1792]{1,0:T(8,128)(2,1)} %grads_ref.3) | copy-start | bytes 22020100
  8.7 1.6 %collective-permute-start = (f32[4,128,128]{2,1,0:T(8,128)S(1)}, f32[4,128,128]{2,1,0:T(8,128)S(1)}, u32[]{:S(2)}, u32[]{:S(2)}) collective-permute-start(f32[4,128,128]{2,1,0:T(8,128)S(1)} %get-tuple-element.12), channel_id=1, source_target_pairs={{0,1},{1,0},{2,3},{3,2},{4,5},{5,4},{6,7},{7,6},{8,9},{9,8},{10,11... | collective-permute-start | bytes 786440 | tf_op jit(solution)/shard_map/ppermute | solution.py:17
  9.0 1.1 %copy-start.5 = (bf16[8,4096]{1,0:T(8,128)(2,1)S(1)}, bf16[8,4096]{1,0:T(8,128)(2,1)}, u32[]{:S(2)}) copy-start(bf16[8,4096]{1,0:T(8,128)(2,1)} %param.11) | copy-start | bytes 196612
  9.0 3.0 %copy-start.4 = (bf16[8192,64]{0,1:T(8,128)(2,1)S(1)}, bf16[8192,64]{0,1:T(8,128)(2,1)}, u32[]{:S(2)}) copy-start(bf16[8192,64]{0,1:T(8,128)(2,1)} %param.9) | copy-start | bytes 3145732
  10.4 4.3 %collective-permute-start.1 = (bf16[2,128,128]{2,1,0:T(8,128)(2,1)S(1)}, bf16[2,128,128]{2,1,0:T(8,128)(2,1)S(1)}, u32[]{:S(2)}, u32[]{:S(2)}) collective-permute-start(bf16[2,128,128]{2,1,0:T(8,128)(2,1)S(1)} %slice.58), channel_id=1, source_target_pairs={{0,2},{1,3},{2,0},{3,1},{4,6},{5,7},{6,4},{7,5},{8,10},{9,11},{10,... | collective-permute-start | bytes 196616 | tf_op jit(solution)/shard_map/ppermute | solution.py:17
  12.8 10.0 %collective-permute-start.4 = (f32[64,128]{1,0:T(8,128)S(1)}, f32[64,128]{1,0:T(8,128)S(1)}, u32[]{:S(2)}, u32[]{:S(2)}) collective-permute-start(f32[64,128]{1,0:T(8,128)S(1)} %fusion.2), channel_id=1, source_target_pairs={{0,4},{1,5},{2,6},{3,7},{4,0},{5,1},{6,2},{7,3},{8,12},{9,13},{10,... | collective-permute-start | bytes 98312 | tf_op jit(solution)/shard_map/ppermute | solution.py:17
  14.7 5.0 %collective-permute-start.6 = (bf16[16,4096]{1,0:T(8,128)(2,1)S(1)}, bf16[16,4096]{1,0:T(8,128)(2,1)S(1)}, u32[]{:S(2)}, u32[]{:S(2)}) collective-permute-start(bf16[16,4096]{1,0:T(8,128)(2,1)S(1)} %pad_maximum_fusion), channel_id=1, source_target_pairs={{0,2},{1,3},{2,0},{3,1},{4,6},{5,7},{6,4},{7,5},{8,10},{9,11},{10,... | collective-permute-start | bytes 393224 | tf_op jit(solution)/shard_map/ppermute | solution.py:17
  16.3 4.9 %collective-permute-start.2 = (bf16[1,128,128]{2,1,0:T(8,128)(2,1)S(1)}, bf16[1,128,128]{2,1,0:T(8,128)(2,1)S(1)}, u32[]{:S(2)}, u32[]{:S(2)}) collective-permute-start(bf16[1,128,128]{2,1,0:T(8,128)(2,1)S(1)} %slice.59), channel_id=1, source_target_pairs={{0,8},{1,9},{2,10},{3,11},{4,12},{5,13},{6,14},{7,15},{8,0},{9,1},... | collective-permute-start | bytes 98312 | tf_op jit(solution)/shard_map/ppermute | solution.py:17
  19.8 3.1 %collective-permute-start.7 = (bf16[32,4096]{1,0:T(8,128)(2,1)S(1)}, bf16[32,4096]{1,0:T(8,128)(2,1)S(1)}, u32[]{:S(2)}, u32[]{:S(2)}) collective-permute-start(bf16[32,4096]{1,0:T(8,128)(2,1)S(1)} %constant_dynamic-update-slice_fusion.refs_0_), channel_id=1, source_target_pairs={{0,1},{1,0},{2,3},{3,2},{4,5},{5,4},{6,7},{7,6},{8,9},{9,8},{10,11... | collective-permute-start | bytes 786440 | tf_op jit(solution)/shard_map/ppermute | solution.py:17
  21.2 4.3 %collective-permute-start.3 = (f32[128,128]{1,0:T(8,128)S(1)}, f32[128,128]{1,0:T(8,128)S(1)}, u32[]{:S(2)}, u32[]{:S(2)}) collective-permute-start(f32[128,128]{1,0:T(8,128)S(1)} %fusion.own_ref), channel_id=1, source_target_pairs={{0,4},{1,5},{2,6},{3,7},{4,0},{5,1},{6,2},{7,3},{8,12},{9,13},{10,... | collective-permute-start | bytes 196616 | tf_op jit(solution)/shard_map/ppermute | solution.py:17
  22.9 2.7 %copy-start.2 = (s32[16]{0:T(128)S(1)}, s32[16]{0:T(128)}, u32[]{:S(2)}) copy-start(s32[16]{0:T(128)} %length_ref.3) | copy-start | bytes 196
  22.9 2.7 %copy-start.3 = (s32[16]{0:T(128)S(1)}, s32[16]{0:T(128)}, u32[]{:S(2)}) copy-start(s32[16]{0:T(128)} %valid_ref.3) | copy-start | bytes 196
  26.7 1.2 %collective-permute-start.9 = (f32[4,8,16]{2,1,0:T(8,128)S(1)}, f32[4,8,16]{2,1,0:T(8,128)S(1)}, u32[]{:S(2)}, u32[]{:S(2)}) collective-permute-start(f32[4,8,16]{2,1,0:T(8,128)S(1)} %slice.37), channel_id=1, source_target_pairs={{0,1},{1,0},{2,3},{3,2},{4,5},{5,4},{6,7},{7,6},{8,9},{9,8},{10,11... | collective-permute-start | bytes 6152 | tf_op jit(solution)/shard_map/ppermute | solution.py:17
  27.9 3.7 %collective-permute-start.10 = (f32[2,8,16]{2,1,0:T(8,128)S(1)}, f32[2,8,16]{2,1,0:T(8,128)S(1)}, u32[]{:S(2)}, u32[]{:S(2)}) collective-permute-start(f32[2,8,16]{2,1,0:T(8,128)S(1)} %slice.47), channel_id=1, source_target_pairs={{0,2},{1,3},{2,0},{3,1},{4,6},{5,7},{6,4},{7,5},{8,10},{9,11},{10,... | collective-permute-start | bytes 3080 | tf_op jit(solution)/shard_map/ppermute | solution.py:17
  28.4 7.7 %collective-permute-start.8 = (f32[64,128]{1,0:T(8,128)S(1)}, f32[64,128]{1,0:T(8,128)S(1)}, u32[]{:S(2)}, u32[]{:S(2)}) collective-permute-start(f32[64,128]{1,0:T(8,128)S(1)} %get-tuple-element.16), channel_id=1, source_target_pairs={{0,4},{1,5},{2,6},{3,7},{4,0},{5,1},{6,2},{7,3},{8,12},{9,13},{10,... | collective-permute-start | bytes 98312 | tf_op jit(solution)/shard_map/ppermute | solution.py:17
  31.6 4.5 %collective-permute-start.11 = (f32[1,8,16]{2,1,0:T(8,128)S(1)}, f32[1,8,16]{2,1,0:T(8,128)S(1)}, u32[]{:S(2)}, u32[]{:S(2)}) collective-permute-start(f32[1,8,16]{2,1,0:T(8,128)S(1)} %get-tuple-element.20), channel_id=1, source_target_pairs={{0,8},{1,9},{2,10},{3,11},{4,12},{5,13},{6,14},{7,15},{8,0},{9,1},... | collective-permute-start | bytes 1544 | tf_op jit(solution)/shard_map/ppermute | solution.py:17

commit v11 on v10

--- a/solution.py
+++ b/solution.py
@@ -1,4 +1,5 @@
 import functools
+import operator
 
 import jax
 import jax.numpy as jnp
@@ -261,41 +262,32 @@
     )(me, lengths, valid, own, other, products)
 
 
-def last_kernel(
-    place, split, me_ref, length_ref, valid_ref, own_ref, other_ref, doc_ref, more_ref, token_out, doc_out, turned_ref
-):
-    own_q, docs = doc_out.shape
+def place_kernel(place, split, me_ref, own_ref, other_ref, out_ref, turned_ref):
+    own_q = own_ref.shape[0] // len(place)
     for r, ref in enumerate((own_ref, other_ref)):
         for k, offset in enumerate(place):
-            spot = pl.multiple_of((me_ref[0] ^ (offset + split * r)) * own_q, own_q)
+            spot = pl.multiple_of((me_ref[0] ^ offset ^ (split * r)) * own_q, own_q)
             turned_ref[pl.ds(spot, own_q)] = ref[k * own_q : (k + 1) * own_q]
-    token_out[...] = turned_ref[...].T
-    doc_of = lax.broadcasted_iota(jnp.int32, (own_q, docs), 1)
-    used = jnp.zeros((own_q, docs), jnp.int32)
-    for d in range(docs):
-        used = jnp.where(doc_of == d, jnp.minimum(valid_ref[d], length_ref[d]), used)
-    doc_out[...] = (doc_ref[0] + more_ref[0]) * (1.0 / jnp.sqrt(used.astype(jnp.float32)))
-
-
-def last(me, lengths, valid, own, other, doc, more, place, split):
+    out_ref[...] = turned_ref[...].T
+
+
+def place_tokens(me, own, other, place, split):
     count, rows = own.shape
-    _, own_q, docs = doc.shape
     return pl.pallas_call(
-        functools.partial(last_kernel, place, split),
-        in_specs=[SMEM] * 3 + [VMEM] * 4,
-        out_specs=(VMEM, VMEM),
-        out_shape=(
-            jax.ShapeDtypeStruct((rows, 2 * count), jnp.float32),
-            jax.ShapeDtypeStruct((own_q, docs), jnp.float32),
-        ),
+        functools.partial(place_kernel, place, split),
+        in_specs=[SMEM, VMEM, VMEM],
+        out_specs=VMEM,
+        out_shape=jax.ShapeDtypeStruct((rows, 2 * count), jnp.float32),
         scratch_shapes=[pltpu.VMEM((2 * count, rows), jnp.float32)],
         compiler_params=pltpu.CompilerParams(vmem_limit_bytes=16 * MIB),
-    )(me, lengths, valid, own, other, doc, more)
+    )(me, own, other)
 
 
 def offset_of(number, bits):
     last_bit = len(bits) - 1
-    return sum(bit for k, bit in enumerate(bits) if (number >> (last_bit - k)) & 1)
+    return functools.reduce(
+        operator.xor, [bit for k, bit in enumerate(bits) if (number >> (last_bit - k)) & 1], 0
+    )
 
 
 def body(size, activations, out_grads, proj_in, proj_out, queries, doc_length, valid_count):
@@ -303,12 +295,12 @@
     width = proj_in.shape[1]
     own_q = queries.shape[0]
     me = lax.axis_index("seq").astype(jnp.int32)[None]
-    split = size // 4
-    middle = [1 << k for k in range(1, size.bit_length() - 1) if 1 << k != split]
+    split = size // 4 + 1
+    middle = [(1 << k) + 1 for k in range(1, size.bit_length() - 1) if 1 << k != size // 4]
 
     proj = proj_out.T
-    spots = [offset_of(m, middle) + split * r for m in range(size // 4) for r in range(2)]
-    theirs, table = grad_blocks(me, proj, out_grads, rows, [s + 1 for s in spots])
+    spots = [offset_of(m, middle) ^ (split * r) for m in range(size // 4) for r in range(2)]
+    theirs, table = grad_blocks(me, proj, out_grads, rows, [s ^ 1 for s in spots])
     from_core = swap(theirs, 1, size)
     panel = queries
     got = swap(panel, middle[-1], size)
@@ -346,10 +338,10 @@
         half = doc.shape[0] // 2
         doc = doc[:half] + swap(doc[half:], bit, size)
     more = swap(doc[1:], bits[-1], size)
-    token_scores, doc = last(
-        me, doc_length, valid_count, mine, others, doc[:1], more, place, split
-    )
-    return (token_scores, doc.T)
+    token_scores = place_tokens(me, mine, others, place, split)
+    more, token_scores = lax.optimization_barrier((more, token_scores))
+    scale = 1.0 / jnp.sqrt(jnp.minimum(valid_count, doc_length).astype(jnp.float32))
+    return (token_scores, ((doc[0] + more[0]) * scale[None, :]).T)
 
 
 def solution(mesh):

time: 37.5 us -> 34.7 us (0.925)
  waiting for transfers between devices: 13.5 us -> 10.7 us
  other arithmetic: 0.08 us -> 0.68 us
  Pallas kernels: 8.13 us -> 7.59 us
    ppermute x12, waiting for transfers between devices: 13.5 us -> 10.7 us  [swap(): return lax.ppermute(value, 'seq', [(i, i ^ offset) for i in range(size)])]
    transpose x0 -> x1, other arithmetic: none -> 0.6 us  [body(): return (token_scores, ((doc[0] + more[0]) * scale[None, :]).T)]
    pallas_call x1, Pallas kernels: 1.29 us -> 0.74 us  [place_tokens(): pl.pallas_call(functools.partial(place_kernel, place, split), in_specs=[S...]
  transfers between devices with their start and end apart: 12 -> 12, of which waited for: 8 -> 7; matrix products, arithmetic and copies ran while one was open for 3% -> 3% of each run, Pallas kernels for 15% -> 7%
where the time goes in v11:
time: 34.7 us; the launch traced here: 34.5 us
  starting transfers between devices  13.9 us (40%)
  waiting for transfers between devices  10.7 us (31%)
  Pallas kernels  7.59 us (22%)
  matrix products  0.88 us (3%)
  between operations  0.8 us (2%)
  other arithmetic  0.68 us (2%)
    ppermute x12, starting transfers between devices, swap(): return lax.ppermute(value, 'seq', [(i, i ^ offset) for i in range(size)])  13.9 us
    ppermute x12, waiting for transfers between devices, swap(): return lax.ppermute(value, 'seq', [(i, i ^ offset) for i in range(size)])  10.7 us
    pallas_call x1, Pallas kernels, grad_blocks(): pl.pallas_call(functools.partial(grad_kernel, offsets), in_specs=[SMEM, H...  3.96 us
    pallas_call x1, Pallas kernels, grad_blocks(): pl.pallas_call(functools.partial(held_kernel, offsets), in_specs=[SMEM, V...  1.1 us
    pallas_call x1, Pallas kernels, score(): pl.pallas_call(functools.partial(score_kernel, steps, split), out_shape=(...  1.08 us
    dot_general x1, matrix products, body(): lax.dot_general(late, activations, (((0,), (1,)), ((), ())), preferred_el...  0.88 us
    pallas_call x1, Pallas kernels, place_tokens(): pl.pallas_call(functools.partial(place_kernel, place, split), in_specs=[S...  0.74 us
    pallas_call x1, Pallas kernels, inner(): pl.pallas_call(functools.partial(inner_kernel, len(panels)), out_shape=ja...  0.71 us
  transfers between devices with their start and end apart: 12, of which 7 were waited for; matrix products, arithmetic and copies ran while one was open for 3% of the time, Pallas kernels for 7%

profile of v11, /device:TPU:0, one launch (start us, length us, event | category | flops | bytes accessed | tf_op | source)
XLA Modules:
  0.0 34.5 jit_solution(15248821479517083261)
XLA Ops:
  0.6 0.0 copy-start
  0.6 0.0 copy-start.5
  0.7 0.0 copy-start.1
  0.7 4.0 %shard_map.86 = (f32[4,128,128]{2,1,0:T(8,128)S(1)}, bf16[2,1792,128]{2,1,0:T(8,128)(2,1)S(1)}) custom-call(s32[1]{0:T(128)} %bitcast.me_ref, bf16[64,1792]{1,0:T(8,128)(2,1)} %bitcast.16, bf16[2048,1792]{1,0:T(8,128)(2,1)} %grads_ref.3), custom_call_target="tpu_custom_call" | custom-call | flops 234881024 | bytes 3670016 | tf_op jit(solution)/shard_map/pallas_call | solution.py:93
  4.6 0.5 %collective-permute-start = (f32[4,128,128]{2,1,0:T(8,128)S(1)}, f32[4,128,128]{2,1,0:T(8,128)S(1)}, u32[]{:S(2)}, u32[]{:S(2)}) collective-permute-start(f32[4,128,128]{2,1,0:T(8,128)S(1)} %get-tuple-element.12), channel_id=1, source_target_pairs={{0,1},{1,0},{2,3},{3,2},{4,5},{5,4},{6,7},{7,6},{8,9},{9,8},{10,11... | collective-permute-start | bytes 786440 | tf_op jit(solution)/shard_map/ppermute | solution.py:18
  5.2 0.0 copy-done.5
  5.2 3.7 %collective-permute-start.5 = (bf16[8,4096]{1,0:T(8,128)(2,1)S(1)}, bf16[8,4096]{1,0:T(8,128)(2,1)S(1)}, u32[]{:S(2)}, u32[]{:S(2)}) collective-permute-start(bf16[8,4096]{1,0:T(8,128)(2,1)S(1)} %copy-done.5), channel_id=1, source_target_pairs={{0,9},{1,8},{2,11},{3,10},{4,13},{5,12},{6,15},{7,14},{8,1},{9,0},... | collective-permute-start | bytes 196616 | tf_op jit(solution)/shard_map/ppermute | solution.py:18
  8.9 0.0 copy-done.1
  8.9 0.0 copy-start.4
  8.9 1.1 %shard_map.87 = f32[4,128,128]{2,1,0:T(8,128)S(1)} custom-call(s32[1]{0:T(128)} %bitcast.me_ref, bf16[2,1792,128]{2,1,0:T(8,128)(2,1)S(1)} %get-tuple-element.11.table, bf16[2048,1792]{1,0:T(8,128)(2,1)S(1)} %copy-done.1), custom_call_target="tpu_custom_call" | custom-call | flops 234881024 | bytes 3670016 | tf_op jit(solution)/shard_map/pallas_call | solution.py:86
  10.0 0.0 collective-permute-done
  10.1 1.3 %collective-permute-start.1 = (bf16[2,128,128]{2,1,0:T(8,128)(2,1)S(1)}, bf16[2,128,128]{2,1,0:T(8,128)(2,1)S(1)}, u32[]{:S(2)}, u32[]{:S(2)}) collective-permute-start(bf16[2,128,128]{2,1,0:T(8,128)(2,1)S(1)} %slice.65), channel_id=1, source_target_pairs={{0,3},{1,2},{2,1},{3,0},{4,7},{5,6},{6,5},{7,4},{8,11},{9,10},{10,... | collective-permute-start | bytes 196616 | tf_op jit(solution)/shard_map/ppermute | solution.py:18
  11.3 0.0 copy-done
  11.3 0.0 copy-done.4
  11.3 0.9 %fusion.4 = f32[64,128]{1,0:T(8,128)S(1)} fusion(bf16[8192,64]{0,1:T(8,128)(2,1)S(1)} %copy-done.4, bf16[128,8192]{1,0:T(8,128)(2,1)S(1)} %copy-done), kind=kOutput, calls=%fused_computation.17 | convolution fusion | flops 134217728 | bytes 3178496 | tf_op jit(solution)/shard_map/dot_general | solution.py:326
  12.2 1.7 %collective-permute-start.4 = (f32[64,128]{1,0:T(8,128)S(1)}, f32[64,128]{1,0:T(8,128)S(1)}, u32[]{:S(2)}, u32[]{:S(2)}) collective-permute-start(f32[64,128]{1,0:T(8,128)S(1)} %fusion.4), channel_id=1, source_target_pairs={{0,5},{1,4},{2,7},{3,6},{4,1},{5,0},{6,3},{7,2},{8,13},{9,12},{10,... | collective-permute-start | bytes 98312 | tf_op jit(solution)/shard_map/ppermute | solution.py:18
  13.9 0.4 %collective-permute-done.1 = bf16[2,128,128]{2,1,0:T(8,128)(2,1)S(1)} collective-permute-done((bf16[2,128,128]{2,1,0:T(8,128)(2,1)S(1)}, bf16[2,128,128]{2,1,0:T(8,128)(2,1)S(1)}, u32[]{:S(2)}, u32[]{:S(2)}) %collective-permute-start.1) | collective-permute-done | bytes 65568 | tf_op jit(solution)/shard_map/ppermute | solution.py:18
  14.3 0.0 collective-permute-done.5
  14.3 1.6 %collective-permute-start.6 = (bf16[16,4096]{1,0:T(8,128)(2,1)S(1)}, bf16[16,4096]{1,0:T(8,128)(2,1)S(1)}, u32[]{:S(2)}, u32[]{:S(2)}) collective-permute-start(bf16[16,4096]{1,0:T(8,128)(2,1)S(1)} %pad_maximum_fusion), channel_id=1, source_target_pairs={{0,3},{1,2},{2,1},{3,0},{4,7},{5,6},{6,5},{7,4},{8,11},{9,10},{10,... | collective-permute-start | bytes 393224 | tf_op jit(solution)/shard_map/ppermute | solution.py:18
  15.9 0.2 collective-permute-start.2
  16.1 3.8 %collective-permute-done.6 = bf16[16,4096]{1,0:T(8,128)(2,1)S(1)} collective-permute-done((bf16[16,4096]{1,0:T(8,128)(2,1)S(1)}, bf16[16,4096]{1,0:T(8,128)(2,1)S(1)}, u32[]{:S(2)}, u32[]{:S(2)}) %collective-permute-start.6) | collective-permute-done | bytes 131104 | tf_op jit(solution)/shard_map/ppermute | solution.py:18
  19.9 0.5 %collective-permute-start.7 = (bf16[32,4096]{1,0:T(8,128)(2,1)S(1)}, bf16[32,4096]{1,0:T(8,128)(2,1)S(1)}, u32[]{:S(2)}, u32[]{:S(2)}) collective-permute-start(bf16[32,4096]{1,0:T(8,128)(2,1)S(1)} %constant_dynamic-update-slice_fusion.refs_0_), channel_id=1, source_target_pairs={{0,1},{1,0},{2,3},{3,2},{4,5},{5,4},{6,7},{7,6},{8,9},{9,8},{10,11... | collective-permute-start | bytes 786440 | tf_op jit(solution)/shard_map/ppermute | solution.py:18
  20.4 0.0 collective-permute-done.2
  20.4 1.3 %collective-permute-start.3 = (f32[128,128]{1,0:T(8,128)S(1)}, f32[128,128]{1,0:T(8,128)S(1)}, u32[]{:S(2)}, u32[]{:S(2)}) collective-permute-start(f32[128,128]{1,0:T(8,128)S(1)} %fusion.own_ref), channel_id=1, source_target_pairs={{0,5},{1,4},{2,7},{3,6},{4,1},{5,0},{6,3},{7,2},{8,13},{9,12},{10,... | collective-permute-start | bytes 196616 | tf_op jit(solution)/shard_map/ppermute | solution.py:18
  21.7 0.0 collective-permute-done.4
  21.7 0.0 copy-start.2
  21.8 0.0 copy-start.3
  21.8 0.0 collective-permute-done.7.refs_1_
  21.8 0.7 %shard_map.88.inner_ref = f32[2048,512]{1,0:T(8,128)S(1)} custom-call(f32[2,64,128]{2,1,0:T(8,128)S(1)} %pad_maximum_fusion.1.act_ref, bf16[32,4096]{1,0:T(8,128)(2,1)S(1)} %constant_dynamic-update-slice_fusion.refs_0_, bf16[32,4096]{1,0:T(8,128)(2,1)S(1)} %collective-permute-done.7.refs_1_), custom_call_target="tpu_custom_call" | custom-call | flops 536870912 | bytes 4194304 | tf_op jit(solution)/shard_map/pallas_call | solution.py:147
  22.5 2.1 %collective-permute-done.3.other_ref = f32[128,128]{1,0:T(8,128)S(1)} collective-permute-done((f32[128,128]{1,0:T(8,128)S(1)}, f32[128,128]{1,0:T(8,128)S(1)}, u32[]{:S(2)}, u32[]{:S(2)}) %collective-permute-start.3) | collective-permute-done | bytes 65568 | tf_op jit(solution)/shard_map/ppermute | solution.py:18
  24.6 0.0 copy-done.2
  24.6 0.0 copy-done.3
  24.6 1.1 %shard_map.89 = (f32[64,128]{1,0:T(8,128)S(1)}, f32[64,128]{1,0:T(8,128)S(1)}, f32[8,8,16]{2,1,0:T(8,128)S(1)}) custom-call(s32[1]{0:T(128)} %bitcast.me_ref, s32[16]{0:T(128)S(1)} %copy-done.2, s32[16]{0:T(128)S(1)} %copy-done.3, f32[128,128]{1,0:T(8,128)S(1)} %fusion.own_ref, f32[128,128]{1,0:T(8,128)S(1)} %collective-permute-done.3.other_ref, ...), custom_call_target="tpu_custom_call" | custom-call | flops 2097152 | bytes 4194304 | tf_op jit(solution)/shard_map/pallas_call | solution.py:247
  25.7 0.2 collective-permute-start.8
  25.9 1.1 %collective-permute-done.8 = f32[4,8,16]{2,1,0:T(8,128)S(1)} collective-permute-done((f32[4,8,16]{2,1,0:T(8,128)S(1)}, f32[4,8,16]{2,1,0:T(8,128)S(1)}, u32[]{:S(2)}, u32[]{:S(2)}) %collective-permute-start.8) | collective-permute-done | bytes 2080 | tf_op jit(solution)/shard_map/ppermute | solution.py:18
  26.9 1.0 %collective-permute-start.9 = (f32[2,8,16]{2,1,0:T(8,128)S(1)}, f32[2,8,16]{2,1,0:T(8,128)S(1)}, u32[]{:S(2)}, u32[]{:S(2)}) collective-permute-start(f32[2,8,16]{2,1,0:T(8,128)S(1)} %slice.47), channel_id=1, source_target_pairs={{0,3},{1,2},{2,1},{3,0},{4,7},{5,6},{6,5},{7,4},{8,11},{9,10},{10,... | collective-permute-start | bytes 3080 | tf_op jit(solution)/shard_map/ppermute | solution.py:18
  27.9 1.5 %collective-permute-start.11 = (f32[64,128]{1,0:T(8,128)S(1)}, f32[64,128]{1,0:T(8,128)S(1)}, u32[]{:S(2)}, u32[]{:S(2)}) collective-permute-start(f32[64,128]{1,0:T(8,128)S(1)} %get-tuple-element.17), channel_id=1, source_target_pairs={{0,5},{1,4},{2,7},{3,6},{4,1},{5,0},{6,3},{7,2},{8,13},{9,12},{10,... | collective-permute-start | bytes 98312 | tf_op jit(solution)/shard_map/ppermute | solution.py:18
  29.4 0.6 %collective-permute-done.9 = f32[2,8,16]{2,1,0:T(8,128)S(1)} collective-permute-done((f32[2,8,16]{2,1,0:T(8,128)S(1)}, f32[2,8,16]{2,1,0:T(8,128)S(1)}, u32[]{:S(2)}, u32[]{:S(2)}) %collective-permute-start.9) | collective-permute-done | bytes 1056 | tf_op jit(solution)/shard_map/ppermute | solution.py:18
  30.0 0.5 %collective-permute-start.10 = (f32[1,8,16]{2,1,0:T(8,128)S(1)}, f32[1,8,16]{2,1,0:T(8,128)S(1)}, u32[]{:S(2)}, u32[]{:S(2)}) collective-permute-start(f32[1,8,16]{2,1,0:T(8,128)S(1)} %slice.48), channel_id=1, source_target_pairs={{0,9},{1,8},{2,11},{3,10},{4,13},{5,12},{6,15},{7,14},{8,1},{9,0},... | collective-permute-start | bytes 1544 | tf_op jit(solution)/shard_map/ppermute | solution.py:18
  30.5 0.8 %collective-permute-done.11.other_ref = f32[64,128]{1,0:T(8,128)S(1)} collective-permute-done((f32[64,128]{1,0:T(8,128)S(1)}, f32[64,128]{1,0:T(8,128)S(1)}, u32[]{:S(2)}, u32[]{:S(2)}) %collective-permute-start.11) | collective-permute-done | bytes 32800 | tf_op jit(solution)/shard_map/ppermute | solution.py:18
  31.2 0.7 %shard_map.90 = f32[128,128]{1,0:T(8,128)} custom-call(s32[1]{0:T(128)} %bitcast.me_ref, f32[64,128]{1,0:T(8,128)S(1)} %get-tuple-element.16.own_ref, f32[64,128]{1,0:T(8,128)S(1)} %collective-permute-done.11.other_ref), custom_call_target="tpu_custom_call" | custom-call | tf_op jit(solution)/shard_map/pallas_call | solution.py:276
  32.0 2.0 %collective-permute-done.10 = f32[1,8,16]{2,1,0:T(8,128)S(1)} collective-permute-done((f32[1,8,16]{2,1,0:T(8,128)S(1)}, f32[1,8,16]{2,1,0:T(8,128)S(1)}, u32[]{:S(2)}, u32[]{:S(2)}) %collective-permute-start.10) | collective-permute-done | bytes 544 | tf_op jit(solution)/shard_map/ppermute | solution.py:18
  34.0 0.6 %fusion.3 = f32[16,8]{0,1:T(8,128)} fusion(f32[1,8,16]{2,1,0:T(8,128)S(1)} %collective-permute-done.10, f32[2,8,16]{2,1,0:T(8,128)S(1)} %slice_add_fusion.3, f32[16]{0:T(128)S(1)} %convert_rsqrt_fusion), kind=kLoop, calls=%fused_computation.15 | loop fusion | flops 256 | bytes 1600 | tf_op jit(solution)/shard_map/transpose | solution.py:344
  (16 shorter events, 0.1 us)
Async XLA Ops:
  0.6 10.7 %copy-start = (bf16[128,8192]{1,0:T(8,128)(2,1)S(1)}, bf16[128,8192]{1,0:T(8,128)(2,1)}, u32[]{:S(2)}) copy-start(bf16[128,8192]{1,0:T(8,128)(2,1)} %param.7) | copy-start | bytes 6291460
  0.6 4.5 %copy-start.5 = (bf16[8,4096]{1,0:T(8,128)(2,1)S(1)}, bf16[8,4096]{1,0:T(8,128)(2,1)}, u32[]{:S(2)}) copy-start(bf16[8,4096]{1,0:T(8,128)(2,1)} %param.11) | copy-start | bytes 196612
  0.7 8.2 %copy-start.1 = (bf16[2048,1792]{1,0:T(8,128)(2,1)S(1)}, bf16[2048,1792]{1,0:T(8,128)(2,1)}, u32[]{:S(2)}) copy-start(bf16[2048,1792]{1,0:T(8,128)(2,1)} %grads_ref.3) | copy-start | bytes 22020100
  4.6 5.4 %collective-permute-start = (f32[4,128,128]{2,1,0:T(8,128)S(1)}, f32[4,128,128]{2,1,0:T(8,128)S(1)}, u32[]{:S(2)}, u32[]{:S(2)}) collective-permute-start(f32[4,128,128]{2,1,0:T(8,128)S(1)} %get-tuple-element.12), channel_id=1, source_target_pairs={{0,1},{1,0},{2,3},{3,2},{4,5},{5,4},{6,7},{7,6},{8,9},{9,8},{10,11... | collective-permute-start | bytes 786440 | tf_op jit(solution)/shard_map/ppermute | solution.py:18
  5.2 9.1 %collective-permute-start.5 = (bf16[8,4096]{1,0:T(8,128)(2,1)S(1)}, bf16[8,4096]{1,0:T(8,128)(2,1)S(1)}, u32[]{:S(2)}, u32[]{:S(2)}) collective-permute-start(bf16[8,4096]{1,0:T(8,128)(2,1)S(1)} %copy-done.5), channel_id=1, source_target_pairs={{0,9},{1,8},{2,11},{3,10},{4,13},{5,12},{6,15},{7,14},{8,1},{9,0},... | collective-permute-start | bytes 196616 | tf_op jit(solution)/shard_map/ppermute | solution.py:18
  8.9 2.5 %copy-start.4 = (bf16[8192,64]{0,1:T(8,128)(2,1)S(1)}, bf16[8192,64]{0,1:T(8,128)(2,1)}, u32[]{:S(2)}) copy-start(bf16[8192,64]{0,1:T(8,128)(2,1)} %param.9) | copy-start | bytes 3145732
  10.1 4.2 %collective-permute-start.1 = (bf16[2,128,128]{2,1,0:T(8,128)(2,1)S(1)}, bf16[2,128,128]{2,1,0:T(8,128)(2,1)S(1)}, u32[]{:S(2)}, u32[]{:S(2)}) collective-permute-start(bf16[2,128,128]{2,1,0:T(8,128)(2,1)S(1)} %slice.65), channel_id=1, source_target_pairs={{0,3},{1,2},{2,1},{3,0},{4,7},{5,6},{6,5},{7,4},{8,11},{9,10},{10,... | collective-permute-start | bytes 196616 | tf_op jit(solution)/shard_map/ppermute | solution.py:18
  12.2 9.5 %collective-permute-start.4 = (f32[64,128]{1,0:T(8,128)S(1)}, f32[64,128]{1,0:T(8,128)S(1)}, u32[]{:S(2)}, u32[]{:S(2)}) collective-permute-start(f32[64,128]{1,0:T(8,128)S(1)} %fusion.4), channel_id=1, source_target_pairs={{0,5},{1,4},{2,7},{3,6},{4,1},{5,0},{6,3},{7,2},{8,13},{9,12},{10,... | collective-permute-start | bytes 98312 | tf_op jit(solution)/shard_map/ppermute | solution.py:18
  14.3 5.6 %collective-permute-start.6 = (bf16[16,4096]{1,0:T(8,128)(2,1)S(1)}, bf16[16,4096]{1,0:T(8,128)(2,1)S(1)}, u32[]{:S(2)}, u32[]{:S(2)}) collective-permute-start(bf16[16,4096]{1,0:T(8,128)(2,1)S(1)} %pad_maximum_fusion), channel_id=1, source_target_pairs={{0,3},{1,2},{2,1},{3,0},{4,7},{5,6},{6,5},{7,4},{8,11},{9,10},{10,... | collective-permute-start | bytes 393224 | tf_op jit(solution)/shard_map/ppermute | solution.py:18
  15.9 4.5 %collective-permute-start.2 = (bf16[1,128,128]{2,1,0:T(8,128)(2,1)S(1)}, bf16[1,128,128]{2,1,0:T(8,128)(2,1)S(1)}, u32[]{:S(2)}, u32[]{:S(2)}) collective-permute-start(bf16[1,128,128]{2,1,0:T(8,128)(2,1)S(1)} %slice.66), channel_id=1, source_target_pairs={{0,9},{1,8},{2,11},{3,10},{4,13},{5,12},{6,15},{7,14},{8,1},{9,0},... | collective-permute-start | bytes 98312 | tf_op jit(solution)/shard_map/ppermute | solution.py:18
  19.9 1.9 %collective-permute-start.7 = (bf16[32,4096]{1,0:T(8,128)(2,1)S(1)}, bf16[32,4096]{1,0:T(8,128)(2,1)S(1)}, u32[]{:S(2)}, u32[]{:S(2)}) collective-permute-start(bf16[32,4096]{1,0:T(8,128)(2,1)S(1)} %constant_dynamic-update-slice_fusion.refs_0_), channel_id=1, source_target_pairs={{0,1},{1,0},{2,3},{3,2},{4,5},{5,4},{6,7},{7,6},{8,9},{9,8},{10,11... | collective-permute-start | bytes 786440 | tf_op jit(solution)/shard_map/ppermute | solution.py:18
  20.4 4.2 %collective-permute-start.3 = (f32[128,128]{1,0:T(8,128)S(1)}, f32[128,128]{1,0:T(8,128)S(1)}, u32[]{:S(2)}, u32[]{:S(2)}) collective-permute-start(f32[128,128]{1,0:T(8,128)S(1)} %fusion.own_ref), channel_id=1, source_target_pairs={{0,5},{1,4},{2,7},{3,6},{4,1},{5,0},{6,3},{7,2},{8,13},{9,12},{10,... | collective-permute-start | bytes 196616 | tf_op jit(solution)/shard_map/ppermute | solution.py:18
  21.7 2.8 %copy-start.2 = (s32[16]{0:T(128)S(1)}, s32[16]{0:T(128)}, u32[]{:S(2)}) copy-start(s32[16]{0:T(128)} %length_ref.1) | copy-start | bytes 196
  21.8 2.8 %copy-start.3 = (s32[16]{0:T(128)S(1)}, s32[16]{0:T(128)}, u32[]{:S(2)}) copy-start(s32[16]{0:T(128)} %valid_ref.1) | copy-start | bytes 196
  25.7 1.2 %collective-permute-start.8 = (f32[4,8,16]{2,1,0:T(8,128)S(1)}, f32[4,8,16]{2,1,0:T(8,128)S(1)}, u32[]{:S(2)}, u32[]{:S(2)}) collective-permute-start(f32[4,8,16]{2,1,0:T(8,128)S(1)} %slice.37), channel_id=1, source_target_pairs={{0,1},{1,0},{2,3},{3,2},{4,5},{5,4},{6,7},{7,6},{8,9},{9,8},{10,11... | collective-permute-start | bytes 6152 | tf_op jit(solution)/shard_map/ppermute | solution.py:18
  26.9 3.1 %collective-permute-start.9 = (f32[2,8,16]{2,1,0:T(8,128)S(1)}, f32[2,8,16]{2,1,0:T(8,128)S(1)}, u32[]{:S(2)}, u32[]{:S(2)}) collective-permute-start(f32[2,8,16]{2,1,0:T(8,128)S(1)} %slice.47), channel_id=1, source_target_pairs={{0,3},{1,2},{2,1},{3,0},{4,7},{5,6},{6,5},{7,4},{8,11},{9,10},{10,... | collective-permute-start | bytes 3080 | tf_op jit(solution)/shard_map/ppermute | solution.py:18
  27.9 3.3 %collective-permute-start.11 = (f32[64,128]{1,0:T(8,128)S(1)}, f32[64,128]{1,0:T(8,128)S(1)}, u32[]{:S(2)}, u32[]{:S(2)}) collective-permute-start(f32[64,128]{1,0:T(8,128)S(1)} %get-tuple-element.17), channel_id=1, source_target_pairs={{0,5},{1,4},{2,7},{3,6},{4,1},{5,0},{6,3},{7,2},{8,13},{9,12},{10,... | collective-permute-start | bytes 98312 | tf_op jit(solution)/shard_map/ppermute | solution.py:18
  30.0 3.9 %collective-permute-start.10 = (f32[1,8,16]{2,1,0:T(8,128)S(1)}, f32[1,8,16]{2,1,0:T(8,128)S(1)}, u32[]{:S(2)}, u32[]{:S(2)}) collective-permute-start(f32[1,8,16]{2,1,0:T(8,128)S(1)} %slice.48), channel_id=1, source_target_pairs={{0,9},{1,8},{2,11},{3,10},{4,13},{5,12},{6,15},{7,14},{8,1},{9,0},... | collective-permute-start | bytes 1544 | tf_op jit(solution)/shard_map/ppermute | solution.py:18

commit v12 on v11

--- a/solution.py
+++ b/solution.py
@@ -306,14 +306,20 @@
     got = swap(panel, middle[-1], size)
     sums = grad_blocks(me, proj, out_grads, rows, spots, table) + from_core
     late, _ = lax.optimization_barrier((proj_in, sums))
+    got, sums = lax.optimization_barrier((got, sums))
     for k, bit in enumerate(middle):
         half = sums.shape[0] // 2
         sent = swap(sums[half:].astype(jnp.bfloat16), bit, size)
         sums = sums[:half] + sent.astype(jnp.float32)
         if k == 0:
-            got, _ = lax.optimization_barrier((got, sums))
+            after = sums
     own = sums[0]
     across = swap(own, split, size)
+    act = lax.dot_general(
+        late, activations, (((0,), (1,)), ((), ())), preferred_element_type=jnp.float32
+    )
+    sent_act = act
+    act = jnp.stack([act, swap(sent_act, split, size)])
 
     panel = jnp.concatenate([panel, got], axis=0)
     place = [0, middle[-1]]
@@ -323,10 +329,6 @@
     panels = [panel, swap(panel, 1, size)]
     place = tuple(place + [p ^ 1 for p in place])
 
-    act = lax.dot_general(
-        late, activations, (((0,), (1,)), ((), ())), preferred_element_type=jnp.float32
-    )
-    act = jnp.stack([act, swap(act, split, size)])
     steps = max(1, 4 * width * size * own_q * rows // (4 * MIB))
     products = inner(act, panels, steps)
     mine, theirs, doc = score(

time: 34.7 us -> 34 us (0.980)
  starting transfers between devices: 13.9 us -> 12.9 us
    ppermute x12, starting transfers between devices: 13.9 us -> 12.9 us  [swap(): return lax.ppermute(value, 'seq', [(i, i ^ offset) for i in range(size)])]
    ppermute x12, waiting for transfers between devices: 10.7 us -> 11 us  [swap(): return lax.ppermute(value, 'seq', [(i, i ^ offset) for i in range(size)])]
  transfers between devices with their start and end apart: 12 -> 12, of which waited for: 7 -> 6; matrix products, arithmetic and copies ran while one was open for 3% -> 3% of each run, Pallas kernels for 7% -> 19%
where the time goes in v12:
time: 34 us; the launch traced here: 33.9 us
  starting transfers between devices  12.9 us (38%)
  waiting for transfers between devices  11 us (32%)
  Pallas kernels  7.59 us (22%)
  matrix products  0.88 us (3%)
  between operations  0.79 us (2%)
  other arithmetic  0.68 us (2%)
    ppermute x12, starting transfers between devices, swap(): return lax.ppermute(value, 'seq', [(i, i ^ offset) for i in range(size)])  12.9 us
    ppermute x12, waiting for transfers between devices, swap(): return lax.ppermute(value, 'seq', [(i, i ^ offset) for i in range(size)])  11 us
    pallas_call x1, Pallas kernels, grad_blocks(): pl.pallas_call(functools.partial(grad_kernel, offsets), in_specs=[SMEM, H...  3.95 us
    pallas_call x1, Pallas kernels, grad_blocks(): pl.pallas_call(functools.partial(held_kernel, offsets), in_specs=[SMEM, V...  1.1 us
    pallas_call x1, Pallas kernels, score(): pl.pallas_call(functools.partial(score_kernel, steps, split), out_shape=(...  1.08 us
    dot_general x1, matrix products, body(): lax.dot_general(late, activations, (((0,), (1,)), ((), ())), preferred_el...  0.88 us
    pallas_call x1, Pallas kernels, place_tokens(): pl.pallas_call(functools.partial(place_kernel, place, split), in_specs=[S...  0.75 us
    pallas_call x1, Pallas kernels, inner(): pl.pallas_call(functools.partial(inner_kernel, len(panels)), out_shape=ja...  0.7 us
  transfers between devices with their start and end apart: 12, of which 6 were waited for; matrix products, arithmetic and copies ran while one was open for 3% of the time, Pallas kernels for 19%

profile of v12, /device:TPU:0, one launch (start us, length us, event | category | flops | bytes accessed | tf_op | source)
XLA Modules:
  0.0 33.9 jit_solution(14629254279973808054)
XLA Ops:
  0.6 0.0 copy-start
  0.6 3.5 %collective-permute-start = (bf16[8,4096]{1,0:T(8,128)(2,1)}, bf16[8,4096]{1,0:T(8,128)(2,1)S(1)}, u32[]{:S(2)}, u32[]{:S(2)}) collective-permute-start(bf16[8,4096]{1,0:T(8,128)(2,1)} %param.11), channel_id=1, source_target_pairs={{0,9},{1,8},{2,11},{3,10},{4,13},{5,12},{6,15},{7,14},{8,1},{9,0},... | collective-permute-start | bytes 196616 | tf_op jit(solution)/shard_map/ppermute | solution.py:18
  4.2 0.0 copy-start.5
  4.2 0.0 copy-start.1
  4.2 4.0 %shard_map.86 = (f32[4,128,128]{2,1,0:T(8,128)S(1)}, bf16[2,1792,128]{2,1,0:T(8,128)(2,1)S(1)}) custom-call(s32[1]{0:T(128)} %bitcast.me_ref, bf16[64,1792]{1,0:T(8,128)(2,1)} %bitcast.16, bf16[2048,1792]{1,0:T(8,128)(2,1)} %grads_ref.3), custom_call_target="tpu_custom_call" | custom-call | flops 234881024 | bytes 3670016 | tf_op jit(solution)/shard_map/pallas_call | solution.py:93
  8.2 0.7 %collective-permute-start.1 = (f32[4,128,128]{2,1,0:T(8,128)S(1)}, f32[4,128,128]{2,1,0:T(8,128)S(1)}, u32[]{:S(2)}, u32[]{:S(2)}) collective-permute-start(f32[4,128,128]{2,1,0:T(8,128)S(1)} %get-tuple-element.13), channel_id=1, source_target_pairs={{0,1},{1,0},{2,3},{3,2},{4,5},{5,4},{6,7},{7,6},{8,9},{9,8},{10,11... | collective-permute-start | bytes 786440 | tf_op jit(solution)/shard_map/ppermute | solution.py:18
  8.9 0.0 copy-done.5
  8.9 0.0 copy-done.1
  8.9 0.0 copy-start.4
  8.9 1.1 %shard_map.87 = f32[4,128,128]{2,1,0:T(8,128)S(1)} custom-call(s32[1]{0:T(128)} %bitcast.me_ref, bf16[2,1792,128]{2,1,0:T(8,128)(2,1)S(1)} %get-tuple-element.12.table, bf16[2048,1792]{1,0:T(8,128)(2,1)S(1)} %copy-done.1), custom_call_target="tpu_custom_call" | custom-call | flops 234881024 | bytes 3670016 | tf_op jit(solution)/shard_map/pallas_call | solution.py:86
  10.0 0.0 collective-permute-done.1
  10.1 0.0 collective-permute-done
  10.1 1.6 %collective-permute-start.2 = (bf16[2,128,128]{2,1,0:T(8,128)(2,1)S(1)}, bf16[2,128,128]{2,1,0:T(8,128)(2,1)S(1)}, u32[]{:S(2)}, u32[]{:S(2)}) collective-permute-start(bf16[2,128,128]{2,1,0:T(8,128)(2,1)S(1)} %slice.64), channel_id=1, source_target_pairs={{0,3},{1,2},{2,1},{3,0},{4,7},{5,6},{6,5},{7,4},{8,11},{9,10},{10,... | collective-permute-start | bytes 196616 | tf_op jit(solution)/shard_map/ppermute | solution.py:18
  11.7 0.0 copy-done
  11.7 0.0 copy-done.4
  11.7 0.9 %fusion.4 = f32[64,128]{1,0:T(8,128)S(1)} fusion(bf16[8192,64]{0,1:T(8,128)(2,1)S(1)} %copy-done.4, bf16[128,8192]{1,0:T(8,128)(2,1)S(1)} %copy-done), kind=kOutput, calls=%fused_computation.17 | convolution fusion | flops 134217728 | bytes 3178496 | tf_op jit(solution)/shard_map/dot_general | solution.py:318
  12.6 1.4 %collective-permute-start.5 = (f32[64,128]{1,0:T(8,128)S(1)}, f32[64,128]{1,0:T(8,128)S(1)}, u32[]{:S(2)}, u32[]{:S(2)}) collective-permute-start(f32[64,128]{1,0:T(8,128)S(1)} %fusion.4), channel_id=1, source_target_pairs={{0,5},{1,4},{2,7},{3,6},{4,1},{5,0},{6,3},{7,2},{8,13},{9,12},{10,... | collective-permute-start | bytes 98312 | tf_op jit(solution)/shard_map/ppermute | solution.py:18
  14.0 0.5 %collective-permute-start.6 = (bf16[16,4096]{1,0:T(8,128)(2,1)S(1)}, bf16[16,4096]{1,0:T(8,128)(2,1)S(1)}, u32[]{:S(2)}, u32[]{:S(2)}) collective-permute-start(bf16[16,4096]{1,0:T(8,128)(2,1)S(1)} %pad_maximum_fusion), channel_id=1, source_target_pairs={{0,3},{1,2},{2,1},{3,0},{4,7},{5,6},{6,5},{7,4},{8,11},{9,10},{10,... | collective-permute-start | bytes 393224 | tf_op jit(solution)/shard_map/ppermute | solution.py:18
  14.5 0.0 collective-permute-done.2
  14.6 1.3 %collective-permute-start.3 = (bf16[1,128,128]{2,1,0:T(8,128)(2,1)S(1)}, bf16[1,128,128]{2,1,0:T(8,128)(2,1)S(1)}, u32[]{:S(2)}, u32[]{:S(2)}) collective-permute-start(bf16[1,128,128]{2,1,0:T(8,128)(2,1)S(1)} %slice.65), channel_id=1, source_target_pairs={{0,9},{1,8},{2,11},{3,10},{4,13},{5,12},{6,15},{7,14},{8,1},{9,0},... | collective-permute-start | bytes 98312 | tf_op jit(solution)/shard_map/ppermute | solution.py:18
  15.9 3.6 %collective-permute-done.6 = bf16[16,4096]{1,0:T(8,128)(2,1)S(1)} collective-permute-done((bf16[16,4096]{1,0:T(8,128)(2,1)S(1)}, bf16[16,4096]{1,0:T(8,128)(2,1)S(1)}, u32[]{:S(2)}, u32[]{:S(2)}) %collective-permute-start.6) | collective-permute-done | bytes 131104 | tf_op jit(solution)/shard_map/ppermute | solution.py:18
  19.4 0.3 %collective-permute-start.7 = (bf16[32,4096]{1,0:T(8,128)(2,1)S(1)}, bf16[32,4096]{1,0:T(8,128)(2,1)S(1)}, u32[]{:S(2)}, u32[]{:S(2)}) collective-permute-start(bf16[32,4096]{1,0:T(8,128)(2,1)S(1)} %constant_dynamic-update-slice_fusion.refs_0_), channel_id=1, source_target_pairs={{0,1},{1,0},{2,3},{3,2},{4,5},{5,4},{6,7},{7,6},{8,9},{9,8},{10,11... | collective-permute-start | bytes 786440 | tf_op jit(solution)/shard_map/ppermute | solution.py:18
  19.8 0.0 collective-permute-done.3
  19.8 0.4 %collective-permute-start.4 = (f32[128,128]{1,0:T(8,128)S(1)}, f32[128,128]{1,0:T(8,128)S(1)}, u32[]{:S(2)}, u32[]{:S(2)}) collective-permute-start(f32[128,128]{1,0:T(8,128)S(1)} %fusion.own_ref), channel_id=1, source_target_pairs={{0,5},{1,4},{2,7},{3,6},{4,1},{5,0},{6,3},{7,2},{8,13},{9,12},{10,... | collective-permute-start | bytes 196616 | tf_op jit(solution)/shard_map/ppermute | solution.py:18
  20.1 0.0 collective-permute-done.5
  20.2 0.0 copy-start.2
  20.2 0.0 copy-start.3
  20.2 0.9 %collective-permute-done.7.refs_1_ = bf16[32,4096]{1,0:T(8,128)(2,1)S(1)} collective-permute-done((bf16[32,4096]{1,0:T(8,128)(2,1)S(1)}, bf16[32,4096]{1,0:T(8,128)(2,1)S(1)}, u32[]{:S(2)}, u32[]{:S(2)}) %collective-permute-start.7) | collective-permute-done | bytes 262176 | tf_op jit(solution)/shard_map/ppermute | solution.py:18
  21.0 0.7 %shard_map.88.inner_ref = f32[2048,512]{1,0:T(8,128)S(1)} custom-call(f32[2,64,128]{2,1,0:T(8,128)S(1)} %pad_maximum_fusion.1.act_ref, bf16[32,4096]{1,0:T(8,128)(2,1)S(1)} %constant_dynamic-update-slice_fusion.refs_0_, bf16[32,4096]{1,0:T(8,128)(2,1)S(1)} %collective-permute-done.7.refs_1_), custom_call_target="tpu_custom_call" | custom-call | flops 536870912 | bytes 4194304 | tf_op jit(solution)/shard_map/pallas_call | solution.py:147
  21.7 2.2 %collective-permute-done.4.other_ref = f32[128,128]{1,0:T(8,128)S(1)} collective-permute-done((f32[128,128]{1,0:T(8,128)S(1)}, f32[128,128]{1,0:T(8,128)S(1)}, u32[]{:S(2)}, u32[]{:S(2)}) %collective-permute-start.4) | collective-permute-done | bytes 65568 | tf_op jit(solution)/shard_map/ppermute | solution.py:18
  23.9 0.0 copy-done.2
  23.9 0.0 copy-done.3
  23.9 1.1 %shard_map.89 = (f32[64,128]{1,0:T(8,128)S(1)}, f32[64,128]{1,0:T(8,128)S(1)}, f32[8,8,16]{2,1,0:T(8,128)S(1)}) custom-call(s32[1]{0:T(128)} %bitcast.me_ref, s32[16]{0:T(128)S(1)} %copy-done.2, s32[16]{0:T(128)S(1)} %copy-done.3, f32[128,128]{1,0:T(8,128)S(1)} %fusion.own_ref, f32[128,128]{1,0:T(8,128)S(1)} %collective-permute-done.4.other_ref, ...), custom_call_target="tpu_custom_call" | custom-call | flops 2097152 | bytes 4194304 | tf_op jit(solution)/shard_map/pallas_call | solution.py:247
  25.0 0.2 collective-permute-start.8
  25.2 1.0 %collective-permute-done.8 = f32[4,8,16]{2,1,0:T(8,128)S(1)} collective-permute-done((f32[4,8,16]{2,1,0:T(8,128)S(1)}, f32[4,8,16]{2,1,0:T(8,128)S(1)}, u32[]{:S(2)}, u32[]{:S(2)}) %collective-permute-start.8) | collective-permute-done | bytes 2080 | tf_op jit(solution)/shard_map/ppermute | solution.py:18
  26.3 0.6 %collective-permute-start.9 = (f32[2,8,16]{2,1,0:T(8,128)S(1)}, f32[2,8,16]{2,1,0:T(8,128)S(1)}, u32[]{:S(2)}, u32[]{:S(2)}) collective-permute-start(f32[2,8,16]{2,1,0:T(8,128)S(1)} %slice.46), channel_id=1, source_target_pairs={{0,3},{1,2},{2,1},{3,0},{4,7},{5,6},{6,5},{7,4},{8,11},{9,10},{10,... | collective-permute-start | bytes 3080 | tf_op jit(solution)/shard_map/ppermute | solution.py:18
  26.8 1.1 %collective-permute-start.11 = (f32[64,128]{1,0:T(8,128)S(1)}, f32[64,128]{1,0:T(8,128)S(1)}, u32[]{:S(2)}, u32[]{:S(2)}) collective-permute-start(f32[64,128]{1,0:T(8,128)S(1)} %get-tuple-element.19), channel_id=1, source_target_pairs={{0,5},{1,4},{2,7},{3,6},{4,1},{5,0},{6,3},{7,2},{8,13},{9,12},{10,... | collective-permute-start | bytes 98312 | tf_op jit(solution)/shard_map/ppermute | solution.py:18
  27.9 1.4 %collective-permute-done.9 = f32[2,8,16]{2,1,0:T(8,128)S(1)} collective-permute-done((f32[2,8,16]{2,1,0:T(8,128)S(1)}, f32[2,8,16]{2,1,0:T(8,128)S(1)}, u32[]{:S(2)}, u32[]{:S(2)}) %collective-permute-start.9) | collective-permute-done | bytes 1056 | tf_op jit(solution)/shard_map/ppermute | solution.py:18
  29.4 1.3 %collective-permute-start.10 = (f32[1,8,16]{2,1,0:T(8,128)S(1)}, f32[1,8,16]{2,1,0:T(8,128)S(1)}, u32[]{:S(2)}, u32[]{:S(2)}) collective-permute-start(f32[1,8,16]{2,1,0:T(8,128)S(1)} %slice.47), channel_id=1, source_target_pairs={{0,9},{1,8},{2,11},{3,10},{4,13},{5,12},{6,15},{7,14},{8,1},{9,0},... | collective-permute-start | bytes 1544 | tf_op jit(solution)/shard_map/ppermute | solution.py:18
  30.6 0.0 collective-permute-done.11.other_ref
  30.6 0.7 %shard_map.90 = f32[128,128]{1,0:T(8,128)} custom-call(s32[1]{0:T(128)} %bitcast.me_ref, f32[64,128]{1,0:T(8,128)S(1)} %get-tuple-element.18.own_ref, f32[64,128]{1,0:T(8,128)S(1)} %collective-permute-done.11.other_ref), custom_call_target="tpu_custom_call" | custom-call | tf_op jit(solution)/shard_map/pallas_call | solution.py:276
  31.4 1.9 %collective-permute-done.10 = f32[1,8,16]{2,1,0:T(8,128)S(1)} collective-permute-done((f32[1,8,16]{2,1,0:T(8,128)S(1)}, f32[1,8,16]{2,1,0:T(8,128)S(1)}, u32[]{:S(2)}, u32[]{:S(2)}) %collective-permute-start.10) | collective-permute-done | bytes 544 | tf_op jit(solution)/shard_map/ppermute | solution.py:18
  33.3 0.6 %fusion.3 = f32[16,8]{0,1:T(8,128)} fusion(f32[1,8,16]{2,1,0:T(8,128)S(1)} %collective-permute-done.10, f32[2,8,16]{2,1,0:T(8,128)S(1)} %slice_add_fusion.2, f32[16]{0:T(128)S(1)} %convert_rsqrt_fusion), kind=kLoop, calls=%fused_computation.15 | loop fusion | flops 256 | bytes 1600 | tf_op jit(solution)/shard_map/transpose | solution.py:346
  (16 shorter events, 0.1 us)
Async XLA Ops:
  0.6 11.1 %copy-start = (bf16[128,8192]{1,0:T(8,128)(2,1)S(1)}, bf16[128,8192]{1,0:T(8,128)(2,1)}, u32[]{:S(2)}) copy-start(bf16[128,8192]{1,0:T(8,128)(2,1)} %param.7) | copy-start | bytes 6291460
  0.6 9.4 %collective-permute-start = (bf16[8,4096]{1,0:T(8,128)(2,1)}, bf16[8,4096]{1,0:T(8,128)(2,1)S(1)}, u32[]{:S(2)}, u32[]{:S(2)}) collective-permute-start(bf16[8,4096]{1,0:T(8,128)(2,1)} %param.11), channel_id=1, source_target_pairs={{0,9},{1,8},{2,11},{3,10},{4,13},{5,12},{6,15},{7,14},{8,1},{9,0},... | collective-permute-start | bytes 196616 | tf_op jit(solution)/shard_map/ppermute | solution.py:18
  4.2 4.7 %copy-start.5 = (bf16[8,4096]{1,0:T(8,128)(2,1)S(1)}, bf16[8,4096]{1,0:T(8,128)(2,1)}, u32[]{:S(2)}) copy-start(bf16[8,4096]{1,0:T(8,128)(2,1)} %param.11) | copy-start | bytes 196612
  4.2 4.7 %copy-start.1 = (bf16[2048,1792]{1,0:T(8,128)(2,1)S(1)}, bf16[2048,1792]{1,0:T(8,128)(2,1)}, u32[]{:S(2)}) copy-start(bf16[2048,1792]{1,0:T(8,128)(2,1)} %grads_ref.3) | copy-start | bytes 22020100
  8.2 1.9 %collective-permute-start.1 = (f32[4,128,128]{2,1,0:T(8,128)S(1)}, f32[4,128,128]{2,1,0:T(8,128)S(1)}, u32[]{:S(2)}, u32[]{:S(2)}) collective-permute-start(f32[4,128,128]{2,1,0:T(8,128)S(1)} %get-tuple-element.13), channel_id=1, source_target_pairs={{0,1},{1,0},{2,3},{3,2},{4,5},{5,4},{6,7},{7,6},{8,9},{9,8},{10,11... | collective-permute-start | bytes 786440 | tf_op jit(solution)/shard_map/ppermute | solution.py:18
  8.9 2.8 %copy-start.4 = (bf16[8192,64]{0,1:T(8,128)(2,1)S(1)}, bf16[8192,64]{0,1:T(8,128)(2,1)}, u32[]{:S(2)}) copy-start(bf16[8192,64]{0,1:T(8,128)(2,1)} %param.9) | copy-start | bytes 3145732
  10.1 4.4 %collective-permute-start.2 = (bf16[2,128,128]{2,1,0:T(8,128)(2,1)S(1)}, bf16[2,128,128]{2,1,0:T(8,128)(2,1)S(1)}, u32[]{:S(2)}, u32[]{:S(2)}) collective-permute-start(bf16[2,128,128]{2,1,0:T(8,128)(2,1)S(1)} %slice.64), channel_id=1, source_target_pairs={{0,3},{1,2},{2,1},{3,0},{4,7},{5,6},{6,5},{7,4},{8,11},{9,10},{10,... | collective-permute-start | bytes 196616 | tf_op jit(solution)/shard_map/ppermute | solution.py:18
  12.6 7.6 %collective-permute-start.5 = (f32[64,128]{1,0:T(8,128)S(1)}, f32[64,128]{1,0:T(8,128)S(1)}, u32[]{:S(2)}, u32[]{:S(2)}) collective-permute-start(f32[64,128]{1,0:T(8,128)S(1)} %fusion.4), channel_id=1, source_target_pairs={{0,5},{1,4},{2,7},{3,6},{4,1},{5,0},{6,3},{7,2},{8,13},{9,12},{10,... | collective-permute-start | bytes 98312 | tf_op jit(solution)/shard_map/ppermute | solution.py:18
  14.0 5.4 %collective-permute-start.6 = (bf16[16,4096]{1,0:T(8,128)(2,1)S(1)}, bf16[16,4096]{1,0:T(8,128)(2,1)S(1)}, u32[]{:S(2)}, u32[]{:S(2)}) collective-permute-start(bf16[16,4096]{1,0:T(8,128)(2,1)S(1)} %pad_maximum_fusion), channel_id=1, source_target_pairs={{0,3},{1,2},{2,1},{3,0},{4,7},{5,6},{6,5},{7,4},{8,11},{9,10},{10,... | collective-permute-start | bytes 393224 | tf_op jit(solution)/shard_map/ppermute | solution.py:18
  14.6 5.2 %collective-permute-start.3 = (bf16[1,128,128]{2,1,0:T(8,128)(2,1)S(1)}, bf16[1,128,128]{2,1,0:T(8,128)(2,1)S(1)}, u32[]{:S(2)}, u32[]{:S(2)}) collective-permute-start(bf16[1,128,128]{2,1,0:T(8,128)(2,1)S(1)} %slice.65), channel_id=1, source_target_pairs={{0,9},{1,8},{2,11},{3,10},{4,13},{5,12},{6,15},{7,14},{8,1},{9,0},... | collective-permute-start | bytes 98312 | tf_op jit(solution)/shard_map/ppermute | solution.py:18
  19.4 1.6 %collective-permute-start.7 = (bf16[32,4096]{1,0:T(8,128)(2,1)S(1)}, bf16[32,4096]{1,0:T(8,128)(2,1)S(1)}, u32[]{:S(2)}, u32[]{:S(2)}) collective-permute-start(bf16[32,4096]{1,0:T(8,128)(2,1)S(1)} %constant_dynamic-update-slice_fusion.refs_0_), channel_id=1, source_target_pairs={{0,1},{1,0},{2,3},{3,2},{4,5},{5,4},{6,7},{7,6},{8,9},{9,8},{10,11... | collective-permute-start | bytes 786440 | tf_op jit(solution)/shard_map/ppermute | solution.py:18
  19.8 4.1 %collective-permute-start.4 = (f32[128,128]{1,0:T(8,128)S(1)}, f32[128,128]{1,0:T(8,128)S(1)}, u32[]{:S(2)}, u32[]{:S(2)}) collective-permute-start(f32[128,128]{1,0:T(8,128)S(1)} %fusion.own_ref), channel_id=1, source_target_pairs={{0,5},{1,4},{2,7},{3,6},{4,1},{5,0},{6,3},{7,2},{8,13},{9,12},{10,... | collective-permute-start | bytes 196616 | tf_op jit(solution)/shard_map/ppermute | solution.py:18
  20.2 3.8 %copy-start.2 = (s32[16]{0:T(128)S(1)}, s32[16]{0:T(128)}, u32[]{:S(2)}) copy-start(s32[16]{0:T(128)} %length_ref.1) | copy-start | bytes 196
  20.2 3.8 %copy-start.3 = (s32[16]{0:T(128)S(1)}, s32[16]{0:T(128)}, u32[]{:S(2)}) copy-start(s32[16]{0:T(128)} %valid_ref.1) | copy-start | bytes 196
  25.0 1.2 %collective-permute-start.8 = (f32[4,8,16]{2,1,0:T(8,128)S(1)}, f32[4,8,16]{2,1,0:T(8,128)S(1)}, u32[]{:S(2)}, u32[]{:S(2)}) collective-permute-start(f32[4,8,16]{2,1,0:T(8,128)S(1)} %slice.37), channel_id=1, source_target_pairs={{0,1},{1,0},{2,3},{3,2},{4,5},{5,4},{6,7},{7,6},{8,9},{9,8},{10,11... | collective-permute-start | bytes 6152 | tf_op jit(solution)/shard_map/ppermute | solution.py:18
  26.3 3.1 %collective-permute-start.9 = (f32[2,8,16]{2,1,0:T(8,128)S(1)}, f32[2,8,16]{2,1,0:T(8,128)S(1)}, u32[]{:S(2)}, u32[]{:S(2)}) collective-permute-start(f32[2,8,16]{2,1,0:T(8,128)S(1)} %slice.46), channel_id=1, source_target_pairs={{0,3},{1,2},{2,1},{3,0},{4,7},{5,6},{6,5},{7,4},{8,11},{9,10},{10,... | collective-permute-start | bytes 3080 | tf_op jit(solution)/shard_map/ppermute | solution.py:18
  26.8 3.8 %collective-permute-start.11 = (f32[64,128]{1,0:T(8,128)S(1)}, f32[64,128]{1,0:T(8,128)S(1)}, u32[]{:S(2)}, u32[]{:S(2)}) collective-permute-start(f32[64,128]{1,0:T(8,128)S(1)} %get-tuple-element.19), channel_id=1, source_target_pairs={{0,5},{1,4},{2,7},{3,6},{4,1},{5,0},{6,3},{7,2},{8,13},{9,12},{10,... | collective-permute-start | bytes 98312 | tf_op jit(solution)/shard_map/ppermute | solution.py:18
  29.4 3.9 %collective-permute-start.10 = (f32[1,8,16]{2,1,0:T(8,128)S(1)}, f32[1,8,16]{2,1,0:T(8,128)S(1)}, u32[]{:S(2)}, u32[]{:S(2)}) collective-permute-start(f32[1,8,16]{2,1,0:T(8,128)S(1)} %slice.47), channel_id=1, source_target_pairs={{0,9},{1,8},{2,11},{3,10},{4,13},{5,12},{6,15},{7,14},{8,1},{9,0},... | collective-permute-start | bytes 1544 | tf_op jit(solution)/shard_map/ppermute | solution.py:18

commit v13 on v12

--- a/solution.py
+++ b/solution.py
@@ -168,7 +168,7 @@
     tokens = (own_tok, other_tok)
 
     def begin():
-        other = other_ref[...].T
+        other = other_ref[...].astype(jnp.float32).T
         grad_ref[...] = own_ref[...].T + jnp.concatenate([other[width:], other[:width]], axis=0)
 
     if steps == 1:
@@ -295,8 +295,8 @@
     width = proj_in.shape[1]
     own_q = queries.shape[0]
     me = lax.axis_index("seq").astype(jnp.int32)[None]
-    split = size // 4 + 1
-    middle = [(1 << k) + 1 for k in range(1, size.bit_length() - 1) if 1 << k != size // 4]
+    split = size // 2 + 1
+    middle = [(1 << k) + 1 for k in range(1, size.bit_length() - 2)]
 
     proj = proj_out.T
     spots = [offset_of(m, middle) ^ (split * r) for m in range(size // 4) for r in range(2)]
@@ -309,17 +309,15 @@
     got, sums = lax.optimization_barrier((got, sums))
     for k, bit in enumerate(middle):
         half = sums.shape[0] // 2
-        sent = swap(sums[half:].astype(jnp.bfloat16), bit, size)
+        kind = jnp.bfloat16 if k == 0 else jnp.float32
+        sent = swap(sums[half:].astype(kind), bit, size)
         sums = sums[:half] + sent.astype(jnp.float32)
-        if k == 0:
-            after = sums
     own = sums[0]
-    across = swap(own, split, size)
+    across = swap(own.astype(jnp.bfloat16), split, size)
     act = lax.dot_general(
         late, activations, (((0,), (1,)), ((), ())), preferred_element_type=jnp.float32
     )
-    sent_act = act
-    act = jnp.stack([act, swap(sent_act, split, size)])
+    act = jnp.stack([act, swap(act, split, size)])
 
     panel = jnp.concatenate([panel, got], axis=0)
     place = [0, middle[-1]]

time: 34 us -> 34.2 us (level)
  waiting for transfers between devices: 11 us -> 14.8 us
  starting transfers between devices: 12.9 us -> 9.27 us
    ppermute x12, waiting for transfers between devices: 11 us -> 14.8 us  [swap(): return lax.ppermute(value, 'seq', [(i, i ^ offset) for i in range(size)])]
    ppermute x12, starting transfers between devices: 12.9 us -> 9.27 us  [swap(): return lax.ppermute(value, 'seq', [(i, i ^ offset) for i in range(size)])]
  transfers between devices with their start and end apart: 12 -> 12, of which waited for: 6 -> 7; matrix products, arithmetic and copies ran while one was open for 3% -> 3% of each run, Pallas kernels for 19% -> 19%
where the time goes in v13:
time: 34.2 us; the launch traced here: 34.1 us
  waiting for transfers between devices  14.8 us (43%)
  starting transfers between devices  9.27 us (27%)
  Pallas kernels  7.59 us (22%)
  matrix products  0.88 us (3%)
  between operations  0.8 us (2%)
  other arithmetic  0.68 us (2%)
    ppermute x12, waiting for transfers between devices, swap(): return lax.ppermute(value, 'seq', [(i, i ^ offset) for i in range(size)])  14.8 us
    ppermute x12, starting transfers between devices, swap(): return lax.ppermute(value, 'seq', [(i, i ^ offset) for i in range(size)])  9.27 us
    pallas_call x1, Pallas kernels, grad_blocks(): pl.pallas_call(functools.partial(grad_kernel, offsets), in_specs=[SMEM, H...  3.96 us
    pallas_call x1, Pallas kernels, grad_blocks(): pl.pallas_call(functools.partial(held_kernel, offsets), in_specs=[SMEM, V...  1.11 us
    pallas_call x1, Pallas kernels, score(): pl.pallas_call(functools.partial(score_kernel, steps, split), out_shape=(...  1.08 us
    dot_general x1, matrix products, body(): lax.dot_general(late, activations, (((0,), (1,)), ((), ())), preferred_el...  0.88 us
    pallas_call x1, Pallas kernels, place_tokens(): pl.pallas_call(functools.partial(place_kernel, place, split), in_specs=[S...  0.74 us
    pallas_call x1, Pallas kernels, inner(): pl.pallas_call(functools.partial(inner_kernel, len(panels)), out_shape=ja...  0.7 us
  transfers between devices with their start and end apart: 12, of which 7 were waited for; matrix products, arithmetic and copies ran while one was open for 3% of the time, Pallas kernels for 19%

profile of v13, /device:TPU:0, one launch (start us, length us, event | category | flops | bytes accessed | tf_op | source)
XLA Modules:
  0.0 34.1 jit_solution(1732282275015067486)
XLA Ops:
  0.6 0.0 copy-start
  0.6 2.5 %collective-permute-start = (bf16[8,4096]{1,0:T(8,128)(2,1)}, bf16[8,4096]{1,0:T(8,128)(2,1)S(1)}, u32[]{:S(2)}, u32[]{:S(2)}) collective-permute-start(bf16[8,4096]{1,0:T(8,128)(2,1)} %param.11), channel_id=1, source_target_pairs={{0,5},{1,4},{2,7},{3,6},{4,1},{5,0},{6,3},{7,2},{8,13},{9,12},{10,... | collective-permute-start | bytes 196616 | tf_op jit(solution)/shard_map/ppermute | solution.py:18
  3.2 0.0 copy-start.5
  3.2 0.0 copy-start.1
  3.2 4.0 %shard_map.86 = (f32[4,128,128]{2,1,0:T(8,128)S(1)}, bf16[2,1792,128]{2,1,0:T(8,128)(2,1)S(1)}) custom-call(s32[1]{0:T(128)} %bitcast.me_ref, bf16[64,1792]{1,0:T(8,128)(2,1)} %bitcast.17, bf16[2048,1792]{1,0:T(8,128)(2,1)} %grads_ref.3), custom_call_target="tpu_custom_call" | custom-call | flops 234881024 | bytes 3670016 | tf_op jit(solution)/shard_map/pallas_call | solution.py:93
  7.1 0.7 %collective-permute-start.1 = (f32[4,128,128]{2,1,0:T(8,128)S(1)}, f32[4,128,128]{2,1,0:T(8,128)S(1)}, u32[]{:S(2)}, u32[]{:S(2)}) collective-permute-start(f32[4,128,128]{2,1,0:T(8,128)S(1)} %get-tuple-element.13), channel_id=1, source_target_pairs={{0,1},{1,0},{2,3},{3,2},{4,5},{5,4},{6,7},{7,6},{8,9},{9,8},{10,11... | collective-permute-start | bytes 786440 | tf_op jit(solution)/shard_map/ppermute | solution.py:18
  7.9 0.0 copy-done.5
  7.9 0.0 copy-done.1
  7.9 0.0 copy-start.4
  7.9 1.1 %shard_map.87 = f32[4,128,128]{2,1,0:T(8,128)S(1)} custom-call(s32[1]{0:T(128)} %bitcast.me_ref, bf16[2,1792,128]{2,1,0:T(8,128)(2,1)S(1)} %get-tuple-element.12.table, bf16[2048,1792]{1,0:T(8,128)(2,1)S(1)} %copy-done.1), custom_call_target="tpu_custom_call" | custom-call | flops 234881024 | bytes 3670016 | tf_op jit(solution)/shard_map/pallas_call | solution.py:86
  9.0 0.0 collective-permute-done.1
  9.1 0.0 collective-permute-done
  9.1 1.6 %collective-permute-start.2 = (bf16[2,128,128]{2,1,0:T(8,128)(2,1)S(1)}, bf16[2,128,128]{2,1,0:T(8,128)(2,1)S(1)}, u32[]{:S(2)}, u32[]{:S(2)}) collective-permute-start(bf16[2,128,128]{2,1,0:T(8,128)(2,1)S(1)} %slice.62), channel_id=1, source_target_pairs={{0,3},{1,2},{2,1},{3,0},{4,7},{5,6},{6,5},{7,4},{8,11},{9,10},{10,... | collective-permute-start | bytes 196616 | tf_op jit(solution)/shard_map/ppermute | solution.py:18
  10.7 0.0 copy-done
  10.7 0.0 copy-done.4
  10.7 0.9 %fusion.6 = f32[64,128]{1,0:T(8,128)S(1)} fusion(bf16[8192,64]{0,1:T(8,128)(2,1)S(1)} %copy-done.4, bf16[128,8192]{1,0:T(8,128)(2,1)S(1)} %copy-done), kind=kOutput, calls=%fused_computation.17 | convolution fusion | flops 134217728 | bytes 3178496 | tf_op jit(solution)/shard_map/dot_general | solution.py:317
  11.6 2.4 %collective-permute-start.5 = (f32[64,128]{1,0:T(8,128)S(1)}, f32[64,128]{1,0:T(8,128)S(1)}, u32[]{:S(2)}, u32[]{:S(2)}) collective-permute-start(f32[64,128]{1,0:T(8,128)S(1)} %fusion.6), channel_id=1, source_target_pairs={{0,9},{1,8},{2,11},{3,10},{4,13},{5,12},{6,15},{7,14},{8,1},{9,0},... | collective-permute-start | bytes 98312 | tf_op jit(solution)/shard_map/ppermute | solution.py:18
  14.0 0.5 %collective-permute-start.6 = (bf16[16,4096]{1,0:T(8,128)(2,1)S(1)}, bf16[16,4096]{1,0:T(8,128)(2,1)S(1)}, u32[]{:S(2)}, u32[]{:S(2)}) collective-permute-start(bf16[16,4096]{1,0:T(8,128)(2,1)S(1)} %pad_maximum_fusion), channel_id=1, source_target_pairs={{0,3},{1,2},{2,1},{3,0},{4,7},{5,6},{6,5},{7,4},{8,11},{9,10},{10,... | collective-permute-start | bytes 393224 | tf_op jit(solution)/shard_map/ppermute | solution.py:18
  14.5 0.0 collective-permute-done.2
  14.6 0.3 collective-permute-start.3
  14.9 4.6 %collective-permute-done.6 = bf16[16,4096]{1,0:T(8,128)(2,1)S(1)} collective-permute-done((bf16[16,4096]{1,0:T(8,128)(2,1)S(1)}, bf16[16,4096]{1,0:T(8,128)(2,1)S(1)}, u32[]{:S(2)}, u32[]{:S(2)}) %collective-permute-start.6) | collective-permute-done | bytes 131104 | tf_op jit(solution)/shard_map/ppermute | solution.py:18
  19.4 0.3 %collective-permute-start.7 = (bf16[32,4096]{1,0:T(8,128)(2,1)S(1)}, bf16[32,4096]{1,0:T(8,128)(2,1)S(1)}, u32[]{:S(2)}, u32[]{:S(2)}) collective-permute-start(bf16[32,4096]{1,0:T(8,128)(2,1)S(1)} %constant_dynamic-update-slice_fusion.refs_0_), channel_id=1, source_target_pairs={{0,1},{1,0},{2,3},{3,2},{4,5},{5,4},{6,7},{7,6},{8,9},{9,8},{10,11... | collective-permute-start | bytes 786440 | tf_op jit(solution)/shard_map/ppermute | solution.py:18
  19.8 0.0 collective-permute-done.5
  19.8 0.0 collective-permute-done.3
  19.8 0.0 copy-start.2
  19.8 0.0 copy-start.3
  19.8 0.2 collective-permute-start.4
  20.1 1.0 %collective-permute-done.7.refs_1_ = bf16[32,4096]{1,0:T(8,128)(2,1)S(1)} collective-permute-done((bf16[32,4096]{1,0:T(8,128)(2,1)S(1)}, bf16[32,4096]{1,0:T(8,128)(2,1)S(1)}, u32[]{:S(2)}, u32[]{:S(2)}) %collective-permute-start.7) | collective-permute-done | bytes 262176 | tf_op jit(solution)/shard_map/ppermute | solution.py:18
  21.0 0.7 %shard_map.88.inner_ref = f32[2048,512]{1,0:T(8,128)S(1)} custom-call(f32[2,64,128]{2,1,0:T(8,128)S(1)} %pad_maximum_fusion.1.act_ref, bf16[32,4096]{1,0:T(8,128)(2,1)S(1)} %constant_dynamic-update-slice_fusion.refs_0_, bf16[32,4096]{1,0:T(8,128)(2,1)S(1)} %collective-permute-done.7.refs_1_), custom_call_target="tpu_custom_call" | custom-call | flops 536870912 | bytes 4194304 | tf_op jit(solution)/shard_map/pallas_call | solution.py:147
  21.7 3.3 %collective-permute-done.4.other_ref = bf16[128,128]{1,0:T(8,128)(2,1)S(1)} collective-permute-done((bf16[128,128]{1,0:T(8,128)(2,1)S(1)}, bf16[128,128]{1,0:T(8,128)(2,1)S(1)}, u32[]{:S(2)}, u32[]{:S(2)}) %collective-permute-start.4) | collective-permute-done | bytes 32800 | tf_op jit(solution)/shard_map/ppermute | solution.py:18
  25.0 0.0 copy-done.2
  25.0 0.0 copy-done.3
  25.0 1.1 %shard_map.89 = (f32[64,128]{1,0:T(8,128)S(1)}, f32[64,128]{1,0:T(8,128)S(1)}, f32[8,8,16]{2,1,0:T(8,128)S(1)}) custom-call(s32[1]{0:T(128)} %bitcast.me_ref, s32[16]{0:T(128)S(1)} %copy-done.2, s32[16]{0:T(128)S(1)} %copy-done.3, f32[128,128]{1,0:T(8,128)S(1)} %get-tuple-element.23.own_ref, bf16[128,128]{1,0:T(8,128)(2,1)S(1)} %collective-permute-done.4.other_ref, ...), custom_call_target="tpu_custom_call" | custom-call | flops 2097152 | bytes 4194304 | tf_op jit(solution)/shard_map/pallas_call | solution.py:247
  26.1 0.2 collective-permute-start.8
  26.3 1.1 %collective-permute-done.8 = f32[4,8,16]{2,1,0:T(8,128)S(1)} collective-permute-done((f32[4,8,16]{2,1,0:T(8,128)S(1)}, f32[4,8,16]{2,1,0:T(8,128)S(1)}, u32[]{:S(2)}, u32[]{:S(2)}) %collective-permute-start.8) | collective-permute-done | bytes 2080 | tf_op jit(solution)/shard_map/ppermute | solution.py:18
  27.4 0.4 %collective-permute-start.9 = (f32[2,8,16]{2,1,0:T(8,128)S(1)}, f32[2,8,16]{2,1,0:T(8,128)S(1)}, u32[]{:S(2)}, u32[]{:S(2)}) collective-permute-start(f32[2,8,16]{2,1,0:T(8,128)S(1)} %slice.45), channel_id=1, source_target_pairs={{0,3},{1,2},{2,1},{3,0},{4,7},{5,6},{6,5},{7,4},{8,11},{9,10},{10,... | collective-permute-start | bytes 3080 | tf_op jit(solution)/shard_map/ppermute | solution.py:18
  27.8 0.0 collective-permute-start.11
  27.8 2.6 %collective-permute-done.9 = f32[2,8,16]{2,1,0:T(8,128)S(1)} collective-permute-done((f32[2,8,16]{2,1,0:T(8,128)S(1)}, f32[2,8,16]{2,1,0:T(8,128)S(1)}, u32[]{:S(2)}, u32[]{:S(2)}) %collective-permute-start.9) | collective-permute-done | bytes 1056 | tf_op jit(solution)/shard_map/ppermute | solution.py:18
  30.5 0.0 collective-permute-start.10
  30.5 1.6 %collective-permute-done.11.other_ref = f32[64,128]{1,0:T(8,128)S(1)} collective-permute-done((f32[64,128]{1,0:T(8,128)S(1)}, f32[64,128]{1,0:T(8,128)S(1)}, u32[]{:S(2)}, u32[]{:S(2)}) %collective-permute-start.11) | collective-permute-done | bytes 32800 | tf_op jit(solution)/shard_map/ppermute | solution.py:18
  32.1 0.7 %shard_map.90 = f32[128,128]{1,0:T(8,128)} custom-call(s32[1]{0:T(128)} %bitcast.me_ref, f32[64,128]{1,0:T(8,128)S(1)} %get-tuple-element.18.own_ref, f32[64,128]{1,0:T(8,128)S(1)} %collective-permute-done.11.other_ref), custom_call_target="tpu_custom_call" | custom-call | tf_op jit(solution)/shard_map/pallas_call | solution.py:276
  32.8 0.7 %collective-permute-done.10 = f32[1,8,16]{2,1,0:T(8,128)S(1)} collective-permute-done((f32[1,8,16]{2,1,0:T(8,128)S(1)}, f32[1,8,16]{2,1,0:T(8,128)S(1)}, u32[]{:S(2)}, u32[]{:S(2)}) %collective-permute-start.10) | collective-permute-done | bytes 544 | tf_op jit(solution)/shard_map/ppermute | solution.py:18
  33.5 0.6 %fusion.3 = f32[16,8]{0,1:T(8,128)} fusion(f32[1,8,16]{2,1,0:T(8,128)S(1)} %collective-permute-done.10, f32[2,8,16]{2,1,0:T(8,128)S(1)} %slice_add_fusion.2, f32[16]{0:T(128)S(1)} %convert_rsqrt_fusion), kind=kLoop, calls=%fused_computation.14 | loop fusion | flops 256 | bytes 1600 | tf_op jit(solution)/shard_map/transpose | solution.py:344
  (16 shorter events, 0.1 us)
Async XLA Ops:
  0.6 10.0 %copy-start = (bf16[128,8192]{1,0:T(8,128)(2,1)S(1)}, bf16[128,8192]{1,0:T(8,128)(2,1)}, u32[]{:S(2)}) copy-start(bf16[128,8192]{1,0:T(8,128)(2,1)} %param.7) | copy-start | bytes 6291460
  0.6 8.4 %collective-permute-start = (bf16[8,4096]{1,0:T(8,128)(2,1)}, bf16[8,4096]{1,0:T(8,128)(2,1)S(1)}, u32[]{:S(2)}, u32[]{:S(2)}) collective-permute-start(bf16[8,4096]{1,0:T(8,128)(2,1)} %param.11), channel_id=1, source_target_pairs={{0,5},{1,4},{2,7},{3,6},{4,1},{5,0},{6,3},{7,2},{8,13},{9,12},{10,... | collective-permute-start | bytes 196616 | tf_op jit(solution)/shard_map/ppermute | solution.py:18
  3.2 4.7 %copy-start.5 = (bf16[8,4096]{1,0:T(8,128)(2,1)S(1)}, bf16[8,4096]{1,0:T(8,128)(2,1)}, u32[]{:S(2)}) copy-start(bf16[8,4096]{1,0:T(8,128)(2,1)} %param.11) | copy-start | bytes 196612
  3.2 4.7 %copy-start.1 = (bf16[2048,1792]{1,0:T(8,128)(2,1)S(1)}, bf16[2048,1792]{1,0:T(8,128)(2,1)}, u32[]{:S(2)}) copy-start(bf16[2048,1792]{1,0:T(8,128)(2,1)} %grads_ref.3) | copy-start | bytes 22020100
  7.1 1.9 %collective-permute-start.1 = (f32[4,128,128]{2,1,0:T(8,128)S(1)}, f32[4,128,128]{2,1,0:T(8,128)S(1)}, u32[]{:S(2)}, u32[]{:S(2)}) collective-permute-start(f32[4,128,128]{2,1,0:T(8,128)S(1)} %get-tuple-element.13), channel_id=1, source_target_pairs={{0,1},{1,0},{2,3},{3,2},{4,5},{5,4},{6,7},{7,6},{8,9},{9,8},{10,11... | collective-permute-start | bytes 786440 | tf_op jit(solution)/shard_map/ppermute | solution.py:18
  7.9 2.8 %copy-start.4 = (bf16[8192,64]{0,1:T(8,128)(2,1)S(1)}, bf16[8192,64]{0,1:T(8,128)(2,1)}, u32[]{:S(2)}) copy-start(bf16[8192,64]{0,1:T(8,128)(2,1)} %param.9) | copy-start | bytes 3145732
  9.1 5.4 %collective-permute-start.2 = (bf16[2,128,128]{2,1,0:T(8,128)(2,1)S(1)}, bf16[2,128,128]{2,1,0:T(8,128)(2,1)S(1)}, u32[]{:S(2)}, u32[]{:S(2)}) collective-permute-start(bf16[2,128,128]{2,1,0:T(8,128)(2,1)S(1)} %slice.62), channel_id=1, source_target_pairs={{0,3},{1,2},{2,1},{3,0},{4,7},{5,6},{6,5},{7,4},{8,11},{9,10},{10,... | collective-permute-start | bytes 196616 | tf_op jit(solution)/shard_map/ppermute | solution.py:18
  11.6 8.2 %collective-permute-start.5 = (f32[64,128]{1,0:T(8,128)S(1)}, f32[64,128]{1,0:T(8,128)S(1)}, u32[]{:S(2)}, u32[]{:S(2)}) collective-permute-start(f32[64,128]{1,0:T(8,128)S(1)} %fusion.6), channel_id=1, source_target_pairs={{0,9},{1,8},{2,11},{3,10},{4,13},{5,12},{6,15},{7,14},{8,1},{9,0},... | collective-permute-start | bytes 98312 | tf_op jit(solution)/shard_map/ppermute | solution.py:18
  14.0 5.4 %collective-permute-start.6 = (bf16[16,4096]{1,0:T(8,128)(2,1)S(1)}, bf16[16,4096]{1,0:T(8,128)(2,1)S(1)}, u32[]{:S(2)}, u32[]{:S(2)}) collective-permute-start(bf16[16,4096]{1,0:T(8,128)(2,1)S(1)} %pad_maximum_fusion), channel_id=1, source_target_pairs={{0,3},{1,2},{2,1},{3,0},{4,7},{5,6},{6,5},{7,4},{8,11},{9,10},{10,... | collective-permute-start | bytes 393224 | tf_op jit(solution)/shard_map/ppermute | solution.py:18
  14.6 5.2 %collective-permute-start.3 = (f32[1,128,128]{2,1,0:T(8,128)S(1)}, f32[1,128,128]{2,1,0:T(8,128)S(1)}, u32[]{:S(2)}, u32[]{:S(2)}) collective-permute-start(f32[1,128,128]{2,1,0:T(8,128)S(1)} %slice.43), channel_id=1, source_target_pairs={{0,5},{1,4},{2,7},{3,6},{4,1},{5,0},{6,3},{7,2},{8,13},{9,12},{10,... | collective-permute-start | bytes 196616 | tf_op jit(solution)/shard_map/ppermute | solution.py:18
  19.4 1.6 %collective-permute-start.7 = (bf16[32,4096]{1,0:T(8,128)(2,1)S(1)}, bf16[32,4096]{1,0:T(8,128)(2,1)S(1)}, u32[]{:S(2)}, u32[]{:S(2)}) collective-permute-start(bf16[32,4096]{1,0:T(8,128)(2,1)S(1)} %constant_dynamic-update-slice_fusion.refs_0_), channel_id=1, source_target_pairs={{0,1},{1,0},{2,3},{3,2},{4,5},{5,4},{6,7},{7,6},{8,9},{9,8},{10,11... | collective-permute-start | bytes 786440 | tf_op jit(solution)/shard_map/ppermute | solution.py:18
  19.8 5.2 %copy-start.2 = (s32[16]{0:T(128)S(1)}, s32[16]{0:T(128)}, u32[]{:S(2)}) copy-start(s32[16]{0:T(128)} %length_ref.1) | copy-start | bytes 196
  19.8 5.2 %copy-start.3 = (s32[16]{0:T(128)S(1)}, s32[16]{0:T(128)}, u32[]{:S(2)}) copy-start(s32[16]{0:T(128)} %valid_ref.1) | copy-start | bytes 196
  19.8 5.2 %collective-permute-start.4 = (bf16[128,128]{1,0:T(8,128)(2,1)S(1)}, bf16[128,128]{1,0:T(8,128)(2,1)S(1)}, u32[]{:S(2)}, u32[]{:S(2)}) collective-permute-start(bf16[128,128]{1,0:T(8,128)(2,1)S(1)} %get-tuple-element.22), channel_id=1, source_target_pairs={{0,9},{1,8},{2,11},{3,10},{4,13},{5,12},{6,15},{7,14},{8,1},{9,0},... | collective-permute-start | bytes 98312 | tf_op jit(solution)/shard_map/ppermute | solution.py:18
  26.1 1.2 %collective-permute-start.8 = (f32[4,8,16]{2,1,0:T(8,128)S(1)}, f32[4,8,16]{2,1,0:T(8,128)S(1)}, u32[]{:S(2)}, u32[]{:S(2)}) collective-permute-start(f32[4,8,16]{2,1,0:T(8,128)S(1)} %slice.36), channel_id=1, source_target_pairs={{0,1},{1,0},{2,3},{3,2},{4,5},{5,4},{6,7},{7,6},{8,9},{9,8},{10,11... | collective-permute-start | bytes 6152 | tf_op jit(solution)/shard_map/ppermute | solution.py:18
  27.4 3.1 %collective-permute-start.9 = (f32[2,8,16]{2,1,0:T(8,128)S(1)}, f32[2,8,16]{2,1,0:T(8,128)S(1)}, u32[]{:S(2)}, u32[]{:S(2)}) collective-permute-start(f32[2,8,16]{2,1,0:T(8,128)S(1)} %slice.45), channel_id=1, source_target_pairs={{0,3},{1,2},{2,1},{3,0},{4,7},{5,6},{6,5},{7,4},{8,11},{9,10},{10,... | collective-permute-start | bytes 3080 | tf_op jit(solution)/shard_map/ppermute | solution.py:18
  27.8 4.2 %collective-permute-start.11 = (f32[64,128]{1,0:T(8,128)S(1)}, f32[64,128]{1,0:T(8,128)S(1)}, u32[]{:S(2)}, u32[]{:S(2)}) collective-permute-start(f32[64,128]{1,0:T(8,128)S(1)} %get-tuple-element.19), channel_id=1, source_target_pairs={{0,9},{1,8},{2,11},{3,10},{4,13},{5,12},{6,15},{7,14},{8,1},{9,0},... | collective-permute-start | bytes 98312 | tf_op jit(solution)/shard_map/ppermute | solution.py:18
  30.5 3.0 %collective-permute-start.10 = (f32[1,8,16]{2,1,0:T(8,128)S(1)}, f32[1,8,16]{2,1,0:T(8,128)S(1)}, u32[]{:S(2)}, u32[]{:S(2)}) collective-permute-start(f32[1,8,16]{2,1,0:T(8,128)S(1)} %slice.46), channel_id=1, source_target_pairs={{0,5},{1,4},{2,7},{3,6},{4,1},{5,0},{6,3},{7,2},{8,13},{9,12},{10,... | collective-permute-start | bytes 1544 | tf_op jit(solution)/shard_map/ppermute | solution.py:18

commit v14 on v13

--- a/solution.py
+++ b/solution.py
@@ -312,12 +312,16 @@
         kind = jnp.bfloat16 if k == 0 else jnp.float32
         sent = swap(sums[half:].astype(kind), bit, size)
         sums = sums[:half] + sent.astype(jnp.float32)
+        if k == 0:
+            after = sums
     own = sums[0]
     across = swap(own.astype(jnp.bfloat16), split, size)
     act = lax.dot_general(
         late, activations, (((0,), (1,)), ((), ())), preferred_element_type=jnp.float32
     )
-    act = jnp.stack([act, swap(act, split, size)])
+    early, _ = lax.optimization_barrier((act, after))
+    more_act, _ = lax.optimization_barrier((swap(early, split, size), own))
+    act = jnp.stack([act, more_act])
 
     panel = jnp.concatenate([panel, got], axis=0)
     place = [0, middle[-1]]

time: 34.2 us -> 32.9 us (0.962)
  waiting for transfers between devices: 14.8 us -> 7.24 us
  starting transfers between devices: 9.27 us -> 15.5 us
    ppermute x12, waiting for transfers between devices: 14.8 us -> 7.24 us  [swap(): return lax.ppermute(value, 'seq', [(i, i ^ offset) for i in range(size)])]
    ppermute x12, starting transfers between devices: 9.27 us -> 15.5 us  [swap(): return lax.ppermute(value, 'seq', [(i, i ^ offset) for i in range(size)])]
  transfers between devices with their start and end apart: 12 -> 12, of which waited for: 7 -> 6; matrix products, arithmetic and copies ran while one was open for 3% -> 3% of each run, Pallas kernels for 19% -> 20%
where the time goes in v14:
time: 32.9 us; the launch traced here: 32.8 us
  starting transfers between devices  15.5 us (47%)
  Pallas kernels  7.59 us (23%)
  waiting for transfers between devices  7.24 us (22%)
  matrix products  0.88 us (3%)
  between operations  0.79 us (2%)
  other arithmetic  0.68 us (2%)
    ppermute x12, starting transfers between devices, swap(): return lax.ppermute(value, 'seq', [(i, i ^ offset) for i in range(size)])  15.5 us
    ppermute x12, waiting for transfers between devices, swap(): return lax.ppermute(value, 'seq', [(i, i ^ offset) for i in range(size)])  7.24 us
    pallas_call x1, Pallas kernels, grad_blocks(): pl.pallas_call(functools.partial(grad_kernel, offsets), in_specs=[SMEM, H...  3.96 us
    pallas_call x1, Pallas kernels, grad_blocks(): pl.pallas_call(functools.partial(held_kernel, offsets), in_specs=[SMEM, V...  1.11 us
    pallas_call x1, Pallas kernels, score(): pl.pallas_call(functools.partial(score_kernel, steps, split), out_shape=(...  1.08 us
    dot_general x1, matrix products, body(): lax.dot_general(late, activations, (((0,), (1,)), ((), ())), preferred_el...  0.88 us
    pallas_call x1, Pallas kernels, place_tokens(): pl.pallas_call(functools.partial(place_kernel, place, split), in_specs=[S...  0.74 us
    pallas_call x1, Pallas kernels, inner(): pl.pallas_call(functools.partial(inner_kernel, len(panels)), out_shape=ja...  0.71 us
  transfers between devices with their start and end apart: 12, of which 6 were waited for; matrix products, arithmetic and copies ran while one was open for 3% of the time, Pallas kernels for 20%

profile of v14, /device:TPU:0, one launch (start us, length us, event | category | flops | bytes accessed | tf_op | source)
XLA Modules:
  0.0 32.8 jit_solution(14386379155607040289)
XLA Ops:
  0.6 0.0 copy-start
  0.6 2.5 %collective-permute-start = (bf16[8,4096]{1,0:T(8,128)(2,1)}, bf16[8,4096]{1,0:T(8,128)(2,1)S(1)}, u32[]{:S(2)}, u32[]{:S(2)}) collective-permute-start(bf16[8,4096]{1,0:T(8,128)(2,1)} %param.11), channel_id=1, source_target_pairs={{0,5},{1,4},{2,7},{3,6},{4,1},{5,0},{6,3},{7,2},{8,13},{9,12},{10,... | collective-permute-start | bytes 196616 | tf_op jit(solution)/shard_map/ppermute | solution.py:18
  3.2 0.0 copy-start.5
  3.2 0.0 copy-start.1
  3.2 4.0 %shard_map.86 = (f32[4,128,128]{2,1,0:T(8,128)S(1)}, bf16[2,1792,128]{2,1,0:T(8,128)(2,1)S(1)}) custom-call(s32[1]{0:T(128)} %bitcast.me_ref, bf16[64,1792]{1,0:T(8,128)(2,1)} %bitcast.17, bf16[2048,1792]{1,0:T(8,128)(2,1)} %grads_ref.3), custom_call_target="tpu_custom_call" | custom-call | flops 234881024 | bytes 3670016 | tf_op jit(solution)/shard_map/pallas_call | solution.py:93
  7.1 0.7 %collective-permute-start.1 = (f32[4,128,128]{2,1,0:T(8,128)S(1)}, f32[4,128,128]{2,1,0:T(8,128)S(1)}, u32[]{:S(2)}, u32[]{:S(2)}) collective-permute-start(f32[4,128,128]{2,1,0:T(8,128)S(1)} %get-tuple-element.15), channel_id=1, source_target_pairs={{0,1},{1,0},{2,3},{3,2},{4,5},{5,4},{6,7},{7,6},{8,9},{9,8},{10,11... | collective-permute-start | bytes 786440 | tf_op jit(solution)/shard_map/ppermute | solution.py:18
  7.9 0.0 copy-done.5
  7.9 0.0 copy-done.1
  7.9 0.0 copy-start.4
  7.9 1.1 %shard_map.87 = f32[4,128,128]{2,1,0:T(8,128)S(1)} custom-call(s32[1]{0:T(128)} %bitcast.me_ref, bf16[2,1792,128]{2,1,0:T(8,128)(2,1)S(1)} %get-tuple-element.14.table, bf16[2048,1792]{1,0:T(8,128)(2,1)S(1)} %copy-done.1), custom_call_target="tpu_custom_call" | custom-call | flops 234881024 | bytes 3670016 | tf_op jit(solution)/shard_map/pallas_call | solution.py:86
  9.0 0.0 collective-permute-done.1
  9.1 0.0 collective-permute-done
  9.1 1.6 %collective-permute-start.2 = (bf16[2,128,128]{2,1,0:T(8,128)(2,1)S(1)}, bf16[2,128,128]{2,1,0:T(8,128)(2,1)S(1)}, u32[]{:S(2)}, u32[]{:S(2)}) collective-permute-start(bf16[2,128,128]{2,1,0:T(8,128)(2,1)S(1)} %slice.62), channel_id=1, source_target_pairs={{0,3},{1,2},{2,1},{3,0},{4,7},{5,6},{6,5},{7,4},{8,11},{9,10},{10,... | collective-permute-start | bytes 196616 | tf_op jit(solution)/shard_map/ppermute | solution.py:18
  10.7 0.3 collective-permute-start.6
  11.0 0.0 copy-done
  11.0 0.0 copy-done.4
  11.0 0.9 %fusion.6 = f32[64,128]{1,0:T(8,128)S(1)} fusion(bf16[8192,64]{0,1:T(8,128)(2,1)S(1)} %copy-done.4, bf16[128,8192]{1,0:T(8,128)(2,1)S(1)} %copy-done), kind=kOutput, calls=%fused_computation.17 | convolution fusion | flops 134217728 | bytes 3178496 | tf_op jit(solution)/shard_map/dot_general | solution.py:319
  11.9 1.2 %collective-permute-done.2 = bf16[2,128,128]{2,1,0:T(8,128)(2,1)S(1)} collective-permute-done((bf16[2,128,128]{2,1,0:T(8,128)(2,1)S(1)}, bf16[2,128,128]{2,1,0:T(8,128)(2,1)S(1)}, u32[]{:S(2)}, u32[]{:S(2)}) %collective-permute-start.2) | collective-permute-done | bytes 65568 | tf_op jit(solution)/shard_map/ppermute | solution.py:18
  13.1 0.3 collective-permute-start.3
  13.4 2.6 %collective-permute-start.5 = (f32[64,128]{1,0:T(8,128)S(1)}, f32[64,128]{1,0:T(8,128)S(1)}, u32[]{:S(2)}, u32[]{:S(2)}) collective-permute-start(f32[64,128]{1,0:T(8,128)S(1)} %fusion.6), channel_id=1, source_target_pairs={{0,9},{1,8},{2,11},{3,10},{4,13},{5,12},{6,15},{7,14},{8,1},{9,0},... | collective-permute-start | bytes 98312 | tf_op jit(solution)/shard_map/ppermute | solution.py:18
  16.0 0.3 collective-permute-done.6
  16.2 0.5 %collective-permute-start.7 = (bf16[32,4096]{1,0:T(8,128)(2,1)S(1)}, bf16[32,4096]{1,0:T(8,128)(2,1)S(1)}, u32[]{:S(2)}, u32[]{:S(2)}) collective-permute-start(bf16[32,4096]{1,0:T(8,128)(2,1)S(1)} %constant_dynamic-update-slice_fusion.refs_0_), channel_id=1, source_target_pairs={{0,1},{1,0},{2,3},{3,2},{4,5},{5,4},{6,7},{7,6},{8,9},{9,8},{10,11... | collective-permute-start | bytes 786440 | tf_op jit(solution)/shard_map/ppermute | solution.py:18
  16.8 0.4 %collective-permute-done.3 = f32[1,128,128]{2,1,0:T(8,128)S(1)} collective-permute-done((f32[1,128,128]{2,1,0:T(8,128)S(1)}, f32[1,128,128]{2,1,0:T(8,128)S(1)}, u32[]{:S(2)}, u32[]{:S(2)}) %collective-permute-start.3) | collective-permute-done | bytes 65568 | tf_op jit(solution)/shard_map/ppermute | solution.py:18
  17.2 3.0 %collective-permute-start.4 = (bf16[128,128]{1,0:T(8,128)(2,1)S(1)}, bf16[128,128]{1,0:T(8,128)(2,1)S(1)}, u32[]{:S(2)}, u32[]{:S(2)}) collective-permute-start(bf16[128,128]{1,0:T(8,128)(2,1)S(1)} %get-tuple-element.26), channel_id=1, source_target_pairs={{0,9},{1,8},{2,11},{3,10},{4,13},{5,12},{6,15},{7,14},{8,1},{9,0},... | collective-permute-start | bytes 98312 | tf_op jit(solution)/shard_map/ppermute | solution.py:18
  20.2 0.0 collective-permute-done.5
  20.2 0.0 copy-start.2
  20.2 0.0 copy-start.3
  20.2 0.0 collective-permute-done.7.refs_1_
  20.2 0.7 %shard_map.88.inner_ref = f32[2048,512]{1,0:T(8,128)S(1)} custom-call(f32[2,64,128]{2,1,0:T(8,128)S(1)} %pad_maximum_fusion.1.act_ref, bf16[32,4096]{1,0:T(8,128)(2,1)S(1)} %constant_dynamic-update-slice_fusion.refs_0_, bf16[32,4096]{1,0:T(8,128)(2,1)S(1)} %collective-permute-done.7.refs_1_), custom_call_target="tpu_custom_call" | custom-call | flops 536870912 | bytes 4194304 | tf_op jit(solution)/shard_map/pallas_call | solution.py:147
  20.9 1.5 %collective-permute-done.4.other_ref = bf16[128,128]{1,0:T(8,128)(2,1)S(1)} collective-permute-done((bf16[128,128]{1,0:T(8,128)(2,1)S(1)}, bf16[128,128]{1,0:T(8,128)(2,1)S(1)}, u32[]{:S(2)}, u32[]{:S(2)}) %collective-permute-start.4) | collective-permute-done | bytes 32800 | tf_op jit(solution)/shard_map/ppermute | solution.py:18
  22.5 0.0 copy-done.2
  22.5 0.0 copy-done.3
  22.5 1.1 %shard_map.89 = (f32[64,128]{1,0:T(8,128)S(1)}, f32[64,128]{1,0:T(8,128)S(1)}, f32[8,8,16]{2,1,0:T(8,128)S(1)}) custom-call(s32[1]{0:T(128)} %bitcast.me_ref, s32[16]{0:T(128)S(1)} %copy-done.2, s32[16]{0:T(128)S(1)} %copy-done.3, f32[128,128]{1,0:T(8,128)S(1)} %get-tuple-element.27.own_ref, bf16[128,128]{1,0:T(8,128)(2,1)S(1)} %collective-permute-done.4.other_ref, ...), custom_call_target="tpu_custom_call" | custom-call | flops 2097152 | bytes 4194304 | tf_op jit(solution)/shard_map/pallas_call | solution.py:247
  23.6 0.2 collective-permute-start.8
  23.8 1.1 %collective-permute-done.8 = f32[4,8,16]{2,1,0:T(8,128)S(1)} collective-permute-done((f32[4,8,16]{2,1,0:T(8,128)S(1)}, f32[4,8,16]{2,1,0:T(8,128)S(1)}, u32[]{:S(2)}, u32[]{:S(2)}) %collective-permute-start.8) | collective-permute-done | bytes 2080 | tf_op jit(solution)/shard_map/ppermute | solution.py:18
  24.9 1.9 %collective-permute-start.9 = (f32[2,8,16]{2,1,0:T(8,128)S(1)}, f32[2,8,16]{2,1,0:T(8,128)S(1)}, u32[]{:S(2)}, u32[]{:S(2)}) collective-permute-start(f32[2,8,16]{2,1,0:T(8,128)S(1)} %slice.45), channel_id=1, source_target_pairs={{0,3},{1,2},{2,1},{3,0},{4,7},{5,6},{6,5},{7,4},{8,11},{9,10},{10,... | collective-permute-start | bytes 3080 | tf_op jit(solution)/shard_map/ppermute | solution.py:18
  26.7 1.8 %collective-permute-start.11 = (f32[64,128]{1,0:T(8,128)S(1)}, f32[64,128]{1,0:T(8,128)S(1)}, u32[]{:S(2)}, u32[]{:S(2)}) collective-permute-start(f32[64,128]{1,0:T(8,128)S(1)} %get-tuple-element.23), channel_id=1, source_target_pairs={{0,9},{1,8},{2,11},{3,10},{4,13},{5,12},{6,15},{7,14},{8,1},{9,0},... | collective-permute-start | bytes 98312 | tf_op jit(solution)/shard_map/ppermute | solution.py:18
  28.5 0.0 collective-permute-done.9
  28.5 0.2 collective-permute-start.10
  28.7 2.7 %collective-permute-done.11.other_ref = f32[64,128]{1,0:T(8,128)S(1)} collective-permute-done((f32[64,128]{1,0:T(8,128)S(1)}, f32[64,128]{1,0:T(8,128)S(1)}, u32[]{:S(2)}, u32[]{:S(2)}) %collective-permute-start.11) | collective-permute-done | bytes 32800 | tf_op jit(solution)/shard_map/ppermute | solution.py:18
  31.4 0.7 %shard_map.90 = f32[128,128]{1,0:T(8,128)} custom-call(s32[1]{0:T(128)} %bitcast.me_ref, f32[64,128]{1,0:T(8,128)S(1)} %get-tuple-element.22.own_ref, f32[64,128]{1,0:T(8,128)S(1)} %collective-permute-done.11.other_ref), custom_call_target="tpu_custom_call" | custom-call | tf_op jit(solution)/shard_map/pallas_call | solution.py:276
  32.2 0.0 collective-permute-done.10
  32.2 0.6 %fusion.3 = f32[16,8]{0,1:T(8,128)} fusion(f32[1,8,16]{2,1,0:T(8,128)S(1)} %collective-permute-done.10, f32[2,8,16]{2,1,0:T(8,128)S(1)} %slice_add_fusion.2, f32[16]{0:T(128)S(1)} %convert_rsqrt_fusion), kind=kLoop, calls=%fused_computation.14 | loop fusion | flops 256 | bytes 1600 | tf_op jit(solution)/shard_map/transpose | solution.py:348
  (16 shorter events, 0.1 us)
Async XLA Ops:
  0.6 10.4 %copy-start = (bf16[128,8192]{1,0:T(8,128)(2,1)S(1)}, bf16[128,8192]{1,0:T(8,128)(2,1)}, u32[]{:S(2)}) copy-start(bf16[128,8192]{1,0:T(8,128)(2,1)} %param.7) | copy-start | bytes 6291460
  0.6 8.4 %collective-permute-start = (bf16[8,4096]{1,0:T(8,128)(2,1)}, bf16[8,4096]{1,0:T(8,128)(2,1)S(1)}, u32[]{:S(2)}, u32[]{:S(2)}) collective-permute-start(bf16[8,4096]{1,0:T(8,128)(2,1)} %param.11), channel_id=1, source_target_pairs={{0,5},{1,4},{2,7},{3,6},{4,1},{5,0},{6,3},{7,2},{8,13},{9,12},{10,... | collective-permute-start | bytes 196616 | tf_op jit(solution)/shard_map/ppermute | solution.py:18
  3.2 4.7 %copy-start.5 = (bf16[8,4096]{1,0:T(8,128)(2,1)S(1)}, bf16[8,4096]{1,0:T(8,128)(2,1)}, u32[]{:S(2)}) copy-start(bf16[8,4096]{1,0:T(8,128)(2,1)} %param.11) | copy-start | bytes 196612
  3.2 4.7 %copy-start.1 = (bf16[2048,1792]{1,0:T(8,128)(2,1)S(1)}, bf16[2048,1792]{1,0:T(8,128)(2,1)}, u32[]{:S(2)}) copy-start(bf16[2048,1792]{1,0:T(8,128)(2,1)} %grads_ref.3) | copy-start | bytes 22020100
  7.1 1.9 %collective-permute-start.1 = (f32[4,128,128]{2,1,0:T(8,128)S(1)}, f32[4,128,128]{2,1,0:T(8,128)S(1)}, u32[]{:S(2)}, u32[]{:S(2)}) collective-permute-start(f32[4,128,128]{2,1,0:T(8,128)S(1)} %get-tuple-element.15), channel_id=1, source_target_pairs={{0,1},{1,0},{2,3},{3,2},{4,5},{5,4},{6,7},{7,6},{8,9},{9,8},{10,11... | collective-permute-start | bytes 786440 | tf_op jit(solution)/shard_map/ppermute | solution.py:18
  7.9 3.1 %copy-start.4 = (bf16[8192,64]{0,1:T(8,128)(2,1)S(1)}, bf16[8192,64]{0,1:T(8,128)(2,1)}, u32[]{:S(2)}) copy-start(bf16[8192,64]{0,1:T(8,128)(2,1)} %param.9) | copy-start | bytes 3145732
  9.1 4.0 %collective-permute-start.2 = (bf16[2,128,128]{2,1,0:T(8,128)(2,1)S(1)}, bf16[2,128,128]{2,1,0:T(8,128)(2,1)S(1)}, u32[]{:S(2)}, u32[]{:S(2)}) collective-permute-start(bf16[2,128,128]{2,1,0:T(8,128)(2,1)S(1)} %slice.62), channel_id=1, source_target_pairs={{0,3},{1,2},{2,1},{3,0},{4,7},{5,6},{6,5},{7,4},{8,11},{9,10},{10,... | collective-permute-start | bytes 196616 | tf_op jit(solution)/shard_map/ppermute | solution.py:18
  10.7 5.5 %collective-permute-start.6 = (bf16[16,4096]{1,0:T(8,128)(2,1)S(1)}, bf16[16,4096]{1,0:T(8,128)(2,1)S(1)}, u32[]{:S(2)}, u32[]{:S(2)}) collective-permute-start(bf16[16,4096]{1,0:T(8,128)(2,1)S(1)} %pad_maximum_fusion), channel_id=1, source_target_pairs={{0,3},{1,2},{2,1},{3,0},{4,7},{5,6},{6,5},{7,4},{8,11},{9,10},{10,... | collective-permute-start | bytes 393224 | tf_op jit(solution)/shard_map/ppermute | solution.py:18
  13.1 4.1 %collective-permute-start.3 = (f32[1,128,128]{2,1,0:T(8,128)S(1)}, f32[1,128,128]{2,1,0:T(8,128)S(1)}, u32[]{:S(2)}, u32[]{:S(2)}) collective-permute-start(f32[1,128,128]{2,1,0:T(8,128)S(1)} %slice.43), channel_id=1, source_target_pairs={{0,5},{1,4},{2,7},{3,6},{4,1},{5,0},{6,3},{7,2},{8,13},{9,12},{10,... | collective-permute-start | bytes 196616 | tf_op jit(solution)/shard_map/ppermute | solution.py:18
  13.4 6.8 %collective-permute-start.5 = (f32[64,128]{1,0:T(8,128)S(1)}, f32[64,128]{1,0:T(8,128)S(1)}, u32[]{:S(2)}, u32[]{:S(2)}) collective-permute-start(f32[64,128]{1,0:T(8,128)S(1)} %fusion.6), channel_id=1, source_target_pairs={{0,9},{1,8},{2,11},{3,10},{4,13},{5,12},{6,15},{7,14},{8,1},{9,0},... | collective-permute-start | bytes 98312 | tf_op jit(solution)/shard_map/ppermute | solution.py:18
  16.2 4.0 %collective-permute-start.7 = (bf16[32,4096]{1,0:T(8,128)(2,1)S(1)}, bf16[32,4096]{1,0:T(8,128)(2,1)S(1)}, u32[]{:S(2)}, u32[]{:S(2)}) collective-permute-start(bf16[32,4096]{1,0:T(8,128)(2,1)S(1)} %constant_dynamic-update-slice_fusion.refs_0_), channel_id=1, source_target_pairs={{0,1},{1,0},{2,3},{3,2},{4,5},{5,4},{6,7},{7,6},{8,9},{9,8},{10,11... | collective-permute-start | bytes 786440 | tf_op jit(solution)/shard_map/ppermute | solution.py:18
  17.2 5.3 %collective-permute-start.4 = (bf16[128,128]{1,0:T(8,128)(2,1)S(1)}, bf16[128,128]{1,0:T(8,128)(2,1)S(1)}, u32[]{:S(2)}, u32[]{:S(2)}) collective-permute-start(bf16[128,128]{1,0:T(8,128)(2,1)S(1)} %get-tuple-element.26), channel_id=1, source_target_pairs={{0,9},{1,8},{2,11},{3,10},{4,13},{5,12},{6,15},{7,14},{8,1},{9,0},... | collective-permute-start | bytes 98312 | tf_op jit(solution)/shard_map/ppermute | solution.py:18
  20.2 2.3 %copy-start.2 = (s32[16]{0:T(128)S(1)}, s32[16]{0:T(128)}, u32[]{:S(2)}) copy-start(s32[16]{0:T(128)} %length_ref.1) | copy-start | bytes 196
  20.2 2.3 %copy-start.3 = (s32[16]{0:T(128)S(1)}, s32[16]{0:T(128)}, u32[]{:S(2)}) copy-start(s32[16]{0:T(128)} %valid_ref.1) | copy-start | bytes 196
  23.6 1.2 %collective-permute-start.8 = (f32[4,8,16]{2,1,0:T(8,128)S(1)}, f32[4,8,16]{2,1,0:T(8,128)S(1)}, u32[]{:S(2)}, u32[]{:S(2)}) collective-permute-start(f32[4,8,16]{2,1,0:T(8,128)S(1)} %slice.36), channel_id=1, source_target_pairs={{0,1},{1,0},{2,3},{3,2},{4,5},{5,4},{6,7},{7,6},{8,9},{9,8},{10,11... | collective-permute-start | bytes 6152 | tf_op jit(solution)/shard_map/ppermute | solution.py:18
  24.9 3.7 %collective-permute-start.9 = (f32[2,8,16]{2,1,0:T(8,128)S(1)}, f32[2,8,16]{2,1,0:T(8,128)S(1)}, u32[]{:S(2)}, u32[]{:S(2)}) collective-permute-start(f32[2,8,16]{2,1,0:T(8,128)S(1)} %slice.45), channel_id=1, source_target_pairs={{0,3},{1,2},{2,1},{3,0},{4,7},{5,6},{6,5},{7,4},{8,11},{9,10},{10,... | collective-permute-start | bytes 3080 | tf_op jit(solution)/shard_map/ppermute | solution.py:18
  26.7 4.7 %collective-permute-start.11 = (f32[64,128]{1,0:T(8,128)S(1)}, f32[64,128]{1,0:T(8,128)S(1)}, u32[]{:S(2)}, u32[]{:S(2)}) collective-permute-start(f32[64,128]{1,0:T(8,128)S(1)} %get-tuple-element.23), channel_id=1, source_target_pairs={{0,9},{1,8},{2,11},{3,10},{4,13},{5,12},{6,15},{7,14},{8,1},{9,0},... | collective-permute-start | bytes 98312 | tf_op jit(solution)/shard_map/ppermute | solution.py:18
  28.5 3.6 %collective-permute-start.10 = (f32[1,8,16]{2,1,0:T(8,128)S(1)}, f32[1,8,16]{2,1,0:T(8,128)S(1)}, u32[]{:S(2)}, u32[]{:S(2)}) collective-permute-start(f32[1,8,16]{2,1,0:T(8,128)S(1)} %slice.46), channel_id=1, source_target_pairs={{0,5},{1,4},{2,7},{3,6},{4,1},{5,0},{6,3},{7,2},{8,13},{9,12},{10,... | collective-permute-start | bytes 1544 | tf_op jit(solution)/shard_map/ppermute | solution.py:18

commit v15 on v14

--- a/solution.py
+++ b/solution.py
@@ -109,6 +109,48 @@
     )
 
 
+def act_kernel(pieces, proj_ref, rows_ref, out_ref, rows_buf, sems):
+    depth = rows_ref.shape[1] // pieces
+    copies = []
+    for k in range(pieces):
+        copy = pltpu.make_async_copy(
+            rows_ref.at[:, pl.ds(k * depth, depth)], rows_buf.at[k], sems.at[k]
+        )
+        copy.start(priority=k % 2)
+        copies.append(copy)
+    total = None
+    for k in range(pieces):
+        copies[k].wait()
+        part = lax.dot_general(
+            proj_ref[:, k * depth : (k + 1) * depth],
+            rows_buf[k],
+            (((1,), (1,)), ((), ())),
+            preferred_element_type=jnp.float32,
+        )
+        total = part if total is None else total + part
+    out_ref[...] = total
+
+
+def act_blocks(proj, activations):
+    width, depth = proj.shape
+    rows = activations.shape[0]
+    pieces = 8
+    return pl.pallas_call(
+        functools.partial(act_kernel, pieces),
+        in_specs=[VMEM, HBM],
+        out_specs=VMEM,
+        out_shape=jax.ShapeDtypeStruct((width, rows), jnp.float32),
+        scratch_shapes=[
+            pltpu.VMEM((pieces, rows, depth // pieces), jnp.bfloat16),
+            pltpu.SemaphoreType.DMA((pieces,)),
+        ],
+        compiler_params=pltpu.CompilerParams(vmem_limit_bytes=24 * MIB),
+        cost_estimate=pl.CostEstimate(
+            flops=2 * width * rows * depth, bytes_accessed=2 * rows * depth, transcendentals=0
+        ),
+    )(proj, pltpu.with_memory_space_constraint(activations, pltpu.HBM))
+
+
 def inner_kernel(pieces, act_ref, *refs):
     out_ref = refs[pieces]
     columns = []
@@ -309,16 +351,13 @@
     got, sums = lax.optimization_barrier((got, sums))
     for k, bit in enumerate(middle):
         half = sums.shape[0] // 2
-        kind = jnp.bfloat16 if k == 0 else jnp.float32
-        sent = swap(sums[half:].astype(kind), bit, size)
+        sent = swap(sums[half:].astype(jnp.bfloat16), bit, size)
         sums = sums[:half] + sent.astype(jnp.float32)
         if k == 0:
             after = sums
     own = sums[0]
     across = swap(own.astype(jnp.bfloat16), split, size)
-    act = lax.dot_general(
-        late, activations, (((0,), (1,)), ((), ())), preferred_element_type=jnp.float32
-    )
+    act = act_blocks(late.T, activations)
     early, _ = lax.optimization_barrier((act, after))
     more_act, _ = lax.optimization_barrier((swap(early, split, size), own))
     act = jnp.stack([act, more_act])

time: 32.9 us -> 31.9 us (0.970)
  waiting for transfers between devices: 7.24 us -> 4.02 us
  Pallas kernels: 7.59 us -> 10.4 us
  matrix products: 0.88 us -> 0 us
    ppermute x12, waiting for transfers between devices: 7.24 us -> 4.02 us  [swap(): return lax.ppermute(value, 'seq', [(i, i ^ offset) for i in range(size)])]
    pallas_call x0 -> x1, Pallas kernels: none -> 2.84 us  [act_blocks(): pl.pallas_call(functools.partial(act_kernel, pieces), in_specs=[VMEM, HBM...]
    dot_general x1 -> x0, matrix products: 0.88 us -> none  [body(): lax.dot_general(late, activations, (((0,), (1,)), ((), ())), preferred_el...]
  transfers between devices with their start and end apart: 12 -> 12, of which waited for: 6 -> 5; matrix products, arithmetic and copies ran while one was open for 3% -> 0% of each run, Pallas kernels for 20% -> 30%
where the time goes in v15:
time: 31.9 us; the launch traced here: 31.7 us
  starting transfers between devices  15.7 us (49%)
  Pallas kernels  10.4 us (33%)
  waiting for transfers between devices  4.02 us (13%)
  between operations  0.79 us (2%)
  other arithmetic  0.7 us (2%)
    ppermute x12, starting transfers between devices, swap(): return lax.ppermute(value, 'seq', [(i, i ^ offset) for i in range(size)])  15.7 us
    ppermute x12, waiting for transfers between devices, swap(): return lax.ppermute(value, 'seq', [(i, i ^ offset) for i in range(size)])  4.02 us
    pallas_call x1, Pallas kernels, grad_blocks(): pl.pallas_call(functools.partial(grad_kernel, offsets), in_specs=[SMEM, H...  3.95 us
    pallas_call x1, Pallas kernels, act_blocks(): pl.pallas_call(functools.partial(act_kernel, pieces), in_specs=[VMEM, HBM...  2.84 us
    pallas_call x1, Pallas kernels, grad_blocks(): pl.pallas_call(functools.partial(held_kernel, offsets), in_specs=[SMEM, V...  1.13 us
    pallas_call x1, Pallas kernels, score(): pl.pallas_call(functools.partial(score_kernel, steps, split), out_shape=(...  1.08 us
    pallas_call x1, Pallas kernels, place_tokens(): pl.pallas_call(functools.partial(place_kernel, place, split), in_specs=[S...  0.74 us
    pallas_call x1, Pallas kernels, inner(): pl.pallas_call(functools.partial(inner_kernel, len(panels)), out_shape=ja...  0.71 us
  transfers between devices with their start and end apart: 12, of which 5 were waited for; matrix products, arithmetic and copies ran while one was open for 0% of the time, Pallas kernels for 30%

profile of v15, /device:TPU:0, one launch (start us, length us, event | category | flops | bytes accessed | tf_op | source)
XLA Modules:
  0.0 31.7 jit_solution(14172541729391237037)
XLA Ops:
  0.6 0.0 copy-start.4
  0.6 2.5 %collective-permute-start = (bf16[8,4096]{1,0:T(8,128)(2,1)}, bf16[8,4096]{1,0:T(8,128)(2,1)S(1)}, u32[]{:S(2)}, u32[]{:S(2)}) collective-permute-start(bf16[8,4096]{1,0:T(8,128)(2,1)} %param.11), channel_id=1, source_target_pairs={{0,5},{1,4},{2,7},{3,6},{4,1},{5,0},{6,3},{7,2},{8,13},{9,12},{10,... | collective-permute-start | bytes 196616 | tf_op jit(solution)/shard_map/ppermute | solution.py:18
  3.2 0.0 copy-start
  3.2 3.9 %shard_map.86 = (f32[4,128,128]{2,1,0:T(8,128)S(1)}, bf16[2,1792,128]{2,1,0:T(8,128)(2,1)S(1)}) custom-call(s32[1]{0:T(128)} %bitcast.me_ref, bf16[64,1792]{1,0:T(8,128)(2,1)} %bitcast.18, bf16[2048,1792]{1,0:T(8,128)(2,1)} %grads_ref.3), custom_call_target="tpu_custom_call" | custom-call | flops 234881024 | bytes 3670016 | tf_op jit(solution)/shard_map/pallas_call | solution.py:93
  7.1 0.7 %collective-permute-start.1 = (f32[4,128,128]{2,1,0:T(8,128)S(1)}, f32[4,128,128]{2,1,0:T(8,128)S(1)}, u32[]{:S(2)}, u32[]{:S(2)}) collective-permute-start(f32[4,128,128]{2,1,0:T(8,128)S(1)} %get-tuple-element.15), channel_id=1, source_target_pairs={{0,1},{1,0},{2,3},{3,2},{4,5},{5,4},{6,7},{7,6},{8,9},{9,8},{10,11... | collective-permute-start | bytes 786440 | tf_op jit(solution)/shard_map/ppermute | solution.py:18
  7.9 0.0 copy-done.4
  7.9 0.0 copy-done
  7.9 0.0 copy-start.1
  7.9 1.1 %shard_map.87 = f32[4,128,128]{2,1,0:T(8,128)S(1)} custom-call(s32[1]{0:T(128)} %bitcast.me_ref, bf16[2,1792,128]{2,1,0:T(8,128)(2,1)S(1)} %get-tuple-element.14.table, bf16[2048,1792]{1,0:T(8,128)(2,1)S(1)} %copy-done), custom_call_target="tpu_custom_call" | custom-call | flops 234881024 | bytes 3670016 | tf_op jit(solution)/shard_map/pallas_call | solution.py:86
  9.0 0.0 collective-permute-done.1
  9.1 0.0 collective-permute-done
  9.1 1.5 %collective-permute-start.2 = (bf16[2,128,128]{2,1,0:T(8,128)(2,1)S(1)}, bf16[2,128,128]{2,1,0:T(8,128)(2,1)S(1)}, u32[]{:S(2)}, u32[]{:S(2)}) collective-permute-start(bf16[2,128,128]{2,1,0:T(8,128)(2,1)S(1)} %slice.64), channel_id=1, source_target_pairs={{0,3},{1,2},{2,1},{3,0},{4,7},{5,6},{6,5},{7,4},{8,11},{9,10},{10,... | collective-permute-start | bytes 196616 | tf_op jit(solution)/shard_map/ppermute | solution.py:18
  10.7 0.3 %collective-permute-start.6 = (bf16[16,4096]{1,0:T(8,128)(2,1)S(1)}, bf16[16,4096]{1,0:T(8,128)(2,1)S(1)}, u32[]{:S(2)}, u32[]{:S(2)}) collective-permute-start(bf16[16,4096]{1,0:T(8,128)(2,1)S(1)} %pad_maximum_fusion), channel_id=1, source_target_pairs={{0,3},{1,2},{2,1},{3,0},{4,7},{5,6},{6,5},{7,4},{8,11},{9,10},{10,... | collective-permute-start | bytes 393224 | tf_op jit(solution)/shard_map/ppermute | solution.py:18
  11.0 0.0 copy-done.1
  11.0 0.0 copy-start.2
  11.0 0.0 copy-start.3
  11.0 2.8 %shard_map.88 = f32[64,128]{1,0:T(8,128)S(1)} custom-call(bf16[64,8192]{1,0:T(8,128)(2,1)S(1)} %bitcast.16, bf16[128,8192]{1,0:T(8,128)(2,1)} %rows_ref.1), custom_call_target="tpu_custom_call" | custom-call | flops 134217728 | bytes 2097152 | tf_op jit(solution)/shard_map/pallas_call | solution.py:138
  13.9 0.0 collective-permute-done.2
  13.9 0.1 collective-permute-start.3
  14.0 2.7 %collective-permute-start.5 = (f32[64,128]{1,0:T(8,128)S(1)}, f32[64,128]{1,0:T(8,128)S(1)}, u32[]{:S(2)}, u32[]{:S(2)}) collective-permute-start(f32[64,128]{1,0:T(8,128)S(1)} %shard_map.88), channel_id=1, source_target_pairs={{0,9},{1,8},{2,11},{3,10},{4,13},{5,12},{6,15},{7,14},{8,1},{9,0},... | collective-permute-start | bytes 98312 | tf_op jit(solution)/shard_map/ppermute | solution.py:18
  16.8 0.0 collective-permute-done.6
  16.8 0.4 %collective-permute-start.7 = (bf16[32,4096]{1,0:T(8,128)(2,1)S(1)}, bf16[32,4096]{1,0:T(8,128)(2,1)S(1)}, u32[]{:S(2)}, u32[]{:S(2)}) collective-permute-start(bf16[32,4096]{1,0:T(8,128)(2,1)S(1)} %constant_dynamic-update-slice_fusion.refs_0_), channel_id=1, source_target_pairs={{0,1},{1,0},{2,3},{3,2},{4,5},{5,4},{6,7},{7,6},{8,9},{9,8},{10,11... | collective-permute-start | bytes 786440 | tf_op jit(solution)/shard_map/ppermute | solution.py:18
  17.2 0.2 collective-permute-done.3
  17.4 2.8 %collective-permute-start.4 = (bf16[128,128]{1,0:T(8,128)(2,1)S(1)}, bf16[128,128]{1,0:T(8,128)(2,1)S(1)}, u32[]{:S(2)}, u32[]{:S(2)}) collective-permute-start(bf16[128,128]{1,0:T(8,128)(2,1)S(1)} %get-tuple-element.26), channel_id=1, source_target_pairs={{0,9},{1,8},{2,11},{3,10},{4,13},{5,12},{6,15},{7,14},{8,1},{9,0},... | collective-permute-start | bytes 98312 | tf_op jit(solution)/shard_map/ppermute | solution.py:18
  20.1 0.0 collective-permute-done.5
  20.1 0.0 collective-permute-done.7.refs_1_
  20.2 0.7 %shard_map.89.inner_ref = f32[2048,512]{1,0:T(8,128)S(1)} custom-call(f32[2,64,128]{2,1,0:T(8,128)S(1)} %pad_maximum_fusion.1.act_ref, bf16[32,4096]{1,0:T(8,128)(2,1)S(1)} %constant_dynamic-update-slice_fusion.refs_0_, bf16[32,4096]{1,0:T(8,128)(2,1)S(1)} %collective-permute-done.7.refs_1_), custom_call_target="tpu_custom_call" | custom-call | flops 536870912 | bytes 4194304 | tf_op jit(solution)/shard_map/pallas_call | solution.py:189
  20.9 0.9 %collective-permute-done.4.other_ref = bf16[128,128]{1,0:T(8,128)(2,1)S(1)} collective-permute-done((bf16[128,128]{1,0:T(8,128)(2,1)S(1)}, bf16[128,128]{1,0:T(8,128)(2,1)S(1)}, u32[]{:S(2)}, u32[]{:S(2)}) %collective-permute-start.4) | collective-permute-done | bytes 32800 | tf_op jit(solution)/shard_map/ppermute | solution.py:18
  21.7 0.0 copy-done.2
  21.7 0.0 copy-done.3
  21.7 1.1 %shard_map.90 = (f32[64,128]{1,0:T(8,128)S(1)}, f32[64,128]{1,0:T(8,128)S(1)}, f32[8,8,16]{2,1,0:T(8,128)S(1)}) custom-call(s32[1]{0:T(128)} %bitcast.me_ref, s32[16]{0:T(128)S(1)} %copy-done.2, s32[16]{0:T(128)S(1)} %copy-done.3, f32[128,128]{1,0:T(8,128)S(1)} %get-tuple-element.27.own_ref, bf16[128,128]{1,0:T(8,128)(2,1)S(1)} %collective-permute-done.4.other_ref, ...), custom_call_target="tpu_custom_call" | custom-call | flops 2097152 | bytes 4194304 | tf_op jit(solution)/shard_map/pallas_call | solution.py:289
  22.8 0.3 %collective-permute-start.8 = (f32[4,8,16]{2,1,0:T(8,128)S(1)}, f32[4,8,16]{2,1,0:T(8,128)S(1)}, u32[]{:S(2)}, u32[]{:S(2)}) collective-permute-start(f32[4,8,16]{2,1,0:T(8,128)S(1)} %slice.37), channel_id=1, source_target_pairs={{0,1},{1,0},{2,3},{3,2},{4,5},{5,4},{6,7},{7,6},{8,9},{9,8},{10,11... | collective-permute-start | bytes 6152 | tf_op jit(solution)/shard_map/ppermute | solution.py:18
  23.2 0.9 %collective-permute-done.8 = f32[4,8,16]{2,1,0:T(8,128)S(1)} collective-permute-done((f32[4,8,16]{2,1,0:T(8,128)S(1)}, f32[4,8,16]{2,1,0:T(8,128)S(1)}, u32[]{:S(2)}, u32[]{:S(2)}) %collective-permute-start.8) | collective-permute-done | bytes 2080 | tf_op jit(solution)/shard_map/ppermute | solution.py:18
  24.1 1.4 %collective-permute-start.9 = (f32[2,8,16]{2,1,0:T(8,128)S(1)}, f32[2,8,16]{2,1,0:T(8,128)S(1)}, u32[]{:S(2)}, u32[]{:S(2)}) collective-permute-start(f32[2,8,16]{2,1,0:T(8,128)S(1)} %slice.46), channel_id=1, source_target_pairs={{0,3},{1,2},{2,1},{3,0},{4,7},{5,6},{6,5},{7,4},{8,11},{9,10},{10,... | collective-permute-start | bytes 3080 | tf_op jit(solution)/shard_map/ppermute | solution.py:18
  25.5 2.5 %collective-permute-start.11 = (f32[64,128]{1,0:T(8,128)S(1)}, f32[64,128]{1,0:T(8,128)S(1)}, u32[]{:S(2)}, u32[]{:S(2)}) collective-permute-start(f32[64,128]{1,0:T(8,128)S(1)} %get-tuple-element.23), channel_id=1, source_target_pairs={{0,9},{1,8},{2,11},{3,10},{4,13},{5,12},{6,15},{7,14},{8,1},{9,0},... | collective-permute-start | bytes 98312 | tf_op jit(solution)/shard_map/ppermute | solution.py:18
  28.0 0.0 collective-permute-done.9
  28.0 0.3 collective-permute-start.10
  28.3 1.4 %collective-permute-done.11.other_ref = f32[64,128]{1,0:T(8,128)S(1)} collective-permute-done((f32[64,128]{1,0:T(8,128)S(1)}, f32[64,128]{1,0:T(8,128)S(1)}, u32[]{:S(2)}, u32[]{:S(2)}) %collective-permute-start.11) | collective-permute-done | bytes 32800 | tf_op jit(solution)/shard_map/ppermute | solution.py:18
  29.7 0.7 %shard_map.91 = f32[128,128]{1,0:T(8,128)} custom-call(s32[1]{0:T(128)} %bitcast.me_ref, f32[64,128]{1,0:T(8,128)S(1)} %get-tuple-element.22.own_ref, f32[64,128]{1,0:T(8,128)S(1)} %collective-permute-done.11.other_ref), custom_call_target="tpu_custom_call" | custom-call | tf_op jit(solution)/shard_map/pallas_call | solution.py:318
  30.5 0.7 %collective-permute-done.10 = f32[1,8,16]{2,1,0:T(8,128)S(1)} collective-permute-done((f32[1,8,16]{2,1,0:T(8,128)S(1)}, f32[1,8,16]{2,1,0:T(8,128)S(1)}, u32[]{:S(2)}, u32[]{:S(2)}) %collective-permute-start.10) | collective-permute-done | bytes 544 | tf_op jit(solution)/shard_map/ppermute | solution.py:18
  31.1 0.6 %fusion.3 = f32[16,8]{0,1:T(8,128)} fusion(f32[1,8,16]{2,1,0:T(8,128)S(1)} %collective-permute-done.10, f32[2,8,16]{2,1,0:T(8,128)S(1)} %slice_add_fusion.2, f32[16]{0:T(128)S(1)} %convert_rsqrt_fusion), kind=kLoop, calls=%fused_computation.15 | loop fusion | flops 256 | bytes 1600 | tf_op jit(solution)/shard_map/transpose | solution.py:387
  (16 shorter events, 0.2 us)
Async XLA Ops:
  0.6 7.2 %copy-start.4 = (bf16[8,4096]{1,0:T(8,128)(2,1)S(1)}, bf16[8,4096]{1,0:T(8,128)(2,1)}, u32[]{:S(2)}) copy-start(bf16[8,4096]{1,0:T(8,128)(2,1)} %param.11) | copy-start | bytes 196612
  0.6 8.4 %collective-permute-start = (bf16[8,4096]{1,0:T(8,128)(2,1)}, bf16[8,4096]{1,0:T(8,128)(2,1)S(1)}, u32[]{:S(2)}, u32[]{:S(2)}) collective-permute-start(bf16[8,4096]{1,0:T(8,128)(2,1)} %param.11), channel_id=1, source_target_pairs={{0,5},{1,4},{2,7},{3,6},{4,1},{5,0},{6,3},{7,2},{8,13},{9,12},{10,... | collective-permute-start | bytes 196616 | tf_op jit(solution)/shard_map/ppermute | solution.py:18
  3.2 4.7 %copy-start = (bf16[2048,1792]{1,0:T(8,128)(2,1)S(1)}, bf16[2048,1792]{1,0:T(8,128)(2,1)}, u32[]{:S(2)}) copy-start(bf16[2048,1792]{1,0:T(8,128)(2,1)} %grads_ref.3) | copy-start | bytes 22020100
  7.1 1.9 %collective-permute-start.1 = (f32[4,128,128]{2,1,0:T(8,128)S(1)}, f32[4,128,128]{2,1,0:T(8,128)S(1)}, u32[]{:S(2)}, u32[]{:S(2)}) collective-permute-start(f32[4,128,128]{2,1,0:T(8,128)S(1)} %get-tuple-element.15), channel_id=1, source_target_pairs={{0,1},{1,0},{2,3},{3,2},{4,5},{5,4},{6,7},{7,6},{8,9},{9,8},{10,11... | collective-permute-start | bytes 786440 | tf_op jit(solution)/shard_map/ppermute | solution.py:18
  7.9 3.1 %copy-start.1 = (bf16[8192,64]{0,1:T(8,128)(2,1)S(1)}, bf16[8192,64]{0,1:T(8,128)(2,1)}, u32[]{:S(2)}) copy-start(bf16[8192,64]{0,1:T(8,128)(2,1)} %param.9) | copy-start | bytes 3145732
  9.1 4.8 %collective-permute-start.2 = (bf16[2,128,128]{2,1,0:T(8,128)(2,1)S(1)}, bf16[2,128,128]{2,1,0:T(8,128)(2,1)S(1)}, u32[]{:S(2)}, u32[]{:S(2)}) collective-permute-start(bf16[2,128,128]{2,1,0:T(8,128)(2,1)S(1)} %slice.64), channel_id=1, source_target_pairs={{0,3},{1,2},{2,1},{3,0},{4,7},{5,6},{6,5},{7,4},{8,11},{9,10},{10,... | collective-permute-start | bytes 196616 | tf_op jit(solution)/shard_map/ppermute | solution.py:18
  10.7 6.1 %collective-permute-start.6 = (bf16[16,4096]{1,0:T(8,128)(2,1)S(1)}, bf16[16,4096]{1,0:T(8,128)(2,1)S(1)}, u32[]{:S(2)}, u32[]{:S(2)}) collective-permute-start(bf16[16,4096]{1,0:T(8,128)(2,1)S(1)} %pad_maximum_fusion), channel_id=1, source_target_pairs={{0,3},{1,2},{2,1},{3,0},{4,7},{5,6},{6,5},{7,4},{8,11},{9,10},{10,... | collective-permute-start | bytes 393224 | tf_op jit(solution)/shard_map/ppermute | solution.py:18
  11.0 10.7 %copy-start.2 = (s32[16]{0:T(128)S(1)}, s32[16]{0:T(128)}, u32[]{:S(2)}) copy-start(s32[16]{0:T(128)} %length_ref.1) | copy-start | bytes 196
  11.0 10.7 %copy-start.3 = (s32[16]{0:T(128)S(1)}, s32[16]{0:T(128)}, u32[]{:S(2)}) copy-start(s32[16]{0:T(128)} %valid_ref.1) | copy-start | bytes 196
  13.9 3.4 %collective-permute-start.3 = (bf16[1,128,128]{2,1,0:T(8,128)(2,1)S(1)}, bf16[1,128,128]{2,1,0:T(8,128)(2,1)S(1)}, u32[]{:S(2)}, u32[]{:S(2)}) collective-permute-start(bf16[1,128,128]{2,1,0:T(8,128)(2,1)S(1)} %slice.65), channel_id=1, source_target_pairs={{0,5},{1,4},{2,7},{3,6},{4,1},{5,0},{6,3},{7,2},{8,13},{9,12},{10,... | collective-permute-start | bytes 98312 | tf_op jit(solution)/shard_map/ppermute | solution.py:18
  14.0 6.1 %collective-permute-start.5 = (f32[64,128]{1,0:T(8,128)S(1)}, f32[64,128]{1,0:T(8,128)S(1)}, u32[]{:S(2)}, u32[]{:S(2)}) collective-permute-start(f32[64,128]{1,0:T(8,128)S(1)} %shard_map.88), channel_id=1, source_target_pairs={{0,9},{1,8},{2,11},{3,10},{4,13},{5,12},{6,15},{7,14},{8,1},{9,0},... | collective-permute-start | bytes 98312 | tf_op jit(solution)/shard_map/ppermute | solution.py:18
  16.8 3.4 %collective-permute-start.7 = (bf16[32,4096]{1,0:T(8,128)(2,1)S(1)}, bf16[32,4096]{1,0:T(8,128)(2,1)S(1)}, u32[]{:S(2)}, u32[]{:S(2)}) collective-permute-start(bf16[32,4096]{1,0:T(8,128)(2,1)S(1)} %constant_dynamic-update-slice_fusion.refs_0_), channel_id=1, source_target_pairs={{0,1},{1,0},{2,3},{3,2},{4,5},{5,4},{6,7},{7,6},{8,9},{9,8},{10,11... | collective-permute-start | bytes 786440 | tf_op jit(solution)/shard_map/ppermute | solution.py:18
  17.4 4.4 %collective-permute-start.4 = (bf16[128,128]{1,0:T(8,128)(2,1)S(1)}, bf16[128,128]{1,0:T(8,128)(2,1)S(1)}, u32[]{:S(2)}, u32[]{:S(2)}) collective-permute-start(bf16[128,128]{1,0:T(8,128)(2,1)S(1)} %get-tuple-element.26), channel_id=1, source_target_pairs={{0,9},{1,8},{2,11},{3,10},{4,13},{5,12},{6,15},{7,14},{8,1},{9,0},... | collective-permute-start | bytes 98312 | tf_op jit(solution)/shard_map/ppermute | solution.py:18
  22.8 1.2 %collective-permute-start.8 = (f32[4,8,16]{2,1,0:T(8,128)S(1)}, f32[4,8,16]{2,1,0:T(8,128)S(1)}, u32[]{:S(2)}, u32[]{:S(2)}) collective-permute-start(f32[4,8,16]{2,1,0:T(8,128)S(1)} %slice.37), channel_id=1, source_target_pairs={{0,1},{1,0},{2,3},{3,2},{4,5},{5,4},{6,7},{7,6},{8,9},{9,8},{10,11... | collective-permute-start | bytes 6152 | tf_op jit(solution)/shard_map/ppermute | solution.py:18
  24.1 3.9 %collective-permute-start.9 = (f32[2,8,16]{2,1,0:T(8,128)S(1)}, f32[2,8,16]{2,1,0:T(8,128)S(1)}, u32[]{:S(2)}, u32[]{:S(2)}) collective-permute-start(f32[2,8,16]{2,1,0:T(8,128)S(1)} %slice.46), channel_id=1, source_target_pairs={{0,3},{1,2},{2,1},{3,0},{4,7},{5,6},{6,5},{7,4},{8,11},{9,10},{10,... | collective-permute-start | bytes 3080 | tf_op jit(solution)/shard_map/ppermute | solution.py:18
  25.5 4.2 %collective-permute-start.11 = (f32[64,128]{1,0:T(8,128)S(1)}, f32[64,128]{1,0:T(8,128)S(1)}, u32[]{:S(2)}, u32[]{:S(2)}) collective-permute-start(f32[64,128]{1,0:T(8,128)S(1)} %get-tuple-element.23), channel_id=1, source_target_pairs={{0,9},{1,8},{2,11},{3,10},{4,13},{5,12},{6,15},{7,14},{8,1},{9,0},... | collective-permute-start | bytes 98312 | tf_op jit(solution)/shard_map/ppermute | solution.py:18
  28.0 3.1 %collective-permute-start.10 = (f32[1,8,16]{2,1,0:T(8,128)S(1)}, f32[1,8,16]{2,1,0:T(8,128)S(1)}, u32[]{:S(2)}, u32[]{:S(2)}) collective-permute-start(f32[1,8,16]{2,1,0:T(8,128)S(1)} %slice.47), channel_id=1, source_target_pairs={{0,5},{1,4},{2,7},{3,6},{4,1},{5,0},{6,3},{7,2},{8,13},{9,12},{10,... | collective-permute-start | bytes 1544 | tf_op jit(solution)/shard_map/ppermute | solution.py:18

commit v16 on v14

--- a/solution.py
+++ b/solution.py
@@ -309,8 +309,7 @@
     got, sums = lax.optimization_barrier((got, sums))
     for k, bit in enumerate(middle):
         half = sums.shape[0] // 2
-        kind = jnp.bfloat16 if k == 0 else jnp.float32
-        sent = swap(sums[half:].astype(kind), bit, size)
+        sent = swap(sums[half:].astype(jnp.bfloat16), bit, size)
         sums = sums[:half] + sent.astype(jnp.float32)
         if k == 0:
             after = sums

time: 32.9 us -> 31.7 us (0.964)
  waiting for transfers between devices: 7.24 us -> 5.41 us
  starting transfers between devices: 15.5 us -> 16.1 us
    ppermute x12, waiting for transfers between devices: 7.24 us -> 5.41 us  [swap(): return lax.ppermute(value, 'seq', [(i, i ^ offset) for i in range(size)])]
    ppermute x12, starting transfers between devices: 15.5 us -> 16.1 us  [swap(): return lax.ppermute(value, 'seq', [(i, i ^ offset) for i in range(size)])]
  transfers between devices with their start and end apart: 12 -> 12, of which waited for: 6 -> 6; matrix products, arithmetic and copies ran while one was open for 3% -> 3% of each run, Pallas kernels for 20% -> 21%
where the time goes in v16:
time: 31.7 us; the launch traced here: 31.6 us
  starting transfers between devices  16.1 us (51%)
  Pallas kernels  7.59 us (24%)
  waiting for transfers between devices  5.41 us (17%)
  matrix products  0.88 us (3%)
  between operations  0.79 us (2%)
  other arithmetic  0.68 us (2%)
    ppermute x12, starting transfers between devices, swap(): return lax.ppermute(value, 'seq', [(i, i ^ offset) for i in range(size)])  16.1 us
    ppermute x12, waiting for transfers between devices, swap(): return lax.ppermute(value, 'seq', [(i, i ^ offset) for i in range(size)])  5.41 us
    pallas_call x1, Pallas kernels, grad_blocks(): pl.pallas_call(functools.partial(grad_kernel, offsets), in_specs=[SMEM, H...  3.96 us
    pallas_call x1, Pallas kernels, grad_blocks(): pl.pallas_call(functools.partial(held_kernel, offsets), in_specs=[SMEM, V...  1.11 us
    pallas_call x1, Pallas kernels, score(): pl.pallas_call(functools.partial(score_kernel, steps, split), out_shape=(...  1.08 us
    dot_general x1, matrix products, body(): lax.dot_general(late, activations, (((0,), (1,)), ((), ())), preferred_el...  0.88 us
    pallas_call x1, Pallas kernels, place_tokens(): pl.pallas_call(functools.partial(place_kernel, place, split), in_specs=[S...  0.74 us
    pallas_call x1, Pallas kernels, inner(): pl.pallas_call(functools.partial(inner_kernel, len(panels)), out_shape=ja...  0.71 us
  transfers between devices with their start and end apart: 12, of which 6 were waited for; matrix products, arithmetic and copies ran while one was open for 3% of the time, Pallas kernels for 21%

profile of v16, /device:TPU:0, one launch (start us, length us, event | category | flops | bytes accessed | tf_op | source)
XLA Modules:
  0.0 31.6 jit_solution(10388758221796539953)
XLA Ops:
  0.6 0.0 copy-start
  0.6 2.5 %collective-permute-start = (bf16[8,4096]{1,0:T(8,128)(2,1)}, bf16[8,4096]{1,0:T(8,128)(2,1)S(1)}, u32[]{:S(2)}, u32[]{:S(2)}) collective-permute-start(bf16[8,4096]{1,0:T(8,128)(2,1)} %param.11), channel_id=1, source_target_pairs={{0,5},{1,4},{2,7},{3,6},{4,1},{5,0},{6,3},{7,2},{8,13},{9,12},{10,... | collective-permute-start | bytes 196616 | tf_op jit(solution)/shard_map/ppermute | solution.py:18
  3.2 0.0 copy-start.5
  3.2 0.0 copy-start.1
  3.2 4.0 %shard_map.86 = (f32[4,128,128]{2,1,0:T(8,128)S(1)}, bf16[2,1792,128]{2,1,0:T(8,128)(2,1)S(1)}) custom-call(s32[1]{0:T(128)} %bitcast.me_ref, bf16[64,1792]{1,0:T(8,128)(2,1)} %bitcast.17, bf16[2048,1792]{1,0:T(8,128)(2,1)} %grads_ref.3), custom_call_target="tpu_custom_call" | custom-call | flops 234881024 | bytes 3670016 | tf_op jit(solution)/shard_map/pallas_call | solution.py:93
  7.1 0.7 %collective-permute-start.1 = (f32[4,128,128]{2,1,0:T(8,128)S(1)}, f32[4,128,128]{2,1,0:T(8,128)S(1)}, u32[]{:S(2)}, u32[]{:S(2)}) collective-permute-start(f32[4,128,128]{2,1,0:T(8,128)S(1)} %get-tuple-element.15), channel_id=1, source_target_pairs={{0,1},{1,0},{2,3},{3,2},{4,5},{5,4},{6,7},{7,6},{8,9},{9,8},{10,11... | collective-permute-start | bytes 786440 | tf_op jit(solution)/shard_map/ppermute | solution.py:18
  7.9 0.0 copy-done.5
  7.9 0.0 copy-done.1
  7.9 0.0 copy-start.4
  7.9 1.1 %shard_map.87 = f32[4,128,128]{2,1,0:T(8,128)S(1)} custom-call(s32[1]{0:T(128)} %bitcast.me_ref, bf16[2,1792,128]{2,1,0:T(8,128)(2,1)S(1)} %get-tuple-element.14.table, bf16[2048,1792]{1,0:T(8,128)(2,1)S(1)} %copy-done.1), custom_call_target="tpu_custom_call" | custom-call | flops 234881024 | bytes 3670016 | tf_op jit(solution)/shard_map/pallas_call | solution.py:86
  9.0 0.0 collective-permute-done.1
  9.1 0.0 collective-permute-done
  9.1 1.6 %collective-permute-start.2 = (bf16[2,128,128]{2,1,0:T(8,128)(2,1)S(1)}, bf16[2,128,128]{2,1,0:T(8,128)(2,1)S(1)}, u32[]{:S(2)}, u32[]{:S(2)}) collective-permute-start(bf16[2,128,128]{2,1,0:T(8,128)(2,1)S(1)} %slice.64), channel_id=1, source_target_pairs={{0,3},{1,2},{2,1},{3,0},{4,7},{5,6},{6,5},{7,4},{8,11},{9,10},{10,... | collective-permute-start | bytes 196616 | tf_op jit(solution)/shard_map/ppermute | solution.py:18
  10.7 0.3 %collective-permute-start.6 = (bf16[16,4096]{1,0:T(8,128)(2,1)S(1)}, bf16[16,4096]{1,0:T(8,128)(2,1)S(1)}, u32[]{:S(2)}, u32[]{:S(2)}) collective-permute-start(bf16[16,4096]{1,0:T(8,128)(2,1)S(1)} %pad_maximum_fusion), channel_id=1, source_target_pairs={{0,3},{1,2},{2,1},{3,0},{4,7},{5,6},{6,5},{7,4},{8,11},{9,10},{10,... | collective-permute-start | bytes 393224 | tf_op jit(solution)/shard_map/ppermute | solution.py:18
  11.0 0.0 copy-done
  11.0 0.0 copy-done.4
  11.0 0.9 %fusion.6 = f32[64,128]{1,0:T(8,128)S(1)} fusion(bf16[8192,64]{0,1:T(8,128)(2,1)S(1)} %copy-done.4, bf16[128,8192]{1,0:T(8,128)(2,1)S(1)} %copy-done), kind=kOutput, calls=%fused_computation.18 | convolution fusion | flops 134217728 | bytes 3178496 | tf_op jit(solution)/shard_map/dot_general | solution.py:318
  11.9 1.2 %collective-permute-done.2 = bf16[2,128,128]{2,1,0:T(8,128)(2,1)S(1)} collective-permute-done((bf16[2,128,128]{2,1,0:T(8,128)(2,1)S(1)}, bf16[2,128,128]{2,1,0:T(8,128)(2,1)S(1)}, u32[]{:S(2)}, u32[]{:S(2)}) %collective-permute-start.2) | collective-permute-done | bytes 65568 | tf_op jit(solution)/shard_map/ppermute | solution.py:18
  13.1 0.3 collective-permute-start.3
  13.4 2.6 %collective-permute-start.5 = (f32[64,128]{1,0:T(8,128)S(1)}, f32[64,128]{1,0:T(8,128)S(1)}, u32[]{:S(2)}, u32[]{:S(2)}) collective-permute-start(f32[64,128]{1,0:T(8,128)S(1)} %fusion.6), channel_id=1, source_target_pairs={{0,9},{1,8},{2,11},{3,10},{4,13},{5,12},{6,15},{7,14},{8,1},{9,0},... | collective-permute-start | bytes 98312 | tf_op jit(solution)/shard_map/ppermute | solution.py:18
  16.0 0.3 collective-permute-done.6
  16.2 0.5 %collective-permute-start.7 = (bf16[32,4096]{1,0:T(8,128)(2,1)S(1)}, bf16[32,4096]{1,0:T(8,128)(2,1)S(1)}, u32[]{:S(2)}, u32[]{:S(2)}) collective-permute-start(bf16[32,4096]{1,0:T(8,128)(2,1)S(1)} %constant_dynamic-update-slice_fusion.refs_0_), channel_id=1, source_target_pairs={{0,1},{1,0},{2,3},{3,2},{4,5},{5,4},{6,7},{7,6},{8,9},{9,8},{10,11... | collective-permute-start | bytes 786440 | tf_op jit(solution)/shard_map/ppermute | solution.py:18
  16.7 0.0 collective-permute-done.3
  16.8 2.6 %collective-permute-start.4 = (bf16[128,128]{1,0:T(8,128)(2,1)S(1)}, bf16[128,128]{1,0:T(8,128)(2,1)S(1)}, u32[]{:S(2)}, u32[]{:S(2)}) collective-permute-start(bf16[128,128]{1,0:T(8,128)(2,1)S(1)} %get-tuple-element.26), channel_id=1, source_target_pairs={{0,9},{1,8},{2,11},{3,10},{4,13},{5,12},{6,15},{7,14},{8,1},{9,0},... | collective-permute-start | bytes 98312 | tf_op jit(solution)/shard_map/ppermute | solution.py:18
  19.3 0.0 collective-permute-done.5
  19.4 0.0 copy-start.2
  19.4 0.0 copy-start.3
  19.4 0.0 collective-permute-done.7.refs_1_
  19.4 0.7 %shard_map.88.inner_ref = f32[2048,512]{1,0:T(8,128)S(1)} custom-call(f32[2,64,128]{2,1,0:T(8,128)S(1)} %pad_maximum_fusion.1.act_ref, bf16[32,4096]{1,0:T(8,128)(2,1)S(1)} %constant_dynamic-update-slice_fusion.refs_0_, bf16[32,4096]{1,0:T(8,128)(2,1)S(1)} %collective-permute-done.7.refs_1_), custom_call_target="tpu_custom_call" | custom-call | flops 536870912 | bytes 4194304 | tf_op jit(solution)/shard_map/pallas_call | solution.py:147
  20.1 1.0 %collective-permute-done.4.other_ref = bf16[128,128]{1,0:T(8,128)(2,1)S(1)} collective-permute-done((bf16[128,128]{1,0:T(8,128)(2,1)S(1)}, bf16[128,128]{1,0:T(8,128)(2,1)S(1)}, u32[]{:S(2)}, u32[]{:S(2)}) %collective-permute-start.4) | collective-permute-done | bytes 32800 | tf_op jit(solution)/shard_map/ppermute | solution.py:18
  21.1 0.0 copy-done.2
  21.1 0.0 copy-done.3
  21.1 1.1 %shard_map.89 = (f32[64,128]{1,0:T(8,128)S(1)}, f32[64,128]{1,0:T(8,128)S(1)}, f32[8,8,16]{2,1,0:T(8,128)S(1)}) custom-call(s32[1]{0:T(128)} %bitcast.me_ref, s32[16]{0:T(128)S(1)} %copy-done.2, s32[16]{0:T(128)S(1)} %copy-done.3, f32[128,128]{1,0:T(8,128)S(1)} %get-tuple-element.27.own_ref, bf16[128,128]{1,0:T(8,128)(2,1)S(1)} %collective-permute-done.4.other_ref, ...), custom_call_target="tpu_custom_call" | custom-call | flops 2097152 | bytes 4194304 | tf_op jit(solution)/shard_map/pallas_call | solution.py:247
  22.2 0.2 collective-permute-start.8
  22.4 1.1 %collective-permute-done.8 = f32[4,8,16]{2,1,0:T(8,128)S(1)} collective-permute-done((f32[4,8,16]{2,1,0:T(8,128)S(1)}, f32[4,8,16]{2,1,0:T(8,128)S(1)}, u32[]{:S(2)}, u32[]{:S(2)}) %collective-permute-start.8) | collective-permute-done | bytes 2080 | tf_op jit(solution)/shard_map/ppermute | solution.py:18
  23.5 1.9 %collective-permute-start.9 = (f32[2,8,16]{2,1,0:T(8,128)S(1)}, f32[2,8,16]{2,1,0:T(8,128)S(1)}, u32[]{:S(2)}, u32[]{:S(2)}) collective-permute-start(f32[2,8,16]{2,1,0:T(8,128)S(1)} %slice.46), channel_id=1, source_target_pairs={{0,3},{1,2},{2,1},{3,0},{4,7},{5,6},{6,5},{7,4},{8,11},{9,10},{10,... | collective-permute-start | bytes 3080 | tf_op jit(solution)/shard_map/ppermute | solution.py:18
  25.4 2.5 %collective-permute-start.11 = (f32[64,128]{1,0:T(8,128)S(1)}, f32[64,128]{1,0:T(8,128)S(1)}, u32[]{:S(2)}, u32[]{:S(2)}) collective-permute-start(f32[64,128]{1,0:T(8,128)S(1)} %get-tuple-element.23), channel_id=1, source_target_pairs={{0,9},{1,8},{2,11},{3,10},{4,13},{5,12},{6,15},{7,14},{8,1},{9,0},... | collective-permute-start | bytes 98312 | tf_op jit(solution)/shard_map/ppermute | solution.py:18
  27.9 0.0 collective-permute-done.9
  27.9 0.5 %collective-permute-start.10 = (f32[1,8,16]{2,1,0:T(8,128)S(1)}, f32[1,8,16]{2,1,0:T(8,128)S(1)}, u32[]{:S(2)}, u32[]{:S(2)}) collective-permute-start(f32[1,8,16]{2,1,0:T(8,128)S(1)} %slice.47), channel_id=1, source_target_pairs={{0,5},{1,4},{2,7},{3,6},{4,1},{5,0},{6,3},{7,2},{8,13},{9,12},{10,... | collective-permute-start | bytes 1544 | tf_op jit(solution)/shard_map/ppermute | solution.py:18
  28.4 1.2 %collective-permute-done.11.other_ref = f32[64,128]{1,0:T(8,128)S(1)} collective-permute-done((f32[64,128]{1,0:T(8,128)S(1)}, f32[64,128]{1,0:T(8,128)S(1)}, u32[]{:S(2)}, u32[]{:S(2)}) %collective-permute-start.11) | collective-permute-done | bytes 32800 | tf_op jit(solution)/shard_map/ppermute | solution.py:18
  29.7 0.7 %shard_map.90 = f32[128,128]{1,0:T(8,128)} custom-call(s32[1]{0:T(128)} %bitcast.me_ref, f32[64,128]{1,0:T(8,128)S(1)} %get-tuple-element.22.own_ref, f32[64,128]{1,0:T(8,128)S(1)} %collective-permute-done.11.other_ref), custom_call_target="tpu_custom_call" | custom-call | tf_op jit(solution)/shard_map/pallas_call | solution.py:276
  30.4 0.6 %collective-permute-done.10 = f32[1,8,16]{2,1,0:T(8,128)S(1)} collective-permute-done((f32[1,8,16]{2,1,0:T(8,128)S(1)}, f32[1,8,16]{2,1,0:T(8,128)S(1)}, u32[]{:S(2)}, u32[]{:S(2)}) %collective-permute-start.10) | collective-permute-done | bytes 544 | tf_op jit(solution)/shard_map/ppermute | solution.py:18
  31.0 0.6 %fusion.3 = f32[16,8]{0,1:T(8,128)} fusion(f32[1,8,16]{2,1,0:T(8,128)S(1)} %collective-permute-done.10, f32[2,8,16]{2,1,0:T(8,128)S(1)} %slice_add_fusion.2, f32[16]{0:T(128)S(1)} %convert_rsqrt_fusion), kind=kLoop, calls=%fused_computation.15 | loop fusion | flops 256 | bytes 1600 | tf_op jit(solution)/shard_map/transpose | solution.py:347
  (16 shorter events, 0.1 us)
Async XLA Ops:
  0.6 10.4 %copy-start = (bf16[128,8192]{1,0:T(8,128)(2,1)S(1)}, bf16[128,8192]{1,0:T(8,128)(2,1)}, u32[]{:S(2)}) copy-start(bf16[128,8192]{1,0:T(8,128)(2,1)} %param.7) | copy-start | bytes 6291460
  0.6 8.4 %collective-permute-start = (bf16[8,4096]{1,0:T(8,128)(2,1)}, bf16[8,4096]{1,0:T(8,128)(2,1)S(1)}, u32[]{:S(2)}, u32[]{:S(2)}) collective-permute-start(bf16[8,4096]{1,0:T(8,128)(2,1)} %param.11), channel_id=1, source_target_pairs={{0,5},{1,4},{2,7},{3,6},{4,1},{5,0},{6,3},{7,2},{8,13},{9,12},{10,... | collective-permute-start | bytes 196616 | tf_op jit(solution)/shard_map/ppermute | solution.py:18
  3.2 4.7 %copy-start.5 = (bf16[8,4096]{1,0:T(8,128)(2,1)S(1)}, bf16[8,4096]{1,0:T(8,128)(2,1)}, u32[]{:S(2)}) copy-start(bf16[8,4096]{1,0:T(8,128)(2,1)} %param.11) | copy-start | bytes 196612
  3.2 4.7 %copy-start.1 = (bf16[2048,1792]{1,0:T(8,128)(2,1)S(1)}, bf16[2048,1792]{1,0:T(8,128)(2,1)}, u32[]{:S(2)}) copy-start(bf16[2048,1792]{1,0:T(8,128)(2,1)} %grads_ref.3) | copy-start | bytes 22020100
  7.1 1.9 %collective-permute-start.1 = (f32[4,128,128]{2,1,0:T(8,128)S(1)}, f32[4,128,128]{2,1,0:T(8,128)S(1)}, u32[]{:S(2)}, u32[]{:S(2)}) collective-permute-start(f32[4,128,128]{2,1,0:T(8,128)S(1)} %get-tuple-element.15), channel_id=1, source_target_pairs={{0,1},{1,0},{2,3},{3,2},{4,5},{5,4},{6,7},{7,6},{8,9},{9,8},{10,11... | collective-permute-start | bytes 786440 | tf_op jit(solution)/shard_map/ppermute | solution.py:18
  7.9 3.1 %copy-start.4 = (bf16[8192,64]{0,1:T(8,128)(2,1)S(1)}, bf16[8192,64]{0,1:T(8,128)(2,1)}, u32[]{:S(2)}) copy-start(bf16[8192,64]{0,1:T(8,128)(2,1)} %param.9) | copy-start | bytes 3145732
  9.1 4.0 %collective-permute-start.2 = (bf16[2,128,128]{2,1,0:T(8,128)(2,1)S(1)}, bf16[2,128,128]{2,1,0:T(8,128)(2,1)S(1)}, u32[]{:S(2)}, u32[]{:S(2)}) collective-permute-start(bf16[2,128,128]{2,1,0:T(8,128)(2,1)S(1)} %slice.64), channel_id=1, source_target_pairs={{0,3},{1,2},{2,1},{3,0},{4,7},{5,6},{6,5},{7,4},{8,11},{9,10},{10,... | collective-permute-start | bytes 196616 | tf_op jit(solution)/shard_map/ppermute | solution.py:18
  10.7 5.5 %collective-permute-start.6 = (bf16[16,4096]{1,0:T(8,128)(2,1)S(1)}, bf16[16,4096]{1,0:T(8,128)(2,1)S(1)}, u32[]{:S(2)}, u32[]{:S(2)}) collective-permute-start(bf16[16,4096]{1,0:T(8,128)(2,1)S(1)} %pad_maximum_fusion), channel_id=1, source_target_pairs={{0,3},{1,2},{2,1},{3,0},{4,7},{5,6},{6,5},{7,4},{8,11},{9,10},{10,... | collective-permute-start | bytes 393224 | tf_op jit(solution)/shard_map/ppermute | solution.py:18
  13.1 3.6 %collective-permute-start.3 = (bf16[1,128,128]{2,1,0:T(8,128)(2,1)S(1)}, bf16[1,128,128]{2,1,0:T(8,128)(2,1)S(1)}, u32[]{:S(2)}, u32[]{:S(2)}) collective-permute-start(bf16[1,128,128]{2,1,0:T(8,128)(2,1)S(1)} %slice.65), channel_id=1, source_target_pairs={{0,5},{1,4},{2,7},{3,6},{4,1},{5,0},{6,3},{7,2},{8,13},{9,12},{10,... | collective-permute-start | bytes 98312 | tf_op jit(solution)/shard_map/ppermute | solution.py:18
  13.4 5.9 %collective-permute-start.5 = (f32[64,128]{1,0:T(8,128)S(1)}, f32[64,128]{1,0:T(8,128)S(1)}, u32[]{:S(2)}, u32[]{:S(2)}) collective-permute-start(f32[64,128]{1,0:T(8,128)S(1)} %fusion.6), channel_id=1, source_target_pairs={{0,9},{1,8},{2,11},{3,10},{4,13},{5,12},{6,15},{7,14},{8,1},{9,0},... | collective-permute-start | bytes 98312 | tf_op jit(solution)/shard_map/ppermute | solution.py:18
  16.2 3.1 %collective-permute-start.7 = (bf16[32,4096]{1,0:T(8,128)(2,1)S(1)}, bf16[32,4096]{1,0:T(8,128)(2,1)S(1)}, u32[]{:S(2)}, u32[]{:S(2)}) collective-permute-start(bf16[32,4096]{1,0:T(8,128)(2,1)S(1)} %constant_dynamic-update-slice_fusion.refs_0_), channel_id=1, source_target_pairs={{0,1},{1,0},{2,3},{3,2},{4,5},{5,4},{6,7},{7,6},{8,9},{9,8},{10,11... | collective-permute-start | bytes 786440 | tf_op jit(solution)/shard_map/ppermute | solution.py:18
  16.8 4.4 %collective-permute-start.4 = (bf16[128,128]{1,0:T(8,128)(2,1)S(1)}, bf16[128,128]{1,0:T(8,128)(2,1)S(1)}, u32[]{:S(2)}, u32[]{:S(2)}) collective-permute-start(bf16[128,128]{1,0:T(8,128)(2,1)S(1)} %get-tuple-element.26), channel_id=1, source_target_pairs={{0,9},{1,8},{2,11},{3,10},{4,13},{5,12},{6,15},{7,14},{8,1},{9,0},... | collective-permute-start | bytes 98312 | tf_op jit(solution)/shard_map/ppermute | solution.py:18
  19.4 1.8 %copy-start.2 = (s32[16]{0:T(128)S(1)}, s32[16]{0:T(128)}, u32[]{:S(2)}) copy-start(s32[16]{0:T(128)} %length_ref.1) | copy-start | bytes 196
  19.4 1.8 %copy-start.3 = (s32[16]{0:T(128)S(1)}, s32[16]{0:T(128)}, u32[]{:S(2)}) copy-start(s32[16]{0:T(128)} %valid_ref.1) | copy-start | bytes 196
  22.2 1.2 %collective-permute-start.8 = (f32[4,8,16]{2,1,0:T(8,128)S(1)}, f32[4,8,16]{2,1,0:T(8,128)S(1)}, u32[]{:S(2)}, u32[]{:S(2)}) collective-permute-start(f32[4,8,16]{2,1,0:T(8,128)S(1)} %slice.37), channel_id=1, source_target_pairs={{0,1},{1,0},{2,3},{3,2},{4,5},{5,4},{6,7},{7,6},{8,9},{9,8},{10,11... | collective-permute-start | bytes 6152 | tf_op jit(solution)/shard_map/ppermute | solution.py:18
  23.5 4.4 %collective-permute-start.9 = (f32[2,8,16]{2,1,0:T(8,128)S(1)}, f32[2,8,16]{2,1,0:T(8,128)S(1)}, u32[]{:S(2)}, u32[]{:S(2)}) collective-permute-start(f32[2,8,16]{2,1,0:T(8,128)S(1)} %slice.46), channel_id=1, source_target_pairs={{0,3},{1,2},{2,1},{3,0},{4,7},{5,6},{6,5},{7,4},{8,11},{9,10},{10,... | collective-permute-start | bytes 3080 | tf_op jit(solution)/shard_map/ppermute | solution.py:18
  25.4 4.2 %collective-permute-start.11 = (f32[64,128]{1,0:T(8,128)S(1)}, f32[64,128]{1,0:T(8,128)S(1)}, u32[]{:S(2)}, u32[]{:S(2)}) collective-permute-start(f32[64,128]{1,0:T(8,128)S(1)} %get-tuple-element.23), channel_id=1, source_target_pairs={{0,9},{1,8},{2,11},{3,10},{4,13},{5,12},{6,15},{7,14},{8,1},{9,0},... | collective-permute-start | bytes 98312 | tf_op jit(solution)/shard_map/ppermute | solution.py:18
  27.9 3.1 %collective-permute-start.10 = (f32[1,8,16]{2,1,0:T(8,128)S(1)}, f32[1,8,16]{2,1,0:T(8,128)S(1)}, u32[]{:S(2)}, u32[]{:S(2)}) collective-permute-start(f32[1,8,16]{2,1,0:T(8,128)S(1)} %slice.47), channel_id=1, source_target_pairs={{0,5},{1,4},{2,7},{3,6},{4,1},{5,0},{6,3},{7,2},{8,13},{9,12},{10,... | collective-permute-start | bytes 1544 | tf_op jit(solution)/shard_map/ppermute | solution.py:18

commit v17 on v16

--- a/solution.py
+++ b/solution.py
@@ -262,25 +262,47 @@
     )(me, lengths, valid, own, other, products)
 
 
-def place_kernel(place, split, me_ref, own_ref, other_ref, out_ref, turned_ref):
-    own_q = own_ref.shape[0] // len(place)
+def last_kernel(
+    place, split, me_ref, length_ref, valid_ref, own_ref, other_ref, doc_ref, more_ref,
+    token_out, doc_out, turned_ref, token_buf, doc_buf, sems,
+):
+    own_q, docs = doc_buf.shape
     for r, ref in enumerate((own_ref, other_ref)):
         for k, offset in enumerate(place):
             spot = pl.multiple_of((me_ref[0] ^ offset ^ (split * r)) * own_q, own_q)
             turned_ref[pl.ds(spot, own_q)] = ref[k * own_q : (k + 1) * own_q]
-    out_ref[...] = turned_ref[...].T
-
-
-def place_tokens(me, own, other, place, split):
+    token_buf[...] = turned_ref[...].T
+    tokens = pltpu.make_async_copy(token_buf, token_out, sems.at[0])
+    tokens.start()
+    doc_of = lax.broadcasted_iota(jnp.int32, (own_q, docs), 1)
+    used = jnp.zeros((own_q, docs), jnp.int32)
+    for d in range(docs):
+        used = jnp.where(doc_of == d, jnp.minimum(valid_ref[d], length_ref[d]), used)
+    doc_buf[...] = (doc_ref[0] + more_ref[0]) * (1.0 / jnp.sqrt(used.astype(jnp.float32)))
+    scores = pltpu.make_async_copy(doc_buf, doc_out, sems.at[1])
+    scores.start()
+    tokens.wait()
+    scores.wait()
+
+
+def last(me, lengths, valid, own, other, doc, more, place, split):
     count, rows = own.shape
+    _, own_q, docs = doc.shape
+    tokens = jax.ShapeDtypeStruct((rows, 2 * count), jnp.float32)
+    scores = jax.ShapeDtypeStruct((own_q, docs), jnp.float32)
     return pl.pallas_call(
-        functools.partial(place_kernel, place, split),
-        in_specs=[SMEM, VMEM, VMEM],
-        out_specs=VMEM,
-        out_shape=jax.ShapeDtypeStruct((rows, 2 * count), jnp.float32),
-        scratch_shapes=[pltpu.VMEM((2 * count, rows), jnp.float32)],
+        functools.partial(last_kernel, place, split),
+        in_specs=[SMEM] * 3 + [VMEM] * 4,
+        out_specs=(HBM, HBM),
+        out_shape=(tokens, scores),
+        scratch_shapes=[
+            pltpu.VMEM((2 * count, rows), jnp.float32),
+            pltpu.VMEM(tokens.shape, jnp.float32),
+            pltpu.VMEM(scores.shape, jnp.float32),
+            pltpu.SemaphoreType.DMA((2,)),
+        ],
         compiler_params=pltpu.CompilerParams(vmem_limit_bytes=16 * MIB),
-    )(me, own, other)
+    )(me, lengths, valid, own, other, doc, more)
 
 
 def offset_of(number, bits):
@@ -341,10 +363,10 @@
         half = doc.shape[0] // 2
         doc = doc[:half] + swap(doc[half:], bit, size)
     more = swap(doc[1:], bits[-1], size)
-    token_scores = place_tokens(me, mine, others, place, split)
-    more, token_scores = lax.optimization_barrier((more, token_scores))
-    scale = 1.0 / jnp.sqrt(jnp.minimum(valid_count, doc_length).astype(jnp.float32))
-    return (token_scores, ((doc[0] + more[0]) * scale[None, :]).T)
+    token_scores, doc = last(
+        me, doc_length, valid_count, mine, others, doc[:1], more, place, split
+    )
+    return (token_scores, doc.T)
 
 
 def solution(mesh):

time: 31.7 us -> 32.5 us (1.025)
  other arithmetic: 0.68 us -> 0.08 us
  Pallas kernels: 7.59 us -> 8.16 us
  waiting for transfers between devices: 5.41 us -> 5.96 us
    transpose x1 -> x0, other arithmetic: 0.6 us -> none  [body(): return (token_scores, ((doc[0] + more[0]) * scale[None, :]).T)]
    pallas_call x1, Pallas kernels: 0.74 us -> 1.31 us  [last(): pl.pallas_call(functools.partial(last_kernel, place, split), in_specs=[SM...]
    ppermute x12, waiting for transfers between devices: 5.41 us -> 5.96 us  [swap(): return lax.ppermute(value, 'seq', [(i, i ^ offset) for i in range(size)])]
  transfers between devices with their start and end apart: 12 -> 12, of which waited for: 6 -> 5; matrix products, arithmetic and copies ran while one was open for 3% -> 3% of each run, Pallas kernels for 21% -> 18%
where the time goes in v17:
time: 32.5 us; the launch traced here: 32.3 us
  starting transfers between devices  16.4 us (50%)
  Pallas kernels  8.16 us (25%)
  waiting for transfers between devices  5.96 us (18%)
  matrix products  0.88 us (3%)
  between operations  0.8 us (2%)
    ppermute x12, starting transfers between devices, swap(): return lax.ppermute(value, 'seq', [(i, i ^ offset) for i in range(size)])  16.4 us
    ppermute x12, waiting for transfers between devices, swap(): return lax.ppermute(value, 'seq', [(i, i ^ offset) for i in range(size)])  5.96 us
    pallas_call x1, Pallas kernels, grad_blocks(): pl.pallas_call(functools.partial(grad_kernel, offsets), in_specs=[SMEM, H...  3.96 us
    pallas_call x1, Pallas kernels, last(): pl.pallas_call(functools.partial(last_kernel, place, split), in_specs=[SM...  1.31 us
    pallas_call x1, Pallas kernels, grad_blocks(): pl.pallas_call(functools.partial(held_kernel, offsets), in_specs=[SMEM, V...  1.11 us
    pallas_call x1, Pallas kernels, score(): pl.pallas_call(functools.partial(score_kernel, steps, split), out_shape=(...  1.08 us
    dot_general x1, matrix products, body(): lax.dot_general(late, activations, (((0,), (1,)), ((), ())), preferred_el...  0.88 us
    pallas_call x1, Pallas kernels, inner(): pl.pallas_call(functools.partial(inner_kernel, len(panels)), out_shape=ja...  0.71 us
  transfers between devices with their start and end apart: 12, of which 5 were waited for; matrix products, arithmetic and copies ran while one was open for 3% of the time, Pallas kernels for 18%

profile of v17, /device:TPU:0, one launch (start us, length us, event | category | flops | bytes accessed | tf_op | source)
XLA Modules:
  0.0 32.3 jit_solution(10212145928519418000)
XLA Ops:
  0.6 0.0 copy-start
  0.6 2.5 %collective-permute-start = (bf16[8,4096]{1,0:T(8,128)(2,1)}, bf16[8,4096]{1,0:T(8,128)(2,1)S(1)}, u32[]{:S(2)}, u32[]{:S(2)}) collective-permute-start(bf16[8,4096]{1,0:T(8,128)(2,1)} %param.11), channel_id=1, source_target_pairs={{0,5},{1,4},{2,7},{3,6},{4,1},{5,0},{6,3},{7,2},{8,13},{9,12},{10,... | collective-permute-start | bytes 196616 | tf_op jit(solution)/shard_map/ppermute | solution.py:18
  3.2 0.0 copy-start.5
  3.2 0.0 copy-start.1
  3.2 4.0 %shard_map.86 = (f32[4,128,128]{2,1,0:T(8,128)S(1)}, bf16[2,1792,128]{2,1,0:T(8,128)(2,1)S(1)}) custom-call(s32[1]{0:T(128)} %bitcast.me_ref, bf16[64,1792]{1,0:T(8,128)(2,1)} %bitcast.10, bf16[2048,1792]{1,0:T(8,128)(2,1)} %grads_ref.3), custom_call_target="tpu_custom_call" | custom-call | flops 234881024 | bytes 3670016 | tf_op jit(solution)/shard_map/pallas_call | solution.py:93
  7.1 0.7 %collective-permute-start.1 = (f32[4,128,128]{2,1,0:T(8,128)S(1)}, f32[4,128,128]{2,1,0:T(8,128)S(1)}, u32[]{:S(2)}, u32[]{:S(2)}) collective-permute-start(f32[4,128,128]{2,1,0:T(8,128)S(1)} %get-tuple-element.15), channel_id=1, source_target_pairs={{0,1},{1,0},{2,3},{3,2},{4,5},{5,4},{6,7},{7,6},{8,9},{9,8},{10,11... | collective-permute-start | bytes 786440 | tf_op jit(solution)/shard_map/ppermute | solution.py:18
  7.9 0.0 copy-done.5
  7.9 0.0 copy-done.1
  7.9 0.0 copy-start.4
  7.9 1.1 %shard_map.87 = f32[4,128,128]{2,1,0:T(8,128)S(1)} custom-call(s32[1]{0:T(128)} %bitcast.me_ref, bf16[2,1792,128]{2,1,0:T(8,128)(2,1)S(1)} %get-tuple-element.14.table, bf16[2048,1792]{1,0:T(8,128)(2,1)S(1)} %copy-done.1), custom_call_target="tpu_custom_call" | custom-call | flops 234881024 | bytes 3670016 | tf_op jit(solution)/shard_map/pallas_call | solution.py:86
  9.0 0.0 collective-permute-done.1
  9.1 0.0 collective-permute-done
  9.1 1.6 %collective-permute-start.2 = (bf16[2,128,128]{2,1,0:T(8,128)(2,1)S(1)}, bf16[2,128,128]{2,1,0:T(8,128)(2,1)S(1)}, u32[]{:S(2)}, u32[]{:S(2)}) collective-permute-start(bf16[2,128,128]{2,1,0:T(8,128)(2,1)S(1)} %slice.57), channel_id=1, source_target_pairs={{0,3},{1,2},{2,1},{3,0},{4,7},{5,6},{6,5},{7,4},{8,11},{9,10},{10,... | collective-permute-start | bytes 196616 | tf_op jit(solution)/shard_map/ppermute | solution.py:18
  10.7 0.3 collective-permute-start.6
  11.0 0.0 copy-done
  11.0 0.0 copy-done.4
  11.0 0.9 %fusion.4 = f32[64,128]{1,0:T(8,128)S(1)} fusion(bf16[8192,64]{0,1:T(8,128)(2,1)S(1)} %copy-done.4, bf16[128,8192]{1,0:T(8,128)(2,1)S(1)} %copy-done), kind=kOutput, calls=%fused_computation.14 | convolution fusion | flops 134217728 | bytes 3178496 | tf_op jit(solution)/shard_map/dot_general | solution.py:340
  11.9 1.3 %collective-permute-done.2 = bf16[2,128,128]{2,1,0:T(8,128)(2,1)S(1)} collective-permute-done((bf16[2,128,128]{2,1,0:T(8,128)(2,1)S(1)}, bf16[2,128,128]{2,1,0:T(8,128)(2,1)S(1)}, u32[]{:S(2)}, u32[]{:S(2)}) %collective-permute-start.2) | collective-permute-done | bytes 65568 | tf_op jit(solution)/shard_map/ppermute | solution.py:18
  13.2 0.2 collective-permute-start.3
  13.4 2.6 %collective-permute-start.5 = (f32[64,128]{1,0:T(8,128)S(1)}, f32[64,128]{1,0:T(8,128)S(1)}, u32[]{:S(2)}, u32[]{:S(2)}) collective-permute-start(f32[64,128]{1,0:T(8,128)S(1)} %fusion.4), channel_id=1, source_target_pairs={{0,9},{1,8},{2,11},{3,10},{4,13},{5,12},{6,15},{7,14},{8,1},{9,0},... | collective-permute-start | bytes 98312 | tf_op jit(solution)/shard_map/ppermute | solution.py:18
  16.0 0.2 collective-permute-done.6
  16.2 0.5 %collective-permute-start.7 = (bf16[32,4096]{1,0:T(8,128)(2,1)S(1)}, bf16[32,4096]{1,0:T(8,128)(2,1)S(1)}, u32[]{:S(2)}, u32[]{:S(2)}) collective-permute-start(bf16[32,4096]{1,0:T(8,128)(2,1)S(1)} %constant_dynamic-update-slice_fusion.refs_0_), channel_id=1, source_target_pairs={{0,1},{1,0},{2,3},{3,2},{4,5},{5,4},{6,7},{7,6},{8,9},{9,8},{10,11... | collective-permute-start | bytes 786440 | tf_op jit(solution)/shard_map/ppermute | solution.py:18
  16.7 0.0 collective-permute-done.3
  16.7 2.7 %collective-permute-start.4 = (bf16[128,128]{1,0:T(8,128)(2,1)S(1)}, bf16[128,128]{1,0:T(8,128)(2,1)S(1)}, u32[]{:S(2)}, u32[]{:S(2)}) collective-permute-start(bf16[128,128]{1,0:T(8,128)(2,1)S(1)} %get-tuple-element.26), channel_id=1, source_target_pairs={{0,9},{1,8},{2,11},{3,10},{4,13},{5,12},{6,15},{7,14},{8,1},{9,0},... | collective-permute-start | bytes 98312 | tf_op jit(solution)/shard_map/ppermute | solution.py:18
  19.4 0.0 collective-permute-done.5
  19.4 0.0 copy-start.2
  19.4 0.0 copy-start.3
  19.4 0.0 collective-permute-done.7.refs_1_
  19.4 0.7 %shard_map.88.inner_ref = f32[2048,512]{1,0:T(8,128)S(1)} custom-call(f32[2,64,128]{2,1,0:T(8,128)S(1)} %pad_maximum_fusion.1.act_ref, bf16[32,4096]{1,0:T(8,128)(2,1)S(1)} %constant_dynamic-update-slice_fusion.refs_0_, bf16[32,4096]{1,0:T(8,128)(2,1)S(1)} %collective-permute-done.7.refs_1_), custom_call_target="tpu_custom_call" | custom-call | flops 536870912 | bytes 4194304 | tf_op jit(solution)/shard_map/pallas_call | solution.py:147
  20.1 0.9 %collective-permute-done.4.other_ref = bf16[128,128]{1,0:T(8,128)(2,1)S(1)} collective-permute-done((bf16[128,128]{1,0:T(8,128)(2,1)S(1)}, bf16[128,128]{1,0:T(8,128)(2,1)S(1)}, u32[]{:S(2)}, u32[]{:S(2)}) %collective-permute-start.4) | collective-permute-done | bytes 32800 | tf_op jit(solution)/shard_map/ppermute | solution.py:18
  21.0 0.0 copy-done.2
  21.0 0.0 copy-done.3
  21.0 1.1 %shard_map.89 = (f32[64,128]{1,0:T(8,128)S(1)}, f32[64,128]{1,0:T(8,128)S(1)}, f32[8,8,16]{2,1,0:T(8,128)S(1)}) custom-call(s32[1]{0:T(128)} %bitcast.me_ref, s32[16]{0:T(128)S(1)} %copy-done.2, s32[16]{0:T(128)S(1)} %copy-done.3, f32[128,128]{1,0:T(8,128)S(1)} %get-tuple-element.27.own_ref, bf16[128,128]{1,0:T(8,128)(2,1)S(1)} %collective-permute-done.4.other_ref, ...), custom_call_target="tpu_custom_call" | custom-call | flops 2097152 | bytes 4194304 | tf_op jit(solution)/shard_map/pallas_call | solution.py:247
  22.1 0.2 collective-permute-start.9
  22.4 1.0 %collective-permute-done.9 = f32[4,8,16]{2,1,0:T(8,128)S(1)} collective-permute-done((f32[4,8,16]{2,1,0:T(8,128)S(1)}, f32[4,8,16]{2,1,0:T(8,128)S(1)}, u32[]{:S(2)}, u32[]{:S(2)}) %collective-permute-start.9) | collective-permute-done | bytes 2080 | tf_op jit(solution)/shard_map/ppermute | solution.py:18
  23.4 2.1 %collective-permute-start.10 = (f32[2,8,16]{2,1,0:T(8,128)S(1)}, f32[2,8,16]{2,1,0:T(8,128)S(1)}, u32[]{:S(2)}, u32[]{:S(2)}) collective-permute-start(f32[2,8,16]{2,1,0:T(8,128)S(1)} %slice.46), channel_id=1, source_target_pairs={{0,3},{1,2},{2,1},{3,0},{4,7},{5,6},{6,5},{7,4},{8,11},{9,10},{10,... | collective-permute-start | bytes 3080 | tf_op jit(solution)/shard_map/ppermute | solution.py:18
  25.5 2.5 %collective-permute-start.8 = (f32[64,128]{1,0:T(8,128)S(1)}, f32[64,128]{1,0:T(8,128)S(1)}, u32[]{:S(2)}, u32[]{:S(2)}) collective-permute-start(f32[64,128]{1,0:T(8,128)S(1)} %get-tuple-element.22), channel_id=1, source_target_pairs={{0,9},{1,8},{2,11},{3,10},{4,13},{5,12},{6,15},{7,14},{8,1},{9,0},... | collective-permute-start | bytes 98312 | tf_op jit(solution)/shard_map/ppermute | solution.py:18
  27.9 0.0 collective-permute-done.10
  27.9 0.5 %collective-permute-start.11 = (f32[1,8,16]{2,1,0:T(8,128)S(1)}, f32[1,8,16]{2,1,0:T(8,128)S(1)}, u32[]{:S(2)}, u32[]{:S(2)}) collective-permute-start(f32[1,8,16]{2,1,0:T(8,128)S(1)} %get-tuple-element.28), channel_id=1, source_target_pairs={{0,5},{1,4},{2,7},{3,6},{4,1},{5,0},{6,3},{7,2},{8,13},{9,12},{10,... | collective-permute-start | bytes 1544 | tf_op jit(solution)/shard_map/ppermute | solution.py:18
  28.5 2.6 %collective-permute-done.11.more_ref = f32[1,8,16]{2,1,0:T(8,128)S(1)} collective-permute-done((f32[1,8,16]{2,1,0:T(8,128)S(1)}, f32[1,8,16]{2,1,0:T(8,128)S(1)}, u32[]{:S(2)}, u32[]{:S(2)}) %collective-permute-start.11) | collective-permute-done | bytes 544 | tf_op jit(solution)/shard_map/ppermute | solution.py:18
  31.0 0.0 collective-permute-done.8.other_ref
  31.0 1.3 %shard_map.90 = (f32[128,128]{1,0:T(8,128)}, f32[8,16]{1,0:T(8,128)}) custom-call(s32[1]{0:T(128)} %bitcast.me_ref, s32[16]{0:T(128)S(1)} %copy-done.2, s32[16]{0:T(128)S(1)} %copy-done.3, f32[64,128]{1,0:T(8,128)S(1)} %get-tuple-element.21.own_ref, f32[64,128]{1,0:T(8,128)S(1)} %collective-permute-done.8.other_ref, ...), custom_call_target="tpu_custom_call" | custom-call | tf_op jit(solution)/shard_map/pallas_call | solution.py:293
  (15 shorter events, 0.1 us)
Async XLA Ops:
  0.6 10.3 %copy-start = (bf16[128,8192]{1,0:T(8,128)(2,1)S(1)}, bf16[128,8192]{1,0:T(8,128)(2,1)}, u32[]{:S(2)}) copy-start(bf16[128,8192]{1,0:T(8,128)(2,1)} %param.7) | copy-start | bytes 6291460
  0.6 8.4 %collective-permute-start = (bf16[8,4096]{1,0:T(8,128)(2,1)}, bf16[8,4096]{1,0:T(8,128)(2,1)S(1)}, u32[]{:S(2)}, u32[]{:S(2)}) collective-permute-start(bf16[8,4096]{1,0:T(8,128)(2,1)} %param.11), channel_id=1, source_target_pairs={{0,5},{1,4},{2,7},{3,6},{4,1},{5,0},{6,3},{7,2},{8,13},{9,12},{10,... | collective-permute-start | bytes 196616 | tf_op jit(solution)/shard_map/ppermute | solution.py:18
  3.2 4.7 %copy-start.5 = (bf16[8,4096]{1,0:T(8,128)(2,1)S(1)}, bf16[8,4096]{1,0:T(8,128)(2,1)}, u32[]{:S(2)}) copy-start(bf16[8,4096]{1,0:T(8,128)(2,1)} %param.11) | copy-start | bytes 196612
  3.2 4.7 %copy-start.1 = (bf16[2048,1792]{1,0:T(8,128)(2,1)S(1)}, bf16[2048,1792]{1,0:T(8,128)(2,1)}, u32[]{:S(2)}) copy-start(bf16[2048,1792]{1,0:T(8,128)(2,1)} %grads_ref.3) | copy-start | bytes 22020100
  7.1 1.9 %collective-permute-start.1 = (f32[4,128,128]{2,1,0:T(8,128)S(1)}, f32[4,128,128]{2,1,0:T(8,128)S(1)}, u32[]{:S(2)}, u32[]{:S(2)}) collective-permute-start(f32[4,128,128]{2,1,0:T(8,128)S(1)} %get-tuple-element.15), channel_id=1, source_target_pairs={{0,1},{1,0},{2,3},{3,2},{4,5},{5,4},{6,7},{7,6},{8,9},{9,8},{10,11... | collective-permute-start | bytes 786440 | tf_op jit(solution)/shard_map/ppermute | solution.py:18
  7.9 3.1 %copy-start.4 = (bf16[8192,64]{0,1:T(8,128)(2,1)S(1)}, bf16[8192,64]{0,1:T(8,128)(2,1)}, u32[]{:S(2)}) copy-start(bf16[8192,64]{0,1:T(8,128)(2,1)} %param.9) | copy-start | bytes 3145732
  9.1 4.0 %collective-permute-start.2 = (bf16[2,128,128]{2,1,0:T(8,128)(2,1)S(1)}, bf16[2,128,128]{2,1,0:T(8,128)(2,1)S(1)}, u32[]{:S(2)}, u32[]{:S(2)}) collective-permute-start(bf16[2,128,128]{2,1,0:T(8,128)(2,1)S(1)} %slice.57), channel_id=1, source_target_pairs={{0,3},{1,2},{2,1},{3,0},{4,7},{5,6},{6,5},{7,4},{8,11},{9,10},{10,... | collective-permute-start | bytes 196616 | tf_op jit(solution)/shard_map/ppermute | solution.py:18
  10.7 5.5 %collective-permute-start.6 = (bf16[16,4096]{1,0:T(8,128)(2,1)S(1)}, bf16[16,4096]{1,0:T(8,128)(2,1)S(1)}, u32[]{:S(2)}, u32[]{:S(2)}) collective-permute-start(bf16[16,4096]{1,0:T(8,128)(2,1)S(1)} %pad_maximum_fusion), channel_id=1, source_target_pairs={{0,3},{1,2},{2,1},{3,0},{4,7},{5,6},{6,5},{7,4},{8,11},{9,10},{10,... | collective-permute-start | bytes 393224 | tf_op jit(solution)/shard_map/ppermute | solution.py:18
  13.2 3.5 %collective-permute-start.3 = (bf16[1,128,128]{2,1,0:T(8,128)(2,1)S(1)}, bf16[1,128,128]{2,1,0:T(8,128)(2,1)S(1)}, u32[]{:S(2)}, u32[]{:S(2)}) collective-permute-start(bf16[1,128,128]{2,1,0:T(8,128)(2,1)S(1)} %slice.58), channel_id=1, source_target_pairs={{0,5},{1,4},{2,7},{3,6},{4,1},{5,0},{6,3},{7,2},{8,13},{9,12},{10,... | collective-permute-start | bytes 98312 | tf_op jit(solution)/shard_map/ppermute | solution.py:18
  13.4 6.0 %collective-permute-start.5 = (f32[64,128]{1,0:T(8,128)S(1)}, f32[64,128]{1,0:T(8,128)S(1)}, u32[]{:S(2)}, u32[]{:S(2)}) collective-permute-start(f32[64,128]{1,0:T(8,128)S(1)} %fusion.4), channel_id=1, source_target_pairs={{0,9},{1,8},{2,11},{3,10},{4,13},{5,12},{6,15},{7,14},{8,1},{9,0},... | collective-permute-start | bytes 98312 | tf_op jit(solution)/shard_map/ppermute | solution.py:18
  16.2 3.2 %collective-permute-start.7 = (bf16[32,4096]{1,0:T(8,128)(2,1)S(1)}, bf16[32,4096]{1,0:T(8,128)(2,1)S(1)}, u32[]{:S(2)}, u32[]{:S(2)}) collective-permute-start(bf16[32,4096]{1,0:T(8,128)(2,1)S(1)} %constant_dynamic-update-slice_fusion.refs_0_), channel_id=1, source_target_pairs={{0,1},{1,0},{2,3},{3,2},{4,5},{5,4},{6,7},{7,6},{8,9},{9,8},{10,11... | collective-permute-start | bytes 786440 | tf_op jit(solution)/shard_map/ppermute | solution.py:18
  16.7 4.3 %collective-permute-start.4 = (bf16[128,128]{1,0:T(8,128)(2,1)S(1)}, bf16[128,128]{1,0:T(8,128)(2,1)S(1)}, u32[]{:S(2)}, u32[]{:S(2)}) collective-permute-start(bf16[128,128]{1,0:T(8,128)(2,1)S(1)} %get-tuple-element.26), channel_id=1, source_target_pairs={{0,9},{1,8},{2,11},{3,10},{4,13},{5,12},{6,15},{7,14},{8,1},{9,0},... | collective-permute-start | bytes 98312 | tf_op jit(solution)/shard_map/ppermute | solution.py:18
  19.4 1.6 %copy-start.2 = (s32[16]{0:T(128)S(1)}, s32[16]{0:T(128)}, u32[]{:S(2)}) copy-start(s32[16]{0:T(128)} %length_ref.3) | copy-start | bytes 196
  19.4 1.6 %copy-start.3 = (s32[16]{0:T(128)S(1)}, s32[16]{0:T(128)}, u32[]{:S(2)}) copy-start(s32[16]{0:T(128)} %valid_ref.3) | copy-start | bytes 196
  22.1 1.2 %collective-permute-start.9 = (f32[4,8,16]{2,1,0:T(8,128)S(1)}, f32[4,8,16]{2,1,0:T(8,128)S(1)}, u32[]{:S(2)}, u32[]{:S(2)}) collective-permute-start(f32[4,8,16]{2,1,0:T(8,128)S(1)} %slice.37), channel_id=1, source_target_pairs={{0,1},{1,0},{2,3},{3,2},{4,5},{5,4},{6,7},{7,6},{8,9},{9,8},{10,11... | collective-permute-start | bytes 6152 | tf_op jit(solution)/shard_map/ppermute | solution.py:18
  23.4 4.5 %collective-permute-start.10 = (f32[2,8,16]{2,1,0:T(8,128)S(1)}, f32[2,8,16]{2,1,0:T(8,128)S(1)}, u32[]{:S(2)}, u32[]{:S(2)}) collective-permute-start(f32[2,8,16]{2,1,0:T(8,128)S(1)} %slice.46), channel_id=1, source_target_pairs={{0,3},{1,2},{2,1},{3,0},{4,7},{5,6},{6,5},{7,4},{8,11},{9,10},{10,... | collective-permute-start | bytes 3080 | tf_op jit(solution)/shard_map/ppermute | solution.py:18
  25.5 5.6 %collective-permute-start.8 = (f32[64,128]{1,0:T(8,128)S(1)}, f32[64,128]{1,0:T(8,128)S(1)}, u32[]{:S(2)}, u32[]{:S(2)}) collective-permute-start(f32[64,128]{1,0:T(8,128)S(1)} %get-tuple-element.22), channel_id=1, source_target_pairs={{0,9},{1,8},{2,11},{3,10},{4,13},{5,12},{6,15},{7,14},{8,1},{9,0},... | collective-permute-start | bytes 98312 | tf_op jit(solution)/shard_map/ppermute | solution.py:18
  27.9 3.1 %collective-permute-start.11 = (f32[1,8,16]{2,1,0:T(8,128)S(1)}, f32[1,8,16]{2,1,0:T(8,128)S(1)}, u32[]{:S(2)}, u32[]{:S(2)}) collective-permute-start(f32[1,8,16]{2,1,0:T(8,128)S(1)} %get-tuple-element.28), channel_id=1, source_target_pairs={{0,5},{1,4},{2,7},{3,6},{4,1},{5,0},{6,3},{7,2},{8,13},{9,12},{10,... | collective-permute-start | bytes 1544 | tf_op jit(solution)/shard_map/ppermute | solution.py:18

commit v18 on v16

--- a/solution.py
+++ b/solution.py
@@ -158,7 +158,7 @@
 
 
 def score_kernel(
-    steps, split, me_ref, length_ref, valid_ref, own_ref, other_ref, inner_ref, own_tok, other_tok, doc_ref, grad_ref
+    steps, member_ref, own_ref, other_ref, inner_ref, own_tok, other_tok, doc_ref, grad_ref
 ):
     rows, wide = own_ref.shape
     halves, width = 2, wide // 2
@@ -194,22 +194,8 @@
             tokens[r][...] = jnp.where(step == 0, total, tokens[r][...] + total)
 
     def finish():
-        me = me_ref[0]
-        docs = length_ref.shape[0]
-        doc_of = lax.broadcasted_iota(jnp.int32, (docs, rows), 0)
-        lower = jnp.zeros((docs, rows), jnp.int32)
-        upper = jnp.zeros((docs, rows), jnp.int32)
-        start = jnp.int32(0)
-        for d in range(docs):
-            lower = jnp.where(doc_of == d, start, lower)
-            used = jnp.minimum(valid_ref[d], length_ref[d])
-            upper = jnp.where(doc_of == d, start + used, upper)
-            start = start + length_ref[d]
-        members, parts = [], []
+        parts = []
         for r in range(halves):
-            token = (me ^ (split * r)) * rows + lax.broadcasted_iota(jnp.int32, (docs, rows), 1)
-            inside = (token >= lower) & (token < upper)
-            members.append(jnp.where(inside, 1.0, 0.0).astype(jnp.bfloat16))
             left = tokens[r][...]
             for _ in range(3):
                 part = left.astype(jnp.bfloat16)
@@ -217,7 +203,7 @@
                 parts.append(part)
         partial = lax.dot_general(
             jnp.concatenate(parts, axis=1),
-            jnp.concatenate([m for m in members for _ in range(3)], axis=1),
+            member_ref[...],
             (((1,), (1,)), ((), ())),
             preferred_element_type=jnp.float32,
         )
@@ -231,21 +217,21 @@
         pl.when(step == steps - 1)(finish)
 
 
-def score(me, lengths, valid, own, other, products, split, own_q, steps):
+def score(members, own, other, products, own_q, steps):
     rows, wide = own.shape
-    docs = lengths.shape[0]
+    docs = members.shape[0]
     count = 4 * products.shape[0] // wide
     if steps == 1:
-        grid = {"in_specs": [SMEM] * 3 + [VMEM] * 3, "out_specs": (VMEM,) * 3}
+        grid = {"in_specs": [VMEM] * 4, "out_specs": (VMEM,) * 3}
     else:
         block = (products.shape[0] // steps, products.shape[1])
         grid = {
             "grid": (steps,),
-            "in_specs": [SMEM] * 3 + [VMEM] * 2 + [pl.BlockSpec(block, lambda s: (s, 0))],
+            "in_specs": [VMEM] * 3 + [pl.BlockSpec(block, lambda s: (s, 0))],
             "out_specs": (VMEM,) * 3,
         }
     return pl.pallas_call(
-        functools.partial(score_kernel, steps, split),
+        functools.partial(score_kernel, steps),
         out_shape=(
             jax.ShapeDtypeStruct((count, rows), jnp.float32),
             jax.ShapeDtypeStruct((count, rows), jnp.float32),
@@ -259,7 +245,7 @@
             transcendentals=0,
         ),
         **grid,
-    )(me, lengths, valid, own, other, products)
+    )(members, own, other, products)
 
 
 def place_kernel(place, split, me_ref, own_ref, other_ref, out_ref, turned_ref):
@@ -281,6 +267,15 @@
         scratch_shapes=[pltpu.VMEM((2 * count, rows), jnp.float32)],
         compiler_params=pltpu.CompilerParams(vmem_limit_bytes=16 * MIB),
     )(me, own, other)
+
+
+def masks(me, split, rows, doc_length, valid_count):
+    lower = jnp.cumsum(doc_length) - doc_length
+    upper = lower + jnp.minimum(valid_count, doc_length)
+    place = jnp.arange(6 * rows, dtype=jnp.int32)
+    token = (me ^ (split * (place // (3 * rows)))) * rows + place % rows
+    inside = (token[None, :] >= lower[:, None]) & (token[None, :] < upper[:, None])
+    return inside.astype(jnp.bfloat16)
 
 
 def offset_of(number, bits):
@@ -319,7 +314,7 @@
         late, activations, (((0,), (1,)), ((), ())), preferred_element_type=jnp.float32
     )
     early, _ = lax.optimization_barrier((act, after))
-    more_act, _ = lax.optimization_barrier((swap(early, split, size), own))
+    more_act = swap(early, split, size)
     act = jnp.stack([act, more_act])
 
     panel = jnp.concatenate([panel, got], axis=0)
@@ -332,9 +327,9 @@
 
     steps = max(1, 4 * width * size * own_q * rows // (4 * MIB))
     products = inner(act, panels, steps)
-    mine, theirs, doc = score(
-        me, doc_length, valid_count, own, across, products, split, own_q, steps
-    )
+    members = masks(me[0], split, rows, doc_length, valid_count)
+    members, _ = lax.optimization_barrier((members, own))
+    mine, theirs, doc = score(members, own, across, products, own_q, steps)
     others = swap(theirs, split, size)
     bits = [1] + middle
     for bit in bits[:-1]:

time: 31.7 us -> 36.6 us (1.15)
  local copies, waits for them, and re-layouts: 0.09 us -> 4.09 us
  other arithmetic: 0.68 us -> 3.4 us
  starting transfers between devices: 16.1 us -> 13.6 us
  waiting for transfers between devices: 5.41 us -> 6.64 us
  Pallas kernels: 7.59 us -> 6.93 us
    unnamed x14 -> x18, local copies, waits for them, and re-layouts: 0.05 us -> 3.97 us
    ppermute x12, starting transfers between devices: 16.1 us -> 13.6 us  [swap(): return lax.ppermute(value, 'seq', [(i, i ^ offset) for i in range(size)])]
    ppermute x12, waiting for transfers between devices: 5.41 us -> 6.64 us  [swap(): return lax.ppermute(value, 'seq', [(i, i ^ offset) for i in range(size)])]
    add x1, other arithmetic: 0.03 us -> 0.98 us  [body(): sums = grad_blocks(me, proj, out_grads, rows, spots, table) + from_core]
    concatenate x1, other arithmetic: 0.01 us -> 0.85 us  [body(): panel = jnp.concatenate([panel, got], axis=0)]
    add x0 -> x2, other arithmetic: none -> 0.69 us  [the longest x1 0.68 us: masks(): upper = lower + jnp.minimum(valid_count, doc_length)]
    pallas_call x1, Pallas kernels: 1.08 us -> 0.52 us  [score(): pl.pallas_call(functools.partial(score_kernel, steps), out_shape=(jax.Sha...]
  transfers between devices with their start and end apart: 12 -> 12, of which waited for: 6 -> 6; matrix products, arithmetic and copies ran while one was open for 3% -> 13% of each run, Pallas kernels for 21% -> 18%
where the time goes in v18:
time: 36.6 us; the launch traced here: 36.3 us
  starting transfers between devices  13.6 us (37%)
  Pallas kernels  6.93 us (19%)
  waiting for transfers between devices  6.64 us (18%)
  local copies, waits for them, and re-layouts  4.09 us (11%)
  other arithmetic  3.4 us (9%)
  matrix products  0.84 us (2%)
  between operations  0.83 us (2%)
    ppermute x12, starting transfers between devices, swap(): return lax.ppermute(value, 'seq', [(i, i ^ offset) for i in range(size)])  13.6 us
    ppermute x12, waiting for transfers between devices, swap(): return lax.ppermute(value, 'seq', [(i, i ^ offset) for i in range(size)])  6.64 us
    unnamed x18, local copies, waits for them, and re-layouts  3.97 us
    pallas_call x1, Pallas kernels, grad_blocks(): pl.pallas_call(functools.partial(grad_kernel, offsets), in_specs=[SMEM, H...  3.82 us
    pallas_call x1, Pallas kernels, grad_blocks(): pl.pallas_call(functools.partial(held_kernel, offsets), in_specs=[SMEM, V...  1.14 us
    add x1, other arithmetic, body(): sums = grad_blocks(me, proj, out_grads, rows, spots, table) + from_core  0.98 us
    concatenate x1, other arithmetic, body(): panel = jnp.concatenate([panel, got], axis=0)  0.85 us
    dot_general x1, matrix products, body(): lax.dot_general(late, activations, (((0,), (1,)), ((), ())), preferred_el...  0.84 us
  transfers between devices with their start and end apart: 12, of which 6 were waited for; matrix products, arithmetic and copies ran while one was open for 13% of the time, Pallas kernels for 18%

profile of v18, /device:TPU:0, one launch (start us, length us, event | category | flops | bytes accessed | tf_op | source)
XLA Modules:
  0.0 36.3 jit_solution(10854600183991280069)
XLA Ops:
  0.6 0.0 copy-start
  0.6 2.5 %collective-permute-start = (bf16[8,4096]{1,0:T(8,128)(2,1)}, bf16[8,4096]{1,0:T(8,128)(2,1)}, u32[]{:S(2)}, u32[]{:S(2)}) collective-permute-start(bf16[8,4096]{1,0:T(8,128)(2,1)} %param.11), channel_id=1, source_target_pairs={{0,5},{1,4},{2,7},{3,6},{4,1},{5,0},{6,3},{7,2},{8,13},{9,12},{10,... | collective-permute-start | bytes 196616 | tf_op jit(solution)/shard_map/ppermute | solution.py:18
  3.2 3.8 %shard_map.86 = (f32[4,128,128]{2,1,0:T(8,128)S(1)}, bf16[2,1792,128]{2,1,0:T(8,128)(2,1)S(1)}) custom-call(s32[1]{0:T(128)} %bitcast.1.me_ref, bf16[64,1792]{1,0:T(8,128)(2,1)} %bitcast.18, bf16[2048,1792]{1,0:T(8,128)(2,1)} %grads_ref.3), custom_call_target="tpu_custom_call" | custom-call | flops 234881024 | bytes 3670016 | tf_op jit(solution)/shard_map/pallas_call | solution.py:93
  7.0 0.7 %collective-permute-start.1 = (f32[4,128,128]{2,1,0:T(8,128)S(1)}, f32[4,128,128]{2,1,0:T(8,128)}, u32[]{:S(2)}, u32[]{:S(2)}) collective-permute-start(f32[4,128,128]{2,1,0:T(8,128)S(1)} %get-tuple-element.15), channel_id=1, source_target_pairs={{0,1},{1,0},{2,3},{3,2},{4,5},{5,4},{6,7},{7,6},{8,9},{9,8},{10,11... | collective-permute-start | bytes 786440 | tf_op jit(solution)/shard_map/ppermute | solution.py:18
  7.8 0.0 copy-done.3
  7.8 0.0 copy-done.5
  7.8 0.1 copy.10
  7.9 0.1 reduce
  8.0 0.7 %minimum_add_fusion = (s32[16]{0:T(128)S(1)}, s32[16]{0:T(128)S(1)}) fusion(s32[16]{0:T(128)} %param.13, s32[16]{0:T(128)} %param.12, s32[16]{0:T(128)S(1)} %reduce), kind=kLoop, calls=%fused_computation.34 | loop fusion | flops 48 | bytes 320 | tf_op jit(solution)/shard_map/add | solution.py:274
  8.7 0.1 and_convert_fusion.member_ref
  8.8 3.1 %copy-done.1 = bf16[2048,1792]{1,0:T(8,128)(2,1)S(1)} copy-done((bf16[2048,1792]{1,0:T(8,128)(2,1)S(1)}, bf16[2048,1792]{1,0:T(8,128)(2,1)}, u32[]{:S(2)}) %copy-start.1) | copy-done | bytes 7340056
  11.9 1.1 %shard_map.87 = f32[4,128,128]{2,1,0:T(8,128)S(1)} custom-call(s32[1]{0:T(128)} %bitcast.1.me_ref, bf16[2,1792,128]{2,1,0:T(8,128)(2,1)S(1)} %get-tuple-element.14.table, bf16[2048,1792]{1,0:T(8,128)(2,1)S(1)} %copy-done.1), custom_call_target="tpu_custom_call" | custom-call | flops 234881024 | bytes 3670016 | tf_op jit(solution)/shard_map/pallas_call | solution.py:86
  13.0 0.0 collective-permute-done.1
  13.0 1.0 %add.49 = f32[4,128,128]{2,1,0:T(8,128)S(1)} add(f32[4,128,128]{2,1,0:T(8,128)S(1)} %shard_map.87, f32[4,128,128]{2,1,0:T(8,128)} %collective-permute-done.1) | non-fusion elementwise | flops 65536 | bytes 786432 | tf_op jit(solution)/shard_map/add | solution.py:302
  14.0 0.0 collective-permute-done
  14.0 1.2 %collective-permute-start.2 = (bf16[2,128,128]{2,1,0:T(8,128)(2,1)S(1)}, bf16[2,128,128]{2,1,0:T(8,128)(2,1)S(1)}, u32[]{:S(2)}, u32[]{:S(2)}) collective-permute-start(bf16[2,128,128]{2,1,0:T(8,128)(2,1)S(1)} %slice.64), channel_id=1, source_target_pairs={{0,3},{1,2},{2,1},{3,0},{4,7},{5,6},{6,5},{7,4},{8,11},{9,10},{10,... | collective-permute-start | bytes 196616 | tf_op jit(solution)/shard_map/ppermute | solution.py:18
  15.3 0.0 copy-done.4
  15.3 0.8 %pad_maximum_fusion = bf16[16,4096]{1,0:T(8,128)(2,1)S(1)} fusion(bf16[8,4096]{1,0:T(8,128)(2,1)} %collective-permute-done, bf16[8,4096]{1,0:T(8,128)(2,1)S(1)} %copy-done.4), kind=kLoop, calls=%fused_computation.1 | loop fusion | flops 262144 | bytes 262144 | tf_op jit(solution)/shard_map/concatenate | solution.py:320
  16.1 0.8 %constant_dynamic-update-slice_fusion.1 = bf16[32,4096]{1,0:T(8,128)(2,1)S(1)} fusion(bf16[32,4096]{1,0:T(8,128)(2,1)S(1)} %constant_dynamic-update-slice_fusion.2, bf16[8,4096]{1,0:T(8,128)(2,1)} %collective-permute-done), kind=kLoop, calls=%fused_computation.11 | loop fusion | bytes 131072
  17.0 0.6 %collective-permute-start.6 = (bf16[16,4096]{1,0:T(8,128)(2,1)S(1)}, bf16[16,4096]{1,0:T(8,128)(2,1)S(1)}, u32[]{:S(2)}, u32[]{:S(2)}) collective-permute-start(bf16[16,4096]{1,0:T(8,128)(2,1)S(1)} %pad_maximum_fusion), channel_id=1, source_target_pairs={{0,3},{1,2},{2,1},{3,0},{4,7},{5,6},{6,5},{7,4},{8,11},{9,10},{10,... | collective-permute-start | bytes 393224 | tf_op jit(solution)/shard_map/ppermute | solution.py:18
  17.6 0.0 copy-done
  17.6 0.0 copy-done.2
  17.6 0.8 %fusion.16 = f32[64,128]{1,0:T(8,128)S(1)} fusion(bf16[8192,64]{0,1:T(8,128)(2,1)S(1)} %copy-done.2, bf16[128,8192]{1,0:T(8,128)(2,1)S(1)} %copy-done), kind=kOutput, calls=%fused_computation.36 | convolution fusion | flops 134217728 | bytes 3178496 | tf_op jit(solution)/shard_map/dot_general | solution.py:313
  18.4 0.0 collective-permute-done.2
  18.5 0.2 collective-permute-start.3
  18.7 2.6 %collective-permute-start.5 = (f32[64,128]{1,0:T(8,128)S(1)}, f32[64,128]{1,0:T(8,128)S(1)}, u32[]{:S(2)}, u32[]{:S(2)}) collective-permute-start(f32[64,128]{1,0:T(8,128)S(1)} %fusion.16), channel_id=1, source_target_pairs={{0,9},{1,8},{2,11},{3,10},{4,13},{5,12},{6,15},{7,14},{8,1},{9,0},... | collective-permute-start | bytes 98312 | tf_op jit(solution)/shard_map/ppermute | solution.py:18
  21.3 0.8 %collective-permute-done.6 = bf16[16,4096]{1,0:T(8,128)(2,1)S(1)} collective-permute-done((bf16[16,4096]{1,0:T(8,128)(2,1)S(1)}, bf16[16,4096]{1,0:T(8,128)(2,1)S(1)}, u32[]{:S(2)}, u32[]{:S(2)}) %collective-permute-start.6) | collective-permute-done | bytes 131104 | tf_op jit(solution)/shard_map/ppermute | solution.py:18
  22.2 0.8 %collective-permute-start.7 = (bf16[32,4096]{1,0:T(8,128)(2,1)S(1)}, bf16[32,4096]{1,0:T(8,128)(2,1)S(1)}, u32[]{:S(2)}, u32[]{:S(2)}) collective-permute-start(bf16[32,4096]{1,0:T(8,128)(2,1)S(1)} %constant_dynamic-update-slice_fusion.refs_0_), channel_id=1, source_target_pairs={{0,1},{1,0},{2,3},{3,2},{4,5},{5,4},{6,7},{7,6},{8,9},{9,8},{10,11... | collective-permute-start | bytes 786440 | tf_op jit(solution)/shard_map/ppermute | solution.py:18
  22.9 0.0 collective-permute-done.3
  23.0 2.3 %collective-permute-start.4 = (bf16[128,128]{1,0:T(8,128)(2,1)S(1)}, bf16[128,128]{1,0:T(8,128)(2,1)S(1)}, u32[]{:S(2)}, u32[]{:S(2)}) collective-permute-start(bf16[128,128]{1,0:T(8,128)(2,1)S(1)} %get-tuple-element.26), channel_id=1, source_target_pairs={{0,9},{1,8},{2,11},{3,10},{4,13},{5,12},{6,15},{7,14},{8,1},{9,0},... | collective-permute-start | bytes 98312 | tf_op jit(solution)/shard_map/ppermute | solution.py:18
  25.3 0.0 collective-permute-done.5
  25.3 0.0 collective-permute-done.7.refs_1_
  25.3 0.7 %shard_map.88.inner_ref = f32[2048,512]{1,0:T(8,128)S(1)} custom-call(f32[2,64,128]{2,1,0:T(8,128)S(1)} %pad_maximum_fusion.1.act_ref, bf16[32,4096]{1,0:T(8,128)(2,1)S(1)} %constant_dynamic-update-slice_fusion.refs_0_, bf16[32,4096]{1,0:T(8,128)(2,1)S(1)} %collective-permute-done.7.refs_1_), custom_call_target="tpu_custom_call" | custom-call | flops 536870912 | bytes 4194304 | tf_op jit(solution)/shard_map/pallas_call | solution.py:147
  26.0 0.0 copy-start.6
  26.0 0.0 copy-start.7
  26.0 1.8 %collective-permute-done.4.other_ref = bf16[128,128]{1,0:T(8,128)(2,1)S(1)} collective-permute-done((bf16[128,128]{1,0:T(8,128)(2,1)S(1)}, bf16[128,128]{1,0:T(8,128)(2,1)S(1)}, u32[]{:S(2)}, u32[]{:S(2)}) %collective-permute-start.4) | collective-permute-done | bytes 32800 | tf_op jit(solution)/shard_map/ppermute | solution.py:18
  27.8 0.5 %shard_map.89 = (f32[64,128]{1,0:T(8,128)S(1)}, f32[64,128]{1,0:T(8,128)S(1)}, f32[8,8,16]{2,1,0:T(8,128)S(1)}) custom-call(bf16[16,768]{1,0:T(8,128)(2,1)S(1)} %and_convert_fusion.member_ref, f32[128,128]{1,0:T(8,128)S(1)} %get-tuple-element.27.own_ref, bf16[128,128]{1,0:T(8,128)(2,1)S(1)} %collective-permute-done.4.other_ref, ...), custom_call_target="tpu_custom_call" | custom-call | flops 2097152 | bytes 4194304 | tf_op jit(solution)/shard_map/pallas_call | solution.py:233
  28.3 0.2 collective-permute-start.8
  28.5 1.1 %collective-permute-done.8 = f32[4,8,16]{2,1,0:T(8,128)S(1)} collective-permute-done((f32[4,8,16]{2,1,0:T(8,128)S(1)}, f32[4,8,16]{2,1,0:T(8,128)S(1)}, u32[]{:S(2)}, u32[]{:S(2)}) %collective-permute-start.8) | collective-permute-done | bytes 2080 | tf_op jit(solution)/shard_map/ppermute | solution.py:18
  29.6 0.2 collective-permute-start.9
  29.8 2.2 %collective-permute-start.11 = (f32[64,128]{1,0:T(8,128)S(1)}, f32[64,128]{1,0:T(8,128)S(1)}, u32[]{:S(2)}, u32[]{:S(2)}) collective-permute-start(f32[64,128]{1,0:T(8,128)S(1)} %get-tuple-element.23), channel_id=1, source_target_pairs={{0,9},{1,8},{2,11},{3,10},{4,13},{5,12},{6,15},{7,14},{8,1},{9,0},... | collective-permute-start | bytes 98312 | tf_op jit(solution)/shard_map/ppermute | solution.py:18
  32.0 0.7 %collective-permute-done.9 = f32[2,8,16]{2,1,0:T(8,128)S(1)} collective-permute-done((f32[2,8,16]{2,1,0:T(8,128)S(1)}, f32[2,8,16]{2,1,0:T(8,128)S(1)}, u32[]{:S(2)}, u32[]{:S(2)}) %collective-permute-start.9) | collective-permute-done | bytes 1056 | tf_op jit(solution)/shard_map/ppermute | solution.py:18
  32.7 0.0 collective-permute-start.10
  32.7 0.0 copy-done.6
  32.7 1.3 %collective-permute-done.11.other_ref = f32[64,128]{1,0:T(8,128)S(1)} collective-permute-done((f32[64,128]{1,0:T(8,128)S(1)}, f32[64,128]{1,0:T(8,128)S(1)}, u32[]{:S(2)}, u32[]{:S(2)}) %collective-permute-start.11) | collective-permute-done | bytes 32800 | tf_op jit(solution)/shard_map/ppermute | solution.py:18
  34.0 0.7 %shard_map.90 = f32[128,128]{1,0:T(8,128)} custom-call(s32[1]{0:T(128)} %bitcast.1.me_ref, f32[64,128]{1,0:T(8,128)S(1)} %get-tuple-element.22.own_ref, f32[64,128]{1,0:T(8,128)S(1)} %collective-permute-done.11.other_ref), custom_call_target="tpu_custom_call" | custom-call | tf_op jit(solution)/shard_map/pallas_call | solution.py:262
  34.8 0.9 %collective-permute-done.10 = f32[1,8,16]{2,1,0:T(8,128)S(1)} collective-permute-done((f32[1,8,16]{2,1,0:T(8,128)S(1)}, f32[1,8,16]{2,1,0:T(8,128)S(1)}, u32[]{:S(2)}, u32[]{:S(2)}) %collective-permute-start.10) | collective-permute-done | bytes 544 | tf_op jit(solution)/shard_map/ppermute | solution.py:18
  35.7 0.6 %fusion.9 = f32[16,8]{0,1:T(8,128)} fusion(f32[1,8,16]{2,1,0:T(8,128)S(1)} %collective-permute-done.10, f32[2,8,16]{2,1,0:T(8,128)S(1)} %slice_add_fusion.2, f32[16]{0:T(128)S(1)} %convert_rsqrt_fusion), kind=kLoop, calls=%fused_computation.27 | loop fusion | flops 256 | bytes 1600 | tf_op jit(solution)/shard_map/transpose | solution.py:342
  (21 shorter events, 0.2 us)
Async XLA Ops:
  0.6 16.9 %copy-start = (bf16[128,8192]{1,0:T(8,128)(2,1)S(1)}, bf16[128,8192]{1,0:T(8,128)(2,1)}, u32[]{:S(2)}) copy-start(bf16[128,8192]{1,0:T(8,128)(2,1)} %param.7) | copy-start | bytes 6291460
  0.6 13.4 %collective-permute-start = (bf16[8,4096]{1,0:T(8,128)(2,1)}, bf16[8,4096]{1,0:T(8,128)(2,1)}, u32[]{:S(2)}, u32[]{:S(2)}) collective-permute-start(bf16[8,4096]{1,0:T(8,128)(2,1)} %param.11), channel_id=1, source_target_pairs={{0,5},{1,4},{2,7},{3,6},{4,1},{5,0},{6,3},{7,2},{8,13},{9,12},{10,... | collective-permute-start | bytes 196616 | tf_op jit(solution)/shard_map/ppermute | solution.py:18
  3.2 4.6 %copy-start.3 = (bf16[8,4096]{1,0:T(8,128)(2,1)S(1)}, bf16[8,4096]{1,0:T(8,128)(2,1)}, u32[]{:S(2)}) copy-start(bf16[8,4096]{1,0:T(8,128)(2,1)} %param.11) | copy-start | bytes 196612
  3.2 4.6 %copy-start.5 = (s32[16]{0:T(128)S(1)}, s32[16]{0:T(128)}, u32[]{:S(2)}) copy-start(s32[16]{0:T(128)} %param.12) | copy-start | bytes 196
  7.0 6.0 %collective-permute-start.1 = (f32[4,128,128]{2,1,0:T(8,128)S(1)}, f32[4,128,128]{2,1,0:T(8,128)}, u32[]{:S(2)}, u32[]{:S(2)}) collective-permute-start(f32[4,128,128]{2,1,0:T(8,128)S(1)} %get-tuple-element.15), channel_id=1, source_target_pairs={{0,1},{1,0},{2,3},{3,2},{4,5},{5,4},{6,7},{7,6},{8,9},{9,8},{10,11... | collective-permute-start | bytes 786440 | tf_op jit(solution)/shard_map/ppermute | solution.py:18
  8.8 3.1 %copy-start.1 = (bf16[2048,1792]{1,0:T(8,128)(2,1)S(1)}, bf16[2048,1792]{1,0:T(8,128)(2,1)}, u32[]{:S(2)}) copy-start(bf16[2048,1792]{1,0:T(8,128)(2,1)} %grads_ref.3) | copy-start | bytes 22020100
  11.9 3.4 %copy-start.4 = (bf16[8,4096]{1,0:T(8,128)(2,1)S(1)}, bf16[8,4096]{1,0:T(8,128)(2,1)}, u32[]{:S(2)}) copy-start(bf16[8,4096]{1,0:T(8,128)(2,1)} %param.11) | copy-start | bytes 196612
  11.9 5.7 %copy-start.2 = (bf16[8192,64]{0,1:T(8,128)(2,1)S(1)}, bf16[8192,64]{0,1:T(8,128)(2,1)}, u32[]{:S(2)}) copy-start(bf16[8192,64]{0,1:T(8,128)(2,1)} %param.9) | copy-start | bytes 3145732
  14.0 4.4 %collective-permute-start.2 = (bf16[2,128,128]{2,1,0:T(8,128)(2,1)S(1)}, bf16[2,128,128]{2,1,0:T(8,128)(2,1)S(1)}, u32[]{:S(2)}, u32[]{:S(2)}) collective-permute-start(bf16[2,128,128]{2,1,0:T(8,128)(2,1)S(1)} %slice.64), channel_id=1, source_target_pairs={{0,3},{1,2},{2,1},{3,0},{4,7},{5,6},{6,5},{7,4},{8,11},{9,10},{10,... | collective-permute-start | bytes 196616 | tf_op jit(solution)/shard_map/ppermute | solution.py:18
  17.0 5.2 %collective-permute-start.6 = (bf16[16,4096]{1,0:T(8,128)(2,1)S(1)}, bf16[16,4096]{1,0:T(8,128)(2,1)S(1)}, u32[]{:S(2)}, u32[]{:S(2)}) collective-permute-start(bf16[16,4096]{1,0:T(8,128)(2,1)S(1)} %pad_maximum_fusion), channel_id=1, source_target_pairs={{0,3},{1,2},{2,1},{3,0},{4,7},{5,6},{6,5},{7,4},{8,11},{9,10},{10,... | collective-permute-start | bytes 393224 | tf_op jit(solution)/shard_map/ppermute | solution.py:18
  18.5 4.5 %collective-permute-start.3 = (bf16[1,128,128]{2,1,0:T(8,128)(2,1)S(1)}, bf16[1,128,128]{2,1,0:T(8,128)(2,1)S(1)}, u32[]{:S(2)}, u32[]{:S(2)}) collective-permute-start(bf16[1,128,128]{2,1,0:T(8,128)(2,1)S(1)} %slice.65), channel_id=1, source_target_pairs={{0,5},{1,4},{2,7},{3,6},{4,1},{5,0},{6,3},{7,2},{8,13},{9,12},{10,... | collective-permute-start | bytes 98312 | tf_op jit(solution)/shard_map/ppermute | solution.py:18
  18.7 6.6 %collective-permute-start.5 = (f32[64,128]{1,0:T(8,128)S(1)}, f32[64,128]{1,0:T(8,128)S(1)}, u32[]{:S(2)}, u32[]{:S(2)}) collective-permute-start(f32[64,128]{1,0:T(8,128)S(1)} %fusion.16), channel_id=1, source_target_pairs={{0,9},{1,8},{2,11},{3,10},{4,13},{5,12},{6,15},{7,14},{8,1},{9,0},... | collective-permute-start | bytes 98312 | tf_op jit(solution)/shard_map/ppermute | solution.py:18
  22.2 3.1 %collective-permute-start.7 = (bf16[32,4096]{1,0:T(8,128)(2,1)S(1)}, bf16[32,4096]{1,0:T(8,128)(2,1)S(1)}, u32[]{:S(2)}, u32[]{:S(2)}) collective-permute-start(bf16[32,4096]{1,0:T(8,128)(2,1)S(1)} %constant_dynamic-update-slice_fusion.refs_0_), channel_id=1, source_target_pairs={{0,1},{1,0},{2,3},{3,2},{4,5},{5,4},{6,7},{7,6},{8,9},{9,8},{10,11... | collective-permute-start | bytes 786440 | tf_op jit(solution)/shard_map/ppermute | solution.py:18
  23.0 4.8 %collective-permute-start.4 = (bf16[128,128]{1,0:T(8,128)(2,1)S(1)}, bf16[128,128]{1,0:T(8,128)(2,1)S(1)}, u32[]{:S(2)}, u32[]{:S(2)}) collective-permute-start(bf16[128,128]{1,0:T(8,128)(2,1)S(1)} %get-tuple-element.26), channel_id=1, source_target_pairs={{0,9},{1,8},{2,11},{3,10},{4,13},{5,12},{6,15},{7,14},{8,1},{9,0},... | collective-permute-start | bytes 98312 | tf_op jit(solution)/shard_map/ppermute | solution.py:18
  26.0 6.7 %copy-start.6 = (s32[16]{0:T(128)S(1)}, s32[16]{0:T(128)}, u32[]{:S(2)}) copy-start(s32[16]{0:T(128)} %param.12) | copy-start | bytes 196
  26.0 6.7 %copy-start.7 = (s32[16]{0:T(128)S(1)}, s32[16]{0:T(128)}, u32[]{:S(2)}) copy-start(s32[16]{0:T(128)} %param.13) | copy-start | bytes 196
  28.3 1.2 %collective-permute-start.8 = (f32[4,8,16]{2,1,0:T(8,128)S(1)}, f32[4,8,16]{2,1,0:T(8,128)S(1)}, u32[]{:S(2)}, u32[]{:S(2)}) collective-permute-start(f32[4,8,16]{2,1,0:T(8,128)S(1)} %slice.37), channel_id=1, source_target_pairs={{0,1},{1,0},{2,3},{3,2},{4,5},{5,4},{6,7},{7,6},{8,9},{9,8},{10,11... | collective-permute-start | bytes 6152 | tf_op jit(solution)/shard_map/ppermute | solution.py:18
  29.6 3.1 %collective-permute-start.9 = (f32[2,8,16]{2,1,0:T(8,128)S(1)}, f32[2,8,16]{2,1,0:T(8,128)S(1)}, u32[]{:S(2)}, u32[]{:S(2)}) collective-permute-start(f32[2,8,16]{2,1,0:T(8,128)S(1)} %slice.46), channel_id=1, source_target_pairs={{0,3},{1,2},{2,1},{3,0},{4,7},{5,6},{6,5},{7,4},{8,11},{9,10},{10,... | collective-permute-start | bytes 3080 | tf_op jit(solution)/shard_map/ppermute | solution.py:18
  29.8 4.2 %collective-permute-start.11 = (f32[64,128]{1,0:T(8,128)S(1)}, f32[64,128]{1,0:T(8,128)S(1)}, u32[]{:S(2)}, u32[]{:S(2)}) collective-permute-start(f32[64,128]{1,0:T(8,128)S(1)} %get-tuple-element.23), channel_id=1, source_target_pairs={{0,9},{1,8},{2,11},{3,10},{4,13},{5,12},{6,15},{7,14},{8,1},{9,0},... | collective-permute-start | bytes 98312 | tf_op jit(solution)/shard_map/ppermute | solution.py:18
  32.7 3.0 %collective-permute-start.10 = (f32[1,8,16]{2,1,0:T(8,128)S(1)}, f32[1,8,16]{2,1,0:T(8,128)S(1)}, u32[]{:S(2)}, u32[]{:S(2)}) collective-permute-start(f32[1,8,16]{2,1,0:T(8,128)S(1)} %slice.47), channel_id=1, source_target_pairs={{0,5},{1,4},{2,7},{3,6},{4,1},{5,0},{6,3},{7,2},{8,13},{9,12},{10,... | collective-permute-start | bytes 1544 | tf_op jit(solution)/shard_map/ppermute | solution.py:18

commit v19 on v18

--- a/solution.py
+++ b/solution.py
@@ -314,7 +314,7 @@
         late, activations, (((0,), (1,)), ((), ())), preferred_element_type=jnp.float32
     )
     early, _ = lax.optimization_barrier((act, after))
-    more_act = swap(early, split, size)
+    more_act, _ = lax.optimization_barrier((swap(early, split, size), own))
     act = jnp.stack([act, more_act])
 
     panel = jnp.concatenate([panel, got], axis=0)
@@ -327,8 +327,8 @@
 
     steps = max(1, 4 * width * size * own_q * rows // (4 * MIB))
     products = inner(act, panels, steps)
-    members = masks(me[0], split, rows, doc_length, valid_count)
-    members, _ = lax.optimization_barrier((members, own))
+    lengths, counts, late_me, _ = lax.optimization_barrier((doc_length, valid_count, me, after))
+    members = masks(late_me[0], split, rows, lengths, counts)
     mine, theirs, doc = score(members, own, across, products, own_q, steps)
     others = swap(theirs, split, size)
     bits = [1] + middle

time: 36.6 us -> 31.5 us (0.86)
  local copies, waits for them, and re-layouts: 4.09 us -> 0.18 us
  starting transfers between devices: 13.6 us -> 16.5 us
  other arithmetic: 3.4 us -> 0.94 us
  waiting for transfers between devices: 6.64 us -> 4.96 us
    unnamed x18 -> x14, local copies, waits for them, and re-layouts: 3.97 us -> 0.05 us
    ppermute x12, starting transfers between devices: 13.6 us -> 16.5 us  [swap(): return lax.ppermute(value, 'seq', [(i, i ^ offset) for i in range(size)])]
    ppermute x12, waiting for transfers between devices: 6.64 us -> 4.96 us  [swap(): return lax.ppermute(value, 'seq', [(i, i ^ offset) for i in range(size)])]
    add x1, other arithmetic: 0.98 us -> 0.03 us  [body(): sums = grad_blocks(me, proj, out_grads, rows, spots, table) + from_core]
    concatenate x1, other arithmetic: 0.85 us -> 0.01 us  [body(): panel = jnp.concatenate([panel, got], axis=0)]
    add x1, other arithmetic: 0.68 us -> 0.01 us  [masks(): upper = lower + jnp.minimum(valid_count, doc_length)]
  transfers between devices with their start and end apart: 12 -> 12, of which waited for: 6 -> 5; matrix products, arithmetic and copies ran while one was open for 13% -> 4% of each run, Pallas kernels for 18% -> 21%
where the time goes in v19:
time: 31.5 us; the launch traced here: 31.3 us
  starting transfers between devices  16.5 us (52%)
  Pallas kernels  7.04 us (22%)
  waiting for transfers between devices  4.96 us (16%)
  other arithmetic  0.94 us (3%)
  matrix products  0.88 us (3%)
  between operations  0.81 us (3%)
    ppermute x12, starting transfers between devices, swap(): return lax.ppermute(value, 'seq', [(i, i ^ offset) for i in range(size)])  16.5 us
    ppermute x12, waiting for transfers between devices, swap(): return lax.ppermute(value, 'seq', [(i, i ^ offset) for i in range(size)])  4.96 us
    pallas_call x1, Pallas kernels, grad_blocks(): pl.pallas_call(functools.partial(grad_kernel, offsets), in_specs=[SMEM, H...  3.96 us
    pallas_call x1, Pallas kernels, grad_blocks(): pl.pallas_call(functools.partial(held_kernel, offsets), in_specs=[SMEM, V...  1.11 us
    dot_general x1, matrix products, body(): lax.dot_general(late, activations, (((0,), (1,)), ((), ())), preferred_el...  0.88 us
    pallas_call x1, Pallas kernels, place_tokens(): pl.pallas_call(functools.partial(place_kernel, place, split), in_specs=[S...  0.74 us
    pallas_call x1, Pallas kernels, inner(): pl.pallas_call(functools.partial(inner_kernel, len(panels)), out_shape=ja...  0.71 us
  transfers between devices with their start and end apart: 12, of which 5 were waited for; matrix products, arithmetic and copies ran while one was open for 4% of the time, Pallas kernels for 21%

profile of v19, /device:TPU:0, one launch (start us, length us, event | category | flops | bytes accessed | tf_op | source)
XLA Modules:
  0.0 31.3 jit_solution(6569929397283305589)
XLA Ops:
  0.6 0.0 copy-start
  0.6 2.5 %collective-permute-start = (bf16[8,4096]{1,0:T(8,128)(2,1)}, bf16[8,4096]{1,0:T(8,128)(2,1)S(1)}, u32[]{:S(2)}, u32[]{:S(2)}) collective-permute-start(bf16[8,4096]{1,0:T(8,128)(2,1)} %param.11), channel_id=1, source_target_pairs={{0,5},{1,4},{2,7},{3,6},{4,1},{5,0},{6,3},{7,2},{8,13},{9,12},{10,... | collective-permute-start | bytes 196616 | tf_op jit(solution)/shard_map/ppermute | solution.py:18
  3.2 0.0 copy-start.3
  3.2 0.0 copy-start.1
  3.2 4.0 %shard_map.86 = (f32[4,128,128]{2,1,0:T(8,128)S(1)}, bf16[2,1792,128]{2,1,0:T(8,128)(2,1)S(1)}) custom-call(s32[1]{0:T(128)} %bitcast.me_ref, bf16[64,1792]{1,0:T(8,128)(2,1)} %bitcast.19, bf16[2048,1792]{1,0:T(8,128)(2,1)} %grads_ref.3), custom_call_target="tpu_custom_call" | custom-call | flops 234881024 | bytes 3670016 | tf_op jit(solution)/shard_map/pallas_call | solution.py:93
  7.1 0.7 %collective-permute-start.1 = (f32[4,128,128]{2,1,0:T(8,128)S(1)}, f32[4,128,128]{2,1,0:T(8,128)S(1)}, u32[]{:S(2)}, u32[]{:S(2)}) collective-permute-start(f32[4,128,128]{2,1,0:T(8,128)S(1)} %get-tuple-element.18), channel_id=1, source_target_pairs={{0,1},{1,0},{2,3},{3,2},{4,5},{5,4},{6,7},{7,6},{8,9},{9,8},{10,11... | collective-permute-start | bytes 786440 | tf_op jit(solution)/shard_map/ppermute | solution.py:18
  7.9 0.0 copy-done.3
  7.9 0.0 copy-done.1
  7.9 0.0 copy-start.2
  7.9 1.1 %shard_map.87 = f32[4,128,128]{2,1,0:T(8,128)S(1)} custom-call(s32[1]{0:T(128)} %bitcast.me_ref, bf16[2,1792,128]{2,1,0:T(8,128)(2,1)S(1)} %get-tuple-element.17.table, bf16[2048,1792]{1,0:T(8,128)(2,1)S(1)} %copy-done.1), custom_call_target="tpu_custom_call" | custom-call | flops 234881024 | bytes 3670016 | tf_op jit(solution)/shard_map/pallas_call | solution.py:86
  9.0 0.0 collective-permute-done.1
  9.1 0.0 copy-start.4
  9.1 0.0 copy-start.5
  9.1 0.0 collective-permute-done
  9.1 1.6 %collective-permute-start.2 = (bf16[2,128,128]{2,1,0:T(8,128)(2,1)S(1)}, bf16[2,128,128]{2,1,0:T(8,128)(2,1)S(1)}, u32[]{:S(2)}, u32[]{:S(2)}) collective-permute-start(bf16[2,128,128]{2,1,0:T(8,128)(2,1)S(1)} %slice.64), channel_id=1, source_target_pairs={{0,3},{1,2},{2,1},{3,0},{4,7},{5,6},{6,5},{7,4},{8,11},{9,10},{10,... | collective-permute-start | bytes 196616 | tf_op jit(solution)/shard_map/ppermute | solution.py:18
  10.7 0.3 %collective-permute-start.6 = (bf16[16,4096]{1,0:T(8,128)(2,1)S(1)}, bf16[16,4096]{1,0:T(8,128)(2,1)S(1)}, u32[]{:S(2)}, u32[]{:S(2)}) collective-permute-start(bf16[16,4096]{1,0:T(8,128)(2,1)S(1)} %pad_maximum_fusion), channel_id=1, source_target_pairs={{0,3},{1,2},{2,1},{3,0},{4,7},{5,6},{6,5},{7,4},{8,11},{9,10},{10,... | collective-permute-start | bytes 393224 | tf_op jit(solution)/shard_map/ppermute | solution.py:18
  11.0 0.0 copy-done
  11.1 0.0 copy-done.2
  11.1 0.9 %fusion.16 = f32[64,128]{1,0:T(8,128)S(1)} fusion(bf16[8192,64]{0,1:T(8,128)(2,1)S(1)} %copy-done.2, bf16[128,8192]{1,0:T(8,128)(2,1)S(1)} %copy-done), kind=kOutput, calls=%fused_computation.36 | convolution fusion | flops 134217728 | bytes 3178496 | tf_op jit(solution)/shard_map/dot_general | solution.py:313
  11.9 1.2 %collective-permute-done.2 = bf16[2,128,128]{2,1,0:T(8,128)(2,1)S(1)} collective-permute-done((bf16[2,128,128]{2,1,0:T(8,128)(2,1)S(1)}, bf16[2,128,128]{2,1,0:T(8,128)(2,1)S(1)}, u32[]{:S(2)}, u32[]{:S(2)}) %collective-permute-start.2) | collective-permute-done | bytes 65568 | tf_op jit(solution)/shard_map/ppermute | solution.py:18
  13.2 0.0 copy-done.4
  13.2 0.1 copy.10
  13.3 0.1 reduce
  13.4 0.3 collective-permute-start.3
  13.7 2.6 %collective-permute-start.5 = (f32[64,128]{1,0:T(8,128)S(1)}, f32[64,128]{1,0:T(8,128)S(1)}, u32[]{:S(2)}, u32[]{:S(2)}) collective-permute-start(f32[64,128]{1,0:T(8,128)S(1)} %fusion.16), channel_id=1, source_target_pairs={{0,9},{1,8},{2,11},{3,10},{4,13},{5,12},{6,15},{7,14},{8,1},{9,0},... | collective-permute-start | bytes 98312 | tf_op jit(solution)/shard_map/ppermute | solution.py:18
  16.2 0.0 copy-done.5
  16.3 0.1 and_convert_fusion.member_ref
  16.3 0.0 collective-permute-done.6
  16.4 0.4 %collective-permute-start.7 = (bf16[32,4096]{1,0:T(8,128)(2,1)S(1)}, bf16[32,4096]{1,0:T(8,128)(2,1)S(1)}, u32[]{:S(2)}, u32[]{:S(2)}) collective-permute-start(bf16[32,4096]{1,0:T(8,128)(2,1)S(1)} %constant_dynamic-update-slice_fusion.refs_0_), channel_id=1, source_target_pairs={{0,1},{1,0},{2,3},{3,2},{4,5},{5,4},{6,7},{7,6},{8,9},{9,8},{10,11... | collective-permute-start | bytes 786440 | tf_op jit(solution)/shard_map/ppermute | solution.py:18
  16.8 0.0 collective-permute-done.3
  16.8 2.8 %collective-permute-start.4 = (bf16[128,128]{1,0:T(8,128)(2,1)S(1)}, bf16[128,128]{1,0:T(8,128)(2,1)S(1)}, u32[]{:S(2)}, u32[]{:S(2)}) collective-permute-start(bf16[128,128]{1,0:T(8,128)(2,1)S(1)} %get-tuple-element.32), channel_id=1, source_target_pairs={{0,9},{1,8},{2,11},{3,10},{4,13},{5,12},{6,15},{7,14},{8,1},{9,0},... | collective-permute-start | bytes 98312 | tf_op jit(solution)/shard_map/ppermute | solution.py:18
  19.6 0.0 collective-permute-done.5
  19.6 0.0 collective-permute-done.7.refs_1_
  19.6 0.7 %shard_map.88.inner_ref = f32[2048,512]{1,0:T(8,128)S(1)} custom-call(f32[2,64,128]{2,1,0:T(8,128)S(1)} %pad_maximum_fusion.1.act_ref, bf16[32,4096]{1,0:T(8,128)(2,1)S(1)} %constant_dynamic-update-slice_fusion.refs_0_, bf16[32,4096]{1,0:T(8,128)(2,1)S(1)} %collective-permute-done.7.refs_1_), custom_call_target="tpu_custom_call" | custom-call | flops 536870912 | bytes 4194304 | tf_op jit(solution)/shard_map/pallas_call | solution.py:147
  20.4 0.9 %collective-permute-done.4.other_ref = bf16[128,128]{1,0:T(8,128)(2,1)S(1)} collective-permute-done((bf16[128,128]{1,0:T(8,128)(2,1)S(1)}, bf16[128,128]{1,0:T(8,128)(2,1)S(1)}, u32[]{:S(2)}, u32[]{:S(2)}) %collective-permute-start.4) | collective-permute-done | bytes 32800 | tf_op jit(solution)/shard_map/ppermute | solution.py:18
  21.2 0.5 %shard_map.89 = (f32[64,128]{1,0:T(8,128)S(1)}, f32[64,128]{1,0:T(8,128)S(1)}, f32[8,8,16]{2,1,0:T(8,128)S(1)}) custom-call(bf16[16,768]{1,0:T(8,128)(2,1)S(1)} %and_convert_fusion.member_ref, f32[128,128]{1,0:T(8,128)S(1)} %get-tuple-element.33.own_ref, bf16[128,128]{1,0:T(8,128)(2,1)S(1)} %collective-permute-done.4.other_ref, ...), custom_call_target="tpu_custom_call" | custom-call | flops 2097152 | bytes 4194304 | tf_op jit(solution)/shard_map/pallas_call | solution.py:233
  21.8 0.3 collective-permute-start.8
  22.1 1.0 %collective-permute-done.8 = f32[4,8,16]{2,1,0:T(8,128)S(1)} collective-permute-done((f32[4,8,16]{2,1,0:T(8,128)S(1)}, f32[4,8,16]{2,1,0:T(8,128)S(1)}, u32[]{:S(2)}, u32[]{:S(2)}) %collective-permute-start.8) | collective-permute-done | bytes 2080 | tf_op jit(solution)/shard_map/ppermute | solution.py:18
  23.0 2.1 %collective-permute-start.9 = (f32[2,8,16]{2,1,0:T(8,128)S(1)}, f32[2,8,16]{2,1,0:T(8,128)S(1)}, u32[]{:S(2)}, u32[]{:S(2)}) collective-permute-start(f32[2,8,16]{2,1,0:T(8,128)S(1)} %slice.46), channel_id=1, source_target_pairs={{0,3},{1,2},{2,1},{3,0},{4,7},{5,6},{6,5},{7,4},{8,11},{9,10},{10,... | collective-permute-start | bytes 3080 | tf_op jit(solution)/shard_map/ppermute | solution.py:18
  25.2 2.4 %collective-permute-start.11 = (f32[64,128]{1,0:T(8,128)S(1)}, f32[64,128]{1,0:T(8,128)S(1)}, u32[]{:S(2)}, u32[]{:S(2)}) collective-permute-start(f32[64,128]{1,0:T(8,128)S(1)} %get-tuple-element.29), channel_id=1, source_target_pairs={{0,9},{1,8},{2,11},{3,10},{4,13},{5,12},{6,15},{7,14},{8,1},{9,0},... | collective-permute-start | bytes 98312 | tf_op jit(solution)/shard_map/ppermute | solution.py:18
  27.6 0.0 collective-permute-done.9
  27.6 0.5 %collective-permute-start.10 = (f32[1,8,16]{2,1,0:T(8,128)S(1)}, f32[1,8,16]{2,1,0:T(8,128)S(1)}, u32[]{:S(2)}, u32[]{:S(2)}) collective-permute-start(f32[1,8,16]{2,1,0:T(8,128)S(1)} %slice.47), channel_id=1, source_target_pairs={{0,5},{1,4},{2,7},{3,6},{4,1},{5,0},{6,3},{7,2},{8,13},{9,12},{10,... | collective-permute-start | bytes 1544 | tf_op jit(solution)/shard_map/ppermute | solution.py:18
  28.1 1.3 %collective-permute-done.11.other_ref = f32[64,128]{1,0:T(8,128)S(1)} collective-permute-done((f32[64,128]{1,0:T(8,128)S(1)}, f32[64,128]{1,0:T(8,128)S(1)}, u32[]{:S(2)}, u32[]{:S(2)}) %collective-permute-start.11) | collective-permute-done | bytes 32800 | tf_op jit(solution)/shard_map/ppermute | solution.py:18
  29.4 0.7 %shard_map.90 = f32[128,128]{1,0:T(8,128)} custom-call(s32[1]{0:T(128)} %bitcast.me_ref, f32[64,128]{1,0:T(8,128)S(1)} %get-tuple-element.28.own_ref, f32[64,128]{1,0:T(8,128)S(1)} %collective-permute-done.11.other_ref), custom_call_target="tpu_custom_call" | custom-call | tf_op jit(solution)/shard_map/pallas_call | solution.py:262
  30.2 0.6 %collective-permute-done.10 = f32[1,8,16]{2,1,0:T(8,128)S(1)} collective-permute-done((f32[1,8,16]{2,1,0:T(8,128)S(1)}, f32[1,8,16]{2,1,0:T(8,128)S(1)}, u32[]{:S(2)}, u32[]{:S(2)}) %collective-permute-start.10) | collective-permute-done | bytes 544 | tf_op jit(solution)/shard_map/ppermute | solution.py:18
  30.7 0.6 %fusion.9 = f32[16,8]{0,1:T(8,128)} fusion(f32[1,8,16]{2,1,0:T(8,128)S(1)} %collective-permute-done.10, f32[2,8,16]{2,1,0:T(8,128)S(1)} %slice_add_fusion.2, f32[16]{0:T(128)S(1)} %convert_rsqrt_fusion), kind=kLoop, calls=%fused_computation.27 | loop fusion | flops 256 | bytes 1600 | tf_op jit(solution)/shard_map/transpose | solution.py:342
  (19 shorter events, 0.2 us)
Async XLA Ops:
  0.6 10.4 %copy-start = (bf16[128,8192]{1,0:T(8,128)(2,1)S(1)}, bf16[128,8192]{1,0:T(8,128)(2,1)}, u32[]{:S(2)}) copy-start(bf16[128,8192]{1,0:T(8,128)(2,1)} %param.7) | copy-start | bytes 6291460
  0.6 8.5 %collective-permute-start = (bf16[8,4096]{1,0:T(8,128)(2,1)}, bf16[8,4096]{1,0:T(8,128)(2,1)S(1)}, u32[]{:S(2)}, u32[]{:S(2)}) collective-permute-start(bf16[8,4096]{1,0:T(8,128)(2,1)} %param.11), channel_id=1, source_target_pairs={{0,5},{1,4},{2,7},{3,6},{4,1},{5,0},{6,3},{7,2},{8,13},{9,12},{10,... | collective-permute-start | bytes 196616 | tf_op jit(solution)/shard_map/ppermute | solution.py:18
  3.2 4.7 %copy-start.3 = (bf16[8,4096]{1,0:T(8,128)(2,1)S(1)}, bf16[8,4096]{1,0:T(8,128)(2,1)}, u32[]{:S(2)}) copy-start(bf16[8,4096]{1,0:T(8,128)(2,1)} %param.11) | copy-start | bytes 196612
  3.2 4.7 %copy-start.1 = (bf16[2048,1792]{1,0:T(8,128)(2,1)S(1)}, bf16[2048,1792]{1,0:T(8,128)(2,1)}, u32[]{:S(2)}) copy-start(bf16[2048,1792]{1,0:T(8,128)(2,1)} %grads_ref.3) | copy-start | bytes 22020100
  7.1 1.9 %collective-permute-start.1 = (f32[4,128,128]{2,1,0:T(8,128)S(1)}, f32[4,128,128]{2,1,0:T(8,128)S(1)}, u32[]{:S(2)}, u32[]{:S(2)}) collective-permute-start(f32[4,128,128]{2,1,0:T(8,128)S(1)} %get-tuple-element.18), channel_id=1, source_target_pairs={{0,1},{1,0},{2,3},{3,2},{4,5},{5,4},{6,7},{7,6},{8,9},{9,8},{10,11... | collective-permute-start | bytes 786440 | tf_op jit(solution)/shard_map/ppermute | solution.py:18
  7.9 3.2 %copy-start.2 = (bf16[8192,64]{0,1:T(8,128)(2,1)S(1)}, bf16[8192,64]{0,1:T(8,128)(2,1)}, u32[]{:S(2)}) copy-start(bf16[8192,64]{0,1:T(8,128)(2,1)} %param.9) | copy-start | bytes 3145732
  9.1 4.1 %copy-start.4 = (s32[16]{0:T(128)S(1)}, s32[16]{0:T(128)}, u32[]{:S(2)}) copy-start(s32[16]{0:T(128)} %param.12) | copy-start | bytes 196
  9.1 7.2 %copy-start.5 = (s32[16]{0:T(128)S(1)}, s32[16]{0:T(128)}, u32[]{:S(2)}) copy-start(s32[16]{0:T(128)} %param.13) | copy-start | bytes 196
  9.1 4.0 %collective-permute-start.2 = (bf16[2,128,128]{2,1,0:T(8,128)(2,1)S(1)}, bf16[2,128,128]{2,1,0:T(8,128)(2,1)S(1)}, u32[]{:S(2)}, u32[]{:S(2)}) collective-permute-start(bf16[2,128,128]{2,1,0:T(8,128)(2,1)S(1)} %slice.64), channel_id=1, source_target_pairs={{0,3},{1,2},{2,1},{3,0},{4,7},{5,6},{6,5},{7,4},{8,11},{9,10},{10,... | collective-permute-start | bytes 196616 | tf_op jit(solution)/shard_map/ppermute | solution.py:18
  10.7 5.6 %collective-permute-start.6 = (bf16[16,4096]{1,0:T(8,128)(2,1)S(1)}, bf16[16,4096]{1,0:T(8,128)(2,1)S(1)}, u32[]{:S(2)}, u32[]{:S(2)}) collective-permute-start(bf16[16,4096]{1,0:T(8,128)(2,1)S(1)} %pad_maximum_fusion), channel_id=1, source_target_pairs={{0,3},{1,2},{2,1},{3,0},{4,7},{5,6},{6,5},{7,4},{8,11},{9,10},{10,... | collective-permute-start | bytes 393224 | tf_op jit(solution)/shard_map/ppermute | solution.py:18
  13.4 3.4 %collective-permute-start.3 = (bf16[1,128,128]{2,1,0:T(8,128)(2,1)S(1)}, bf16[1,128,128]{2,1,0:T(8,128)(2,1)S(1)}, u32[]{:S(2)}, u32[]{:S(2)}) collective-permute-start(bf16[1,128,128]{2,1,0:T(8,128)(2,1)S(1)} %slice.65), channel_id=1, source_target_pairs={{0,5},{1,4},{2,7},{3,6},{4,1},{5,0},{6,3},{7,2},{8,13},{9,12},{10,... | collective-permute-start | bytes 98312 | tf_op jit(solution)/shard_map/ppermute | solution.py:18
  13.7 5.9 %collective-permute-start.5 = (f32[64,128]{1,0:T(8,128)S(1)}, f32[64,128]{1,0:T(8,128)S(1)}, u32[]{:S(2)}, u32[]{:S(2)}) collective-permute-start(f32[64,128]{1,0:T(8,128)S(1)} %fusion.16), channel_id=1, source_target_pairs={{0,9},{1,8},{2,11},{3,10},{4,13},{5,12},{6,15},{7,14},{8,1},{9,0},... | collective-permute-start | bytes 98312 | tf_op jit(solution)/shard_map/ppermute | solution.py:18
  16.4 3.3 %collective-permute-start.7 = (bf16[32,4096]{1,0:T(8,128)(2,1)S(1)}, bf16[32,4096]{1,0:T(8,128)(2,1)S(1)}, u32[]{:S(2)}, u32[]{:S(2)}) collective-permute-start(bf16[32,4096]{1,0:T(8,128)(2,1)S(1)} %constant_dynamic-update-slice_fusion.refs_0_), channel_id=1, source_target_pairs={{0,1},{1,0},{2,3},{3,2},{4,5},{5,4},{6,7},{7,6},{8,9},{9,8},{10,11... | collective-permute-start | bytes 786440 | tf_op jit(solution)/shard_map/ppermute | solution.py:18
  16.8 4.4 %collective-permute-start.4 = (bf16[128,128]{1,0:T(8,128)(2,1)S(1)}, bf16[128,128]{1,0:T(8,128)(2,1)S(1)}, u32[]{:S(2)}, u32[]{:S(2)}) collective-permute-start(bf16[128,128]{1,0:T(8,128)(2,1)S(1)} %get-tuple-element.32), channel_id=1, source_target_pairs={{0,9},{1,8},{2,11},{3,10},{4,13},{5,12},{6,15},{7,14},{8,1},{9,0},... | collective-permute-start | bytes 98312 | tf_op jit(solution)/shard_map/ppermute | solution.py:18
  21.8 1.2 %collective-permute-start.8 = (f32[4,8,16]{2,1,0:T(8,128)S(1)}, f32[4,8,16]{2,1,0:T(8,128)S(1)}, u32[]{:S(2)}, u32[]{:S(2)}) collective-permute-start(f32[4,8,16]{2,1,0:T(8,128)S(1)} %slice.37), channel_id=1, source_target_pairs={{0,1},{1,0},{2,3},{3,2},{4,5},{5,4},{6,7},{7,6},{8,9},{9,8},{10,11... | collective-permute-start | bytes 6152 | tf_op jit(solution)/shard_map/ppermute | solution.py:18
  23.0 4.6 %collective-permute-start.9 = (f32[2,8,16]{2,1,0:T(8,128)S(1)}, f32[2,8,16]{2,1,0:T(8,128)S(1)}, u32[]{:S(2)}, u32[]{:S(2)}) collective-permute-start(f32[2,8,16]{2,1,0:T(8,128)S(1)} %slice.46), channel_id=1, source_target_pairs={{0,3},{1,2},{2,1},{3,0},{4,7},{5,6},{6,5},{7,4},{8,11},{9,10},{10,... | collective-permute-start | bytes 3080 | tf_op jit(solution)/shard_map/ppermute | solution.py:18
  25.2 4.2 %collective-permute-start.11 = (f32[64,128]{1,0:T(8,128)S(1)}, f32[64,128]{1,0:T(8,128)S(1)}, u32[]{:S(2)}, u32[]{:S(2)}) collective-permute-start(f32[64,128]{1,0:T(8,128)S(1)} %get-tuple-element.29), channel_id=1, source_target_pairs={{0,9},{1,8},{2,11},{3,10},{4,13},{5,12},{6,15},{7,14},{8,1},{9,0},... | collective-permute-start | bytes 98312 | tf_op jit(solution)/shard_map/ppermute | solution.py:18
  27.6 3.1 %collective-permute-start.10 = (f32[1,8,16]{2,1,0:T(8,128)S(1)}, f32[1,8,16]{2,1,0:T(8,128)S(1)}, u32[]{:S(2)}, u32[]{:S(2)}) collective-permute-start(f32[1,8,16]{2,1,0:T(8,128)S(1)} %slice.47), channel_id=1, source_target_pairs={{0,5},{1,4},{2,7},{3,6},{4,1},{5,0},{6,3},{7,2},{8,13},{9,12},{10,... | collective-permute-start | bytes 1544 | tf_op jit(solution)/shard_map/ppermute | solution.py:18

commit v20 on v19

--- a/solution.py
+++ b/solution.py
@@ -109,8 +109,9 @@
     )
 
 
-def inner_kernel(pieces, act_ref, *refs):
-    out_ref = refs[pieces]
+def inner_kernel(pieces, own_ref, act_ref, *refs):
+    out_ref, turned_ref = refs[pieces:]
+    turned_ref[...] = own_ref[...].T
     columns = []
     for r in range(act_ref.shape[0]):
         act = act_ref[r]
@@ -130,23 +131,29 @@
     out_ref[...] = jnp.dot(left, table, preferred_element_type=jnp.float32)
 
 
-def inner(act, panels, steps):
+def inner(own, act, panels, steps):
     halves, width, rows = act.shape
     count = sum(p.shape[0] for p in panels)
     pairs = panels[0].shape[1] // (2 * width)
     total = pairs * count
     if steps == 1:
-        grid = {"in_specs": [VMEM] * (1 + len(panels)), "out_specs": VMEM}
+        grid = {"in_specs": [VMEM] * (2 + len(panels)), "out_specs": (VMEM, VMEM)}
     else:
         grid = {
             "grid": (steps,),
-            "in_specs": [VMEM]
+            "in_specs": [VMEM] * 2
             + [pl.BlockSpec((p.shape[0], p.shape[1] // steps), lambda s: (0, s)) for p in panels],
-            "out_specs": pl.BlockSpec((total // steps, 2 * halves * rows), lambda s: (s, 0)),
+            "out_specs": (
+                pl.BlockSpec((total // steps, 2 * halves * rows), lambda s: (s, 0)),
+                VMEM,
+            ),
         }
     return pl.pallas_call(
         functools.partial(inner_kernel, len(panels)),
-        out_shape=jax.ShapeDtypeStruct((total, 2 * halves * rows), jnp.float32),
+        out_shape=(
+            jax.ShapeDtypeStruct((total, 2 * halves * rows), jnp.float32),
+            jax.ShapeDtypeStruct((halves * width, rows), jnp.float32),
+        ),
         compiler_params=pltpu.CompilerParams(vmem_limit_bytes=32 * MIB),
         cost_estimate=pl.CostEstimate(
             flops=16 * total * width * halves * rows,
@@ -154,13 +161,13 @@
             transcendentals=0,
         ),
         **grid,
-    )(act, *panels)
+    )(own, act, *panels)
 
 
 def score_kernel(
     steps, member_ref, own_ref, other_ref, inner_ref, own_tok, other_tok, doc_ref, grad_ref
 ):
-    rows, wide = own_ref.shape
+    wide, rows = own_ref.shape
     halves, width = 2, wide // 2
     count = own_tok.shape[0]
     pairs = inner_ref.shape[0] // count
@@ -169,7 +176,7 @@
 
     def begin():
         other = other_ref[...].astype(jnp.float32).T
-        grad_ref[...] = own_ref[...].T + jnp.concatenate([other[width:], other[:width]], axis=0)
+        grad_ref[...] = own_ref[...] + jnp.concatenate([other[width:], other[:width]], axis=0)
 
     if steps == 1:
         begin()
@@ -218,7 +225,7 @@
 
 
 def score(members, own, other, products, own_q, steps):
-    rows, wide = own.shape
+    wide, rows = own.shape
     docs = members.shape[0]
     count = 4 * products.shape[0] // wide
     if steps == 1:
@@ -314,7 +321,7 @@
         late, activations, (((0,), (1,)), ((), ())), preferred_element_type=jnp.float32
     )
     early, _ = lax.optimization_barrier((act, after))
-    more_act, _ = lax.optimization_barrier((swap(early, split, size), own))
+    more_act = swap(early, split, size)
     act = jnp.stack([act, more_act])
 
     panel = jnp.concatenate([panel, got], axis=0)
@@ -326,10 +333,10 @@
     place = tuple(place + [p ^ 1 for p in place])
 
     steps = max(1, 4 * width * size * own_q * rows // (4 * MIB))
-    products = inner(act, panels, steps)
+    products, turned = inner(own, act, panels, steps)
     lengths, counts, late_me, _ = lax.optimization_barrier((doc_length, valid_count, me, after))
     members = masks(late_me[0], split, rows, lengths, counts)
-    mine, theirs, doc = score(members, own, across, products, own_q, steps)
+    mine, theirs, doc = score(members, turned, across, products, own_q, steps)
     others = swap(theirs, split, size)
     bits = [1] + middle
     for bit in bits[:-1]:

time: 31.5 us -> 31.4 us (level)
  no operation moved by 1% of the time
where the time goes in v20:
time: 31.4 us; the launch traced here: 31.3 us
  starting transfers between devices  16.5 us (53%)
  Pallas kernels  7 us (22%)
  waiting for transfers between devices  4.96 us (16%)
  other arithmetic  0.93 us (3%)
  matrix products  0.88 us (3%)
  between operations  0.81 us (3%)
    ppermute x12, starting transfers between devices, swap(): return lax.ppermute(value, 'seq', [(i, i ^ offset) for i in range(size)])  16.5 us
    ppermute x12, waiting for transfers between devices, swap(): return lax.ppermute(value, 'seq', [(i, i ^ offset) for i in range(size)])  4.96 us
    pallas_call x1, Pallas kernels, grad_blocks(): pl.pallas_call(functools.partial(grad_kernel, offsets), in_specs=[SMEM, H...  3.96 us
    pallas_call x1, Pallas kernels, grad_blocks(): pl.pallas_call(functools.partial(held_kernel, offsets), in_specs=[SMEM, V...  1.11 us
    dot_general x1, matrix products, body(): lax.dot_general(late, activations, (((0,), (1,)), ((), ())), preferred_el...  0.88 us
    pallas_call x1, Pallas kernels, place_tokens(): pl.pallas_call(functools.partial(place_kernel, place, split), in_specs=[S...  0.74 us
    pallas_call x1, Pallas kernels, inner(): pl.pallas_call(functools.partial(inner_kernel, len(panels)), out_shape=(j...  0.71 us
  transfers between devices with their start and end apart: 12, of which 5 were waited for; matrix products, arithmetic and copies ran while one was open for 4% of the time, Pallas kernels for 21%

profile of v20, /device:TPU:0, one launch (start us, length us, event | category | flops | bytes accessed | tf_op | source)
XLA Modules:
  0.0 31.3 jit_solution(15596620841917279234)
XLA Ops:
  0.6 0.0 copy-start
  0.6 2.5 %collective-permute-start = (bf16[8,4096]{1,0:T(8,128)(2,1)}, bf16[8,4096]{1,0:T(8,128)(2,1)S(1)}, u32[]{:S(2)}, u32[]{:S(2)}) collective-permute-start(bf16[8,4096]{1,0:T(8,128)(2,1)} %param.11), channel_id=1, source_target_pairs={{0,5},{1,4},{2,7},{3,6},{4,1},{5,0},{6,3},{7,2},{8,13},{9,12},{10,... | collective-permute-start | bytes 196616 | tf_op jit(solution)/shard_map/ppermute | solution.py:18
  3.2 0.0 copy-start.3
  3.2 0.0 copy-start.1
  3.2 4.0 %shard_map.86 = (f32[4,128,128]{2,1,0:T(8,128)S(1)}, bf16[2,1792,128]{2,1,0:T(8,128)(2,1)S(1)}) custom-call(s32[1]{0:T(128)} %bitcast.me_ref, bf16[64,1792]{1,0:T(8,128)(2,1)} %bitcast.19, bf16[2048,1792]{1,0:T(8,128)(2,1)} %grads_ref.3), custom_call_target="tpu_custom_call" | custom-call | flops 234881024 | bytes 3670016 | tf_op jit(solution)/shard_map/pallas_call | solution.py:93
  7.1 0.7 %collective-permute-start.1 = (f32[4,128,128]{2,1,0:T(8,128)S(1)}, f32[4,128,128]{2,1,0:T(8,128)S(1)}, u32[]{:S(2)}, u32[]{:S(2)}) collective-permute-start(f32[4,128,128]{2,1,0:T(8,128)S(1)} %get-tuple-element.19), channel_id=1, source_target_pairs={{0,1},{1,0},{2,3},{3,2},{4,5},{5,4},{6,7},{7,6},{8,9},{9,8},{10,11... | collective-permute-start | bytes 786440 | tf_op jit(solution)/shard_map/ppermute | solution.py:18
  7.9 0.0 copy-done.3
  7.9 0.0 copy-done.1
  7.9 0.0 copy-start.2
  7.9 1.1 %shard_map.87 = f32[4,128,128]{2,1,0:T(8,128)S(1)} custom-call(s32[1]{0:T(128)} %bitcast.me_ref, bf16[2,1792,128]{2,1,0:T(8,128)(2,1)S(1)} %get-tuple-element.18.table, bf16[2048,1792]{1,0:T(8,128)(2,1)S(1)} %copy-done.1), custom_call_target="tpu_custom_call" | custom-call | flops 234881024 | bytes 3670016 | tf_op jit(solution)/shard_map/pallas_call | solution.py:86
  9.0 0.0 collective-permute-done.1
  9.1 0.0 copy-start.4
  9.1 0.0 copy-start.5
  9.1 0.0 collective-permute-done
  9.1 1.6 %collective-permute-start.2 = (bf16[2,128,128]{2,1,0:T(8,128)(2,1)S(1)}, bf16[2,128,128]{2,1,0:T(8,128)(2,1)S(1)}, u32[]{:S(2)}, u32[]{:S(2)}) collective-permute-start(bf16[2,128,128]{2,1,0:T(8,128)(2,1)S(1)} %slice.64), channel_id=1, source_target_pairs={{0,3},{1,2},{2,1},{3,0},{4,7},{5,6},{6,5},{7,4},{8,11},{9,10},{10,... | collective-permute-start | bytes 196616 | tf_op jit(solution)/shard_map/ppermute | solution.py:18
  10.7 0.3 %collective-permute-start.5 = (bf16[16,4096]{1,0:T(8,128)(2,1)S(1)}, bf16[16,4096]{1,0:T(8,128)(2,1)S(1)}, u32[]{:S(2)}, u32[]{:S(2)}) collective-permute-start(bf16[16,4096]{1,0:T(8,128)(2,1)S(1)} %pad_maximum_fusion), channel_id=1, source_target_pairs={{0,3},{1,2},{2,1},{3,0},{4,7},{5,6},{6,5},{7,4},{8,11},{9,10},{10,... | collective-permute-start | bytes 393224 | tf_op jit(solution)/shard_map/ppermute | solution.py:18
  11.0 0.0 copy-done
  11.1 0.0 copy-done.2
  11.1 0.9 %fusion.16 = f32[64,128]{1,0:T(8,128)S(1)} fusion(bf16[8192,64]{0,1:T(8,128)(2,1)S(1)} %copy-done.2, bf16[128,8192]{1,0:T(8,128)(2,1)S(1)} %copy-done), kind=kOutput, calls=%fused_computation.36 | convolution fusion | flops 134217728 | bytes 3178496 | tf_op jit(solution)/shard_map/dot_general | solution.py:320
  11.9 1.2 %collective-permute-done.2 = bf16[2,128,128]{2,1,0:T(8,128)(2,1)S(1)} collective-permute-done((bf16[2,128,128]{2,1,0:T(8,128)(2,1)S(1)}, bf16[2,128,128]{2,1,0:T(8,128)(2,1)S(1)}, u32[]{:S(2)}, u32[]{:S(2)}) %collective-permute-start.2) | collective-permute-done | bytes 65568 | tf_op jit(solution)/shard_map/ppermute | solution.py:18
  13.2 0.0 copy-done.4
  13.2 0.1 copy.10
  13.3 0.1 reduce
  13.4 0.3 collective-permute-start.3
  13.7 2.6 %collective-permute-start.4 = (f32[64,128]{1,0:T(8,128)S(1)}, f32[64,128]{1,0:T(8,128)S(1)}, u32[]{:S(2)}, u32[]{:S(2)}) collective-permute-start(f32[64,128]{1,0:T(8,128)S(1)} %fusion.16), channel_id=1, source_target_pairs={{0,9},{1,8},{2,11},{3,10},{4,13},{5,12},{6,15},{7,14},{8,1},{9,0},... | collective-permute-start | bytes 98312 | tf_op jit(solution)/shard_map/ppermute | solution.py:18
  16.2 0.0 copy-done.5
  16.3 0.1 and_convert_fusion.member_ref
  16.3 0.0 collective-permute-done.5
  16.4 0.4 %collective-permute-start.6 = (bf16[32,4096]{1,0:T(8,128)(2,1)S(1)}, bf16[32,4096]{1,0:T(8,128)(2,1)S(1)}, u32[]{:S(2)}, u32[]{:S(2)}) collective-permute-start(bf16[32,4096]{1,0:T(8,128)(2,1)S(1)} %constant_dynamic-update-slice_fusion.refs_0_), channel_id=1, source_target_pairs={{0,1},{1,0},{2,3},{3,2},{4,5},{5,4},{6,7},{7,6},{8,9},{9,8},{10,11... | collective-permute-start | bytes 786440 | tf_op jit(solution)/shard_map/ppermute | solution.py:18
  16.8 0.0 collective-permute-done.3
  16.8 2.8 %collective-permute-start.7 = (bf16[128,128]{1,0:T(8,128)(2,1)S(1)}, bf16[128,128]{1,0:T(8,128)(2,1)S(1)}, u32[]{:S(2)}, u32[]{:S(2)}) collective-permute-start(bf16[128,128]{1,0:T(8,128)(2,1)S(1)} %get-tuple-element.34), channel_id=1, source_target_pairs={{0,9},{1,8},{2,11},{3,10},{4,13},{5,12},{6,15},{7,14},{8,1},{9,0},... | collective-permute-start | bytes 98312 | tf_op jit(solution)/shard_map/ppermute | solution.py:18
  19.6 0.0 collective-permute-done.4
  19.6 0.0 collective-permute-done.6.refs_1_
  19.6 0.7 %shard_map.88 = (f32[2048,512]{1,0:T(8,128)S(1)}, f32[128,128]{1,0:T(8,128)S(1)}) custom-call(f32[128,128]{1,0:T(8,128)S(1)} %get-tuple-element.35.own_ref, f32[2,64,128]{2,1,0:T(8,128)S(1)} %pad_maximum_fusion.1.act_ref, bf16[32,4096]{1,0:T(8,128)(2,1)S(1)} %constant_dynamic-update-slice_fusion.refs_0_, bf16[32,4096]{1,0:T(8,128)(2,1)S(1)} %collective-permute-done.6.refs_1_), custom_call_target="tpu_custom_call" | custom-call | flops 536870912 | bytes 4194304 | tf_op jit(solution)/shard_map/pallas_call | solution.py:151
  20.4 0.9 %collective-permute-done.7.other_ref = bf16[128,128]{1,0:T(8,128)(2,1)S(1)} collective-permute-done((bf16[128,128]{1,0:T(8,128)(2,1)S(1)}, bf16[128,128]{1,0:T(8,128)(2,1)S(1)}, u32[]{:S(2)}, u32[]{:S(2)}) %collective-permute-start.7) | collective-permute-done | bytes 32800 | tf_op jit(solution)/shard_map/ppermute | solution.py:18
  21.2 0.5 %shard_map.89 = (f32[64,128]{1,0:T(8,128)S(1)}, f32[64,128]{1,0:T(8,128)S(1)}, f32[8,8,16]{2,1,0:T(8,128)S(1)}) custom-call(bf16[16,768]{1,0:T(8,128)(2,1)S(1)} %and_convert_fusion.member_ref, f32[128,128]{1,0:T(8,128)S(1)} %get-tuple-element.27.own_ref, bf16[128,128]{1,0:T(8,128)(2,1)S(1)} %collective-permute-done.7.other_ref, ...), custom_call_target="tpu_custom_call" | custom-call | flops 2097152 | bytes 4194304 | tf_op jit(solution)/shard_map/pallas_call | solution.py:240
  21.7 0.3 collective-permute-start.8
  22.0 1.0 %collective-permute-done.8 = f32[4,8,16]{2,1,0:T(8,128)S(1)} collective-permute-done((f32[4,8,16]{2,1,0:T(8,128)S(1)}, f32[4,8,16]{2,1,0:T(8,128)S(1)}, u32[]{:S(2)}, u32[]{:S(2)}) %collective-permute-start.8) | collective-permute-done | bytes 2080 | tf_op jit(solution)/shard_map/ppermute | solution.py:18
  23.0 2.1 %collective-permute-start.9 = (f32[2,8,16]{2,1,0:T(8,128)S(1)}, f32[2,8,16]{2,1,0:T(8,128)S(1)}, u32[]{:S(2)}, u32[]{:S(2)}) collective-permute-start(f32[2,8,16]{2,1,0:T(8,128)S(1)} %slice.46), channel_id=1, source_target_pairs={{0,3},{1,2},{2,1},{3,0},{4,7},{5,6},{6,5},{7,4},{8,11},{9,10},{10,... | collective-permute-start | bytes 3080 | tf_op jit(solution)/shard_map/ppermute | solution.py:18
  25.1 2.4 %collective-permute-start.11 = (f32[64,128]{1,0:T(8,128)S(1)}, f32[64,128]{1,0:T(8,128)S(1)}, u32[]{:S(2)}, u32[]{:S(2)}) collective-permute-start(f32[64,128]{1,0:T(8,128)S(1)} %get-tuple-element.31), channel_id=1, source_target_pairs={{0,9},{1,8},{2,11},{3,10},{4,13},{5,12},{6,15},{7,14},{8,1},{9,0},... | collective-permute-start | bytes 98312 | tf_op jit(solution)/shard_map/ppermute | solution.py:18
  27.6 0.0 collective-permute-done.9
  27.6 0.5 %collective-permute-start.10 = (f32[1,8,16]{2,1,0:T(8,128)S(1)}, f32[1,8,16]{2,1,0:T(8,128)S(1)}, u32[]{:S(2)}, u32[]{:S(2)}) collective-permute-start(f32[1,8,16]{2,1,0:T(8,128)S(1)} %slice.47), channel_id=1, source_target_pairs={{0,5},{1,4},{2,7},{3,6},{4,1},{5,0},{6,3},{7,2},{8,13},{9,12},{10,... | collective-permute-start | bytes 1544 | tf_op jit(solution)/shard_map/ppermute | solution.py:18
  28.1 1.3 %collective-permute-done.11.other_ref = f32[64,128]{1,0:T(8,128)S(1)} collective-permute-done((f32[64,128]{1,0:T(8,128)S(1)}, f32[64,128]{1,0:T(8,128)S(1)}, u32[]{:S(2)}, u32[]{:S(2)}) %collective-permute-start.11) | collective-permute-done | bytes 32800 | tf_op jit(solution)/shard_map/ppermute | solution.py:18
  29.4 0.7 %shard_map.90 = f32[128,128]{1,0:T(8,128)} custom-call(s32[1]{0:T(128)} %bitcast.me_ref, f32[64,128]{1,0:T(8,128)S(1)} %get-tuple-element.30.own_ref, f32[64,128]{1,0:T(8,128)S(1)} %collective-permute-done.11.other_ref), custom_call_target="tpu_custom_call" | custom-call | tf_op jit(solution)/shard_map/pallas_call | solution.py:269
  30.1 0.6 %collective-permute-done.10 = f32[1,8,16]{2,1,0:T(8,128)S(1)} collective-permute-done((f32[1,8,16]{2,1,0:T(8,128)S(1)}, f32[1,8,16]{2,1,0:T(8,128)S(1)}, u32[]{:S(2)}, u32[]{:S(2)}) %collective-permute-start.10) | collective-permute-done | bytes 544 | tf_op jit(solution)/shard_map/ppermute | solution.py:18
  30.7 0.6 %fusion.9 = f32[16,8]{0,1:T(8,128)} fusion(f32[1,8,16]{2,1,0:T(8,128)S(1)} %collective-permute-done.10, f32[2,8,16]{2,1,0:T(8,128)S(1)} %slice_add_fusion.2, f32[16]{0:T(128)S(1)} %convert_rsqrt_fusion), kind=kLoop, calls=%fused_computation.27 | loop fusion | flops 256 | bytes 1600 | tf_op jit(solution)/shard_map/transpose | solution.py:349
  (19 shorter events, 0.2 us)
Async XLA Ops:
  0.6 10.4 %copy-start = (bf16[128,8192]{1,0:T(8,128)(2,1)S(1)}, bf16[128,8192]{1,0:T(8,128)(2,1)}, u32[]{:S(2)}) copy-start(bf16[128,8192]{1,0:T(8,128)(2,1)} %param.7) | copy-start | bytes 6291460
  0.6 8.5 %collective-permute-start = (bf16[8,4096]{1,0:T(8,128)(2,1)}, bf16[8,4096]{1,0:T(8,128)(2,1)S(1)}, u32[]{:S(2)}, u32[]{:S(2)}) collective-permute-start(bf16[8,4096]{1,0:T(8,128)(2,1)} %param.11), channel_id=1, source_target_pairs={{0,5},{1,4},{2,7},{3,6},{4,1},{5,0},{6,3},{7,2},{8,13},{9,12},{10,... | collective-permute-start | bytes 196616 | tf_op jit(solution)/shard_map/ppermute | solution.py:18
  3.2 4.7 %copy-start.3 = (bf16[8,4096]{1,0:T(8,128)(2,1)S(1)}, bf16[8,4096]{1,0:T(8,128)(2,1)}, u32[]{:S(2)}) copy-start(bf16[8,4096]{1,0:T(8,128)(2,1)} %param.11) | copy-start | bytes 196612
  3.2 4.7 %copy-start.1 = (bf16[2048,1792]{1,0:T(8,128)(2,1)S(1)}, bf16[2048,1792]{1,0:T(8,128)(2,1)}, u32[]{:S(2)}) copy-start(bf16[2048,1792]{1,0:T(8,128)(2,1)} %grads_ref.3) | copy-start | bytes 22020100
  7.1 1.9 %collective-permute-start.1 = (f32[4,128,128]{2,1,0:T(8,128)S(1)}, f32[4,128,128]{2,1,0:T(8,128)S(1)}, u32[]{:S(2)}, u32[]{:S(2)}) collective-permute-start(f32[4,128,128]{2,1,0:T(8,128)S(1)} %get-tuple-element.19), channel_id=1, source_target_pairs={{0,1},{1,0},{2,3},{3,2},{4,5},{5,4},{6,7},{7,6},{8,9},{9,8},{10,11... | collective-permute-start | bytes 786440 | tf_op jit(solution)/shard_map/ppermute | solution.py:18
  7.9 3.2 %copy-start.2 = (bf16[8192,64]{0,1:T(8,128)(2,1)S(1)}, bf16[8192,64]{0,1:T(8,128)(2,1)}, u32[]{:S(2)}) copy-start(bf16[8192,64]{0,1:T(8,128)(2,1)} %param.9) | copy-start | bytes 3145732
  9.1 4.1 %copy-start.4 = (s32[16]{0:T(128)S(1)}, s32[16]{0:T(128)}, u32[]{:S(2)}) copy-start(s32[16]{0:T(128)} %param.12) | copy-start | bytes 196
  9.1 7.2 %copy-start.5 = (s32[16]{0:T(128)S(1)}, s32[16]{0:T(128)}, u32[]{:S(2)}) copy-start(s32[16]{0:T(128)} %param.13) | copy-start | bytes 196
  9.1 4.0 %collective-permute-start.2 = (bf16[2,128,128]{2,1,0:T(8,128)(2,1)S(1)}, bf16[2,128,128]{2,1,0:T(8,128)(2,1)S(1)}, u32[]{:S(2)}, u32[]{:S(2)}) collective-permute-start(bf16[2,128,128]{2,1,0:T(8,128)(2,1)S(1)} %slice.64), channel_id=1, source_target_pairs={{0,3},{1,2},{2,1},{3,0},{4,7},{5,6},{6,5},{7,4},{8,11},{9,10},{10,... | collective-permute-start | bytes 196616 | tf_op jit(solution)/shard_map/ppermute | solution.py:18
  10.7 5.6 %collective-permute-start.5 = (bf16[16,4096]{1,0:T(8,128)(2,1)S(1)}, bf16[16,4096]{1,0:T(8,128)(2,1)S(1)}, u32[]{:S(2)}, u32[]{:S(2)}) collective-permute-start(bf16[16,4096]{1,0:T(8,128)(2,1)S(1)} %pad_maximum_fusion), channel_id=1, source_target_pairs={{0,3},{1,2},{2,1},{3,0},{4,7},{5,6},{6,5},{7,4},{8,11},{9,10},{10,... | collective-permute-start | bytes 393224 | tf_op jit(solution)/shard_map/ppermute | solution.py:18
  13.4 3.4 %collective-permute-start.3 = (bf16[1,128,128]{2,1,0:T(8,128)(2,1)S(1)}, bf16[1,128,128]{2,1,0:T(8,128)(2,1)S(1)}, u32[]{:S(2)}, u32[]{:S(2)}) collective-permute-start(bf16[1,128,128]{2,1,0:T(8,128)(2,1)S(1)} %slice.65), channel_id=1, source_target_pairs={{0,5},{1,4},{2,7},{3,6},{4,1},{5,0},{6,3},{7,2},{8,13},{9,12},{10,... | collective-permute-start | bytes 98312 | tf_op jit(solution)/shard_map/ppermute | solution.py:18
  13.7 5.9 %collective-permute-start.4 = (f32[64,128]{1,0:T(8,128)S(1)}, f32[64,128]{1,0:T(8,128)S(1)}, u32[]{:S(2)}, u32[]{:S(2)}) collective-permute-start(f32[64,128]{1,0:T(8,128)S(1)} %fusion.16), channel_id=1, source_target_pairs={{0,9},{1,8},{2,11},{3,10},{4,13},{5,12},{6,15},{7,14},{8,1},{9,0},... | collective-permute-start | bytes 98312 | tf_op jit(solution)/shard_map/ppermute | solution.py:18
  16.4 3.3 %collective-permute-start.6 = (bf16[32,4096]{1,0:T(8,128)(2,1)S(1)}, bf16[32,4096]{1,0:T(8,128)(2,1)S(1)}, u32[]{:S(2)}, u32[]{:S(2)}) collective-permute-start(bf16[32,4096]{1,0:T(8,128)(2,1)S(1)} %constant_dynamic-update-slice_fusion.refs_0_), channel_id=1, source_target_pairs={{0,1},{1,0},{2,3},{3,2},{4,5},{5,4},{6,7},{7,6},{8,9},{9,8},{10,11... | collective-permute-start | bytes 786440 | tf_op jit(solution)/shard_map/ppermute | solution.py:18
  16.8 4.4 %collective-permute-start.7 = (bf16[128,128]{1,0:T(8,128)(2,1)S(1)}, bf16[128,128]{1,0:T(8,128)(2,1)S(1)}, u32[]{:S(2)}, u32[]{:S(2)}) collective-permute-start(bf16[128,128]{1,0:T(8,128)(2,1)S(1)} %get-tuple-element.34), channel_id=1, source_target_pairs={{0,9},{1,8},{2,11},{3,10},{4,13},{5,12},{6,15},{7,14},{8,1},{9,0},... | collective-permute-start | bytes 98312 | tf_op jit(solution)/shard_map/ppermute | solution.py:18
  21.7 1.2 %collective-permute-start.8 = (f32[4,8,16]{2,1,0:T(8,128)S(1)}, f32[4,8,16]{2,1,0:T(8,128)S(1)}, u32[]{:S(2)}, u32[]{:S(2)}) collective-permute-start(f32[4,8,16]{2,1,0:T(8,128)S(1)} %slice.37), channel_id=1, source_target_pairs={{0,1},{1,0},{2,3},{3,2},{4,5},{5,4},{6,7},{7,6},{8,9},{9,8},{10,11... | collective-permute-start | bytes 6152 | tf_op jit(solution)/shard_map/ppermute | solution.py:18
  23.0 4.6 %collective-permute-start.9 = (f32[2,8,16]{2,1,0:T(8,128)S(1)}, f32[2,8,16]{2,1,0:T(8,128)S(1)}, u32[]{:S(2)}, u32[]{:S(2)}) collective-permute-start(f32[2,8,16]{2,1,0:T(8,128)S(1)} %slice.46), channel_id=1, source_target_pairs={{0,3},{1,2},{2,1},{3,0},{4,7},{5,6},{6,5},{7,4},{8,11},{9,10},{10,... | collective-permute-start | bytes 3080 | tf_op jit(solution)/shard_map/ppermute | solution.py:18
  25.1 4.2 %collective-permute-start.11 = (f32[64,128]{1,0:T(8,128)S(1)}, f32[64,128]{1,0:T(8,128)S(1)}, u32[]{:S(2)}, u32[]{:S(2)}) collective-permute-start(f32[64,128]{1,0:T(8,128)S(1)} %get-tuple-element.31), channel_id=1, source_target_pairs={{0,9},{1,8},{2,11},{3,10},{4,13},{5,12},{6,15},{7,14},{8,1},{9,0},... | collective-permute-start | bytes 98312 | tf_op jit(solution)/shard_map/ppermute | solution.py:18
  27.6 3.1 %collective-permute-start.10 = (f32[1,8,16]{2,1,0:T(8,128)S(1)}, f32[1,8,16]{2,1,0:T(8,128)S(1)}, u32[]{:S(2)}, u32[]{:S(2)}) collective-permute-start(f32[1,8,16]{2,1,0:T(8,128)S(1)} %slice.47), channel_id=1, source_target_pairs={{0,5},{1,4},{2,7},{3,6},{4,1},{5,0},{6,3},{7,2},{8,13},{9,12},{10,... | collective-permute-start | bytes 1544 | tf_op jit(solution)/shard_map/ppermute | solution.py:18
